TPU v7x, 128 devices: a whole 4x4x4 slice. The times are simulated.
128 devices in a mesh: tx: 16 (over y, x), ty: 8 (over z, core).
Axes of the slice: x: 4, y: 4, z: 4, core: 2. Of those that a mesh axis runs over, the one named last changes fastest.
Arguments:
- earlier: bfloat16 [64, 32, 256, 128], P('tx', 'ty'), may hold values from -6 to 6
- innovation: bfloat16 [64, 32, 256, 128], P('tx', 'ty'), may hold values from -6 to 6
- conditioner: bfloat16 [64, 32, 1024, 128], P('tx', 'ty'), may hold values from -0.125 to 0.125
- chol_factor: bfloat16 [64, 32, 128, 128], P('tx', 'ty'), may hold values from -0.5 to 0.5
- block_level: int32 [64, 32], P('tx', 'ty'), may hold values from 0 to 3, as said below
- neighbours: int32 [64, 32, 8], P('tx', 'ty'), may hold values from 0 to 17, as said below
Outputs:
- window: bfloat16 [64, 32, 256, 128], P('tx', 'ty')
Inputs may be any that keep to these rules, and one draw needn't show every extreme that they name: `block_level`: in each device's tile of 4 x 4 cells no level holds more than 8 blocks, and one level holds exactly 8. `neighbours`: A code q < 9 names the earlier-level block at cell offset (q // 3 - 1, q mod 3 - 1), with periodic wrap; a code q >= 9 names the window block at offset ((q - 9) // 3 - 1, (q - 9) mod 3 - 1), whose level is always lower than the block's own. The 8 codes of a block are distinct.
All inputs are finite; a program needn't handle non-finite values.
Results may differ from a plain program's by a relative error of at most 0.0023.
Values may be sent and summed in bfloat16 or wider, within the bound.
No kernel may reach another device: no remote copies, remote signals or barrier semaphores. Data moves between devices by JAX's collectives and lax.ppermute only.
A program may use at most 64 MiB of HBM per device.

v0:
```python
import jax
import jax.numpy as jnp
from jax import lax
from jax.sharding import PartitionSpec as P

LEVELS = 4


def with_halo(shard, sides, width):
    for axis, dim in sides:
        size, length = (lax.axis_size(axis), shard.shape[dim])
        up = [(i, (i + 1) % size) for i in range(size)]
        down = [(j, i) for i, j in up]
        last = lax.slice_in_dim(shard, length - width, length, axis=dim)
        initial = lax.slice_in_dim(shard, 0, width, axis=dim)
        before = lax.ppermute(last, axis, up)
        after = lax.ppermute(initial, axis, down)
        shard = jnp.concatenate([before, shard, after], axis=dim)
    return shard


def advance(window, lookup, section, innovation, conditioner, chol_factor, block_level, neighbours):
    tile_x, tile_y, realize, block_size = window.shape
    tile_cells = tile_x * tile_y
    capacity = tile_cells // 2
    near_count = neighbours.shape[2]
    is_now = block_level.reshape(tile_cells) == section
    order_rank = jnp.cumsum(is_now.astype(jnp.int32)) - 1
    picked = is_now[None, :] & (
        order_rank[None, :] == jnp.arange(capacity, dtype=jnp.int32)[:, None]
    )
    filled = jnp.any(picked, axis=1)
    chosen = jnp.sum(jnp.where(picked, jnp.arange(tile_cells, dtype=jnp.int32)[None, :], 0), axis=1)
    near_codes = neighbours.reshape(tile_cells, near_count)[chosen]
    offset = near_codes % 9
    source_kind = near_codes // 9
    row_index = (chosen // tile_y)[:, None] + offset // 3
    col_index = (chosen % tile_y)[:, None] + offset % 3
    gathered = lookup[source_kind, row_index, col_index]
    matrices = conditioner.reshape(tile_cells, near_count, block_size, block_size)[chosen]
    shocks = innovation.reshape(tile_cells, realize, block_size)[chosen]
    factors = jnp.triu(chol_factor.reshape(tile_cells, block_size, block_size)[chosen])
    summed = jnp.einsum("ckrb,ckbo->cro", gathered, matrices, preferred_element_type=jnp.float32)
    summed = summed + jnp.einsum(
        "crb,cbo->cro", shocks, factors, preferred_element_type=jnp.float32
    )
    values = summed.astype(jnp.bfloat16)
    target = jnp.where(filled, chosen, tile_cells)
    flat_window = (
        window.reshape(tile_cells, realize, block_size).at[target].set(values, mode="drop")
    )
    return flat_window.reshape(window.shape)


def local(earlier, innovation, conditioner, chol_factor, block_level, neighbours):
    window = jnp.zeros(earlier.shape, jnp.bfloat16)
    for section in range(LEVELS):
        lookup = with_halo(jnp.stack([earlier, window]), (("tx", 1), ("ty", 2)), 1)
        window = advance(
            window, lookup, section, innovation, conditioner, chol_factor, block_level, neighbours
        )
    return window


def solution(mesh):
    placed = (
        P("tx", "ty", None, None),
        P("tx", "ty", None, None),
        P("tx", "ty", None, None),
        P("tx", "ty", None, None),
        P("tx", "ty"),
        P("tx", "ty", None),
    )
    return jax.shard_map(
        local, mesh=mesh, in_specs=placed, out_specs=P("tx", "ty", None, None), check_vma=False
    )
```

profile of v0, /device:TPU:0, one launch (start us, length us, event | category | flops | bytes accessed | tf_op | source)
XLA Modules:
  0.0 201.9 jit_solution(18251890068833825596)
XLA Ops:
  3.8 3.8 %collective-permute-start.1 = (bf16[2,1,4,256,128]{4,3,2,1,0:T(8,128)(2,1)}, bf16[2,1,4,256,128]{4,3,2,1,0:T(8,128)(2,1)}, u32[]{:S(2)}, u32[]{:S(2)}) collective-permute-start(bf16[2,1,4,256,128]{4,3,2,1,0:T(8,128)(2,1)} %get-tuple-element.28), channel_id=1, source_target_pairs={{8,0},{16,8},{24,16},{32,24},{40,32},{48,40},{56,48},{64,56},{72,6... | collective-permute-start | bytes 1572872 | tf_op jit(solution)/shard_map/ppermute | solution.py:17
  10.9 8.8 %collective-permute-done = bf16[2,1,4,256,128]{4,3,2,1,0:T(8,128)(2,1)} collective-permute-done((bf16[2,1,4,256,128]{4,3,2,1,0:T(8,128)(2,1)}, bf16[2,1,4,256,128]{4,3,2,1,0:T(8,128)(2,1)}, u32[]{:S(2)}, u32[]{:S(2)}) %collective-permute-start) | collective-permute-done | bytes 524320 | tf_op jit(solution)/shard_map/ppermute | solution.py:16
  19.7 2.4 %pad_maximum_fusion.9 = (bf16[2,6,1,256,128]{4,3,2,1,0:T(8,128)(2,1)}, bf16[2,6,1,256,128]{4,3,2,1,0:T(8,128)(2,1)}) fusion(bf16[2,1,4,256,128]{4,3,2,1,0:T(8,128)(2,1)} %collective-permute-done.1, bf16[2,4,4,256,128]{4,3,2,1,0:T(8,128)(2,1)S(1)} %stack.19, bf16[2,1,4,256,128]{4,3,2,1,0:T(8,128)(2,1)} %collective-permute-done), kind=kLoop, calls=%fused_computation.67 | loop fusion | flops 1572864 | bytes 4718592 | tf_op jit(solution)/shard_map/slice | solution.py:14
  22.2 3.0 %collective-permute-start.3 = (bf16[2,6,1,256,128]{4,3,2,1,0:T(8,128)(2,1)}, bf16[2,6,1,256,128]{4,3,2,1,0:T(8,128)(2,1)}, u32[]{:S(2)}, u32[]{:S(2)}) collective-permute-start(bf16[2,6,1,256,128]{4,3,2,1,0:T(8,128)(2,1)} %get-tuple-element.20), channel_id=1, source_target_pairs={{1,0},{2,1},{3,2},{4,3},{5,4},{6,5},{7,6},{0,7},{9,8},{10,9},{11,1... | collective-permute-start | bytes 2359304 | tf_op jit(solution)/shard_map/ppermute | solution.py:17
  28.3 4.4 %gather_fusion.2 = bf16[8,8,128,128]{3,2,1,0:T(8,128)(2,1)} fusion(bf16[16,8,128,128]{3,2,1,0:T(8,128)(2,1)} %bitcast.229, s32[1024]{0:T(1024)S(1)} %pad_clamp_fusion.3), kind=kCustom, calls=%fused_computation.2 | custom fusion | bytes 4194336 | tf_op jit(solution)/shard_map/gather | solution.py:40
  35.3 3.8 %pad_maximum_fusion.3 = bf16[2,6,6,256,128]{4,3,2,1,0:T(8,128)(2,1)} fusion(bf16[2,6,1,256,128]{4,3,2,1,0:T(8,128)(2,1)} %collective-permute-done.3, bf16[2,1,4,256,128]{4,3,2,1,0:T(8,128)(2,1)} %collective-permute-done.1, bf16[2,4,4,256,128]{4,3,2,1,0:T(8,128)(2,1)S(1)} %stack.19, bf16[2,1,4,256,128]{4,3,2,1,0:T(8,128)(2,1)} %collective-permute-done, ...), kind=kLoop, calls=%fused_computation.39 | loop fusion | flops 9437184 | bytes 9437184 | tf_op jit(solution)/shard_map/concatenate | solution.py:18
  39.1 5.5 %gather_fusion.1 = bf16[64,256,128]{2,1,0:T(8,128)(2,1)} fusion(bf16[2,6,6,256,128]{4,3,2,1,0:T(8,128)(2,1)} %pad_maximum_fusion.3, s32[64]{0:T(128)S(1)} %reshape.1152), kind=kCustom, calls=%fused_computation.1 | custom fusion | bytes 8389376 | tf_op jit(solution)/shard_map/gather | solution.py:39
  44.6 5.0 %fusion.25 = bf16[8,256,128]{2,1,0:T(8,128)(2,1)} fusion(f32[8,256,128]{2,1,0:T(8,128)S(1)} %copy-done.3, bf16[8,8,256,128]{3,2,1,0:T(8,128)(2,1)} %bitcast.225, bf16[8,8,128,128]{3,2,1,0:T(8,128)(2,1)} %gather_fusion.2), kind=kOutput, calls=%fused_computation.64 | convolution fusion | flops 537395200 | bytes 7864320 | tf_op jit(solution)/shard_map/ckrb,ckbo->cro/dot_general | solution.py:43
  51.8 5.3 %collective-permute-start.5 = (bf16[2,1,4,256,128]{4,3,2,1,0:T(8,128)(2,1)S(1)}, bf16[2,1,4,256,128]{4,3,2,1,0:T(8,128)(2,1)S(1)}, u32[]{:S(2)}, u32[]{:S(2)}) collective-permute-start(bf16[2,1,4,256,128]{4,3,2,1,0:T(8,128)(2,1)S(1)} %get-tuple-element.26), channel_id=1, source_target_pairs={{8,0},{16,8},{24,16},{32,24},{40,32},{48,40},{56,48},{64,56},{72,6... | collective-permute-start | bytes 1572872 | tf_op jit(solution)/shard_map/ppermute | solution.py:17
  57.5 12.0 %collective-permute-done.4 = bf16[2,1,4,256,128]{4,3,2,1,0:T(8,128)(2,1)S(1)} collective-permute-done((bf16[2,1,4,256,128]{4,3,2,1,0:T(8,128)(2,1)S(1)}, bf16[2,1,4,256,128]{4,3,2,1,0:T(8,128)(2,1)S(1)}, u32[]{:S(2)}, u32[]{:S(2)}) %collective-permute-start.4) | collective-permute-done | bytes 524320 | tf_op jit(solution)/shard_map/ppermute | solution.py:16
  71.3 3.0 %collective-permute-start.7 = (bf16[2,6,1,256,128]{4,3,2,1,0:T(8,128)(2,1)}, bf16[2,6,1,256,128]{4,3,2,1,0:T(8,128)(2,1)}, u32[]{:S(2)}, u32[]{:S(2)}) collective-permute-start(bf16[2,6,1,256,128]{4,3,2,1,0:T(8,128)(2,1)} %get-tuple-element.18), channel_id=1, source_target_pairs={{1,0},{2,1},{3,2},{4,3},{5,4},{6,5},{7,6},{0,7},{9,8},{10,9},{11,1... | collective-permute-start | bytes 2359304 | tf_op jit(solution)/shard_map/ppermute | solution.py:17
  77.9 4.4 %gather_fusion.7 = bf16[8,8,128,128]{3,2,1,0:T(8,128)(2,1)} fusion(bf16[16,8,128,128]{3,2,1,0:T(8,128)(2,1)} %bitcast.230, s32[1024]{0:T(1024)S(1)} %pad_clamp_fusion.2), kind=kCustom, calls=%fused_computation.7 | custom fusion | bytes 4194336 | tf_op jit(solution)/shard_map/gather | solution.py:40
  82.6 2.3 %fusion.33 = f32[8,256,128]{2,1,0:T(8,128)} fusion(bf16[8,256,128]{2,1,0:T(8,128)(2,1)} %gather_fusion.8, bf16[8,128,128]{2,1,0:T(8,128)(2,1)S(1)} %gather_fusion.9, pred[128,128]{1,0:T(8,128)(4,1)S(1)} %iota_compare_fusion), kind=kOutput, calls=%fused_computation.80 | convolution fusion | flops 67239936 | bytes 1851392 | tf_op jit(solution)/shard_map/crb,cbo->cro/dot_general | solution.py:44
  84.9 5.1 %fusion.3 = bf16[2,6,6,256,128]{4,3,2,1,0:T(8,128)(2,1)} fusion(bf16[1,4,4,256,128]{4,3,2,1,0:T(8,128)(2,1)S(1)} %bitcast.218, bf16[2,6,1,256,128]{4,3,2,1,0:T(8,128)(2,1)} %collective-permute-done.7, bf16[2,1,4,256,128]{4,3,2,1,0:T(8,128)(2,1)} %copy-done.8, bf16[1,4,4,256,128]{4,3,2,1,0:T(8,128)(2,1)S(1)} %bitcast.207, ...), kind=kLoop, calls=%fused_computation.30 | loop fusion | flops 11796480 | bytes 9437184 | tf_op jit(solution)/shard_map/concatenate | solution.py:18
  90.0 5.4 %gather_fusion.6 = bf16[64,256,128]{2,1,0:T(8,128)(2,1)} fusion(bf16[2,6,6,256,128]{4,3,2,1,0:T(8,128)(2,1)} %fusion.3, s32[64]{0:T(128)S(1)} %reshape.1190), kind=kCustom, calls=%fused_computation.6 | custom fusion | bytes 8389376 | tf_op jit(solution)/shard_map/gather | solution.py:39
  95.5 5.1 %fusion.24 = bf16[8,256,128]{2,1,0:T(8,128)(2,1)} fusion(f32[8,256,128]{2,1,0:T(8,128)} %fusion.33, bf16[8,8,256,128]{3,2,1,0:T(8,128)(2,1)} %bitcast.226, bf16[8,8,128,128]{3,2,1,0:T(8,128)(2,1)} %gather_fusion.7), kind=kOutput, calls=%fused_computation.63 | convolution fusion | flops 537395200 | bytes 7864320 | tf_op jit(solution)/shard_map/ckrb,ckbo->cro/dot_general | solution.py:43
  102.6 5.4 %collective-permute-start.9 = (bf16[2,1,4,256,128]{4,3,2,1,0:T(8,128)(2,1)S(1)}, bf16[2,1,4,256,128]{4,3,2,1,0:T(8,128)(2,1)S(1)}, u32[]{:S(2)}, u32[]{:S(2)}) collective-permute-start(bf16[2,1,4,256,128]{4,3,2,1,0:T(8,128)(2,1)S(1)} %get-tuple-element.24), channel_id=1, source_target_pairs={{8,0},{16,8},{24,16},{32,24},{40,32},{48,40},{56,48},{64,56},{72,6... | collective-permute-start | bytes 1572872 | tf_op jit(solution)/shard_map/ppermute | solution.py:17
  108.3 10.6 %collective-permute-done.8 = bf16[2,1,4,256,128]{4,3,2,1,0:T(8,128)(2,1)S(1)} collective-permute-done((bf16[2,1,4,256,128]{4,3,2,1,0:T(8,128)(2,1)S(1)}, bf16[2,1,4,256,128]{4,3,2,1,0:T(8,128)(2,1)S(1)}, u32[]{:S(2)}, u32[]{:S(2)}) %collective-permute-start.8) | collective-permute-done | bytes 524320 | tf_op jit(solution)/shard_map/ppermute | solution.py:16
  120.7 3.0 %collective-permute-start.11 = (bf16[2,6,1,256,128]{4,3,2,1,0:T(8,128)(2,1)}, bf16[2,6,1,256,128]{4,3,2,1,0:T(8,128)(2,1)}, u32[]{:S(2)}, u32[]{:S(2)}) collective-permute-start(bf16[2,6,1,256,128]{4,3,2,1,0:T(8,128)(2,1)} %get-tuple-element.16), channel_id=1, source_target_pairs={{1,0},{2,1},{3,2},{4,3},{5,4},{6,5},{7,6},{0,7},{9,8},{10,9},{11,1... | collective-permute-start | bytes 2359304 | tf_op jit(solution)/shard_map/ppermute | solution.py:17
  127.3 4.4 %gather_fusion.12 = bf16[8,8,128,128]{3,2,1,0:T(8,128)(2,1)} fusion(bf16[16,8,128,128]{3,2,1,0:T(8,128)(2,1)} %bitcast.231, s32[1024]{0:T(1024)S(1)} %pad_clamp_fusion.1), kind=kCustom, calls=%fused_computation.12 | custom fusion | bytes 4194336 | tf_op jit(solution)/shard_map/gather | solution.py:40
  132.0 2.3 %fusion.31 = f32[8,256,128]{2,1,0:T(8,128)} fusion(bf16[8,256,128]{2,1,0:T(8,128)(2,1)} %gather_fusion.13, bf16[8,128,128]{2,1,0:T(8,128)(2,1)S(1)} %gather_fusion.14, pred[128,128]{1,0:T(8,128)(4,1)S(1)} %iota_compare_fusion), kind=kOutput, calls=%fused_computation.78 | convolution fusion | flops 67239936 | bytes 1851392 | tf_op jit(solution)/shard_map/crb,cbo->cro/dot_general | solution.py:44
  134.3 5.1 %fusion.7 = bf16[2,6,6,256,128]{4,3,2,1,0:T(8,128)(2,1)} fusion(bf16[1,4,4,256,128]{4,3,2,1,0:T(8,128)(2,1)S(1)} %bitcast.221, bf16[2,6,1,256,128]{4,3,2,1,0:T(8,128)(2,1)} %collective-permute-done.11, bf16[2,1,4,256,128]{4,3,2,1,0:T(8,128)(2,1)} %copy-done.7, bf16[1,4,4,256,128]{4,3,2,1,0:T(8,128)(2,1)S(1)} %bitcast.210, ...), kind=kLoop, calls=%fused_computation.34 | loop fusion | flops 11796480 | bytes 9437184 | tf_op jit(solution)/shard_map/concatenate | solution.py:18
  139.4 5.4 %gather_fusion.11 = bf16[64,256,128]{2,1,0:T(8,128)(2,1)} fusion(bf16[2,6,6,256,128]{4,3,2,1,0:T(8,128)(2,1)} %fusion.7, s32[64]{0:T(128)S(1)} %reshape.1228), kind=kCustom, calls=%fused_computation.11 | custom fusion | bytes 8389376 | tf_op jit(solution)/shard_map/gather | solution.py:39
  144.9 5.1 %fusion.23 = bf16[8,256,128]{2,1,0:T(8,128)(2,1)} fusion(f32[8,256,128]{2,1,0:T(8,128)} %fusion.31, bf16[8,8,256,128]{3,2,1,0:T(8,128)(2,1)} %bitcast.227, bf16[8,8,128,128]{3,2,1,0:T(8,128)(2,1)} %gather_fusion.12), kind=kOutput, calls=%fused_computation.62 | convolution fusion | flops 537395200 | bytes 7864320 | tf_op jit(solution)/shard_map/ckrb,ckbo->cro/dot_general | solution.py:43
  151.9 5.4 %collective-permute-start.13 = (bf16[2,1,4,256,128]{4,3,2,1,0:T(8,128)(2,1)S(1)}, bf16[2,1,4,256,128]{4,3,2,1,0:T(8,128)(2,1)S(1)}, u32[]{:S(2)}, u32[]{:S(2)}) collective-permute-start(bf16[2,1,4,256,128]{4,3,2,1,0:T(8,128)(2,1)S(1)} %get-tuple-element.22), channel_id=1, source_target_pairs={{8,0},{16,8},{24,16},{32,24},{40,32},{48,40},{56,48},{64,56},{72,6... | collective-permute-start | bytes 1572872 | tf_op jit(solution)/shard_map/ppermute | solution.py:17
  157.7 10.7 %collective-permute-done.12 = bf16[2,1,4,256,128]{4,3,2,1,0:T(8,128)(2,1)S(1)} collective-permute-done((bf16[2,1,4,256,128]{4,3,2,1,0:T(8,128)(2,1)S(1)}, bf16[2,1,4,256,128]{4,3,2,1,0:T(8,128)(2,1)S(1)}, u32[]{:S(2)}, u32[]{:S(2)}) %collective-permute-start.12) | collective-permute-done | bytes 524320 | tf_op jit(solution)/shard_map/ppermute | solution.py:16
  170.2 3.0 %collective-permute-start.15 = (bf16[2,6,1,256,128]{4,3,2,1,0:T(8,128)(2,1)}, bf16[2,6,1,256,128]{4,3,2,1,0:T(8,128)(2,1)}, u32[]{:S(2)}, u32[]{:S(2)}) collective-permute-start(bf16[2,6,1,256,128]{4,3,2,1,0:T(8,128)(2,1)} %get-tuple-element.14), channel_id=1, source_target_pairs={{1,0},{2,1},{3,2},{4,3},{5,4},{6,5},{7,6},{0,7},{9,8},{10,9},{11,1... | collective-permute-start | bytes 2359304 | tf_op jit(solution)/shard_map/ppermute | solution.py:17
  176.8 4.4 %gather_fusion.17 = bf16[8,8,128,128]{3,2,1,0:T(8,128)(2,1)} fusion(bf16[16,8,128,128]{3,2,1,0:T(8,128)(2,1)} %bitcast.232, s32[1024]{0:T(1024)S(1)} %pad_clamp_fusion), kind=kCustom, calls=%fused_computation.17 | custom fusion | bytes 4194336 | tf_op jit(solution)/shard_map/gather | solution.py:40
  181.3 2.3 %fusion.29 = f32[8,256,128]{2,1,0:T(8,128)} fusion(bf16[8,256,128]{2,1,0:T(8,128)(2,1)} %gather_fusion.18, bf16[8,128,128]{2,1,0:T(8,128)(2,1)S(1)} %gather_fusion.19, pred[128,128]{1,0:T(8,128)(4,1)S(1)} %iota_compare_fusion), kind=kOutput, calls=%fused_computation.76 | convolution fusion | flops 67239936 | bytes 1851392 | tf_op jit(solution)/shard_map/crb,cbo->cro/dot_general | solution.py:44
  183.6 5.1 %fusion.11 = bf16[2,6,6,256,128]{4,3,2,1,0:T(8,128)(2,1)} fusion(bf16[1,4,4,256,128]{4,3,2,1,0:T(8,128)(2,1)S(1)} %bitcast.224, bf16[2,6,1,256,128]{4,3,2,1,0:T(8,128)(2,1)} %collective-permute-done.15, bf16[2,1,4,256,128]{4,3,2,1,0:T(8,128)(2,1)} %copy-done.10, bf16[1,4,4,256,128]{4,3,2,1,0:T(8,128)(2,1)S(1)} %bitcast.213, ...), kind=kLoop, calls=%fused_computation.38 | loop fusion | flops 11796480 | bytes 9437184 | tf_op jit(solution)/shard_map/concatenate | solution.py:18
  188.7 5.5 %gather_fusion.16 = bf16[64,256,128]{2,1,0:T(8,128)(2,1)} fusion(bf16[2,6,6,256,128]{4,3,2,1,0:T(8,128)(2,1)} %fusion.11, s32[64]{0:T(128)S(1)} %reshape.1266), kind=kCustom, calls=%fused_computation.16 | custom fusion | bytes 8389376 | tf_op jit(solution)/shard_map/gather | solution.py:39
  194.3 4.9 %fusion.22 = bf16[8,256,128]{2,1,0:T(8,128)(2,1)} fusion(f32[8,256,128]{2,1,0:T(8,128)S(1)} %copy-done.4, bf16[8,8,256,128]{3,2,1,0:T(8,128)(2,1)} %bitcast.228, bf16[8,8,128,128]{3,2,1,0:T(8,128)(2,1)} %gather_fusion.17), kind=kOutput, calls=%fused_computation.61 | convolution fusion | flops 537395200 | bytes 7864320 | tf_op jit(solution)/shard_map/ckrb,ckbo->cro/dot_general | solution.py:43
  (120 shorter events, 39.7 us)
Async XLA Ops:
  0.0 25.3 %copy-start = (bf16[4,4,256,128]{3,2,1,0:T(8,128)(2,1)S(1)}, bf16[4,4,256,128]{3,2,1,0:T(8,128)(2,1)}, u32[]{:S(2)}) copy-start(bf16[4,4,256,128]{3,2,1,0:T(8,128)(2,1)} %param.7) | copy-start | bytes 3145732
  0.0 10.4 %copy-start.11 = (s32[4,4,8]{2,1,0:T(4,128)S(1)}, s32[4,4,8]{2,1,0:T(4,128)}, u32[]{:S(2)}) copy-start(s32[4,4,8]{2,1,0:T(4,128)} %param.11) | copy-start | bytes 1540
  2.2 17.5 %collective-permute-start = (bf16[2,1,4,256,128]{4,3,2,1,0:T(8,128)(2,1)}, bf16[2,1,4,256,128]{4,3,2,1,0:T(8,128)(2,1)}, u32[]{:S(2)}, u32[]{:S(2)}) collective-permute-start(bf16[2,1,4,256,128]{4,3,2,1,0:T(8,128)(2,1)} %get-tuple-element.27), channel_id=1, source_target_pairs={{0,8},{8,16},{16,24},{24,32},{32,40},{40,48},{48,56},{56,64},{64,7... | collective-permute-start | bytes 1572872 | tf_op jit(solution)/shard_map/ppermute | solution.py:16
  3.8 16.0 %collective-permute-start.1 = (bf16[2,1,4,256,128]{4,3,2,1,0:T(8,128)(2,1)}, bf16[2,1,4,256,128]{4,3,2,1,0:T(8,128)(2,1)}, u32[]{:S(2)}, u32[]{:S(2)}) collective-permute-start(bf16[2,1,4,256,128]{4,3,2,1,0:T(8,128)(2,1)} %get-tuple-element.28), channel_id=1, source_target_pairs={{8,0},{16,8},{24,16},{32,24},{40,32},{48,40},{56,48},{64,56},{72,6... | collective-permute-start | bytes 1572872 | tf_op jit(solution)/shard_map/ppermute | solution.py:17
  22.2 13.1 %collective-permute-start.2 = (bf16[2,6,1,256,128]{4,3,2,1,0:T(8,128)(2,1)}, bf16[2,6,1,256,128]{4,3,2,1,0:T(8,128)(2,1)}, u32[]{:S(2)}, u32[]{:S(2)}) collective-permute-start(bf16[2,6,1,256,128]{4,3,2,1,0:T(8,128)(2,1)} %get-tuple-element.19), channel_id=1, source_target_pairs={{0,1},{1,2},{2,3},{3,4},{4,5},{5,6},{6,7},{7,0},{8,9},{9,10},{10,1... | collective-permute-start | bytes 2359304 | tf_op jit(solution)/shard_map/ppermute | solution.py:16
  22.2 13.1 %collective-permute-start.3 = (bf16[2,6,1,256,128]{4,3,2,1,0:T(8,128)(2,1)}, bf16[2,6,1,256,128]{4,3,2,1,0:T(8,128)(2,1)}, u32[]{:S(2)}, u32[]{:S(2)}) collective-permute-start(bf16[2,6,1,256,128]{4,3,2,1,0:T(8,128)(2,1)} %get-tuple-element.20), channel_id=1, source_target_pairs={{1,0},{2,1},{3,2},{4,3},{5,4},{6,5},{7,6},{0,7},{9,8},{10,9},{11,1... | collective-permute-start | bytes 2359304 | tf_op jit(solution)/shard_map/ppermute | solution.py:17
  39.1 5.5 %copy-start.3 = (f32[8,256,128]{2,1,0:T(8,128)S(1)}, f32[8,256,128]{2,1,0:T(8,128)}, u32[]{:S(2)}) copy-start(f32[8,256,128]{2,1,0:T(8,128)} %fusion.35) | copy-start | bytes 3145732
  44.6 7.0 %copy-start.2 = (bf16[4,4,256,128]{3,2,1,0:T(8,128)(2,1)S(1)}, bf16[4,4,256,128]{3,2,1,0:T(8,128)(2,1)}, u32[]{:S(2)}) copy-start(bf16[4,4,256,128]{3,2,1,0:T(8,128)(2,1)} %param.6) | copy-start | bytes 3145732
  51.7 17.8 %collective-permute-start.4 = (bf16[2,1,4,256,128]{4,3,2,1,0:T(8,128)(2,1)S(1)}, bf16[2,1,4,256,128]{4,3,2,1,0:T(8,128)(2,1)S(1)}, u32[]{:S(2)}, u32[]{:S(2)}) collective-permute-start(bf16[2,1,4,256,128]{4,3,2,1,0:T(8,128)(2,1)S(1)} %get-tuple-element.25), channel_id=1, source_target_pairs={{0,8},{8,16},{16,24},{24,32},{32,40},{40,48},{48,56},{56,64},{64,7... | collective-permute-start | bytes 1572872 | tf_op jit(solution)/shard_map/ppermute | solution.py:16
  51.8 17.7 %collective-permute-start.5 = (bf16[2,1,4,256,128]{4,3,2,1,0:T(8,128)(2,1)S(1)}, bf16[2,1,4,256,128]{4,3,2,1,0:T(8,128)(2,1)S(1)}, u32[]{:S(2)}, u32[]{:S(2)}) collective-permute-start(bf16[2,1,4,256,128]{4,3,2,1,0:T(8,128)(2,1)S(1)} %get-tuple-element.26), channel_id=1, source_target_pairs={{8,0},{16,8},{24,16},{32,24},{40,32},{48,40},{56,48},{64,56},{72,6... | collective-permute-start | bytes 1572872 | tf_op jit(solution)/shard_map/ppermute | solution.py:17
  69.5 1.8 copy-start.6
  69.5 1.8 copy-start.8
  71.3 13.6 %collective-permute-start.6 = (bf16[2,6,1,256,128]{4,3,2,1,0:T(8,128)(2,1)}, bf16[2,6,1,256,128]{4,3,2,1,0:T(8,128)(2,1)}, u32[]{:S(2)}, u32[]{:S(2)}) collective-permute-start(bf16[2,6,1,256,128]{4,3,2,1,0:T(8,128)(2,1)} %get-tuple-element.17), channel_id=1, source_target_pairs={{0,1},{1,2},{2,3},{3,4},{4,5},{5,6},{6,7},{7,0},{8,9},{9,10},{10,1... | collective-permute-start | bytes 2359304 | tf_op jit(solution)/shard_map/ppermute | solution.py:16
  71.3 13.6 %collective-permute-start.7 = (bf16[2,6,1,256,128]{4,3,2,1,0:T(8,128)(2,1)}, bf16[2,6,1,256,128]{4,3,2,1,0:T(8,128)(2,1)}, u32[]{:S(2)}, u32[]{:S(2)}) collective-permute-start(bf16[2,6,1,256,128]{4,3,2,1,0:T(8,128)(2,1)} %get-tuple-element.18), channel_id=1, source_target_pairs={{1,0},{2,1},{3,2},{4,3},{5,4},{6,5},{7,6},{0,7},{9,8},{10,9},{11,1... | collective-permute-start | bytes 2359304 | tf_op jit(solution)/shard_map/ppermute | solution.py:17
  102.5 16.5 %collective-permute-start.8 = (bf16[2,1,4,256,128]{4,3,2,1,0:T(8,128)(2,1)S(1)}, bf16[2,1,4,256,128]{4,3,2,1,0:T(8,128)(2,1)S(1)}, u32[]{:S(2)}, u32[]{:S(2)}) collective-permute-start(bf16[2,1,4,256,128]{4,3,2,1,0:T(8,128)(2,1)S(1)} %get-tuple-element.23), channel_id=1, source_target_pairs={{0,8},{8,16},{16,24},{24,32},{32,40},{40,48},{48,56},{56,64},{64,7... | collective-permute-start | bytes 1572872 | tf_op jit(solution)/shard_map/ppermute | solution.py:16
  102.6 16.4 %collective-permute-start.9 = (bf16[2,1,4,256,128]{4,3,2,1,0:T(8,128)(2,1)S(1)}, bf16[2,1,4,256,128]{4,3,2,1,0:T(8,128)(2,1)S(1)}, u32[]{:S(2)}, u32[]{:S(2)}) collective-permute-start(bf16[2,1,4,256,128]{4,3,2,1,0:T(8,128)(2,1)S(1)} %get-tuple-element.24), channel_id=1, source_target_pairs={{8,0},{16,8},{24,16},{32,24},{40,32},{48,40},{56,48},{64,56},{72,6... | collective-permute-start | bytes 1572872 | tf_op jit(solution)/shard_map/ppermute | solution.py:17
  118.9 1.8 copy-start.5
  118.9 1.8 copy-start.7
  120.7 13.6 %collective-permute-start.10 = (bf16[2,6,1,256,128]{4,3,2,1,0:T(8,128)(2,1)}, bf16[2,6,1,256,128]{4,3,2,1,0:T(8,128)(2,1)}, u32[]{:S(2)}, u32[]{:S(2)}) collective-permute-start(bf16[2,6,1,256,128]{4,3,2,1,0:T(8,128)(2,1)} %get-tuple-element.15), channel_id=1, source_target_pairs={{0,1},{1,2},{2,3},{3,4},{4,5},{5,6},{6,7},{7,0},{8,9},{9,10},{10,1... | collective-permute-start | bytes 2359304 | tf_op jit(solution)/shard_map/ppermute | solution.py:16
  120.7 13.6 %collective-permute-start.11 = (bf16[2,6,1,256,128]{4,3,2,1,0:T(8,128)(2,1)}, bf16[2,6,1,256,128]{4,3,2,1,0:T(8,128)(2,1)}, u32[]{:S(2)}, u32[]{:S(2)}) collective-permute-start(bf16[2,6,1,256,128]{4,3,2,1,0:T(8,128)(2,1)} %get-tuple-element.16), channel_id=1, source_target_pairs={{1,0},{2,1},{3,2},{4,3},{5,4},{6,5},{7,6},{0,7},{9,8},{10,9},{11,1... | collective-permute-start | bytes 2359304 | tf_op jit(solution)/shard_map/ppermute | solution.py:17
  151.9 16.6 %collective-permute-start.12 = (bf16[2,1,4,256,128]{4,3,2,1,0:T(8,128)(2,1)S(1)}, bf16[2,1,4,256,128]{4,3,2,1,0:T(8,128)(2,1)S(1)}, u32[]{:S(2)}, u32[]{:S(2)}) collective-permute-start(bf16[2,1,4,256,128]{4,3,2,1,0:T(8,128)(2,1)S(1)} %get-tuple-element.21), channel_id=1, source_target_pairs={{0,8},{8,16},{16,24},{24,32},{32,40},{40,48},{48,56},{56,64},{64,7... | collective-permute-start | bytes 1572872 | tf_op jit(solution)/shard_map/ppermute | solution.py:16
  151.9 16.5 %collective-permute-start.13 = (bf16[2,1,4,256,128]{4,3,2,1,0:T(8,128)(2,1)S(1)}, bf16[2,1,4,256,128]{4,3,2,1,0:T(8,128)(2,1)S(1)}, u32[]{:S(2)}, u32[]{:S(2)}) collective-permute-start(bf16[2,1,4,256,128]{4,3,2,1,0:T(8,128)(2,1)S(1)} %get-tuple-element.22), channel_id=1, source_target_pairs={{8,0},{16,8},{24,16},{32,24},{40,32},{48,40},{56,48},{64,56},{72,6... | collective-permute-start | bytes 1572872 | tf_op jit(solution)/shard_map/ppermute | solution.py:17
  168.4 1.8 copy-start.9
  168.4 1.8 copy-start.10
  170.2 13.4 %collective-permute-start.14 = (bf16[2,6,1,256,128]{4,3,2,1,0:T(8,128)(2,1)}, bf16[2,6,1,256,128]{4,3,2,1,0:T(8,128)(2,1)}, u32[]{:S(2)}, u32[]{:S(2)}) collective-permute-start(bf16[2,6,1,256,128]{4,3,2,1,0:T(8,128)(2,1)} %get-tuple-element.13), channel_id=1, source_target_pairs={{0,1},{1,2},{2,3},{3,4},{4,5},{5,6},{6,7},{7,0},{8,9},{9,10},{10,1... | collective-permute-start | bytes 2359304 | tf_op jit(solution)/shard_map/ppermute | solution.py:16
  170.2 13.4 %collective-permute-start.15 = (bf16[2,6,1,256,128]{4,3,2,1,0:T(8,128)(2,1)}, bf16[2,6,1,256,128]{4,3,2,1,0:T(8,128)(2,1)}, u32[]{:S(2)}, u32[]{:S(2)}) collective-permute-start(bf16[2,6,1,256,128]{4,3,2,1,0:T(8,128)(2,1)} %get-tuple-element.14), channel_id=1, source_target_pairs={{1,0},{2,1},{3,2},{4,3},{5,4},{6,5},{7,6},{0,7},{9,8},{10,9},{11,1... | collective-permute-start | bytes 2359304 | tf_op jit(solution)/shard_map/ppermute | solution.py:17
  188.7 5.5 %copy-start.4 = (f32[8,256,128]{2,1,0:T(8,128)S(1)}, f32[8,256,128]{2,1,0:T(8,128)}, u32[]{:S(2)}) copy-start(f32[8,256,128]{2,1,0:T(8,128)} %fusion.29) | copy-start | bytes 3145732
  201.0 1.0 copy-start.1
where the time goes:
time: 203 us; the launch traced here: 202 us
  local copies, waits for them, and re-layouts  70.6 us (35%)
  waiting for transfers between devices  42.2 us (21%)
  starting transfers between devices  33.5 us (17%)
  matrix products  29.3 us (14%)
  other arithmetic  26 us (13%)
    ppermute x8, waiting for transfers between devices, with_halo(): before = lax.ppermute(last, axis, up)  42.2 us
    ppermute x8, starting transfers between devices, with_halo(): after = lax.ppermute(initial, axis, down)  31.7 us
    gather x4, local copies, waits for them, and re-layouts, advance(): gathered = lookup[source_kind, row_index, col_index]  22 us
    concatenate x7, other arithmetic, with_halo(): shard = jnp.concatenate([before, shard, after], axis=dim)  20.6 us
    dot_general x4, matrix products, advance(): jnp.einsum('ckrb,ckbo->cro', gathered, matrices, preferred_element_type=j...  20.1 us
    gather x4, local copies, waits for them, and re-layouts, advance(): conditioner.reshape(tile_cells, near_count, block_size, block_size)[chosen]  17.5 us
    dot_general x4, matrix products, advance(): jnp.einsum('crb,cbo->cro', shocks, factors, preferred_element_type=jnp.fl...  9.22 us
    scatter x4, local copies, waits for them, and re-layouts, advance(): window.reshape(tile_cells, realize, block_size).at[target]  7.09 us
  transfers between devices with their start and end apart: 16, of which 4 were waited for; matrix products, arithmetic and copies ran while one was open for 23% of the time, Pallas kernels for 0%

commit v1 on v0

v1 whole, which is shorter than its diff:
```python
import functools

import jax
import jax.numpy as jnp
import numpy as np
from jax import lax
from jax.experimental import pallas as pl
from jax.experimental.pallas import tpu as pltpu
from jax.sharding import PartitionSpec as P

LEVELS = 4
BOTH = ("tx", "ty")
PIECES = (("ty_in", 4), ("ty_out_ends", 2), ("ty_out_mid", 2), ("tx_out", 4), ("tx_in", 4), ("tx_out_ends", 2), ("tx_in_ends", 2))
TILE = 16
HALO = 20
SLOTS = TILE + HALO


def slot_table():
    table = np.zeros((2, 2, TILE, 9), np.int32)
    for odd_x in range(2):
        for odd_y in range(2):
            in_x, out_x = (-1, 4) if odd_x else (4, -1)
            in_y, out_y = (-1, 4) if odd_y else (4, -1)
            place = {(x, y): 4 * x + y for x in range(4) for y in range(4)}
            order = [(x, in_y) for x in range(4)] + [(0, out_y), (3, out_y), (1, out_y), (2, out_y)]
            order += [(out_x, y) for y in range(4)] + [(in_x, y) for y in range(4)]
            order += [(out_x, in_y), (out_x, out_y), (in_x, in_y), (in_x, out_y)]
            for at, cell in enumerate(order):
                place[cell] = TILE + at
            for x in range(4):
                for y in range(4):
                    for j in range(9):
                        table[odd_x, odd_y, 4 * x + y, j] = place[(x + j // 3 - 1, y + j % 3 - 1)]
    return table


def send_table():
    table = np.zeros((2, 2, 16), np.int32)
    for odd_x in range(2):
        for odd_y in range(2):
            in_x, out_x = (0, 3) if odd_x else (3, 0)
            in_y, out_y = (0, 3) if odd_y else (3, 0)
            order = [(x, in_y) for x in range(4)] + [(0, out_y), (3, out_y), (1, out_y), (2, out_y)]
            order += [(out_x, y) for y in range(4)] + [(in_x, y) for y in range(4)]
            table[odd_x, odd_y] = [4 * x + y for x, y in order]
    return table


def partners(size_x, size_y, along_x, along_y):
    def other(at, size, kind):
        if kind == "in":
            return at ^ 1
        if kind == "out":
            return (((at + 1) % size) ^ 1) - 1 if at % 2 == 0 and at else (at + 1) % size if at % 2 else size - 1
        return at

    return [
        (x * size_y + y, other(x, size_x, along_x) * size_y + other(y, size_y, along_y))
        for x in range(size_x)
        for y in range(size_y)
    ]


def exchange(sends, odd_x):
    size_x, size_y = lax.axis_size("tx"), lax.axis_size("ty")
    swap = lambda value, x, y: lax.ppermute(value, BOTH, partners(size_x, size_y, x, y))
    ty_in, ty_ends, ty_mid, tx_out, tx_in = sends
    got_ty_ends = swap(ty_ends, None, "out")
    got_ty_in = swap(ty_in, None, "in")
    got_tx_out = swap(tx_out, "out", None)
    got_tx_in = swap(tx_in, "in", None)
    got_ty_mid = swap(ty_mid, None, "out")
    first = jnp.stack([got_ty_in[0], got_ty_ends[0]])
    last = jnp.stack([got_ty_in[3], got_ty_ends[1]])
    got_tx_out_ends = swap(jnp.where(odd_x, last, first), "out", None)
    got_tx_in_ends = swap(jnp.where(odd_x, first, last), "in", None)
    return got_ty_in, got_ty_ends, got_ty_mid, got_tx_out, got_tx_in, got_tx_out_ends, got_tx_in_ends


def level_kernel(section, send, level, slots, order, earlier, window, innovation, conditioner, chol_factor, *rest):
    pieces = len(PIECES)
    halos = [rest[:pieces]]
    rest = rest[pieces:]
    if section:
        halos.append(rest[:pieces])
        rest = rest[pieces:]
    result, *sends, sources = rest
    sources[0:TILE] = earlier[...]
    for half, halo in enumerate(halos):
        base = half * SLOTS + TILE
        for ref in halo:
            sources[base : base + ref.shape[0]] = ref[...]
            base += ref.shape[0]
    if section:
        sources[SLOTS : SLOTS + TILE] = window[...]
    rows = lax.broadcasted_iota(jnp.int32, (128, 128), 0)
    columns = lax.broadcasted_iota(jnp.int32, (128, 128), 1)
    upper = rows <= columns

    def one_cell(cell, carry):
        @pl.when(level[cell] == section)
        def _():
            gathered = jnp.concatenate([sources[slots[cell * 8 + k]] for k in range(8)], axis=1)
            factor = jnp.where(upper, chol_factor[cell].astype(jnp.float32), 0.0).astype(jnp.bfloat16)
            summed = jnp.dot(gathered, conditioner[cell], preferred_element_type=jnp.float32)
            summed += jnp.dot(innovation[cell], factor, preferred_element_type=jnp.float32)
            sources[SLOTS + cell] = summed.astype(jnp.bfloat16)

        return carry

    lax.fori_loop(0, TILE, one_cell, 0)
    at = 0
    for ref in sends:
        for i in range(ref.shape[0]):
            ref[i] = sources[SLOTS + order[at]]
            at += 1
    result[...] = sources[SLOTS : SLOTS + TILE]


def run_level(section, level, slots, order, earlier, window, innovation, conditioner, chol_factor, halos):
    block = earlier.shape[1:]
    send = section < LEVELS - 1
    smem = pl.BlockSpec(memory_space=pltpu.SMEM)
    vmem = pl.BlockSpec(memory_space=pltpu.VMEM)
    flat = [piece for halo in halos for piece in halo]
    shapes = [jax.ShapeDtypeStruct((TILE, *block), jnp.bfloat16)]
    if send:
        shapes += [jax.ShapeDtypeStruct((count, *block), jnp.bfloat16) for _, count in PIECES[:5]]
    return pl.pallas_call(
        functools.partial(level_kernel, section, send),
        out_shape=shapes,
        in_specs=[smem] * 3 + [vmem] * (5 + len(flat)),
        out_specs=[vmem] * len(shapes),
        scratch_shapes=[pltpu.VMEM((2 * SLOTS, *block), jnp.bfloat16)],
        compiler_params=pltpu.CompilerParams(vmem_limit_bytes=32 * 1024 * 1024),
        cost_estimate=pl.CostEstimate(flops=4 * 2 * 256 * 1152 * 128, bytes_accessed=8 << 20, transcendentals=0),
        name=f"level_{section}",
    )(level, slots, order, earlier, window, innovation, conditioner, chol_factor, *flat)


def local(earlier, innovation, conditioner, chol_factor, block_level, neighbours):
    block = earlier.shape[2:]
    odd_x = lax.axis_index("tx") % 2
    odd_y = lax.axis_index("ty") % 2
    in_x, out_x = 3 - 3 * odd_x, 3 * odd_x
    in_y, out_y = 3 - 3 * odd_y, 3 * odd_y
    out_column = lax.dynamic_index_in_dim(earlier, out_y, 1, keepdims=False)
    sends = (
        lax.dynamic_index_in_dim(earlier, in_y, 1, keepdims=False),
        jnp.stack([out_column[0], out_column[3]]),
        out_column[1:3],
        lax.dynamic_index_in_dim(earlier, out_x, 0, keepdims=False),
        lax.dynamic_index_in_dim(earlier, in_x, 0, keepdims=False),
    )
    halos = [exchange(sends, odd_x)]

    table = jnp.asarray(slot_table().reshape(4, TILE, 9))[2 * odd_x + odd_y]
    order = jnp.asarray(send_table().reshape(4, 16))[2 * odd_x + odd_y]
    codes = neighbours.reshape(TILE, 8)
    hits = (codes % 9)[:, :, None] == jnp.arange(9, dtype=jnp.int32)
    slots = jnp.sum(jnp.where(hits, table[:, None, :], 0), axis=-1) + SLOTS * (codes // 9)
    slots = slots.reshape(TILE * 8)
    level = block_level.reshape(TILE)

    own = earlier.reshape(TILE, *block)
    noise = innovation.reshape(TILE, *block)
    matrices = conditioner.reshape(TILE, *conditioner.shape[2:])
    factors = chol_factor.reshape(TILE, *chol_factor.shape[2:])
    window = own
    for section in range(LEVELS):
        window, *sends = run_level(section, level, slots, order, own, window, noise, matrices, factors, halos)
        if sends:
            halos = [halos[0], exchange(sends, odd_x)]
    return window.reshape(earlier.shape)


def solution(mesh):
    placed = (
        P("tx", "ty", None, None),
        P("tx", "ty", None, None),
        P("tx", "ty", None, None),
        P("tx", "ty", None, None),
        P("tx", "ty"),
        P("tx", "ty", None),
    )
    return jax.shard_map(
        local, mesh=mesh, in_specs=placed, out_specs=P("tx", "ty", None, None), check_vma=False
    )
```

time: 203 us -> 97.2 us (0.48)
  local copies, waits for them, and re-layouts: 70.6 us -> 13.7 us
  matrix products: 29.3 us -> 0 us
  other arithmetic: 26 us -> 4.12 us
  waiting for transfers between devices: 42.2 us -> 27.7 us
  Pallas kernels: 0 us -> 10.4 us
  starting transfers between devices: 33.5 us -> 40.2 us
    gather x20 -> x0, local copies, waits for them, and re-layouts: 53.8 us -> none  [the longest x4 22 us: advance(): gathered = lookup[source_kind, row_index, col_index]]
    dot_general x8 -> x0, matrix products: 29.3 us -> none  [the longest x4 20.1 us: advance(): jnp.einsum('ckrb,ckbo->cro', gathered, matrices, preferred_element_type=j...]
    concatenate x11 -> x0, other arithmetic: 20.9 us -> none  [the longest x7 20.6 us: with_halo(): shard = jnp.concatenate([before, shard, after], axis=dim)]
    ppermute x16 -> x28, waiting for transfers between devices: 42.2 us -> 27.7 us  [exchange(): lax.ppermute(value, BOTH, partners(size_x, size_y, x, y))]
    pallas_call x0 -> x4, Pallas kernels: none -> 10.4 us  [run_level(): pl.pallas_call(functools.partial(level_kernel, section, send), out_shape=...]
    scatter x4 -> x0, local copies, waits for them, and re-layouts: 7.09 us -> none  [advance(): window.reshape(tile_cells, realize, block_size).at[target]]
    ppermute x16 -> x28, starting transfers between devices: 33.5 us -> 40.2 us  [exchange(): lax.ppermute(value, BOTH, partners(size_x, size_y, x, y))]
    squeeze x0 -> x3, local copies, waits for them, and re-layouts: none -> 3.53 us  [the longest x1 1.87 us: local(): lax.dynamic_index_in_dim(earlier, in_x, 0, keepdims=False)]
  transfers between devices with their start and end apart: 16 -> 28, of which waited for: 4 -> 11; matrix products, arithmetic and copies ran while one was open for 23% -> 14% of each run, Pallas kernels for 0% -> 0%
where the time goes in v1:
time: 97.2 us; the launch traced here: 96.3 us
  starting transfers between devices  40.2 us (41%)
  waiting for transfers between devices  27.7 us (28%)
  local copies, waits for them, and re-layouts  13.7 us (14%)
  Pallas kernels  10.4 us (11%)
  other arithmetic  4.12 us (4%)
    ppermute x28, starting transfers between devices, exchange(): lax.ppermute(value, BOTH, partners(size_x, size_y, x, y))  40.2 us
    ppermute x28, waiting for transfers between devices, exchange(): lax.ppermute(value, BOTH, partners(size_x, size_y, x, y))  27.7 us
    pallas_call x4, Pallas kernels, run_level(): pl.pallas_call(functools.partial(level_kernel, section, send), out_shape=...  10.4 us
    unnamed x8, local copies, waits for them, and re-layouts  3.24 us
  transfers between devices with their start and end apart: 28, of which 11 were waited for; matrix products, arithmetic and copies ran while one was open for 14% of the time, Pallas kernels for 0%

profile of v1, /device:TPU:0, one launch (start us, length us, event | category | flops | bytes accessed | tf_op | source)
XLA Modules:
  0.0 96.3 jit_solution(17767421432805302349)
XLA Ops:
  1.1 3.6 %collective-permute-start.1 = (bf16[2,256,128]{2,1,0:T(8,128)(2,1)S(1)}, bf16[2,256,128]{2,1,0:T(8,128)(2,1)S(1)}, u32[]{:S(2)}, u32[]{:S(2)}) collective-permute-start(bf16[2,256,128]{2,1,0:T(8,128)(2,1)S(1)} %pad_maximum_fusion), channel_id=1, source_target_pairs={{0,7},{1,2},{2,1},{3,4},{4,3},{5,6},{6,5},{7,0},{8,15},{9,10},{10,... | collective-permute-start | bytes 393224 | tf_op jit(solution)/shard_map/ppermute | solution.py:67
  4.7 1.6 %dynamic-slice_bitcast_fusion.3 = bf16[2,256,128]{2,1,0:T(8,128)(2,1)} fusion(bf16[4,4,256,128]{3,2,1,0:T(8,128)(2,1)} %param.8, s32[]{:T(128)S(6)} %add.58, s32[]{:T(128)S(6)} %select_n.92), kind=kLoop, calls=%fused_computation.3 | loop fusion | bytes 262152 | tf_op jit(solution)/shard_map/slice | solution.py:152
  7.4 1.9 %dynamic-slice_bitcast_fusion = (bf16[4,256,128]{2,1,0:T(8,128)(2,1)}, bf16[4,256,128]{2,1,0:T(8,128)(2,1)}) fusion(bf16[4,4,256,128]{3,2,1,0:T(8,128)(2,1)} %param.8, s32[]{:T(128)S(6)} %select_n.94, s32[]{:T(128)S(6)} %select_n.93), kind=kLoop, calls=%fused_computation | loop fusion | bytes 1048584 | tf_op jit(solution)/shard_map/jit(dynamic_index_in_dim)/squeeze | solution.py:154
  9.2 1.5 %collective-permute-start.4 = (bf16[4,256,128]{2,1,0:T(8,128)(2,1)}, bf16[4,256,128]{2,1,0:T(8,128)(2,1)S(1)}, u32[]{:S(2)}, u32[]{:S(2)}) collective-permute-start(bf16[4,256,128]{2,1,0:T(8,128)(2,1)} %get-tuple-element.41), channel_id=1, source_target_pairs={{0,8},{1,9},{2,10},{3,11},{4,12},{5,13},{6,14},{7,15},{8,0},{9,1},... | collective-permute-start | bytes 786440 | tf_op jit(solution)/shard_map/ppermute | solution.py:67
  10.7 4.5 %collective-permute-start.3 = (bf16[4,256,128]{2,1,0:T(8,128)(2,1)}, bf16[4,256,128]{2,1,0:T(8,128)(2,1)S(1)}, u32[]{:S(2)}, u32[]{:S(2)}) collective-permute-start(bf16[4,256,128]{2,1,0:T(8,128)(2,1)} %get-tuple-element.42), channel_id=1, source_target_pairs={{0,120},{1,121},{2,122},{3,123},{4,124},{5,125},{6,126},{7,127},{8... | collective-permute-start | bytes 786440 | tf_op jit(solution)/shard_map/ppermute | solution.py:67
  15.3 1.3 %fusion = pred[4,4,8]{2,1,0:T(4,128)(4,1)} fusion(s32[4,4,8]{2,1,0:T(4,128)} %param.13), kind=kLoop, calls=%fused_computation.28 | loop fusion | flops 640 | bytes 640 | tf_op jit(solution)/shard_map/jit(floor_divide)/and | solution.py:162
  17.3 1.3 %dynamic-slice_bitcast_fusion.6 = s32[16,9]{0,1:T(8,128)} fusion(s32[4,16,9]{1,2,0:T(8,128)} %constant.79.clone, s32[]{:T(128)S(6)} %select_n.88), kind=kLoop, calls=%fused_computation.27 | loop fusion | bytes 1156 | tf_op jit(solution)/shard_map/jit(_where)/broadcast_in_dim | solution.py:162
  22.2 1.2 %collective-permute-start.5 = (bf16[2,256,128]{2,1,0:T(8,128)(2,1)S(1)}, bf16[2,256,128]{2,1,0:T(8,128)(2,1)S(1)}, u32[]{:S(2)}, u32[]{:S(2)}) collective-permute-start(bf16[2,256,128]{2,1,0:T(8,128)(2,1)S(1)} %get-tuple-element.58), channel_id=1, source_target_pairs={{0,120},{1,121},{2,122},{3,123},{4,124},{5,125},{6,126},{7,127},{8... | collective-permute-start | bytes 393224 | tf_op jit(solution)/shard_map/ppermute | solution.py:67
  25.6 2.2 %collective-permute-done.6.rest_6_ = bf16[2,256,128]{2,1,0:T(8,128)(2,1)S(1)} collective-permute-done((bf16[2,256,128]{2,1,0:T(8,128)(2,1)}, bf16[2,256,128]{2,1,0:T(8,128)(2,1)S(1)}, u32[]{:S(2)}, u32[]{:S(2)}) %collective-permute-start.6) | collective-permute-done | bytes 131104 | tf_op jit(solution)/shard_map/ppermute | solution.py:67
  27.8 3.1 %collective-permute-done.5.rest_5_ = bf16[2,256,128]{2,1,0:T(8,128)(2,1)S(1)} collective-permute-done((bf16[2,256,128]{2,1,0:T(8,128)(2,1)S(1)}, bf16[2,256,128]{2,1,0:T(8,128)(2,1)S(1)}, u32[]{:S(2)}, u32[]{:S(2)}) %collective-permute-start.5) | collective-permute-done | bytes 131104 | tf_op jit(solution)/shard_map/ppermute | solution.py:67
  30.9 2.2 %copy-done = bf16[4,4,1024,128]{3,2,1,0:T(8,128)(2,1)S(1)} copy-done((bf16[4,4,1024,128]{3,2,1,0:T(8,128)(2,1)S(1)}, bf16[4,4,1024,128]{3,2,1,0:T(8,128)(2,1)}, u32[]{:S(2)}) %copy-start) | copy-done | bytes 4194328
  34.1 2.6 %level_0.1 = (bf16[16,256,128]{2,1,0:T(8,128)(2,1)S(1)}, bf16[4,256,128]{2,1,0:T(8,128)(2,1)S(1)}, bf16[2,256,128]{2,1,0:T(8,128)(2,1)S(1)}, bf16[2,256,128]{2,1...) custom-call(s32[16]{0:T(128)S(1)} %reshape.48.level, s32[128]{0:T(128)S(1)} %fusion.2.slots, ...), custom_call_target="tpu_custom_call" | custom-call | flops 301989888 | bytes 8388608 | tf_op jit(solution)/shard_map/level_0/pallas_call | solution.py:130
  37.1 2.7 %collective-permute-start.9 = (bf16[2,256,128]{2,1,0:T(8,128)(2,1)S(1)}, bf16[2,256,128]{2,1,0:T(8,128)(2,1)S(1)}, u32[]{:S(2)}, u32[]{:S(2)}) collective-permute-start(bf16[2,256,128]{2,1,0:T(8,128)(2,1)S(1)} %get-tuple-element.26), channel_id=1, source_target_pairs={{0,7},{1,2},{2,1},{3,4},{4,3},{5,6},{6,5},{7,0},{8,15},{9,10},{10,... | collective-permute-start | bytes 393224 | tf_op jit(solution)/shard_map/ppermute | solution.py:67
  40.6 1.7 %collective-permute-done.8.rest_8_ = bf16[2,256,128]{2,1,0:T(8,128)(2,1)S(1)} collective-permute-done((bf16[2,256,128]{2,1,0:T(8,128)(2,1)S(1)}, bf16[2,256,128]{2,1,0:T(8,128)(2,1)S(1)}, u32[]{:S(2)}, u32[]{:S(2)}) %collective-permute-start.8) | collective-permute-done | bytes 131104 | tf_op jit(solution)/shard_map/ppermute | solution.py:67
  42.8 4.4 %collective-permute-start.12 = (bf16[2,256,128]{2,1,0:T(8,128)(2,1)S(1)}, bf16[2,256,128]{2,1,0:T(8,128)(2,1)S(1)}, u32[]{:S(2)}, u32[]{:S(2)}) collective-permute-start(bf16[2,256,128]{2,1,0:T(8,128)(2,1)S(1)} %get-tuple-element.54), channel_id=1, source_target_pairs={{0,120},{1,121},{2,122},{3,123},{4,124},{5,125},{6,126},{7,127},{8... | collective-permute-start | bytes 393224 | tf_op jit(solution)/shard_map/ppermute | solution.py:67
  47.3 4.9 %collective-permute-done.10.rest_10_ = bf16[4,256,128]{2,1,0:T(8,128)(2,1)S(1)} collective-permute-done((bf16[4,256,128]{2,1,0:T(8,128)(2,1)S(1)}, bf16[4,256,128]{2,1,0:T(8,128)(2,1)S(1)}, u32[]{:S(2)}, u32[]{:S(2)}) %collective-permute-start.10) | collective-permute-done | bytes 262176 | tf_op jit(solution)/shard_map/ppermute | solution.py:67
  52.2 2.1 %collective-permute-done.12.rest_12_ = bf16[2,256,128]{2,1,0:T(8,128)(2,1)S(1)} collective-permute-done((bf16[2,256,128]{2,1,0:T(8,128)(2,1)S(1)}, bf16[2,256,128]{2,1,0:T(8,128)(2,1)S(1)}, u32[]{:S(2)}, u32[]{:S(2)}) %collective-permute-start.12) | collective-permute-done | bytes 131104 | tf_op jit(solution)/shard_map/ppermute | solution.py:67
  54.3 1.8 %level_1.1 = (bf16[16,256,128]{2,1,0:T(8,128)(2,1)S(1)}, bf16[4,256,128]{2,1,0:T(8,128)(2,1)S(1)}, bf16[2,256,128]{2,1,0:T(8,128)(2,1)S(1)}, bf16[2,256,128]{2,1...) custom-call(s32[16]{0:T(128)S(1)} %reshape.48.level, s32[128]{0:T(128)S(1)} %fusion.2.slots, ...), custom_call_target="tpu_custom_call" | custom-call | flops 301989888 | bytes 8388608 | tf_op jit(solution)/shard_map/level_1/pallas_call | solution.py:130
  56.7 2.2 %collective-permute-start.14 = (bf16[4,256,128]{2,1,0:T(8,128)(2,1)S(1)}, bf16[4,256,128]{2,1,0:T(8,128)(2,1)S(1)}, u32[]{:S(2)}, u32[]{:S(2)}) collective-permute-start(bf16[4,256,128]{2,1,0:T(8,128)(2,1)S(1)} %get-tuple-element.30), channel_id=1, source_target_pairs={{0,1},{1,0},{2,3},{3,2},{4,5},{5,4},{6,7},{7,6},{8,9},{9,8},{10,11... | collective-permute-start | bytes 786440 | tf_op jit(solution)/shard_map/ppermute | solution.py:67
  59.2 3.6 %collective-permute-start.17 = (bf16[4,256,128]{2,1,0:T(8,128)(2,1)S(1)}, bf16[4,256,128]{2,1,0:T(8,128)(2,1)S(1)}, u32[]{:S(2)}, u32[]{:S(2)}) collective-permute-start(bf16[4,256,128]{2,1,0:T(8,128)(2,1)S(1)} %get-tuple-element.33), channel_id=1, source_target_pairs={{0,120},{1,121},{2,122},{3,123},{4,124},{5,125},{6,126},{7,127},{8... | collective-permute-start | bytes 786440 | tf_op jit(solution)/shard_map/ppermute | solution.py:67
  62.8 2.1 %collective-permute-start.20 = (bf16[2,256,128]{2,1,0:T(8,128)(2,1)S(1)}, bf16[2,256,128]{2,1,0:T(8,128)(2,1)S(1)}, u32[]{:S(2)}, u32[]{:S(2)}) collective-permute-start(bf16[2,256,128]{2,1,0:T(8,128)(2,1)S(1)} %get-tuple-element.49), channel_id=1, source_target_pairs={{0,8},{1,9},{2,10},{3,11},{4,12},{5,13},{6,14},{7,15},{8,0},{9,1},... | collective-permute-start | bytes 393224 | tf_op jit(solution)/shard_map/ppermute | solution.py:67
  64.9 1.8 %collective-permute-start.19 = (bf16[2,256,128]{2,1,0:T(8,128)(2,1)S(1)}, bf16[2,256,128]{2,1,0:T(8,128)(2,1)S(1)}, u32[]{:S(2)}, u32[]{:S(2)}) collective-permute-start(bf16[2,256,128]{2,1,0:T(8,128)(2,1)S(1)} %get-tuple-element.50), channel_id=1, source_target_pairs={{0,120},{1,121},{2,122},{3,123},{4,124},{5,125},{6,126},{7,127},{8... | collective-permute-start | bytes 393224 | tf_op jit(solution)/shard_map/ppermute | solution.py:67
  66.7 5.0 %collective-permute-done.17.rest_10_ = bf16[4,256,128]{2,1,0:T(8,128)(2,1)S(1)} collective-permute-done((bf16[4,256,128]{2,1,0:T(8,128)(2,1)S(1)}, bf16[4,256,128]{2,1,0:T(8,128)(2,1)S(1)}, u32[]{:S(2)}, u32[]{:S(2)}) %collective-permute-start.17) | collective-permute-done | bytes 262176 | tf_op jit(solution)/shard_map/ppermute | solution.py:67
  71.7 1.8 %collective-permute-done.19.rest_12_ = bf16[2,256,128]{2,1,0:T(8,128)(2,1)S(1)} collective-permute-done((bf16[2,256,128]{2,1,0:T(8,128)(2,1)S(1)}, bf16[2,256,128]{2,1,0:T(8,128)(2,1)S(1)}, u32[]{:S(2)}, u32[]{:S(2)}) %collective-permute-start.19) | collective-permute-done | bytes 131104 | tf_op jit(solution)/shard_map/ppermute | solution.py:67
  73.5 1.5 %level_2.1 = (bf16[16,256,128]{2,1,0:T(8,128)(2,1)S(1)}, bf16[4,256,128]{2,1,0:T(8,128)(2,1)S(1)}, bf16[2,256,128]{2,1,0:T(8,128)(2,1)S(1)}, bf16[2,256,128]{2,1...) custom-call(s32[16]{0:T(128)S(1)} %reshape.48.level, s32[128]{0:T(128)S(1)} %fusion.2.slots, ...), custom_call_target="tpu_custom_call" | custom-call | flops 301989888 | bytes 8388608 | tf_op jit(solution)/shard_map/level_2/pallas_call | solution.py:130
  75.0 2.0 %collective-permute-start.22 = (bf16[2,256,128]{2,1,0:T(8,128)(2,1)S(1)}, bf16[2,256,128]{2,1,0:T(8,128)(2,1)S(1)}, u32[]{:S(2)}, u32[]{:S(2)}) collective-permute-start(bf16[2,256,128]{2,1,0:T(8,128)(2,1)S(1)} %get-tuple-element.37), channel_id=1, source_target_pairs={{0,7},{1,2},{2,1},{3,4},{4,3},{5,6},{6,5},{7,0},{8,15},{9,10},{10,... | collective-permute-start | bytes 393224 | tf_op jit(solution)/shard_map/ppermute | solution.py:67
  78.0 2.1 %collective-permute-start.24 = (bf16[4,256,128]{2,1,0:T(8,128)(2,1)S(1)}, bf16[4,256,128]{2,1,0:T(8,128)(2,1)S(1)}, u32[]{:S(2)}, u32[]{:S(2)}) collective-permute-start(bf16[4,256,128]{2,1,0:T(8,128)(2,1)S(1)} %get-tuple-element.39), channel_id=1, source_target_pairs={{0,120},{1,121},{2,122},{3,123},{4,124},{5,125},{6,126},{7,127},{8... | collective-permute-start | bytes 786440 | tf_op jit(solution)/shard_map/ppermute | solution.py:67
  80.8 1.6 %collective-permute-start.27 = (bf16[2,256,128]{2,1,0:T(8,128)(2,1)S(1)}, bf16[2,256,128]{2,1,0:T(8,128)(2,1)S(1)}, u32[]{:S(2)}, u32[]{:S(2)}) collective-permute-start(bf16[2,256,128]{2,1,0:T(8,128)(2,1)S(1)} %get-tuple-element.45), channel_id=1, source_target_pairs={{0,8},{1,9},{2,10},{3,11},{4,12},{5,13},{6,14},{7,15},{8,0},{9,1},... | collective-permute-start | bytes 393224 | tf_op jit(solution)/shard_map/ppermute | solution.py:67
  82.3 3.3 %collective-permute-start.26 = (bf16[2,256,128]{2,1,0:T(8,128)(2,1)S(1)}, bf16[2,256,128]{2,1,0:T(8,128)(2,1)S(1)}, u32[]{:S(2)}, u32[]{:S(2)}) collective-permute-start(bf16[2,256,128]{2,1,0:T(8,128)(2,1)S(1)} %get-tuple-element.46), channel_id=1, source_target_pairs={{0,120},{1,121},{2,122},{3,123},{4,124},{5,125},{6,126},{7,127},{8... | collective-permute-start | bytes 393224 | tf_op jit(solution)/shard_map/ppermute | solution.py:67
  85.6 4.8 %collective-permute-done.24.rest_10_ = bf16[4,256,128]{2,1,0:T(8,128)(2,1)S(1)} collective-permute-done((bf16[4,256,128]{2,1,0:T(8,128)(2,1)S(1)}, bf16[4,256,128]{2,1,0:T(8,128)(2,1)S(1)}, u32[]{:S(2)}, u32[]{:S(2)}) %collective-permute-start.24) | collective-permute-done | bytes 262176 | tf_op jit(solution)/shard_map/ppermute | solution.py:67
  90.6 1.2 %collective-permute-done.26.rest_12_ = bf16[2,256,128]{2,1,0:T(8,128)(2,1)S(1)} collective-permute-done((bf16[2,256,128]{2,1,0:T(8,128)(2,1)S(1)}, bf16[2,256,128]{2,1,0:T(8,128)(2,1)S(1)}, u32[]{:S(2)}, u32[]{:S(2)}) %collective-permute-start.26) | collective-permute-done | bytes 131104 | tf_op jit(solution)/shard_map/ppermute | solution.py:67
  91.8 4.5 %level_3.1 = bf16[16,256,128]{2,1,0:T(8,128)(2,1)} custom-call(s32[16]{0:T(128)S(1)} %reshape.48.level, s32[128]{0:T(128)S(1)} %fusion.2.slots, s32[16]{0:T(128)S(1)} %fusion.3.order, bf16[16,256,128]{2,1,0:T(8,128)(2,1)S(1)} %bitcast.30, bf16[16,256,128]{2,1,0:T(8,128)(2,1)S(1)} %get-tuple-element.35.window, bf16[16,256,128]{2,1,0:T(8,128)(2,1)S(1)} %bitcast.34, ...), custom_call_target="tpu_custom_call" | custom-call | flops 301989888 | bytes 8388608 | tf_op jit(solution)/shard_map/level_3/pallas_call | solution.py:130
  (66 shorter events, 14.0 us)
Async XLA Ops:
  0.0 30.9 %copy-start.1 = (bf16[4,4,256,128]{3,2,1,0:T(8,128)(2,1)S(1)}, bf16[4,4,256,128]{3,2,1,0:T(8,128)(2,1)}, u32[]{:S(2)}) copy-start(bf16[4,4,256,128]{3,2,1,0:T(8,128)(2,1)} %param.8) | copy-start | bytes 3145732
  0.0 30.9 %copy-start.2 = (bf16[4,4,256,128]{3,2,1,0:T(8,128)(2,1)S(1)}, bf16[4,4,256,128]{3,2,1,0:T(8,128)(2,1)}, u32[]{:S(2)}) copy-start(bf16[4,4,256,128]{3,2,1,0:T(8,128)(2,1)} %param.9) | copy-start | bytes 3145732
  1.1 20.4 %collective-permute-start.1 = (bf16[2,256,128]{2,1,0:T(8,128)(2,1)S(1)}, bf16[2,256,128]{2,1,0:T(8,128)(2,1)S(1)}, u32[]{:S(2)}, u32[]{:S(2)}) collective-permute-start(bf16[2,256,128]{2,1,0:T(8,128)(2,1)S(1)} %pad_maximum_fusion), channel_id=1, source_target_pairs={{0,7},{1,2},{2,1},{3,4},{4,3},{5,6},{6,5},{7,0},{8,15},{9,10},{10,... | collective-permute-start | bytes 393224 | tf_op jit(solution)/shard_map/ppermute | solution.py:67
  6.3 19.3 %collective-permute-start.2 = (bf16[2,256,128]{2,1,0:T(8,128)(2,1)}, bf16[2,256,128]{2,1,0:T(8,128)(2,1)S(1)}, u32[]{:S(2)}, u32[]{:S(2)}) collective-permute-start(bf16[2,256,128]{2,1,0:T(8,128)(2,1)} %dynamic-slice_bitcast_fusion.3), channel_id=1, source_target_pairs={{0,7},{1,2},{2,1},{3,4},{4,3},{5,6},{6,5},{7,0},{8,15},{9,10},{10,... | collective-permute-start | bytes 393224 | tf_op jit(solution)/shard_map/ppermute | solution.py:67
  7.3 14.3 %collective-permute-start = (bf16[4,256,128]{2,1,0:T(8,128)(2,1)S(1)}, bf16[4,256,128]{2,1,0:T(8,128)(2,1)S(1)}, u32[]{:S(2)}, u32[]{:S(2)}) collective-permute-start(bf16[4,256,128]{2,1,0:T(8,128)(2,1)S(1)} %dynamic-slice_bitcast_fusion.2), channel_id=1, source_target_pairs={{0,1},{1,0},{2,3},{3,2},{4,5},{5,4},{6,7},{7,6},{8,9},{9,8},{10,11... | collective-permute-start | bytes 786440 | tf_op jit(solution)/shard_map/ppermute | solution.py:67
  9.2 16.3 %collective-permute-start.4 = (bf16[4,256,128]{2,1,0:T(8,128)(2,1)}, bf16[4,256,128]{2,1,0:T(8,128)(2,1)S(1)}, u32[]{:S(2)}, u32[]{:S(2)}) collective-permute-start(bf16[4,256,128]{2,1,0:T(8,128)(2,1)} %get-tuple-element.41), channel_id=1, source_target_pairs={{0,8},{1,9},{2,10},{3,11},{4,12},{5,13},{6,14},{7,15},{8,0},{9,1},... | collective-permute-start | bytes 786440 | tf_op jit(solution)/shard_map/ppermute | solution.py:67
  10.7 14.8 %collective-permute-start.3 = (bf16[4,256,128]{2,1,0:T(8,128)(2,1)}, bf16[4,256,128]{2,1,0:T(8,128)(2,1)S(1)}, u32[]{:S(2)}, u32[]{:S(2)}) collective-permute-start(bf16[4,256,128]{2,1,0:T(8,128)(2,1)} %get-tuple-element.42), channel_id=1, source_target_pairs={{0,120},{1,121},{2,122},{3,123},{4,124},{5,125},{6,126},{7,127},{8... | collective-permute-start | bytes 786440 | tf_op jit(solution)/shard_map/ppermute | solution.py:67
  22.2 5.5 %collective-permute-start.6 = (bf16[2,256,128]{2,1,0:T(8,128)(2,1)}, bf16[2,256,128]{2,1,0:T(8,128)(2,1)S(1)}, u32[]{:S(2)}, u32[]{:S(2)}) collective-permute-start(bf16[2,256,128]{2,1,0:T(8,128)(2,1)} %get-tuple-element.57), channel_id=1, source_target_pairs={{0,8},{1,9},{2,10},{3,11},{4,12},{5,13},{6,14},{7,15},{8,0},{9,1},... | collective-permute-start | bytes 393224 | tf_op jit(solution)/shard_map/ppermute | solution.py:67
  22.2 8.6 %collective-permute-start.5 = (bf16[2,256,128]{2,1,0:T(8,128)(2,1)S(1)}, bf16[2,256,128]{2,1,0:T(8,128)(2,1)S(1)}, u32[]{:S(2)}, u32[]{:S(2)}) collective-permute-start(bf16[2,256,128]{2,1,0:T(8,128)(2,1)S(1)} %get-tuple-element.58), channel_id=1, source_target_pairs={{0,120},{1,121},{2,122},{3,123},{4,124},{5,125},{6,126},{7,127},{8... | collective-permute-start | bytes 393224 | tf_op jit(solution)/shard_map/ppermute | solution.py:67
  30.9 2.2 %copy-start = (bf16[4,4,1024,128]{3,2,1,0:T(8,128)(2,1)S(1)}, bf16[4,4,1024,128]{3,2,1,0:T(8,128)(2,1)}, u32[]{:S(2)}) copy-start(bf16[4,4,1024,128]{3,2,1,0:T(8,128)(2,1)} %param.10) | copy-start | bytes 12582916
  33.1 1.0 %copy-start.3 = (bf16[4,4,128,128]{3,2,1,0:T(8,128)(2,1)S(1)}, bf16[4,4,128,128]{3,2,1,0:T(8,128)(2,1)}, u32[]{:S(2)}) copy-start(bf16[4,4,128,128]{3,2,1,0:T(8,128)(2,1)} %param.11) | copy-start | bytes 1572868
  36.7 5.7 %collective-permute-start.8 = (bf16[2,256,128]{2,1,0:T(8,128)(2,1)S(1)}, bf16[2,256,128]{2,1,0:T(8,128)(2,1)S(1)}, u32[]{:S(2)}, u32[]{:S(2)}) collective-permute-start(bf16[2,256,128]{2,1,0:T(8,128)(2,1)S(1)} %get-tuple-element.25), channel_id=1, source_target_pairs={{0,7},{1,2},{2,1},{3,4},{4,3},{5,6},{6,5},{7,0},{8,15},{9,10},{10,... | collective-permute-start | bytes 393224 | tf_op jit(solution)/shard_map/ppermute | solution.py:67
  37.0 5.3 %collective-permute-start.7 = (bf16[4,256,128]{2,1,0:T(8,128)(2,1)S(1)}, bf16[4,256,128]{2,1,0:T(8,128)(2,1)S(1)}, u32[]{:S(2)}, u32[]{:S(2)}) collective-permute-start(bf16[4,256,128]{2,1,0:T(8,128)(2,1)S(1)} %get-tuple-element.24), channel_id=1, source_target_pairs={{0,1},{1,0},{2,3},{3,2},{4,5},{5,4},{6,7},{7,6},{8,9},{9,8},{10,11... | collective-permute-start | bytes 786440 | tf_op jit(solution)/shard_map/ppermute | solution.py:67
  37.1 10.2 %collective-permute-start.9 = (bf16[2,256,128]{2,1,0:T(8,128)(2,1)S(1)}, bf16[2,256,128]{2,1,0:T(8,128)(2,1)S(1)}, u32[]{:S(2)}, u32[]{:S(2)}) collective-permute-start(bf16[2,256,128]{2,1,0:T(8,128)(2,1)S(1)} %get-tuple-element.26), channel_id=1, source_target_pairs={{0,7},{1,2},{2,1},{3,4},{4,3},{5,6},{6,5},{7,0},{8,15},{9,10},{10,... | collective-permute-start | bytes 393224 | tf_op jit(solution)/shard_map/ppermute | solution.py:67
  39.7 12.5 %collective-permute-start.10 = (bf16[4,256,128]{2,1,0:T(8,128)(2,1)S(1)}, bf16[4,256,128]{2,1,0:T(8,128)(2,1)S(1)}, u32[]{:S(2)}, u32[]{:S(2)}) collective-permute-start(bf16[4,256,128]{2,1,0:T(8,128)(2,1)S(1)} %get-tuple-element.27), channel_id=1, source_target_pairs={{0,120},{1,121},{2,122},{3,123},{4,124},{5,125},{6,126},{7,127},{8... | collective-permute-start | bytes 786440 | tf_op jit(solution)/shard_map/ppermute | solution.py:67
  40.6 11.6 %collective-permute-start.11 = (bf16[4,256,128]{2,1,0:T(8,128)(2,1)S(1)}, bf16[4,256,128]{2,1,0:T(8,128)(2,1)S(1)}, u32[]{:S(2)}, u32[]{:S(2)}) collective-permute-start(bf16[4,256,128]{2,1,0:T(8,128)(2,1)S(1)} %get-tuple-element.28), channel_id=1, source_target_pairs={{0,8},{1,9},{2,10},{3,11},{4,12},{5,13},{6,14},{7,15},{8,0},{9,1},... | collective-permute-start | bytes 786440 | tf_op jit(solution)/shard_map/ppermute | solution.py:67
  42.5 9.7 %collective-permute-start.13 = (bf16[2,256,128]{2,1,0:T(8,128)(2,1)S(1)}, bf16[2,256,128]{2,1,0:T(8,128)(2,1)S(1)}, u32[]{:S(2)}, u32[]{:S(2)}) collective-permute-start(bf16[2,256,128]{2,1,0:T(8,128)(2,1)S(1)} %get-tuple-element.53), channel_id=1, source_target_pairs={{0,8},{1,9},{2,10},{3,11},{4,12},{5,13},{6,14},{7,15},{8,0},{9,1},... | collective-permute-start | bytes 393224 | tf_op jit(solution)/shard_map/ppermute | solution.py:67
  42.8 11.5 %collective-permute-start.12 = (bf16[2,256,128]{2,1,0:T(8,128)(2,1)S(1)}, bf16[2,256,128]{2,1,0:T(8,128)(2,1)S(1)}, u32[]{:S(2)}, u32[]{:S(2)}) collective-permute-start(bf16[2,256,128]{2,1,0:T(8,128)(2,1)S(1)} %get-tuple-element.54), channel_id=1, source_target_pairs={{0,120},{1,121},{2,122},{3,123},{4,124},{5,125},{6,126},{7,127},{8... | collective-permute-start | bytes 393224 | tf_op jit(solution)/shard_map/ppermute | solution.py:67
  56.1 6.6 %collective-permute-start.15 = (bf16[2,256,128]{2,1,0:T(8,128)(2,1)S(1)}, bf16[2,256,128]{2,1,0:T(8,128)(2,1)S(1)}, u32[]{:S(2)}, u32[]{:S(2)}) collective-permute-start(bf16[2,256,128]{2,1,0:T(8,128)(2,1)S(1)} %get-tuple-element.31), channel_id=1, source_target_pairs={{0,7},{1,2},{2,1},{3,4},{4,3},{5,6},{6,5},{7,0},{8,15},{9,10},{10,... | collective-permute-start | bytes 393224 | tf_op jit(solution)/shard_map/ppermute | solution.py:67
  56.7 6.1 %collective-permute-start.14 = (bf16[4,256,128]{2,1,0:T(8,128)(2,1)S(1)}, bf16[4,256,128]{2,1,0:T(8,128)(2,1)S(1)}, u32[]{:S(2)}, u32[]{:S(2)}) collective-permute-start(bf16[4,256,128]{2,1,0:T(8,128)(2,1)S(1)} %get-tuple-element.30), channel_id=1, source_target_pairs={{0,1},{1,0},{2,3},{3,2},{4,5},{5,4},{6,7},{7,6},{8,9},{9,8},{10,11... | collective-permute-start | bytes 786440 | tf_op jit(solution)/shard_map/ppermute | solution.py:67
  58.9 7.8 %collective-permute-start.16 = (bf16[2,256,128]{2,1,0:T(8,128)(2,1)S(1)}, bf16[2,256,128]{2,1,0:T(8,128)(2,1)S(1)}, u32[]{:S(2)}, u32[]{:S(2)}) collective-permute-start(bf16[2,256,128]{2,1,0:T(8,128)(2,1)S(1)} %get-tuple-element.32), channel_id=1, source_target_pairs={{0,7},{1,2},{2,1},{3,4},{4,3},{5,6},{6,5},{7,0},{8,15},{9,10},{10,... | collective-permute-start | bytes 393224 | tf_op jit(solution)/shard_map/ppermute | solution.py:67
  59.2 12.5 %collective-permute-start.17 = (bf16[4,256,128]{2,1,0:T(8,128)(2,1)S(1)}, bf16[4,256,128]{2,1,0:T(8,128)(2,1)S(1)}, u32[]{:S(2)}, u32[]{:S(2)}) collective-permute-start(bf16[4,256,128]{2,1,0:T(8,128)(2,1)S(1)} %get-tuple-element.33), channel_id=1, source_target_pairs={{0,120},{1,121},{2,122},{3,123},{4,124},{5,125},{6,126},{7,127},{8... | collective-permute-start | bytes 786440 | tf_op jit(solution)/shard_map/ppermute | solution.py:67
  62.7 8.9 %collective-permute-start.18 = (bf16[4,256,128]{2,1,0:T(8,128)(2,1)S(1)}, bf16[4,256,128]{2,1,0:T(8,128)(2,1)S(1)}, u32[]{:S(2)}, u32[]{:S(2)}) collective-permute-start(bf16[4,256,128]{2,1,0:T(8,128)(2,1)S(1)} %get-tuple-element.34), channel_id=1, source_target_pairs={{0,8},{1,9},{2,10},{3,11},{4,12},{5,13},{6,14},{7,15},{8,0},{9,1},... | collective-permute-start | bytes 786440 | tf_op jit(solution)/shard_map/ppermute | solution.py:67
  62.8 8.9 %collective-permute-start.20 = (bf16[2,256,128]{2,1,0:T(8,128)(2,1)S(1)}, bf16[2,256,128]{2,1,0:T(8,128)(2,1)S(1)}, u32[]{:S(2)}, u32[]{:S(2)}) collective-permute-start(bf16[2,256,128]{2,1,0:T(8,128)(2,1)S(1)} %get-tuple-element.49), channel_id=1, source_target_pairs={{0,8},{1,9},{2,10},{3,11},{4,12},{5,13},{6,14},{7,15},{8,0},{9,1},... | collective-permute-start | bytes 393224 | tf_op jit(solution)/shard_map/ppermute | solution.py:67
  64.9 8.5 %collective-permute-start.19 = (bf16[2,256,128]{2,1,0:T(8,128)(2,1)S(1)}, bf16[2,256,128]{2,1,0:T(8,128)(2,1)S(1)}, u32[]{:S(2)}, u32[]{:S(2)}) collective-permute-start(bf16[2,256,128]{2,1,0:T(8,128)(2,1)S(1)} %get-tuple-element.50), channel_id=1, source_target_pairs={{0,120},{1,121},{2,122},{3,123},{4,124},{5,125},{6,126},{7,127},{8... | collective-permute-start | bytes 393224 | tf_op jit(solution)/shard_map/ppermute | solution.py:67
  75.0 5.7 %collective-permute-start.22 = (bf16[2,256,128]{2,1,0:T(8,128)(2,1)S(1)}, bf16[2,256,128]{2,1,0:T(8,128)(2,1)S(1)}, u32[]{:S(2)}, u32[]{:S(2)}) collective-permute-start(bf16[2,256,128]{2,1,0:T(8,128)(2,1)S(1)} %get-tuple-element.37), channel_id=1, source_target_pairs={{0,7},{1,2},{2,1},{3,4},{4,3},{5,6},{6,5},{7,0},{8,15},{9,10},{10,... | collective-permute-start | bytes 393224 | tf_op jit(solution)/shard_map/ppermute | solution.py:67
  77.0 3.7 %collective-permute-start.21 = (bf16[4,256,128]{2,1,0:T(8,128)(2,1)S(1)}, bf16[4,256,128]{2,1,0:T(8,128)(2,1)S(1)}, u32[]{:S(2)}, u32[]{:S(2)}) collective-permute-start(bf16[4,256,128]{2,1,0:T(8,128)(2,1)S(1)} %get-tuple-element.36), channel_id=1, source_target_pairs={{0,1},{1,0},{2,3},{3,2},{4,5},{5,4},{6,7},{7,6},{8,9},{9,8},{10,11... | collective-permute-start | bytes 786440 | tf_op jit(solution)/shard_map/ppermute | solution.py:67
  77.0 8.6 %collective-permute-start.23 = (bf16[2,256,128]{2,1,0:T(8,128)(2,1)S(1)}, bf16[2,256,128]{2,1,0:T(8,128)(2,1)S(1)}, u32[]{:S(2)}, u32[]{:S(2)}) collective-permute-start(bf16[2,256,128]{2,1,0:T(8,128)(2,1)S(1)} %get-tuple-element.38), channel_id=1, source_target_pairs={{0,7},{1,2},{2,1},{3,4},{4,3},{5,6},{6,5},{7,0},{8,15},{9,10},{10,... | collective-permute-start | bytes 393224 | tf_op jit(solution)/shard_map/ppermute | solution.py:67
  78.0 12.4 %collective-permute-start.24 = (bf16[4,256,128]{2,1,0:T(8,128)(2,1)S(1)}, bf16[4,256,128]{2,1,0:T(8,128)(2,1)S(1)}, u32[]{:S(2)}, u32[]{:S(2)}) collective-permute-start(bf16[4,256,128]{2,1,0:T(8,128)(2,1)S(1)} %get-tuple-element.39), channel_id=1, source_target_pairs={{0,120},{1,121},{2,122},{3,123},{4,124},{5,125},{6,126},{7,127},{8... | collective-permute-start | bytes 786440 | tf_op jit(solution)/shard_map/ppermute | solution.py:67
  80.1 10.3 %collective-permute-start.25 = (bf16[4,256,128]{2,1,0:T(8,128)(2,1)S(1)}, bf16[4,256,128]{2,1,0:T(8,128)(2,1)S(1)}, u32[]{:S(2)}, u32[]{:S(2)}) collective-permute-start(bf16[4,256,128]{2,1,0:T(8,128)(2,1)S(1)} %get-tuple-element.40), channel_id=1, source_target_pairs={{0,8},{1,9},{2,10},{3,11},{4,12},{5,13},{6,14},{7,15},{8,0},{9,1},... | collective-permute-start | bytes 786440 | tf_op jit(solution)/shard_map/ppermute | solution.py:67
  80.8 9.8 %collective-permute-start.27 = (bf16[2,256,128]{2,1,0:T(8,128)(2,1)S(1)}, bf16[2,256,128]{2,1,0:T(8,128)(2,1)S(1)}, u32[]{:S(2)}, u32[]{:S(2)}) collective-permute-start(bf16[2,256,128]{2,1,0:T(8,128)(2,1)S(1)} %get-tuple-element.45), channel_id=1, source_target_pairs={{0,8},{1,9},{2,10},{3,11},{4,12},{5,13},{6,14},{7,15},{8,0},{9,1},... | collective-permute-start | bytes 393224 | tf_op jit(solution)/shard_map/ppermute | solution.py:67
  82.3 9.5 %collective-permute-start.26 = (bf16[2,256,128]{2,1,0:T(8,128)(2,1)S(1)}, bf16[2,256,128]{2,1,0:T(8,128)(2,1)S(1)}, u32[]{:S(2)}, u32[]{:S(2)}) collective-permute-start(bf16[2,256,128]{2,1,0:T(8,128)(2,1)S(1)} %get-tuple-element.46), channel_id=1, source_target_pairs={{0,120},{1,121},{2,122},{3,123},{4,124},{5,125},{6,126},{7,127},{8... | collective-permute-start | bytes 393224 | tf_op jit(solution)/shard_map/ppermute | solution.py:67

commit v2 on v0

v2 whole, which is shorter than its diff:
```python
import functools

import jax
import jax.numpy as jnp
from jax import lax
from jax.experimental import pallas as pl
from jax.experimental.pallas import tpu as pltpu
from jax.sharding import PartitionSpec as P

LEVELS = 4
BOTH = ("tx", "ty")
SIDE = 4
GRID = 6
PLANE = GRID * GRID
BLANK = 2 * PLANE
CORNERS = ((0, 0), (0, 3), (3, 0), (3, 3))
VMEM = pl.BlockSpec(memory_space=pltpu.VMEM)
SMEM = pl.BlockSpec(memory_space=pltpu.SMEM)
ANY = pl.BlockSpec(memory_space=pl.ANY)
PARAMS = pltpu.CompilerParams(vmem_limit_bytes=20 * 1024 * 1024)


def partner(at, size, kind):
    if kind == "in":
        return at ^ 1
    if kind == "out":
        return (at + 1) % size if at % 2 else (at - 1) % size
    return at


def swap(value, along_x, along_y):
    size_x, size_y = lax.axis_size("tx"), lax.axis_size("ty")
    pairs = [
        (x * size_y + y, partner(x, size_x, along_x) * size_y + partner(y, size_y, along_y))
        for x in range(size_x)
        for y in range(size_y)
    ]
    return lax.ppermute(value, BOTH, pairs)


def edges():
    odd_x = lax.rem(lax.axis_index("tx"), 2)
    odd_y = lax.rem(lax.axis_index("ty"), 2)
    return 3 * odd_x, 3 - 3 * odd_x, 3 * odd_y, 3 - 3 * odd_y


def exchange_edges(sends):
    tx_out, tx_in, ty_out, ty_in = sends
    return swap(tx_out, "out", None), swap(tx_in, "in", None), swap(ty_out, None, "out"), swap(ty_in, None, "in")


def exchange_corners(halo, odd_y):
    tx_out, tx_in = halo[:2]
    first = jnp.stack([tx_out[0], tx_in[0]])
    last = jnp.stack([tx_out[3], tx_in[3]])
    return swap(jnp.where(odd_y, last, first), None, "out"), swap(jnp.where(odd_y, first, last), None, "in")


def pack_kernel(earlier, tx_out, tx_in, ty_out, ty_in, sems):
    out_x, in_x, out_y, in_y = edges()
    copies = [
        pltpu.make_async_copy(earlier.at[out_x], tx_out, sems.at[0]),
        pltpu.make_async_copy(earlier.at[in_x], tx_in, sems.at[1]),
        pltpu.make_async_copy(earlier.at[:, out_y], ty_out, sems.at[2]),
        pltpu.make_async_copy(earlier.at[:, in_y], ty_in, sems.at[3]),
    ]
    for copy in copies:
        copy.start()
    for copy in copies:
        copy.wait()


def load_kernel(earlier, innovation, conditioner, chol_factor, plane, matrices, noise, shocks, factors, sems):
    copies = [
        pltpu.make_async_copy(innovation, shocks, sems.at[0]),
        pltpu.make_async_copy(chol_factor, factors, sems.at[1]),
        pltpu.make_async_copy(conditioner, matrices, sems.at[2]),
    ]
    copies += [
        pltpu.make_async_copy(earlier.at[x], plane.at[pl.ds((x + 1) * GRID + 1, SIDE)], sems.at[3 + x])
        for x in range(SIDE)
    ]
    for copy in copies:
        copy.start()
    plane[BLANK] = jnp.zeros(plane.shape[1:], plane.dtype)
    rows = lax.broadcasted_iota(jnp.int32, factors.shape[2:], 0)
    columns = lax.broadcasted_iota(jnp.int32, factors.shape[2:], 1)
    upper = rows <= columns
    copies[0].wait()
    copies[1].wait()

    def one_cell(cell, carry):
        x, y = cell // SIDE, cell % SIDE
        factor = jnp.where(upper, factors[x, y].astype(jnp.float32), 0.0).astype(jnp.bfloat16)
        noise[cell] = jnp.dot(shocks[x, y], factor, preferred_element_type=jnp.float32)
        return carry

    lax.fori_loop(0, SIDE * SIDE, one_cell, 0)
    for copy in copies[2:]:
        copy.wait()


def slot_of(code, x, y):
    old = (code >= 9).astype(jnp.int32)
    offset = code - 9 * old
    down = (offset >= 3).astype(jnp.int32) + (offset >= 6).astype(jnp.int32)
    return (x + down) * GRID + y + (offset - 3 * down) + PLANE * old


def main_kernel(section, levels, codes, plane_in, matrices, noise, tx_out, tx_in, ty_out, ty_in, plane, partial, *rest):
    base = PLANE if section else 0
    out_x, in_x, out_y, in_y = edges()
    for i in range(SIDE):
        plane[base + (out_x // 3) * 5 * GRID + i + 1] = tx_out[i]
        plane[base + (in_x // 3) * 5 * GRID + i + 1] = tx_in[i]
        plane[base + (i + 1) * GRID + (out_y // 3) * 5] = ty_out[i]
        plane[base + (i + 1) * GRID + (in_y // 3) * 5] = ty_in[i]
    late = tuple(base + row * GRID + column for row in (0, 5) for column in (0, 5))

    def one_cell(cell, carry):
        x, y = cell // SIDE, cell % SIDE

        @pl.when(levels[x, y] == section)
        def _():
            parts = []
            for k in range(8):
                slot = slot_of(codes[x, y, k], x, y)
                for corner in late:
                    slot = jnp.where(slot == corner, BLANK, slot)
                parts.append(plane[slot])
            summed = noise[cell] + jnp.dot(
                jnp.concatenate(parts, axis=1), matrices[x, y], preferred_element_type=jnp.float32
            )
            plane[PLANE + (x + 1) * GRID + y + 1] = summed.astype(jnp.bfloat16)
            at_corner = ((x == 0) | (x == 3)) & ((y == 0) | (y == 3))

            @pl.when(at_corner)
            def _():
                partial[(x // 3) * 2 + y // 3] = summed

        return carry

    lax.fori_loop(0, SIDE * SIDE, one_cell, 0)
    if rest:
        result, sems = rest
        copies = [
            pltpu.make_async_copy(
                plane.at[pl.ds(PLANE + (x + 1) * GRID + 1, SIDE)], result.at[x], sems.at[x]
            )
            for x in range(SIDE)
        ]
        for copy in copies:
            copy.start()
        for copy in copies:
            copy.wait()


def corner_kernel(section, levels, codes, plane_in, matrices, partial, far, near, *rest):
    if section == LEVELS - 1:
        result_in, plane, result, sems = rest
    else:
        plane, tx_out, tx_in, ty_out, ty_in = rest
    out_x, in_x, out_y, in_y = edges()
    for at, (x, y) in enumerate(CORNERS):
        side = jnp.where(out_x == x, 0, 1)
        code = 2 * x + 2 * y // 3 + 9 * (section > 0)
        late = (PLANE if section else 0) + (x // 3) * 5 * GRID + (y // 3) * 5
        outward = out_y == y

        def block():
            return jnp.where(outward, far[side], near[side])

        if section == 0:
            plane[late] = block()

        @pl.when(levels[x, y] == section)
        def _():
            for k in range(8):

                @pl.when(codes[x, y, k] == code)
                def _():
                    summed = partial[at] + jnp.dot(
                        block(), matrices[x, y, 128 * k : 128 * (k + 1)], preferred_element_type=jnp.float32
                    )
                    plane[PLANE + (x + 1) * GRID + y + 1] = summed.astype(jnp.bfloat16)

    if section == LEVELS - 1:
        copies = [
            pltpu.make_async_copy(plane.at[PLANE + (x + 1) * GRID + y + 1], result.at[x, y], sems.at[at])
            for at, (x, y) in enumerate(CORNERS)
        ]
        for copy in copies:
            copy.start()
        for copy in copies:
            copy.wait()
    else:
        for i in range(SIDE):
            tx_out[i] = plane[PLANE + (out_x + 1) * GRID + i + 1]
            tx_in[i] = plane[PLANE + (in_x + 1) * GRID + i + 1]
            ty_out[i] = plane[PLANE + (i + 1) * GRID + out_y + 1]
            ty_in[i] = plane[PLANE + (i + 1) * GRID + in_y + 1]


def local(earlier, innovation, conditioner, chol_factor, block_level, neighbours):
    block = earlier.shape[2:]
    odd_y = lax.rem(lax.axis_index("ty"), 2) == 1
    edge = jax.ShapeDtypeStruct((SIDE, *block), jnp.bfloat16)
    plane_shape = jax.ShapeDtypeStruct((BLANK + 1, *block), jnp.bfloat16)
    whole = jax.ShapeDtypeStruct(earlier.shape, jnp.bfloat16)
    sends = pl.pallas_call(
        pack_kernel,
        out_shape=[edge] * 4,
        in_specs=[ANY],
        out_specs=[VMEM] * 4,
        scratch_shapes=[pltpu.SemaphoreType.DMA((4,))],
        compiler_params=PARAMS,
        name="pack",
    )(earlier)
    plane, matrices, noise = pl.pallas_call(
        load_kernel,
        out_shape=[
            plane_shape,
            jax.ShapeDtypeStruct(conditioner.shape, jnp.bfloat16),
            jax.ShapeDtypeStruct((SIDE * SIDE, *block), jnp.float32),
        ],
        in_specs=[ANY] * 4,
        out_specs=[VMEM] * 3,
        scratch_shapes=[
            pltpu.VMEM(innovation.shape, jnp.bfloat16),
            pltpu.VMEM(chol_factor.shape, jnp.bfloat16),
            pltpu.SemaphoreType.DMA((7,)),
        ],
        compiler_params=PARAMS,
        cost_estimate=pl.CostEstimate(flops=2 * 16 * 256 * 128 * 128, bytes_accessed=14 << 20, transcendentals=0),
        name="load",
    )(earlier, innovation, conditioner, chol_factor)
    for section in range(LEVELS):
        final = section == LEVELS - 1
        halo = exchange_edges(sends)
        far, near = exchange_corners(halo, odd_y)
        plane, partial, *result = pl.pallas_call(
            functools.partial(main_kernel, section),
            out_shape=[plane_shape, jax.ShapeDtypeStruct((4, *block), jnp.float32)] + [whole] * final,
            in_specs=[SMEM] * 2 + [VMEM] * 7,
            out_specs=[VMEM] * 2 + [ANY] * final,
            scratch_shapes=[pltpu.SemaphoreType.DMA((4,))] * final,
            input_output_aliases={2: 0},
            compiler_params=PARAMS,
            cost_estimate=pl.CostEstimate(flops=8 * 2 * 256 * 1024 * 128, bytes_accessed=4 << 20, transcendentals=0),
            name=f"main_{section}",
        )(block_level, neighbours, plane, matrices, noise, *halo)
        plane, *sends = pl.pallas_call(
            functools.partial(corner_kernel, section),
            out_shape=[plane_shape] + ([whole] if final else [edge] * 4),
            in_specs=[SMEM] * 2 + [VMEM] * 5 + [ANY] * final,
            out_specs=[VMEM] + ([ANY] if final else [VMEM] * 4),
            scratch_shapes=[pltpu.SemaphoreType.DMA((4,))] * final,
            input_output_aliases={2: 0, 7: 1} if final else {2: 0},
            compiler_params=PARAMS,
            cost_estimate=pl.CostEstimate(flops=2 * 256 * 128 * 128, bytes_accessed=1 << 20, transcendentals=0),
            name=f"corner_{section}",
        )(block_level, neighbours, plane, matrices, partial, far, near, *result)
    return sends[0]


def solution(mesh):
    placed = (
        P("tx", "ty", None, None),
        P("tx", "ty", None, None),
        P("tx", "ty", None, None),
        P("tx", "ty", None, None),
        P("tx", "ty"),
        P("tx", "ty", None),
    )
    return jax.shard_map(
        local, mesh=mesh, in_specs=placed, out_specs=P("tx", "ty", None, None), check_vma=False
    )
```

time: 203 us -> 85.2 us (0.42)
  local copies, waits for them, and re-layouts: 70.6 us -> 6.98 us
  matrix products: 29.3 us -> 0 us
  other arithmetic: 26 us -> 0.11 us
  Pallas kernels: 0 us -> 18.4 us
  waiting for transfers between devices: 42.2 us -> 25.6 us
    gather x20 -> x0, local copies, waits for them, and re-layouts: 53.8 us -> none  [the longest x4 22 us: advance(): gathered = lookup[source_kind, row_index, col_index]]
    dot_general x8 -> x0, matrix products: 29.3 us -> none  [the longest x4 20.1 us: advance(): jnp.einsum('ckrb,ckbo->cro', gathered, matrices, preferred_element_type=j...]
    concatenate x11 -> x0, other arithmetic: 20.9 us -> none  [the longest x7 20.6 us: with_halo(): shard = jnp.concatenate([before, shard, after], axis=dim)]
    pallas_call x0 -> x10, Pallas kernels: none -> 18.4 us  [the longest x4 10.6 us: local(): pl.pallas_call(functools.partial(main_kernel, section), out_shape=[plane_...]
    ppermute x16 -> x24, waiting for transfers between devices: 42.2 us -> 25.6 us  [swap(): return lax.ppermute(value, BOTH, pairs)]
    scatter x4 -> x0, local copies, waits for them, and re-layouts: 7.09 us -> none  [advance(): window.reshape(tile_cells, realize, block_size).at[target]]
    unnamed x24 -> x14, local copies, waits for them, and re-layouts: 1.01 us -> 6.91 us
    slice x4 -> x8, local copies, waits for them, and re-layouts: 5.94 us -> 0.08 us  [exchange_corners(): last = jnp.stack([tx_out[3], tx_in[3]])]
  transfers between devices with their start and end apart: 16 -> 24, of which waited for: 4 -> 9; matrix products, arithmetic and copies ran while one was open for 23% -> 0% of each run, Pallas kernels for 0% -> 16%
where the time goes in v2:
time: 85.2 us; the launch traced here: 83.6 us
  starting transfers between devices  32.1 us (38%)
  waiting for transfers between devices  25.6 us (30%)
  Pallas kernels  18.4 us (22%)
  local copies, waits for them, and re-layouts  6.98 us (8%)
    ppermute x24, starting transfers between devices, swap(): return lax.ppermute(value, BOTH, pairs)  32.1 us
    ppermute x24, waiting for transfers between devices, swap(): return lax.ppermute(value, BOTH, pairs)  25.6 us
    pallas_call x4, Pallas kernels, local(): pl.pallas_call(functools.partial(main_kernel, section), out_shape=[plane_...  10.6 us
    unnamed x14, local copies, waits for them, and re-layouts  6.91 us
    pallas_call x4, Pallas kernels, local(): pl.pallas_call(functools.partial(corner_kernel, section), out_shape=[plan...  4.76 us
    pallas_call x1, Pallas kernels, local(): pl.pallas_call(load_kernel, out_shape=[plane_shape, jax.ShapeDtypeStruct(...  2.96 us
  transfers between devices with their start and end apart: 24, of which 9 were waited for; matrix products, arithmetic and copies ran while one was open for 0% of the time, Pallas kernels for 16%

profile of v2, /device:TPU:0, one launch (start us, length us, event | category | flops | bytes accessed | tf_op | source)
XLA Modules:
  0.0 83.6 jit_solution(7996755135131329768)
XLA Ops:
  0.0 1.2 %copy-done.1 = bf16[4,4,256,128]{3,2,1,0:T(8,128)(2,1)S(1)} copy-done((bf16[4,4,256,128]{3,2,1,0:T(8,128)(2,1)S(1)}, bf16[4,4,256,128]{3,2,1,0:T(8,128)(2,1)}, u32[]{:S(2)}) %copy-start.1) | copy-done | bytes 1048600
  1.4 1.7 %collective-permute-start.1 = (bf16[4,256,128]{2,1,0:T(8,128)(2,1)S(1)}, bf16[4,256,128]{2,1,0:T(8,128)(2,1)S(1)}, u32[]{:S(2)}, u32[]{:S(2)}) collective-permute-start(bf16[4,256,128]{2,1,0:T(8,128)(2,1)S(1)} %get-tuple-element.41), channel_id=1, source_target_pairs={{0,8},{1,9},{2,10},{3,11},{4,12},{5,13},{6,14},{7,15},{8,0},{9,1},... | collective-permute-start | bytes 786440 | tf_op jit(solution)/shard_map/ppermute | solution.py:38
  3.0 4.5 %collective-permute-start = (bf16[4,256,128]{2,1,0:T(8,128)(2,1)S(1)}, bf16[4,256,128]{2,1,0:T(8,128)(2,1)S(1)}, u32[]{:S(2)}, u32[]{:S(2)}) collective-permute-start(bf16[4,256,128]{2,1,0:T(8,128)(2,1)S(1)} %get-tuple-element.40), channel_id=1, source_target_pairs={{0,120},{1,121},{2,122},{3,123},{4,124},{5,125},{6,126},{7,127},{8... | collective-permute-start | bytes 786440 | tf_op jit(solution)/shard_map/ppermute | solution.py:38
  7.6 2.9 %collective-permute-start.2 = (bf16[4,256,128]{2,1,0:T(8,128)(2,1)S(1)}, bf16[4,256,128]{2,1,0:T(8,128)(2,1)S(1)}, u32[]{:S(2)}, u32[]{:S(2)}) collective-permute-start(bf16[4,256,128]{2,1,0:T(8,128)(2,1)S(1)} %get-tuple-element.42), channel_id=1, source_target_pairs={{0,7},{1,2},{2,1},{3,4},{4,3},{5,6},{6,5},{7,0},{8,15},{9,10},{10,... | collective-permute-start | bytes 786440 | tf_op jit(solution)/shard_map/ppermute | solution.py:38
  10.5 3.6 %collective-permute-done.tx_out = bf16[4,256,128]{2,1,0:T(8,128)(2,1)S(1)} collective-permute-done((bf16[4,256,128]{2,1,0:T(8,128)(2,1)S(1)}, bf16[4,256,128]{2,1,0:T(8,128)(2,1)S(1)}, u32[]{:S(2)}, u32[]{:S(2)}) %collective-permute-start) | collective-permute-done | bytes 262176 | tf_op jit(solution)/shard_map/ppermute | solution.py:38
  14.1 2.4 %collective-permute-start.4 = (bf16[2,256,128]{2,1,0:T(8,128)(2,1)S(1)}, bf16[2,256,128]{2,1,0:T(8,128)(2,1)S(1)}, u32[]{:S(2)}, u32[]{:S(2)}) collective-permute-start(bf16[2,256,128]{2,1,0:T(8,128)(2,1)S(1)} %get-tuple-element.88), channel_id=1, source_target_pairs={{0,7},{1,2},{2,1},{3,4},{4,3},{5,6},{6,5},{7,0},{8,15},{9,10},{10,... | collective-permute-start | bytes 393224 | tf_op jit(solution)/shard_map/ppermute | solution.py:38
  16.5 2.2 %copy-done = bf16[4,4,1024,128]{3,2,1,0:T(8,128)(2,1)S(1)} copy-done((bf16[4,4,1024,128]{3,2,1,0:T(8,128)(2,1)S(1)}, bf16[4,4,1024,128]{3,2,1,0:T(8,128)(2,1)}, u32[]{:S(2)}) %copy-start) | copy-done | bytes 4194328
  18.7 1.2 %copy-done.2 = bf16[4,4,256,128]{3,2,1,0:T(8,128)(2,1)S(1)} copy-done((bf16[4,4,256,128]{3,2,1,0:T(8,128)(2,1)S(1)}, bf16[4,4,256,128]{3,2,1,0:T(8,128)(2,1)}, u32[]{:S(2)}) %copy-start.2) | copy-done | bytes 1048600
  19.9 1.2 %copy-done.3 = bf16[4,4,256,128]{3,2,1,0:T(8,128)(2,1)S(1)} copy-done((bf16[4,4,256,128]{3,2,1,0:T(8,128)(2,1)S(1)}, bf16[4,4,256,128]{3,2,1,0:T(8,128)(2,1)}, u32[]{:S(2)}) %copy-start.3) | copy-done | bytes 1048600
  21.2 1.0 %copy-done.4 = bf16[4,4,128,128]{3,2,1,0:T(8,128)(2,1)S(1)} copy-done((bf16[4,4,128,128]{3,2,1,0:T(8,128)(2,1)S(1)}, bf16[4,4,128,128]{3,2,1,0:T(8,128)(2,1)}, u32[]{:S(2)}) %copy-start.4) | copy-done | bytes 524312
  22.2 3.0 %load.1 = (bf16[73,256,128]{2,1,0:T(8,128)(2,1)S(1)}, bf16[4,4,1024,128]{3,2,1,0:T(8,128)(2,1)S(1)}, f32[16,256,128]{2,1,0:T(8,128)S(1)}) custom-call(bf16[4,4,256,128]{3,2,1,0:T(8,128)(2,1)S(1)} %copy-done.2, bf16[4,4,256,128]{3,2,1,0:T(8,128)(2,1)S(1)} %copy-done.3, bf16[4,4,1024,128]{3,2,1,0:T(8,128)(2,1)S(1)} %copy-done, ...), custom_call_target="tpu_custom_call" | custom-call | flops 134217728 | bytes 14680064 | tf_op jit(solution)/shard_map/load/pallas_call | solution.py:219
  25.2 3.7 %main_0.1 = (bf16[73,256,128]{2,1,0:T(8,128)(2,1)S(1)}, f32[4,256,128]{2,1,0:T(8,128)S(1)}) custom-call(s32[4,4]{1,0:T(4,128)S(1)} %copy-done.6, s32[4,4,8]{2,1,0:T(4,128)S(1)} %copy-done.5, bf16[73,256,128]{2,1,0:T(8,128)(2,1)S(1)} %get-tuple-element.37.plane_in, ...), custom_call_target="tpu_custom_call", output_to_operand_aliasing={{0}: (2, {})} | custom-call | flops 536870912 | bytes 4194304 | tf_op jit(solution)/shard_map/main_0/pallas_call | solution.py:241
  28.9 1.1 %corner_0.1 = (bf16[73,256,128]{2,1,0:T(8,128)(2,1)S(1)}, bf16[4,256,128]{2,1,0:T(8,128)(2,1)S(1)}, bf16[4,256,128]{2,1,0:T(8,128)(2,1)S(1)}, bf16[4,256,128]{2,1,0:T(8,128)(2,1)S(1)}, bf16[4,256,128]{2,1,0:T(8,128)(2,1)S(1)}) custom-call(s32[4,4]{1,0:T(4,128)S(1)} %copy-done.6, s32[4,4,8]{2,1,0:T(4,128)S(1)} %copy-done.5, ...), custom_call_target="tpu_custom_call", output_to_operand_aliasing={{0}: (2, {})} | custom-call | flops 8388608 | bytes 1048576 | tf_op jit(solution)/shard_map/corner_0/pallas_call | solution.py:252
  30.1 3.8 %collective-permute-start.6 = (bf16[4,256,128]{2,1,0:T(8,128)(2,1)S(1)}, bf16[4,256,128]{2,1,0:T(8,128)(2,1)S(1)}, u32[]{:S(2)}, u32[]{:S(2)}) collective-permute-start(bf16[4,256,128]{2,1,0:T(8,128)(2,1)S(1)} %get-tuple-element.47), channel_id=1, source_target_pairs={{0,120},{1,121},{2,122},{3,123},{4,124},{5,125},{6,126},{7,127},{8... | collective-permute-start | bytes 786440 | tf_op jit(solution)/shard_map/ppermute | solution.py:38
  34.3 0.9 %collective-permute-start.9 = (bf16[4,256,128]{2,1,0:T(8,128)(2,1)S(1)}, bf16[4,256,128]{2,1,0:T(8,128)(2,1)S(1)}, u32[]{:S(2)}, u32[]{:S(2)}) collective-permute-start(bf16[4,256,128]{2,1,0:T(8,128)(2,1)S(1)} %get-tuple-element.50), channel_id=1, source_target_pairs={{0,1},{1,0},{2,3},{3,2},{4,5},{5,4},{6,7},{7,6},{8,9},{9,8},{10,11... | collective-permute-start | bytes 786440 | tf_op jit(solution)/shard_map/ppermute | solution.py:38
  35.2 2.3 %collective-permute-done.7.tx_in = bf16[4,256,128]{2,1,0:T(8,128)(2,1)S(1)} collective-permute-done((bf16[4,256,128]{2,1,0:T(8,128)(2,1)S(1)}, bf16[4,256,128]{2,1,0:T(8,128)(2,1)S(1)}, u32[]{:S(2)}, u32[]{:S(2)}) %collective-permute-start.7) | collective-permute-done | bytes 262176 | tf_op jit(solution)/shard_map/ppermute | solution.py:38
  37.5 4.1 %collective-permute-done.6.tx_out = bf16[4,256,128]{2,1,0:T(8,128)(2,1)S(1)} collective-permute-done((bf16[4,256,128]{2,1,0:T(8,128)(2,1)S(1)}, bf16[4,256,128]{2,1,0:T(8,128)(2,1)S(1)}, u32[]{:S(2)}, u32[]{:S(2)}) %collective-permute-start.6) | collective-permute-done | bytes 262176 | tf_op jit(solution)/shard_map/ppermute | solution.py:38
  42.0 1.5 %main_1.1 = (bf16[73,256,128]{2,1,0:T(8,128)(2,1)S(1)}, f32[4,256,128]{2,1,0:T(8,128)S(1)}) custom-call(s32[4,4]{1,0:T(4,128)S(1)} %copy-done.6, s32[4,4,8]{2,1,0:T(4,128)S(1)} %copy-done.5, bf16[73,256,128]{2,1,0:T(8,128)(2,1)S(1)} %get-tuple-element.46.plane_in, ...), custom_call_target="tpu_custom_call", output_to_operand_aliasing={{0}: (2, {})} | custom-call | flops 536870912 | bytes 4194304 | tf_op jit(solution)/shard_map/main_1/pallas_call | solution.py:241
  43.4 4.0 %collective-permute-done.10.far = bf16[2,256,128]{2,1,0:T(8,128)(2,1)S(1)} collective-permute-done((bf16[2,256,128]{2,1,0:T(8,128)(2,1)S(1)}, bf16[2,256,128]{2,1,0:T(8,128)(2,1)S(1)}, u32[]{:S(2)}, u32[]{:S(2)}) %collective-permute-start.10) | collective-permute-done | bytes 131104 | tf_op jit(solution)/shard_map/ppermute | solution.py:38
  48.3 4.6 %collective-permute-start.12 = (bf16[4,256,128]{2,1,0:T(8,128)(2,1)S(1)}, bf16[4,256,128]{2,1,0:T(8,128)(2,1)S(1)}, u32[]{:S(2)}, u32[]{:S(2)}) collective-permute-start(bf16[4,256,128]{2,1,0:T(8,128)(2,1)S(1)} %get-tuple-element.54), channel_id=1, source_target_pairs={{0,120},{1,121},{2,122},{3,123},{4,124},{5,125},{6,126},{7,127},{8... | collective-permute-start | bytes 786440 | tf_op jit(solution)/shard_map/ppermute | solution.py:38
  53.1 1.5 %collective-permute-done.13.tx_in = bf16[4,256,128]{2,1,0:T(8,128)(2,1)S(1)} collective-permute-done((bf16[4,256,128]{2,1,0:T(8,128)(2,1)S(1)}, bf16[4,256,128]{2,1,0:T(8,128)(2,1)S(1)}, u32[]{:S(2)}, u32[]{:S(2)}) %collective-permute-start.13) | collective-permute-done | bytes 262176 | tf_op jit(solution)/shard_map/ppermute | solution.py:38
  54.7 3.9 %collective-permute-done.12.tx_out = bf16[4,256,128]{2,1,0:T(8,128)(2,1)S(1)} collective-permute-done((bf16[4,256,128]{2,1,0:T(8,128)(2,1)S(1)}, bf16[4,256,128]{2,1,0:T(8,128)(2,1)S(1)}, u32[]{:S(2)}, u32[]{:S(2)}) %collective-permute-start.12) | collective-permute-done | bytes 262176 | tf_op jit(solution)/shard_map/ppermute | solution.py:38
  59.1 1.1 %collective-permute-start.17 = (bf16[2,256,128]{2,1,0:T(8,128)(2,1)S(1)}, bf16[2,256,128]{2,1,0:T(8,128)(2,1)S(1)}, u32[]{:S(2)}, u32[]{:S(2)}) collective-permute-start(bf16[2,256,128]{2,1,0:T(8,128)(2,1)S(1)} %get-tuple-element.75), channel_id=1, source_target_pairs={{0,1},{1,0},{2,3},{3,2},{4,5},{5,4},{6,7},{7,6},{8,9},{9,8},{10,11... | collective-permute-start | bytes 393224 | tf_op jit(solution)/shard_map/ppermute | solution.py:38
  60.2 2.1 %main_2.1 = (bf16[73,256,128]{2,1,0:T(8,128)(2,1)S(1)}, f32[4,256,128]{2,1,0:T(8,128)S(1)}) custom-call(s32[4,4]{1,0:T(4,128)S(1)} %copy-done.6, s32[4,4,8]{2,1,0:T(4,128)S(1)} %copy-done.5, bf16[73,256,128]{2,1,0:T(8,128)(2,1)S(1)} %get-tuple-element.53.plane_in, ...), custom_call_target="tpu_custom_call", output_to_operand_aliasing={{0}: (2, {})} | custom-call | flops 536870912 | bytes 4194304 | tf_op jit(solution)/shard_map/main_2/pallas_call | solution.py:241
  62.3 1.9 %collective-permute-done.16.far = bf16[2,256,128]{2,1,0:T(8,128)(2,1)S(1)} collective-permute-done((bf16[2,256,128]{2,1,0:T(8,128)(2,1)S(1)}, bf16[2,256,128]{2,1,0:T(8,128)(2,1)S(1)}, u32[]{:S(2)}, u32[]{:S(2)}) %collective-permute-start.16) | collective-permute-done | bytes 131104 | tf_op jit(solution)/shard_map/ppermute | solution.py:38
  64.3 1.0 %corner_2.1 = (bf16[73,256,128]{2,1,0:T(8,128)(2,1)S(1)}, bf16[4,256,128]{2,1,0:T(8,128)(2,1)S(1)}, bf16[4,256,128]{2,1,0:T(8,128)(2,1)S(1)}, bf16[4,256,128]{2,1,0:T(8,128)(2,1)S(1)}, bf16[4,256,128]{2,1,0:T(8,128)(2,1)S(1)}) custom-call(s32[4,4]{1,0:T(4,128)S(1)} %copy-done.6, s32[4,4,8]{2,1,0:T(4,128)S(1)} %copy-done.5, ...), custom_call_target="tpu_custom_call", output_to_operand_aliasing={{0}: (2, {})} | custom-call | flops 8388608 | bytes 1048576 | tf_op jit(solution)/shard_map/corner_2/pallas_call | solution.py:252
  65.4 4.9 %collective-permute-start.18 = (bf16[4,256,128]{2,1,0:T(8,128)(2,1)S(1)}, bf16[4,256,128]{2,1,0:T(8,128)(2,1)S(1)}, u32[]{:S(2)}, u32[]{:S(2)}) collective-permute-start(bf16[4,256,128]{2,1,0:T(8,128)(2,1)S(1)} %get-tuple-element.61), channel_id=1, source_target_pairs={{0,120},{1,121},{2,122},{3,123},{4,124},{5,125},{6,126},{7,127},{8... | collective-permute-start | bytes 786440 | tf_op jit(solution)/shard_map/ppermute | solution.py:38
  70.3 0.9 %collective-permute-start.20 = (bf16[4,256,128]{2,1,0:T(8,128)(2,1)S(1)}, bf16[4,256,128]{2,1,0:T(8,128)(2,1)S(1)}, u32[]{:S(2)}, u32[]{:S(2)}) collective-permute-start(bf16[4,256,128]{2,1,0:T(8,128)(2,1)S(1)} %get-tuple-element.63), channel_id=1, source_target_pairs={{0,7},{1,2},{2,1},{3,4},{4,3},{5,6},{6,5},{7,0},{8,15},{9,10},{10,... | collective-permute-start | bytes 786440 | tf_op jit(solution)/shard_map/ppermute | solution.py:38
  72.3 3.5 %collective-permute-done.18.tx_out = bf16[4,256,128]{2,1,0:T(8,128)(2,1)S(1)} collective-permute-done((bf16[4,256,128]{2,1,0:T(8,128)(2,1)S(1)}, bf16[4,256,128]{2,1,0:T(8,128)(2,1)S(1)}, u32[]{:S(2)}, u32[]{:S(2)}) %collective-permute-start.18) | collective-permute-done | bytes 262176 | tf_op jit(solution)/shard_map/ppermute | solution.py:38
  75.9 1.5 %collective-permute-start.22 = (bf16[2,256,128]{2,1,0:T(8,128)(2,1)S(1)}, bf16[2,256,128]{2,1,0:T(8,128)(2,1)S(1)}, u32[]{:S(2)}, u32[]{:S(2)}) collective-permute-start(bf16[2,256,128]{2,1,0:T(8,128)(2,1)S(1)} %get-tuple-element.70), channel_id=1, source_target_pairs={{0,7},{1,2},{2,1},{3,4},{4,3},{5,6},{6,5},{7,0},{8,15},{9,10},{10,... | collective-permute-start | bytes 393224 | tf_op jit(solution)/shard_map/ppermute | solution.py:38
  78.2 3.4 %main_3.1 = (bf16[73,256,128]{2,1,0:T(8,128)(2,1)S(1)}, f32[4,256,128]{2,1,0:T(8,128)S(1)}, bf16[4,4,256,128]{3,2,1,0:T(8,128)(2,1)}) custom-call(s32[4,4]{1,0:T(4,128)S(1)} %copy-done.6, s32[4,4,8]{2,1,0:T(4,128)S(1)} %copy-done.5, bf16[73,256,128]{2,1,0:T(8,128)(2,1)S(1)} %get-tuple-element.60.plane_in, ...), custom_call_target="tpu_custom_call", output_to_operand_aliasing={{0}: (2, {})} | custom-call | flops 536870912 | bytes 4194304 | tf_op jit(solution)/shard_map/main_3/pallas_call | solution.py:241
  81.6 1.9 %corner_3.1 = (bf16[73,256,128]{2,1,0:T(8,128)(2,1)S(1)}, bf16[4,4,256,128]{3,2,1,0:T(8,128)(2,1)}) custom-call(s32[4,4]{1,0:T(4,128)S(1)} %copy-done.6, s32[4,4,8]{2,1,0:T(4,128)S(1)} %copy-done.5, bf16[73,256,128]{2,1,0:T(8,128)(2,1)S(1)} %get-tuple-element.65.plane_in, ...), custom_call_target="tpu_custom_call", output_to_operand_aliasing={{0}: (2, {}), {1}: (7, {})} | custom-call | flops 8388608 | bytes 1048576 | tf_op jit(solution)/shard_map/corner_3/pallas_call | solution.py:252
  (52 shorter events, 4.7 us)
Async XLA Ops:
  0.0 1.2 %copy-start.1 = (bf16[4,4,256,128]{3,2,1,0:T(8,128)(2,1)S(1)}, bf16[4,4,256,128]{3,2,1,0:T(8,128)(2,1)}, u32[]{:S(2)}) copy-start(bf16[4,4,256,128]{3,2,1,0:T(8,128)(2,1)} %earlier.3) | copy-start | bytes 3145732
  1.2 24.0 %copy-start.5 = (s32[4,4,8]{2,1,0:T(4,128)S(1)}, s32[4,4,8]{2,1,0:T(4,128)}, u32[]{:S(2)}) copy-start(s32[4,4,8]{2,1,0:T(4,128)} %codes.15) | copy-start | bytes 1540
  1.2 24.0 %copy-start.6 = (s32[4,4]{1,0:T(4,128)S(1)}, s32[4,4]{1,0:T(4,128)}, u32[]{:S(2)}) copy-start(s32[4,4]{1,0:T(4,128)} %levels.15) | copy-start | bytes 196
  1.4 9.1 %collective-permute-start.1 = (bf16[4,256,128]{2,1,0:T(8,128)(2,1)S(1)}, bf16[4,256,128]{2,1,0:T(8,128)(2,1)S(1)}, u32[]{:S(2)}, u32[]{:S(2)}) collective-permute-start(bf16[4,256,128]{2,1,0:T(8,128)(2,1)S(1)} %get-tuple-element.41), channel_id=1, source_target_pairs={{0,8},{1,9},{2,10},{3,11},{4,12},{5,13},{6,14},{7,15},{8,0},{9,1},... | collective-permute-start | bytes 786440 | tf_op jit(solution)/shard_map/ppermute | solution.py:38
  3.0 11.1 %collective-permute-start = (bf16[4,256,128]{2,1,0:T(8,128)(2,1)S(1)}, bf16[4,256,128]{2,1,0:T(8,128)(2,1)S(1)}, u32[]{:S(2)}, u32[]{:S(2)}) collective-permute-start(bf16[4,256,128]{2,1,0:T(8,128)(2,1)S(1)} %get-tuple-element.40), channel_id=1, source_target_pairs={{0,120},{1,121},{2,122},{3,123},{4,124},{5,125},{6,126},{7,127},{8... | collective-permute-start | bytes 786440 | tf_op jit(solution)/shard_map/ppermute | solution.py:38
  7.6 17.6 %collective-permute-start.2 = (bf16[4,256,128]{2,1,0:T(8,128)(2,1)S(1)}, bf16[4,256,128]{2,1,0:T(8,128)(2,1)S(1)}, u32[]{:S(2)}, u32[]{:S(2)}) collective-permute-start(bf16[4,256,128]{2,1,0:T(8,128)(2,1)S(1)} %get-tuple-element.42), channel_id=1, source_target_pairs={{0,7},{1,2},{2,1},{3,4},{4,3},{5,6},{6,5},{7,0},{8,15},{9,10},{10,... | collective-permute-start | bytes 786440 | tf_op jit(solution)/shard_map/ppermute | solution.py:38
  10.5 14.7 %collective-permute-start.3 = (bf16[4,256,128]{2,1,0:T(8,128)(2,1)S(1)}, bf16[4,256,128]{2,1,0:T(8,128)(2,1)S(1)}, u32[]{:S(2)}, u32[]{:S(2)}) collective-permute-start(bf16[4,256,128]{2,1,0:T(8,128)(2,1)S(1)} %get-tuple-element.43), channel_id=1, source_target_pairs={{0,1},{1,0},{2,3},{3,2},{4,5},{5,4},{6,7},{7,6},{8,9},{9,8},{10,11... | collective-permute-start | bytes 786440 | tf_op jit(solution)/shard_map/ppermute | solution.py:38
  14.1 14.7 %collective-permute-start.4 = (bf16[2,256,128]{2,1,0:T(8,128)(2,1)S(1)}, bf16[2,256,128]{2,1,0:T(8,128)(2,1)S(1)}, u32[]{:S(2)}, u32[]{:S(2)}) collective-permute-start(bf16[2,256,128]{2,1,0:T(8,128)(2,1)S(1)} %get-tuple-element.88), channel_id=1, source_target_pairs={{0,7},{1,2},{2,1},{3,4},{4,3},{5,6},{6,5},{7,0},{8,15},{9,10},{10,... | collective-permute-start | bytes 393224 | tf_op jit(solution)/shard_map/ppermute | solution.py:38
  16.5 12.4 %collective-permute-start.5 = (bf16[2,256,128]{2,1,0:T(8,128)(2,1)S(1)}, bf16[2,256,128]{2,1,0:T(8,128)(2,1)S(1)}, u32[]{:S(2)}, u32[]{:S(2)}) collective-permute-start(bf16[2,256,128]{2,1,0:T(8,128)(2,1)S(1)} %get-tuple-element.87), channel_id=1, source_target_pairs={{0,1},{1,0},{2,3},{3,2},{4,5},{5,4},{6,7},{7,6},{8,9},{9,8},{10,11... | collective-permute-start | bytes 393224 | tf_op jit(solution)/shard_map/ppermute | solution.py:38
  16.5 2.2 %copy-start = (bf16[4,4,1024,128]{3,2,1,0:T(8,128)(2,1)S(1)}, bf16[4,4,1024,128]{3,2,1,0:T(8,128)(2,1)}, u32[]{:S(2)}) copy-start(bf16[4,4,1024,128]{3,2,1,0:T(8,128)(2,1)} %conditioner.1) | copy-start | bytes 12582916
  18.7 1.2 %copy-start.2 = (bf16[4,4,256,128]{3,2,1,0:T(8,128)(2,1)S(1)}, bf16[4,4,256,128]{3,2,1,0:T(8,128)(2,1)}, u32[]{:S(2)}) copy-start(bf16[4,4,256,128]{3,2,1,0:T(8,128)(2,1)} %earlier.3) | copy-start | bytes 3145732
  19.9 1.2 %copy-start.3 = (bf16[4,4,256,128]{3,2,1,0:T(8,128)(2,1)S(1)}, bf16[4,4,256,128]{3,2,1,0:T(8,128)(2,1)}, u32[]{:S(2)}) copy-start(bf16[4,4,256,128]{3,2,1,0:T(8,128)(2,1)} %innovation.1) | copy-start | bytes 3145732
  21.2 1.0 %copy-start.4 = (bf16[4,4,128,128]{3,2,1,0:T(8,128)(2,1)S(1)}, bf16[4,4,128,128]{3,2,1,0:T(8,128)(2,1)}, u32[]{:S(2)}) copy-start(bf16[4,4,128,128]{3,2,1,0:T(8,128)(2,1)} %chol_factor.1) | copy-start | bytes 1572868
  30.0 7.6 %collective-permute-start.7 = (bf16[4,256,128]{2,1,0:T(8,128)(2,1)S(1)}, bf16[4,256,128]{2,1,0:T(8,128)(2,1)S(1)}, u32[]{:S(2)}, u32[]{:S(2)}) collective-permute-start(bf16[4,256,128]{2,1,0:T(8,128)(2,1)S(1)} %get-tuple-element.48), channel_id=1, source_target_pairs={{0,8},{1,9},{2,10},{3,11},{4,12},{5,13},{6,14},{7,15},{8,0},{9,1},... | collective-permute-start | bytes 786440 | tf_op jit(solution)/shard_map/ppermute | solution.py:38
  30.1 11.6 %collective-permute-start.6 = (bf16[4,256,128]{2,1,0:T(8,128)(2,1)S(1)}, bf16[4,256,128]{2,1,0:T(8,128)(2,1)S(1)}, u32[]{:S(2)}, u32[]{:S(2)}) collective-permute-start(bf16[4,256,128]{2,1,0:T(8,128)(2,1)S(1)} %get-tuple-element.47), channel_id=1, source_target_pairs={{0,120},{1,121},{2,122},{3,123},{4,124},{5,125},{6,126},{7,127},{8... | collective-permute-start | bytes 786440 | tf_op jit(solution)/shard_map/ppermute | solution.py:38
  33.9 8.1 %collective-permute-start.8 = (bf16[4,256,128]{2,1,0:T(8,128)(2,1)S(1)}, bf16[4,256,128]{2,1,0:T(8,128)(2,1)S(1)}, u32[]{:S(2)}, u32[]{:S(2)}) collective-permute-start(bf16[4,256,128]{2,1,0:T(8,128)(2,1)S(1)} %get-tuple-element.49), channel_id=1, source_target_pairs={{0,7},{1,2},{2,1},{3,4},{4,3},{5,6},{6,5},{7,0},{8,15},{9,10},{10,... | collective-permute-start | bytes 786440 | tf_op jit(solution)/shard_map/ppermute | solution.py:38
  34.3 7.7 %collective-permute-start.9 = (bf16[4,256,128]{2,1,0:T(8,128)(2,1)S(1)}, bf16[4,256,128]{2,1,0:T(8,128)(2,1)S(1)}, u32[]{:S(2)}, u32[]{:S(2)}) collective-permute-start(bf16[4,256,128]{2,1,0:T(8,128)(2,1)S(1)} %get-tuple-element.50), channel_id=1, source_target_pairs={{0,1},{1,0},{2,3},{3,2},{4,5},{5,4},{6,7},{7,6},{8,9},{9,8},{10,11... | collective-permute-start | bytes 786440 | tf_op jit(solution)/shard_map/ppermute | solution.py:38
  41.7 5.7 %collective-permute-start.10 = (bf16[2,256,128]{2,1,0:T(8,128)(2,1)S(1)}, bf16[2,256,128]{2,1,0:T(8,128)(2,1)S(1)}, u32[]{:S(2)}, u32[]{:S(2)}) collective-permute-start(bf16[2,256,128]{2,1,0:T(8,128)(2,1)S(1)} %get-tuple-element.82), channel_id=1, source_target_pairs={{0,7},{1,2},{2,1},{3,4},{4,3},{5,6},{6,5},{7,0},{8,15},{9,10},{10,... | collective-permute-start | bytes 393224 | tf_op jit(solution)/shard_map/ppermute | solution.py:38
  41.8 5.6 %collective-permute-start.11 = (bf16[2,256,128]{2,1,0:T(8,128)(2,1)S(1)}, bf16[2,256,128]{2,1,0:T(8,128)(2,1)S(1)}, u32[]{:S(2)}, u32[]{:S(2)}) collective-permute-start(bf16[2,256,128]{2,1,0:T(8,128)(2,1)S(1)} %get-tuple-element.81), channel_id=1, source_target_pairs={{0,1},{1,0},{2,3},{3,2},{4,5},{5,4},{6,7},{7,6},{8,9},{9,8},{10,11... | collective-permute-start | bytes 393224 | tf_op jit(solution)/shard_map/ppermute | solution.py:38
  48.2 6.5 %collective-permute-start.13 = (bf16[4,256,128]{2,1,0:T(8,128)(2,1)S(1)}, bf16[4,256,128]{2,1,0:T(8,128)(2,1)S(1)}, u32[]{:S(2)}, u32[]{:S(2)}) collective-permute-start(bf16[4,256,128]{2,1,0:T(8,128)(2,1)S(1)} %get-tuple-element.55), channel_id=1, source_target_pairs={{0,8},{1,9},{2,10},{3,11},{4,12},{5,13},{6,14},{7,15},{8,0},{9,1},... | collective-permute-start | bytes 786440 | tf_op jit(solution)/shard_map/ppermute | solution.py:38
  48.3 10.2 %collective-permute-start.12 = (bf16[4,256,128]{2,1,0:T(8,128)(2,1)S(1)}, bf16[4,256,128]{2,1,0:T(8,128)(2,1)S(1)}, u32[]{:S(2)}, u32[]{:S(2)}) collective-permute-start(bf16[4,256,128]{2,1,0:T(8,128)(2,1)S(1)} %get-tuple-element.54), channel_id=1, source_target_pairs={{0,120},{1,121},{2,122},{3,123},{4,124},{5,125},{6,126},{7,127},{8... | collective-permute-start | bytes 786440 | tf_op jit(solution)/shard_map/ppermute | solution.py:38
  52.9 7.4 %collective-permute-start.14 = (bf16[4,256,128]{2,1,0:T(8,128)(2,1)S(1)}, bf16[4,256,128]{2,1,0:T(8,128)(2,1)S(1)}, u32[]{:S(2)}, u32[]{:S(2)}) collective-permute-start(bf16[4,256,128]{2,1,0:T(8,128)(2,1)S(1)} %get-tuple-element.56), channel_id=1, source_target_pairs={{0,7},{1,2},{2,1},{3,4},{4,3},{5,6},{6,5},{7,0},{8,15},{9,10},{10,... | collective-permute-start | bytes 786440 | tf_op jit(solution)/shard_map/ppermute | solution.py:38
  52.9 7.4 %collective-permute-start.15 = (bf16[4,256,128]{2,1,0:T(8,128)(2,1)S(1)}, bf16[4,256,128]{2,1,0:T(8,128)(2,1)S(1)}, u32[]{:S(2)}, u32[]{:S(2)}) collective-permute-start(bf16[4,256,128]{2,1,0:T(8,128)(2,1)S(1)} %get-tuple-element.57), channel_id=1, source_target_pairs={{0,1},{1,0},{2,3},{3,2},{4,5},{5,4},{6,7},{7,6},{8,9},{9,8},{10,11... | collective-permute-start | bytes 786440 | tf_op jit(solution)/shard_map/ppermute | solution.py:38
  58.6 5.7 %collective-permute-start.16 = (bf16[2,256,128]{2,1,0:T(8,128)(2,1)S(1)}, bf16[2,256,128]{2,1,0:T(8,128)(2,1)S(1)}, u32[]{:S(2)}, u32[]{:S(2)}) collective-permute-start(bf16[2,256,128]{2,1,0:T(8,128)(2,1)S(1)} %get-tuple-element.76), channel_id=1, source_target_pairs={{0,7},{1,2},{2,1},{3,4},{4,3},{5,6},{6,5},{7,0},{8,15},{9,10},{10,... | collective-permute-start | bytes 393224 | tf_op jit(solution)/shard_map/ppermute | solution.py:38
  59.1 5.1 %collective-permute-start.17 = (bf16[2,256,128]{2,1,0:T(8,128)(2,1)S(1)}, bf16[2,256,128]{2,1,0:T(8,128)(2,1)S(1)}, u32[]{:S(2)}, u32[]{:S(2)}) collective-permute-start(bf16[2,256,128]{2,1,0:T(8,128)(2,1)S(1)} %get-tuple-element.75), channel_id=1, source_target_pairs={{0,1},{1,0},{2,3},{3,2},{4,5},{5,4},{6,7},{7,6},{8,9},{9,8},{10,11... | collective-permute-start | bytes 393224 | tf_op jit(solution)/shard_map/ppermute | solution.py:38
  65.3 7.0 %collective-permute-start.19 = (bf16[4,256,128]{2,1,0:T(8,128)(2,1)S(1)}, bf16[4,256,128]{2,1,0:T(8,128)(2,1)S(1)}, u32[]{:S(2)}, u32[]{:S(2)}) collective-permute-start(bf16[4,256,128]{2,1,0:T(8,128)(2,1)S(1)} %get-tuple-element.62), channel_id=1, source_target_pairs={{0,8},{1,9},{2,10},{3,11},{4,12},{5,13},{6,14},{7,15},{8,0},{9,1},... | collective-permute-start | bytes 786440 | tf_op jit(solution)/shard_map/ppermute | solution.py:38
  65.4 10.5 %collective-permute-start.18 = (bf16[4,256,128]{2,1,0:T(8,128)(2,1)S(1)}, bf16[4,256,128]{2,1,0:T(8,128)(2,1)S(1)}, u32[]{:S(2)}, u32[]{:S(2)}) collective-permute-start(bf16[4,256,128]{2,1,0:T(8,128)(2,1)S(1)} %get-tuple-element.61), channel_id=1, source_target_pairs={{0,120},{1,121},{2,122},{3,123},{4,124},{5,125},{6,126},{7,127},{8... | collective-permute-start | bytes 786440 | tf_op jit(solution)/shard_map/ppermute | solution.py:38
  70.3 7.8 %collective-permute-start.20 = (bf16[4,256,128]{2,1,0:T(8,128)(2,1)S(1)}, bf16[4,256,128]{2,1,0:T(8,128)(2,1)S(1)}, u32[]{:S(2)}, u32[]{:S(2)}) collective-permute-start(bf16[4,256,128]{2,1,0:T(8,128)(2,1)S(1)} %get-tuple-element.63), channel_id=1, source_target_pairs={{0,7},{1,2},{2,1},{3,4},{4,3},{5,6},{6,5},{7,0},{8,15},{9,10},{10,... | collective-permute-start | bytes 786440 | tf_op jit(solution)/shard_map/ppermute | solution.py:38
  71.2 6.9 %collective-permute-start.21 = (bf16[4,256,128]{2,1,0:T(8,128)(2,1)S(1)}, bf16[4,256,128]{2,1,0:T(8,128)(2,1)S(1)}, u32[]{:S(2)}, u32[]{:S(2)}) collective-permute-start(bf16[4,256,128]{2,1,0:T(8,128)(2,1)S(1)} %get-tuple-element.64), channel_id=1, source_target_pairs={{0,1},{1,0},{2,3},{3,2},{4,5},{5,4},{6,7},{7,6},{8,9},{9,8},{10,11... | collective-permute-start | bytes 786440 | tf_op jit(solution)/shard_map/ppermute | solution.py:38
  75.9 5.7 %collective-permute-start.22 = (bf16[2,256,128]{2,1,0:T(8,128)(2,1)S(1)}, bf16[2,256,128]{2,1,0:T(8,128)(2,1)S(1)}, u32[]{:S(2)}, u32[]{:S(2)}) collective-permute-start(bf16[2,256,128]{2,1,0:T(8,128)(2,1)S(1)} %get-tuple-element.70), channel_id=1, source_target_pairs={{0,7},{1,2},{2,1},{3,4},{4,3},{5,6},{6,5},{7,0},{8,15},{9,10},{10,... | collective-permute-start | bytes 393224 | tf_op jit(solution)/shard_map/ppermute | solution.py:38
  77.4 4.2 %collective-permute-start.23 = (bf16[2,256,128]{2,1,0:T(8,128)(2,1)S(1)}, bf16[2,256,128]{2,1,0:T(8,128)(2,1)S(1)}, u32[]{:S(2)}, u32[]{:S(2)}) collective-permute-start(bf16[2,256,128]{2,1,0:T(8,128)(2,1)S(1)} %get-tuple-element.69), channel_id=1, source_target_pairs={{0,1},{1,0},{2,3},{3,2},{4,5},{5,4},{6,7},{7,6},{8,9},{9,8},{10,11... | collective-permute-start | bytes 393224 | tf_op jit(solution)/shard_map/ppermute | solution.py:38

commit v3 on v2

v3 whole, which is shorter than its diff:
```python
import functools

import jax
import jax.numpy as jnp
from jax import lax
from jax.experimental import pallas as pl
from jax.experimental.pallas import tpu as pltpu
from jax.sharding import PartitionSpec as P

LEVELS = 4
BOTH = ("tx", "ty")
SIDE = 4
GRID = 6
PLANE = GRID * GRID
BLANK = 2 * PLANE
ROWS = 256
LANES = 128
MARK = 16
EXTRA = 2 * (LANES + MARK)
CORNERS = ((0, 0), (0, 3), (3, 0), (3, 3))
VMEM = pl.BlockSpec(memory_space=pltpu.VMEM)
SMEM = pl.BlockSpec(memory_space=pltpu.SMEM)
HBM = pl.BlockSpec(memory_space=pltpu.HBM)
PARAMS = pltpu.CompilerParams(vmem_limit_bytes=20 * 1024 * 1024)


def partner(at, size, kind):
    if kind == "in":
        return at ^ 1
    if kind == "out":
        return (at + 1) % size if at % 2 else (at - 1) % size
    return at


def swap(value, along_x, along_y):
    size_x, size_y = lax.axis_size("tx"), lax.axis_size("ty")
    pairs = [
        (x * size_y + y, partner(x, size_x, along_x) * size_y + partner(y, size_y, along_y))
        for x in range(size_x)
        for y in range(size_y)
    ]
    return lax.ppermute(value, BOTH, pairs)


def exchange(sends):
    tx_out, tx_in, ty_out, ty_in = sends
    return swap(tx_out, "out", None), swap(tx_in, "in", None), swap(ty_out, None, "out"), swap(ty_in, None, "in")


def forward_corners(halo, odd_y):
    blocks = [piece[: SIDE * ROWS].reshape(SIDE, ROWS, LANES) for piece in halo[:2]]
    first = jnp.stack([piece[0] for piece in blocks]).reshape(2 * ROWS, LANES)
    last = jnp.stack([piece[3] for piece in blocks]).reshape(2 * ROWS, LANES)
    return swap(jnp.where(odd_y, last, first), None, "out"), swap(jnp.where(odd_y, first, last), None, "in")


def edges():
    odd_x = lax.rem(lax.axis_index("tx"), 2)
    odd_y = lax.rem(lax.axis_index("ty"), 2)
    return 3 * odd_x, 3 - 3 * odd_x, 3 * odd_y, 3 - 3 * odd_y


def beyond(edge):
    return (edge // 3) * 5


def own_slot(x, y):
    return PLANE + (x + 1) * GRID + y + 1


def piece(ref, at):
    return ref[at * ROWS : (at + 1) * ROWS]


def pack_kernel(earlier, tx_out, tx_in, ty_out, ty_in, sems):
    out_x, in_x, out_y, in_y = edges()
    copies = [
        pltpu.make_async_copy(earlier.at[out_x], tx_out, sems.at[0]),
        pltpu.make_async_copy(earlier.at[in_x], tx_in, sems.at[1]),
        pltpu.make_async_copy(earlier.at[:, out_y], ty_out, sems.at[2]),
        pltpu.make_async_copy(earlier.at[:, in_y], ty_in, sems.at[3]),
    ]
    for copy in copies:
        copy.start()
    for copy in copies:
        copy.wait()


def load_kernel(
    levels, codes, earlier, innovation, conditioner, chol_factor, plane, matrices, noise, late, *rest
):
    extras = rest[:4]
    shocks, factors, sems = rest[4:]
    copies = [
        pltpu.make_async_copy(innovation, shocks, sems.at[0]),
        pltpu.make_async_copy(chol_factor, factors, sems.at[1]),
        pltpu.make_async_copy(conditioner, matrices, sems.at[2]),
    ]
    copies += [
        pltpu.make_async_copy(earlier.at[x], plane.at[pl.ds((x + 1) * GRID + 1, SIDE)], sems.at[3 + x])
        for x in range(SIDE)
    ]
    for copy in copies:
        copy.start()

    def clear(at, carry):
        plane[at] = jnp.zeros(plane.shape[1:], plane.dtype)
        return carry

    lax.fori_loop(PLANE, BLANK + 1, clear, 0)
    rows = lax.broadcasted_iota(jnp.int32, factors.shape[2:], 0)
    columns = lax.broadcasted_iota(jnp.int32, factors.shape[2:], 1)
    upper = rows <= columns
    copies[0].wait()
    copies[1].wait()

    def one_cell(cell, carry):
        x, y = cell // SIDE, cell % SIDE
        factor = jnp.where(upper, factors[x, y].astype(jnp.float32), 0.0).astype(jnp.bfloat16)
        noise[cell] = jnp.dot(shocks[x, y], factor, preferred_element_type=jnp.float32)
        return carry

    lax.fori_loop(0, SIDE * SIDE, one_cell, 0)
    for copy in copies[2:]:
        copy.wait()
    out_x, in_x, out_y, in_y = edges()
    for at, (x, y) in enumerate(CORNERS):
        level = levels[x, y]
        code = 2 * x + 2 * y // 3 + jnp.where(level > 0, 9, 0)
        found = jnp.int32(-1)
        for k in range(8):
            found = jnp.where(codes[x, y, k] == code, k, found)
        late[at] = found
        mark = jnp.full((MARK, LANES), jnp.where(found >= 0, level, -1).astype(jnp.float32)).astype(jnp.bfloat16)
        start = pl.multiple_of(LANES * jnp.maximum(found, 0), LANES)
        matrix = matrices[x, y, pl.ds(start, LANES)]
        for ref, facing, place in (
            (extras[0], out_x == x, y // 3),
            (extras[1], in_x == x, y // 3),
            (extras[2], out_y == y, x // 3),
            (extras[3], in_y == y, x // 3),
        ):

            @pl.when(facing)
            def _(ref=ref, place=place, matrix=matrix, mark=mark):
                ref[place * LANES : (place + 1) * LANES] = matrix
                ref[2 * LANES + place * MARK : 2 * LANES + (place + 1) * MARK] = mark


def slot_of(code, x, y):
    old = (code >= 9).astype(jnp.int32)
    offset = code - 9 * old
    down = (offset >= 3).astype(jnp.int32) + (offset >= 6).astype(jnp.int32)
    return (x + down) * GRID + y + (offset - 3 * down) + PLANE * old


def store_halo(base, plane, halo):
    tx_out, tx_in, ty_out, ty_in = halo
    out_x, in_x, out_y, in_y = edges()
    for i in range(SIDE):
        plane[base + beyond(out_x) * GRID + i + 1] = piece(tx_out, i)
        plane[base + beyond(in_x) * GRID + i + 1] = piece(tx_in, i)
        plane[base + (i + 1) * GRID + beyond(out_y)] = piece(ty_out, i)
        plane[base + (i + 1) * GRID + beyond(in_y)] = piece(ty_in, i)


def complete_halo(recent, plane, extras):
    out_x, in_x, out_y, in_y = edges()
    source = PLANE if recent else 0

    def complete(cell, other, extra, place):
        mark = extra[2 * LANES + place * MARK : 2 * LANES + place * MARK + 1].astype(jnp.float32)
        product = jnp.dot(
            plane[source + other], extra[place * LANES : (place + 1) * LANES], preferred_element_type=jnp.float32
        )
        product *= jnp.where(mark == recent, 1.0, 0.0)
        plane[PLANE + cell] = (plane[PLANE + cell].astype(jnp.float32) + product).astype(jnp.bfloat16)

    for side_x, extra_x in ((out_x, extras[0]), (in_x, extras[1])):
        for place in (0, 1):
            complete(beyond(side_x) * GRID + 1 + 3 * place, (side_x + 1) * GRID + 5 * place, extra_x, place)
    for side_y, extra_y in ((out_y, extras[2]), (in_y, extras[3])):
        for place in (0, 1):
            complete((1 + 3 * place) * GRID + beyond(side_y), 5 * place * GRID + side_y + 1, extra_y, place)


def finish_corners(recent, levels, late, plane, matrices, partial, far, near):
    out_x, _, out_y, _ = edges()
    for at, (x, y) in enumerate(CORNERS):
        start = jnp.where(out_x == x, 0, ROWS)
        outward = out_y == y

        @pl.when((levels[x, y] == recent) & (late[at] >= 0))
        def _(at=at, x=x, y=y, start=start, outward=outward):
            rows = pl.ds(pl.multiple_of(start, ROWS), ROWS)
            block = jnp.where(outward, far[rows], near[rows])
            matrix = matrices[x, y, pl.ds(pl.multiple_of(LANES * late[at], LANES), LANES)]
            summed = partial[at] + jnp.dot(block, matrix, preferred_element_type=jnp.float32)
            plane[own_slot(x, y)] = summed.astype(jnp.bfloat16)


def store_corners(plane, far, near):
    out_x, _, out_y, _ = edges()
    for x, y in CORNERS:
        rows = pl.ds(pl.multiple_of(jnp.where(out_x == x, 0, ROWS), ROWS), ROWS)
        plane[beyond(x) * GRID + beyond(y)] = jnp.where(out_y == y, far[rows], near[rows])


def main_kernel(section, levels, codes, late, plane_in, partial_in, matrices, noise, *rest):
    halo, rest = rest[:4], rest[4:]
    extras = halo
    if section != 1:
        extras, rest = rest[:4], rest[4:]
    if section:
        extras = [ref.at[pl.ds(ref.shape[0] - EXTRA, EXTRA)] for ref in extras]
    plane, partial, *rest = rest
    base = PLANE if section else 0
    out_x, in_x, out_y, in_y = edges()
    store_halo(base, plane, halo)
    if section:
        corners = [ref.at[pl.ds(SIDE * ROWS, 2 * ROWS)] for ref in halo[2:]]
        if section == 1:
            store_corners(plane, *corners)
        complete_halo(section - 1, plane, extras)
        finish_corners(section - 1, levels, late, plane, matrices, partial, *corners)
    waiting = tuple(base + row * GRID + column for row in (0, 5) for column in (0, 5))

    def one_cell(cell, carry):
        x, y = cell // SIDE, cell % SIDE

        @pl.when(levels[x, y] == section)
        def _():
            parts = []
            for k in range(8):
                slot = slot_of(codes[x, y, k], x, y)
                for corner in waiting:
                    slot = jnp.where(slot == corner, BLANK, slot)
                parts.append(plane[slot])
            summed = noise[cell] + jnp.dot(
                jnp.concatenate(parts, axis=1), matrices[x, y], preferred_element_type=jnp.float32
            )
            plane[own_slot(x, y)] = summed.astype(jnp.bfloat16)
            at_corner = ((x == 0) | (x == 3)) & ((y == 0) | (y == 3))

            @pl.when(at_corner)
            def _():
                partial[(x // 3) * 2 + y // 3] = summed

        return carry

    lax.fori_loop(0, SIDE * SIDE, one_cell, 0)
    if section == LEVELS - 1:
        result, sems = rest
        copies = [
            pltpu.make_async_copy(plane.at[pl.ds(own_slot(x, 0), SIDE)], result.at[x], sems.at[x])
            for x in range(SIDE)
        ]
        for copy in copies:
            copy.start()
        for copy in copies:
            copy.wait()
    else:
        tx_out, tx_in, ty_out, ty_in = rest
        for i in range(SIDE):
            rows = pl.ds(i * ROWS, ROWS)
            tx_out[rows] = plane[own_slot(out_x, i)]
            tx_in[rows] = plane[own_slot(in_x, i)]
            ty_out[rows] = plane[own_slot(i, out_y)]
            ty_in[rows] = plane[own_slot(i, in_y)]
        for i, side in enumerate((out_x, in_x)):
            rows = pl.ds((SIDE + i) * ROWS, ROWS)
            ty_out[rows] = plane[base + beyond(side) * GRID + out_y + 1]
            ty_in[rows] = plane[base + beyond(side) * GRID + in_y + 1]
        if section == 0:
            for ref, extra in zip(rest, extras, strict=True):
                ref[ref.shape[0] - EXTRA :] = extra[...]


def corner_kernel(levels, late, plane_in, matrices, partial, far, near, result_in, plane, result, sems):
    finish_corners(LEVELS - 1, levels, late, plane, matrices, partial, far, near)
    copies = [
        pltpu.make_async_copy(plane.at[own_slot(x, y)], result.at[x, y], sems.at[at])
        for at, (x, y) in enumerate(CORNERS)
    ]
    for copy in copies:
        copy.start()
    for copy in copies:
        copy.wait()


def rows_of(rows):
    return jax.ShapeDtypeStruct((rows, LANES), jnp.bfloat16)


def local(earlier, innovation, conditioner, chol_factor, block_level, neighbours):
    block = earlier.shape[2:]
    odd_y = lax.rem(lax.axis_index("ty"), 2) == 1
    in_hbm = lambda value: pltpu.with_memory_space_constraint(value, pltpu.HBM)
    plane_shape = jax.ShapeDtypeStruct((BLANK + 1, *block), jnp.bfloat16)
    whole = jax.ShapeDtypeStruct(earlier.shape, jnp.bfloat16)
    partial_shape = jax.ShapeDtypeStruct((len(CORNERS), *block), jnp.float32)
    late_shape = jax.ShapeDtypeStruct((len(CORNERS),), jnp.int32)
    sends = pl.pallas_call(
        pack_kernel,
        out_shape=[jax.ShapeDtypeStruct((SIDE, *block), jnp.bfloat16)] * 4,
        in_specs=[HBM],
        out_specs=[VMEM] * 4,
        scratch_shapes=[pltpu.SemaphoreType.DMA((4,))],
        compiler_params=PARAMS,
        name="pack",
    )(in_hbm(earlier))
    sends = [send.reshape(SIDE * ROWS, LANES) for send in sends]
    plane, matrices, noise, late, *extras = pl.pallas_call(
        load_kernel,
        out_shape=[
            plane_shape,
            jax.ShapeDtypeStruct(conditioner.shape, jnp.bfloat16),
            jax.ShapeDtypeStruct((SIDE * SIDE, *block), jnp.float32),
            late_shape,
        ]
        + [rows_of(EXTRA)] * 4,
        in_specs=[SMEM] * 2 + [HBM] * 4,
        out_specs=[VMEM] * 3 + [SMEM] + [VMEM] * 4,
        scratch_shapes=[
            pltpu.VMEM(innovation.shape, jnp.bfloat16),
            pltpu.VMEM(chol_factor.shape, jnp.bfloat16),
            pltpu.SemaphoreType.DMA((7,)),
        ],
        compiler_params=PARAMS,
        cost_estimate=pl.CostEstimate(flops=2 * 16 * 256 * 128 * 128, bytes_accessed=14 << 20, transcendentals=0),
        name="load",
    )(block_level, neighbours, in_hbm(earlier), in_hbm(innovation), in_hbm(conditioner), in_hbm(chol_factor))
    partial = jnp.zeros(partial_shape.shape, partial_shape.dtype)
    for section in range(LEVELS):
        final = section == LEVELS - 1
        halo = exchange(sends)
        if section == 1:
            extras = halo
        if final:
            far, near = forward_corners(halo, odd_y)
        tail = EXTRA if section == 0 else 0
        send_rows = [SIDE * ROWS + tail] * 2 + [(SIDE + 2) * ROWS + tail] * 2
        plane, partial, *sends = pl.pallas_call(
            functools.partial(main_kernel, section),
            out_shape=[plane_shape, partial_shape] + ([whole] if final else [rows_of(rows) for rows in send_rows]),
            in_specs=[SMEM] * 3 + [VMEM] * (8 if section == 1 else 12),
            out_specs=[VMEM] * 2 + ([HBM] if final else [VMEM] * 4),
            scratch_shapes=[pltpu.SemaphoreType.DMA((4,))] * final,
            input_output_aliases={3: 0, 4: 1},
            compiler_params=PARAMS,
            cost_estimate=pl.CostEstimate(flops=8 * 2 * 256 * 1024 * 128, bytes_accessed=4 << 20, transcendentals=0),
            name=f"main_{section}",
        )(block_level, neighbours, late, plane, partial, matrices, noise, *halo, *([] if section == 1 else extras))
    _, result = pl.pallas_call(
        corner_kernel,
        out_shape=[plane_shape, whole],
        in_specs=[SMEM] * 2 + [VMEM] * 5 + [HBM],
        out_specs=[VMEM, HBM],
        scratch_shapes=[pltpu.SemaphoreType.DMA((4,))],
        input_output_aliases={2: 0, 7: 1},
        compiler_params=PARAMS,
        cost_estimate=pl.CostEstimate(flops=2 * 256 * 128 * 128, bytes_accessed=1 << 20, transcendentals=0),
        name="last_corners",
    )(block_level, late, plane, matrices, partial, far, near, sends[0])
    return result


def solution(mesh):
    placed = (
        P("tx", "ty", None, None),
        P("tx", "ty", None, None),
        P("tx", "ty", None, None),
        P("tx", "ty", None, None),
        P("tx", "ty"),
        P("tx", "ty", None),
    )
    return jax.shard_map(
        local, mesh=mesh, in_specs=placed, out_specs=P("tx", "ty", None, None), check_vma=False
    )
```

time: 85.2 us -> 96.6 us (1.13); the launches traced: 83.6 us -> 96.2 us
  local copies, waits for them, and re-layouts: 6.98 us -> 19.8 us
  starting transfers between devices: 32.1 us -> 26 us
  Pallas kernels: 18.4 us -> 24.2 us
    unnamed x14 -> x38, local copies, waits for them, and re-layouts: 6.91 us -> 18 us
    ppermute x24 -> x18, starting transfers between devices: 32.1 us -> 26 us  [swap(): return lax.ppermute(value, BOTH, pairs)]
    pallas_call x4, Pallas kernels: 10.6 us -> 16.2 us  [local(): pl.pallas_call(functools.partial(main_kernel, section), out_shape=[plane_...]
    pallas_call x1, Pallas kernels: 2.96 us -> 5.27 us  [local(): pl.pallas_call(load_kernel, out_shape=[plane_shape, jax.ShapeDtypeStruct(...]
    pallas_call x5 -> x2, Pallas kernels: 4.87 us -> 2.73 us  [the longest x1 1.49 us: local(): pl.pallas_call(corner_kernel, out_shape=[plane_shape, whole], in_specs=[S...]
    slice x8 -> x2, local copies, waits for them, and re-layouts: 0.08 us -> 1.76 us  [forward_corners(): last = jnp.stack([piece[3] for piece in blocks]).reshape(2 * ROWS, LANES)]
    ppermute x24 -> x18, waiting for transfers between devices: 25.6 us -> 25.9 us  [swap(): return lax.ppermute(value, BOTH, pairs)]
  transfers between devices with their start and end apart: 24 -> 18, of which waited for: 9 -> 3; matrix products, arithmetic and copies ran while one was open for 0% -> 2% of each run, Pallas kernels for 16% -> 12%
where the time goes in v3:
time: 96.6 us; the launch traced here: 96.2 us
  starting transfers between devices  26 us (27%)
  waiting for transfers between devices  25.9 us (27%)
  Pallas kernels  24.2 us (25%)
  local copies, waits for them, and re-layouts  19.8 us (20%)
    ppermute x18, starting transfers between devices, swap(): return lax.ppermute(value, BOTH, pairs)  26 us
    ppermute x18, waiting for transfers between devices, swap(): return lax.ppermute(value, BOTH, pairs)  25.9 us
    unnamed x38, local copies, waits for them, and re-layouts  18 us
    pallas_call x4, Pallas kernels, local(): pl.pallas_call(functools.partial(main_kernel, section), out_shape=[plane_...  16.2 us
    pallas_call x1, Pallas kernels, local(): pl.pallas_call(load_kernel, out_shape=[plane_shape, jax.ShapeDtypeStruct(...  5.27 us
  transfers between devices with their start and end apart: 18, of which 3 were waited for; matrix products, arithmetic and copies ran while one was open for 2% of the time, Pallas kernels for 12%

profile of v3, /device:TPU:0, one launch (start us, length us, event | category | flops | bytes accessed | tf_op | source)
XLA Modules:
  0.0 96.2 jit_solution(6974957239259840220)
XLA Ops:
  0.0 1.2 %pack.1 = (bf16[4,256,128]{2,1,0:T(8,128)(2,1)S(1)}, bf16[4,256,128]{2,1,0:T(8,128)(2,1)S(1)}, bf16[4,256,128]{2,1,0:T(8,128)(2,1)S(1)}, bf16[4,256,128]{2,1,0:T(8,128)(2,1)S(1)}) custom-call(bf16[4,4,256,128]{3,2,1,0:T(8,128)(2,1)} %earlier.3), custom_call_target="tpu_custom_call" | custom-call | tf_op jit(solution)/shard_map/pack/pallas_call | solution.py:303
  1.3 5.4 %collective-permute-start = (bf16[1024,128]{1,0:T(8,128)(2,1)S(1)}, bf16[1024,128]{1,0:T(8,128)(2,1)S(1)}, u32[]{:S(2)}, u32[]{:S(2)}) collective-permute-start(bf16[1024,128]{1,0:T(8,128)(2,1)S(1)} %bitcast.17), channel_id=1, source_target_pairs={{0,120},{1,121},{2,122},{3,123},{4,124},{5,125},{6,126},{7,127},{8... | collective-permute-start | bytes 786440 | tf_op jit(solution)/shard_map/ppermute | solution.py:42
  6.6 3.2 %collective-permute-start.2 = (bf16[1024,128]{1,0:T(8,128)(2,1)S(1)}, bf16[1024,128]{1,0:T(8,128)(2,1)S(1)}, u32[]{:S(2)}, u32[]{:S(2)}) collective-permute-start(bf16[1024,128]{1,0:T(8,128)(2,1)S(1)} %bitcast.15), channel_id=1, source_target_pairs={{0,7},{1,2},{2,1},{3,4},{4,3},{5,6},{6,5},{7,0},{8,15},{9,10},{10,... | collective-permute-start | bytes 786440 | tf_op jit(solution)/shard_map/ppermute | solution.py:42
  11.2 5.3 %load.1 = (bf16[73,256,128]{2,1,0:T(8,128)(2,1)S(1)}, bf16[4,4,1024,128]{3,2,1,0:T(8,128)(2,1)S(1)}, f32[16,256,128]{2,1,0:T(8,128)S(1)}, s32[4]{0:T(128)S(1)}, ...) custom-call(s32[4,4]{1,0:T(4,128)S(1)} %copy-done.13, ...), custom_call_target="tpu_custom_call" | custom-call | flops 134217728 | bytes 14680064 | tf_op jit(solution)/shard_map/load/pallas_call | solution.py:313
  16.6 1.9 %main_0.1 = (bf16[73,256,128]{2,1,0:T(8,128)(2,1)S(1)}, f32[4,256,128]{2,1,0:T(8,128)S(1)}, bf16[1312,128]{1,0:T(8,128)(2,1)S(1)}, bf16[1312,128]{1,0:T(8,128)(2...) custom-call(s32[4,4]{1,0:T(4,128)S(1)} %copy-done.13, ...), custom_call_target="tpu_custom_call", output_to_operand_aliasing={{0}: (3, {}), {1}: (4, {})} | custom-call | flops 536870912 | bytes 4194304 | tf_op jit(solution)/shard_map/main_0/pallas_call | solution.py:343
  18.5 1.0 %collective-permute-start.6 = (bf16[1824,128]{1,0:T(8,128)(2,1)S(1)}, bf16[1824,128]{1,0:T(8,128)(2,1)S(1)}, u32[]{:S(2)}, u32[]{:S(2)}) collective-permute-start(bf16[1824,128]{1,0:T(8,128)(2,1)S(1)} %get-tuple-element.55), channel_id=1, source_target_pairs={{0,7},{1,2},{2,1},{3,4},{4,3},{5,6},{6,5},{7,0},{8,15},{9,10},{10,... | collective-permute-start | bytes 1400840 | tf_op jit(solution)/shard_map/ppermute | solution.py:42
  19.5 1.6 %collective-permute-start.7 = (bf16[1824,128]{1,0:T(8,128)(2,1)S(1)}, bf16[1824,128]{1,0:T(8,128)(2,1)S(1)}, u32[]{:S(2)}, u32[]{:S(2)}) collective-permute-start(bf16[1824,128]{1,0:T(8,128)(2,1)S(1)} %get-tuple-element.56), channel_id=1, source_target_pairs={{0,1},{1,0},{2,3},{3,2},{4,5},{5,4},{6,7},{7,6},{8,9},{9,8},{10,11... | collective-permute-start | bytes 1400840 | tf_op jit(solution)/shard_map/ppermute | solution.py:42
  21.1 2.9 %collective-permute-start.4 = (bf16[1312,128]{1,0:T(8,128)(2,1)S(1)}, bf16[1312,128]{1,0:T(8,128)(2,1)S(1)}, u32[]{:S(2)}, u32[]{:S(2)}) collective-permute-start(bf16[1312,128]{1,0:T(8,128)(2,1)S(1)} %get-tuple-element.53), channel_id=1, source_target_pairs={{0,120},{1,121},{2,122},{3,123},{4,124},{5,125},{6,126},{7,127},{8... | collective-permute-start | bytes 1007624 | tf_op jit(solution)/shard_map/ppermute | solution.py:42
  24.0 10.3 %collective-permute-done.4.rest_0_.rest_4_ = bf16[1312,128]{1,0:T(8,128)(2,1)S(1)} collective-permute-done((bf16[1312,128]{1,0:T(8,128)(2,1)S(1)}, bf16[1312,128]{1,0:T(8,128)(2,1)S(1)}, u32[]{:S(2)}, u32[]{:S(2)}) %collective-permute-start.4) | collective-permute-done | bytes 335904 | tf_op jit(solution)/shard_map/ppermute | solution.py:42
  34.3 2.9 %main_1.1 = (bf16[73,256,128]{2,1,0:T(8,128)(2,1)S(1)}, f32[4,256,128]{2,1,0:T(8,128)S(1)}, bf16[1024,128]{1,0:T(8,128)(2,1)S(1)}, bf16[1024,128]{1,0:T(8,128)(2...) custom-call(s32[4,4]{1,0:T(4,128)S(1)} %copy-done.13, ...), custom_call_target="tpu_custom_call", output_to_operand_aliasing={{0}: (3, {}), {1}: (4, {})} | custom-call | flops 536870912 | bytes 4194304 | tf_op jit(solution)/shard_map/main_1/pallas_call | solution.py:343
  37.2 2.1 %collective-permute-start.10 = (bf16[1536,128]{1,0:T(8,128)(2,1)S(1)}, bf16[1536,128]{1,0:T(8,128)(2,1)S(1)}, u32[]{:S(2)}, u32[]{:S(2)}) collective-permute-start(bf16[1536,128]{1,0:T(8,128)(2,1)S(1)} %get-tuple-element.61), channel_id=1, source_target_pairs={{0,7},{1,2},{2,1},{3,4},{4,3},{5,6},{6,5},{7,0},{8,15},{9,10},{10,... | collective-permute-start | bytes 1179656 | tf_op jit(solution)/shard_map/ppermute | solution.py:42
  39.3 0.8 collective-permute-start.11
  40.1 2.3 %collective-permute-start.8 = (bf16[1024,128]{1,0:T(8,128)(2,1)S(1)}, bf16[1024,128]{1,0:T(8,128)(2,1)S(1)}, u32[]{:S(2)}, u32[]{:S(2)}) collective-permute-start(bf16[1024,128]{1,0:T(8,128)(2,1)S(1)} %get-tuple-element.59), channel_id=1, source_target_pairs={{0,120},{1,121},{2,122},{3,123},{4,124},{5,125},{6,126},{7,127},{8... | collective-permute-start | bytes 786440 | tf_op jit(solution)/shard_map/ppermute | solution.py:42
  42.4 9.2 %collective-permute-done.8.rest_0_ = bf16[1024,128]{1,0:T(8,128)(2,1)S(1)} collective-permute-done((bf16[1024,128]{1,0:T(8,128)(2,1)S(1)}, bf16[1024,128]{1,0:T(8,128)(2,1)S(1)}, u32[]{:S(2)}, u32[]{:S(2)}) %collective-permute-start.8) | collective-permute-done | bytes 262176 | tf_op jit(solution)/shard_map/ppermute | solution.py:42
  51.7 4.9 %main_2.1 = (bf16[73,256,128]{2,1,0:T(8,128)(2,1)S(1)}, f32[4,256,128]{2,1,0:T(8,128)S(1)}, bf16[1024,128]{1,0:T(8,128)(2,1)}, bf16[1024,128]{1,0:T(8,128)(2,1)}...) custom-call(s32[4,4]{1,0:T(4,128)S(1)} %copy-done.13, ...), custom_call_target="tpu_custom_call", output_to_operand_aliasing={{0}: (3, {}), {1}: (4, {})} | custom-call | flops 536870912 | bytes 4194304 | tf_op jit(solution)/shard_map/main_2/pallas_call | solution.py:343
  56.6 2.2 %copy-done = bf16[73,256,128]{2,1,0:T(8,128)(2,1)} copy-done((bf16[73,256,128]{2,1,0:T(8,128)(2,1)}, bf16[73,256,128]{2,1,0:T(8,128)(2,1)S(1)}, u32[]{:S(2)}) %copy-start) | copy-done | bytes 4784152
  58.7 0.8 copy-done.17
  59.5 0.7 copy-done.18
  60.3 3.2 %collective-permute-start.12 = (bf16[1024,128]{1,0:T(8,128)(2,1)}, bf16[1024,128]{1,0:T(8,128)(2,1)}, u32[]{:S(2)}, u32[]{:S(2)}) collective-permute-start(bf16[1024,128]{1,0:T(8,128)(2,1)} %get-tuple-element.65), channel_id=1, source_target_pairs={{0,120},{1,121},{2,122},{3,123},{4,124},{5,125},{6,126},{7,127},{8... | collective-permute-start | bytes 786440 | tf_op jit(solution)/shard_map/ppermute | solution.py:42
  63.5 0.8 collective-permute-start.14
  64.3 6.3 %collective-permute-done.12.rest_0_ = bf16[1024,128]{1,0:T(8,128)(2,1)} collective-permute-done((bf16[1024,128]{1,0:T(8,128)(2,1)}, bf16[1024,128]{1,0:T(8,128)(2,1)}, u32[]{:S(2)}, u32[]{:S(2)}) %collective-permute-start.12) | collective-permute-done | bytes 262176 | tf_op jit(solution)/shard_map/ppermute | solution.py:42
  70.6 0.9 slice_bitcast_fusion.3
  71.5 0.9 slice_bitcast_fusion.2
  72.4 2.7 %collective-permute-start.16 = (bf16[512,128]{1,0:T(8,128)(2,1)S(1)}, bf16[512,128]{1,0:T(8,128)(2,1)S(1)}, u32[]{:S(2)}, u32[]{:S(2)}) collective-permute-start(bf16[512,128]{1,0:T(8,128)(2,1)S(1)} %bitcast.19), channel_id=1, source_target_pairs={{0,7},{1,2},{2,1},{3,4},{4,3},{5,6},{6,5},{7,0},{8,15},{9,10},{10,... | collective-permute-start | bytes 393224 | tf_op jit(solution)/shard_map/ppermute | solution.py:42
  75.1 2.3 %copy-done.1 = bf16[73,256,128]{2,1,0:T(8,128)(2,1)S(1)} copy-done((bf16[73,256,128]{2,1,0:T(8,128)(2,1)S(1)}, bf16[73,256,128]{2,1,0:T(8,128)(2,1)}, u32[]{:S(2)}) %copy-start.1) | copy-done | bytes 4784152
  77.5 2.2 %copy-done.5 = bf16[4,4,1024,128]{3,2,1,0:T(8,128)(2,1)S(1)} copy-done((bf16[4,4,1024,128]{3,2,1,0:T(8,128)(2,1)S(1)}, bf16[4,4,1024,128]{3,2,1,0:T(8,128)(2,1)}, u32[]{:S(2)}) %copy-start.5) | copy-done | bytes 4194328
  79.7 1.0 %copy-done.8 = bf16[1312,128]{1,0:T(8,128)(2,1)S(1)} copy-done((bf16[1312,128]{1,0:T(8,128)(2,1)S(1)}, bf16[1312,128]{1,0:T(8,128)(2,1)}, u32[]{:S(2)}) %copy-start.8) | copy-done | bytes 335896
  80.7 1.0 %copy-done.10 = bf16[1312,128]{1,0:T(8,128)(2,1)S(1)} copy-done((bf16[1312,128]{1,0:T(8,128)(2,1)S(1)}, bf16[1312,128]{1,0:T(8,128)(2,1)}, u32[]{:S(2)}) %copy-start.10) | copy-done | bytes 335896
  83.6 6.6 %main_3.1 = (bf16[73,256,128]{2,1,0:T(8,128)(2,1)S(1)}, f32[4,256,128]{2,1,0:T(8,128)S(1)}, bf16[4,4,256,128]{3,2,1,0:T(8,128)(2,1)}) custom-call(s32[4,4]{1,0:T(4,128)S(1)} %copy-done.14, s32[4,4,8]{2,1,0:T(4,128)S(1)} %copy-done.12, s32[4]{0:T(128)S(1)} %copy-done.16, ...), custom_call_target="tpu_custom_call", output_to_operand_aliasing={{0}: (3, {}), {1}: (4, {})} | custom-call | flops 536870912 | bytes 4194304 | tf_op jit(solution)/shard_map/main_3/pallas_call | solution.py:343
  90.2 2.2 %copy-done.2 = bf16[73,256,128]{2,1,0:T(8,128)(2,1)} copy-done((bf16[73,256,128]{2,1,0:T(8,128)(2,1)}, bf16[73,256,128]{2,1,0:T(8,128)(2,1)S(1)}, u32[]{:S(2)}) %copy-start.2) | copy-done | bytes 4784152
  92.4 2.3 %copy-done.3 = bf16[73,256,128]{2,1,0:T(8,128)(2,1)S(1)} copy-done((bf16[73,256,128]{2,1,0:T(8,128)(2,1)S(1)}, bf16[73,256,128]{2,1,0:T(8,128)(2,1)}, u32[]{:S(2)}) %copy-start.3) | copy-done | bytes 4784152
  94.7 1.5 %last_corners.1 = (bf16[73,256,128]{2,1,0:T(8,128)(2,1)S(1)}, bf16[4,4,256,128]{3,2,1,0:T(8,128)(2,1)}) custom-call(s32[4,4]{1,0:T(4,128)S(1)} %copy-done.14, s32[4]{0:T(128)S(1)} %copy-done.16, bf16[73,256,128]{2,1,0:T(8,128)(2,1)S(1)} %copy-done.3, bf16[4,4,1024,128]{3,2,1,0:T(8,128)(2,1)S(1)} %copy-done.6, ...), custom_call_target="tpu_custom_call", output_to_operand_aliasing={{0}: (2, {}), {1}: (7, {})} | custom-call | flops 8388608 | bytes 1048576 | tf_op jit(solution)/shard_map/last_corners/pallas_call | solution.py:354
  (53 shorter events, 3.5 us)
Async XLA Ops:
  1.3 15.2 %collective-permute-start = (bf16[1024,128]{1,0:T(8,128)(2,1)S(1)}, bf16[1024,128]{1,0:T(8,128)(2,1)S(1)}, u32[]{:S(2)}, u32[]{:S(2)}) collective-permute-start(bf16[1024,128]{1,0:T(8,128)(2,1)S(1)} %bitcast.17), channel_id=1, source_target_pairs={{0,120},{1,121},{2,122},{3,123},{4,124},{5,125},{6,126},{7,127},{8... | collective-permute-start | bytes 786440 | tf_op jit(solution)/shard_map/ppermute | solution.py:42
  6.6 9.9 %collective-permute-start.1 = (bf16[1024,128]{1,0:T(8,128)(2,1)S(1)}, bf16[1024,128]{1,0:T(8,128)(2,1)S(1)}, u32[]{:S(2)}, u32[]{:S(2)}) collective-permute-start(bf16[1024,128]{1,0:T(8,128)(2,1)S(1)} %bitcast.16), channel_id=1, source_target_pairs={{0,8},{1,9},{2,10},{3,11},{4,12},{5,13},{6,14},{7,15},{8,0},{9,1},... | collective-permute-start | bytes 786440 | tf_op jit(solution)/shard_map/ppermute | solution.py:42
  6.6 9.9 %collective-permute-start.2 = (bf16[1024,128]{1,0:T(8,128)(2,1)S(1)}, bf16[1024,128]{1,0:T(8,128)(2,1)S(1)}, u32[]{:S(2)}, u32[]{:S(2)}) collective-permute-start(bf16[1024,128]{1,0:T(8,128)(2,1)S(1)} %bitcast.15), channel_id=1, source_target_pairs={{0,7},{1,2},{2,1},{3,4},{4,3},{5,6},{6,5},{7,0},{8,15},{9,10},{10,... | collective-permute-start | bytes 786440 | tf_op jit(solution)/shard_map/ppermute | solution.py:42
  9.8 6.7 %collective-permute-start.3 = (bf16[1024,128]{1,0:T(8,128)(2,1)S(1)}, bf16[1024,128]{1,0:T(8,128)(2,1)S(1)}, u32[]{:S(2)}, u32[]{:S(2)}) collective-permute-start(bf16[1024,128]{1,0:T(8,128)(2,1)S(1)} %bitcast.14), channel_id=1, source_target_pairs={{0,1},{1,0},{2,3},{3,2},{4,5},{5,4},{6,7},{7,6},{8,9},{9,8},{10,11... | collective-permute-start | bytes 786440 | tf_op jit(solution)/shard_map/ppermute | solution.py:42
  16.5 35.2 %copy-start.4 = (bf16[4,4,1024,128]{3,2,1,0:T(8,128)(2,1)}, bf16[4,4,1024,128]{3,2,1,0:T(8,128)(2,1)S(1)}, u32[]{:S(2)}) copy-start(bf16[4,4,1024,128]{3,2,1,0:T(8,128)(2,1)S(1)} %get-tuple-element.41.matrices) | copy-start | bytes 12582916
  16.5 35.2 %copy-start.15 = (s32[4]{0:T(128)}, s32[4]{0:T(128)S(1)}, u32[]{:S(2)}) copy-start(s32[4]{0:T(128)S(1)} %get-tuple-element.39.late) | copy-start | bytes 52
  18.5 15.8 %collective-permute-start.6 = (bf16[1824,128]{1,0:T(8,128)(2,1)S(1)}, bf16[1824,128]{1,0:T(8,128)(2,1)S(1)}, u32[]{:S(2)}, u32[]{:S(2)}) collective-permute-start(bf16[1824,128]{1,0:T(8,128)(2,1)S(1)} %get-tuple-element.55), channel_id=1, source_target_pairs={{0,7},{1,2},{2,1},{3,4},{4,3},{5,6},{6,5},{7,0},{8,15},{9,10},{10,... | collective-permute-start | bytes 1400840 | tf_op jit(solution)/shard_map/ppermute | solution.py:42
  19.5 14.8 %collective-permute-start.7 = (bf16[1824,128]{1,0:T(8,128)(2,1)S(1)}, bf16[1824,128]{1,0:T(8,128)(2,1)S(1)}, u32[]{:S(2)}, u32[]{:S(2)}) collective-permute-start(bf16[1824,128]{1,0:T(8,128)(2,1)S(1)} %get-tuple-element.56), channel_id=1, source_target_pairs={{0,1},{1,0},{2,3},{3,2},{4,5},{5,4},{6,7},{7,6},{8,9},{9,8},{10,11... | collective-permute-start | bytes 1400840 | tf_op jit(solution)/shard_map/ppermute | solution.py:42
  21.1 13.2 %collective-permute-start.4 = (bf16[1312,128]{1,0:T(8,128)(2,1)S(1)}, bf16[1312,128]{1,0:T(8,128)(2,1)S(1)}, u32[]{:S(2)}, u32[]{:S(2)}) collective-permute-start(bf16[1312,128]{1,0:T(8,128)(2,1)S(1)} %get-tuple-element.53), channel_id=1, source_target_pairs={{0,120},{1,121},{2,122},{3,123},{4,124},{5,125},{6,126},{7,127},{8... | collective-permute-start | bytes 1007624 | tf_op jit(solution)/shard_map/ppermute | solution.py:42
  24.0 10.3 %collective-permute-start.5 = (bf16[1312,128]{1,0:T(8,128)(2,1)S(1)}, bf16[1312,128]{1,0:T(8,128)(2,1)S(1)}, u32[]{:S(2)}, u32[]{:S(2)}) collective-permute-start(bf16[1312,128]{1,0:T(8,128)(2,1)S(1)} %get-tuple-element.54), channel_id=1, source_target_pairs={{0,8},{1,9},{2,10},{3,11},{4,12},{5,13},{6,14},{7,15},{8,0},{9,1},... | collective-permute-start | bytes 1007624 | tf_op jit(solution)/shard_map/ppermute | solution.py:42
  34.3 17.4 %copy-start.7 = (bf16[1312,128]{1,0:T(8,128)(2,1)}, bf16[1312,128]{1,0:T(8,128)(2,1)S(1)}, u32[]{:S(2)}) copy-start(bf16[1312,128]{1,0:T(8,128)(2,1)S(1)} %collective-permute-done.4.rest_0_.rest_4_) | copy-start | bytes 1007620
  34.3 17.4 %copy-start.9 = (bf16[1312,128]{1,0:T(8,128)(2,1)}, bf16[1312,128]{1,0:T(8,128)(2,1)S(1)}, u32[]{:S(2)}) copy-start(bf16[1312,128]{1,0:T(8,128)(2,1)S(1)} %collective-permute-done.5.rest_1_.rest_5_) | copy-start | bytes 1007620
  37.2 14.5 %collective-permute-start.10 = (bf16[1536,128]{1,0:T(8,128)(2,1)S(1)}, bf16[1536,128]{1,0:T(8,128)(2,1)S(1)}, u32[]{:S(2)}, u32[]{:S(2)}) collective-permute-start(bf16[1536,128]{1,0:T(8,128)(2,1)S(1)} %get-tuple-element.61), channel_id=1, source_target_pairs={{0,7},{1,2},{2,1},{3,4},{4,3},{5,6},{6,5},{7,0},{8,15},{9,10},{10,... | collective-permute-start | bytes 1179656 | tf_op jit(solution)/shard_map/ppermute | solution.py:42
  39.3 12.4 %collective-permute-start.11 = (bf16[1536,128]{1,0:T(8,128)(2,1)S(1)}, bf16[1536,128]{1,0:T(8,128)(2,1)S(1)}, u32[]{:S(2)}, u32[]{:S(2)}) collective-permute-start(bf16[1536,128]{1,0:T(8,128)(2,1)S(1)} %get-tuple-element.62), channel_id=1, source_target_pairs={{0,1},{1,0},{2,3},{3,2},{4,5},{5,4},{6,7},{7,6},{8,9},{9,8},{10,11... | collective-permute-start | bytes 1179656 | tf_op jit(solution)/shard_map/ppermute | solution.py:42
  40.1 11.5 %collective-permute-start.8 = (bf16[1024,128]{1,0:T(8,128)(2,1)S(1)}, bf16[1024,128]{1,0:T(8,128)(2,1)S(1)}, u32[]{:S(2)}, u32[]{:S(2)}) collective-permute-start(bf16[1024,128]{1,0:T(8,128)(2,1)S(1)} %get-tuple-element.59), channel_id=1, source_target_pairs={{0,120},{1,121},{2,122},{3,123},{4,124},{5,125},{6,126},{7,127},{8... | collective-permute-start | bytes 786440 | tf_op jit(solution)/shard_map/ppermute | solution.py:42
  42.4 9.2 %collective-permute-start.9 = (bf16[1024,128]{1,0:T(8,128)(2,1)S(1)}, bf16[1024,128]{1,0:T(8,128)(2,1)S(1)}, u32[]{:S(2)}, u32[]{:S(2)}) collective-permute-start(bf16[1024,128]{1,0:T(8,128)(2,1)S(1)} %get-tuple-element.60), channel_id=1, source_target_pairs={{0,8},{1,9},{2,10},{3,11},{4,12},{5,13},{6,14},{7,15},{8,0},{9,1},... | collective-permute-start | bytes 786440 | tf_op jit(solution)/shard_map/ppermute | solution.py:42
  56.6 2.2 %copy-start = (bf16[73,256,128]{2,1,0:T(8,128)(2,1)}, bf16[73,256,128]{2,1,0:T(8,128)(2,1)S(1)}, u32[]{:S(2)}) copy-start(bf16[73,256,128]{2,1,0:T(8,128)(2,1)S(1)} %get-tuple-element.63.plane_in) | copy-start | bytes 14352388
  58.7 0.8 copy-start.17
  59.5 0.7 copy-start.18
  60.3 10.4 %collective-permute-start.12 = (bf16[1024,128]{1,0:T(8,128)(2,1)}, bf16[1024,128]{1,0:T(8,128)(2,1)}, u32[]{:S(2)}, u32[]{:S(2)}) collective-permute-start(bf16[1024,128]{1,0:T(8,128)(2,1)} %get-tuple-element.65), channel_id=1, source_target_pairs={{0,120},{1,121},{2,122},{3,123},{4,124},{5,125},{6,126},{7,127},{8... | collective-permute-start | bytes 786440 | tf_op jit(solution)/shard_map/ppermute | solution.py:42
  63.5 8.0 %collective-permute-start.13 = (bf16[1024,128]{1,0:T(8,128)(2,1)}, bf16[1024,128]{1,0:T(8,128)(2,1)}, u32[]{:S(2)}, u32[]{:S(2)}) collective-permute-start(bf16[1024,128]{1,0:T(8,128)(2,1)} %get-tuple-element.66), channel_id=1, source_target_pairs={{0,8},{1,9},{2,10},{3,11},{4,12},{5,13},{6,14},{7,15},{8,0},{9,1},... | collective-permute-start | bytes 786440 | tf_op jit(solution)/shard_map/ppermute | solution.py:42
  63.5 11.7 %collective-permute-start.14 = (bf16[1536,128]{1,0:T(8,128)(2,1)}, bf16[1536,128]{1,0:T(8,128)(2,1)S(1)}, u32[]{:S(2)}, u32[]{:S(2)}) collective-permute-start(bf16[1536,128]{1,0:T(8,128)(2,1)} %copy-done.18), channel_id=1, source_target_pairs={{0,7},{1,2},{2,1},{3,4},{4,3},{5,6},{6,5},{7,0},{8,15},{9,10},{10,... | collective-permute-start | bytes 1179656 | tf_op jit(solution)/shard_map/ppermute | solution.py:42
  64.3 10.9 %collective-permute-start.15 = (bf16[1536,128]{1,0:T(8,128)(2,1)}, bf16[1536,128]{1,0:T(8,128)(2,1)S(1)}, u32[]{:S(2)}, u32[]{:S(2)}) collective-permute-start(bf16[1536,128]{1,0:T(8,128)(2,1)} %copy-done.17), channel_id=1, source_target_pairs={{0,1},{1,0},{2,3},{3,2},{4,5},{5,4},{6,7},{7,6},{8,9},{9,8},{10,11... | collective-permute-start | bytes 1179656 | tf_op jit(solution)/shard_map/ppermute | solution.py:42
  72.4 19.9 %collective-permute-start.16 = (bf16[512,128]{1,0:T(8,128)(2,1)S(1)}, bf16[512,128]{1,0:T(8,128)(2,1)S(1)}, u32[]{:S(2)}, u32[]{:S(2)}) collective-permute-start(bf16[512,128]{1,0:T(8,128)(2,1)S(1)} %bitcast.19), channel_id=1, source_target_pairs={{0,7},{1,2},{2,1},{3,4},{4,3},{5,6},{6,5},{7,0},{8,15},{9,10},{10,... | collective-permute-start | bytes 393224 | tf_op jit(solution)/shard_map/ppermute | solution.py:42
  75.1 17.2 %collective-permute-start.17 = (bf16[512,128]{1,0:T(8,128)(2,1)S(1)}, bf16[512,128]{1,0:T(8,128)(2,1)S(1)}, u32[]{:S(2)}, u32[]{:S(2)}) collective-permute-start(bf16[512,128]{1,0:T(8,128)(2,1)S(1)} %bitcast.18), channel_id=1, source_target_pairs={{0,1},{1,0},{2,3},{3,2},{4,5},{5,4},{6,7},{7,6},{8,9},{9,8},{10,11... | collective-permute-start | bytes 393224 | tf_op jit(solution)/shard_map/ppermute | solution.py:42
  75.1 2.4 %copy-start.1 = (bf16[73,256,128]{2,1,0:T(8,128)(2,1)S(1)}, bf16[73,256,128]{2,1,0:T(8,128)(2,1)}, u32[]{:S(2)}) copy-start(bf16[73,256,128]{2,1,0:T(8,128)(2,1)} %copy-done) | copy-start | bytes 14352388
  77.5 2.2 %copy-start.5 = (bf16[4,4,1024,128]{3,2,1,0:T(8,128)(2,1)S(1)}, bf16[4,4,1024,128]{3,2,1,0:T(8,128)(2,1)}, u32[]{:S(2)}) copy-start(bf16[4,4,1024,128]{3,2,1,0:T(8,128)(2,1)} %copy-done.4) | copy-start | bytes 12582916
  79.7 1.0 %copy-start.8 = (bf16[1312,128]{1,0:T(8,128)(2,1)S(1)}, bf16[1312,128]{1,0:T(8,128)(2,1)}, u32[]{:S(2)}) copy-start(bf16[1312,128]{1,0:T(8,128)(2,1)} %copy-done.7) | copy-start | bytes 1007620
  80.7 1.0 %copy-start.10 = (bf16[1312,128]{1,0:T(8,128)(2,1)S(1)}, bf16[1312,128]{1,0:T(8,128)(2,1)}, u32[]{:S(2)}) copy-start(bf16[1312,128]{1,0:T(8,128)(2,1)} %copy-done.9) | copy-start | bytes 1007620
  83.6 8.8 %copy-start.6 = (bf16[4,4,1024,128]{3,2,1,0:T(8,128)(2,1)S(1)}, bf16[4,4,1024,128]{3,2,1,0:T(8,128)(2,1)}, u32[]{:S(2)}) copy-start(bf16[4,4,1024,128]{3,2,1,0:T(8,128)(2,1)} %copy-done.4) | copy-start | bytes 12582916
  90.2 2.2 %copy-start.2 = (bf16[73,256,128]{2,1,0:T(8,128)(2,1)}, bf16[73,256,128]{2,1,0:T(8,128)(2,1)S(1)}, u32[]{:S(2)}) copy-start(bf16[73,256,128]{2,1,0:T(8,128)(2,1)S(1)} %get-tuple-element.69.plane_in) | copy-start | bytes 14352388
  92.4 2.4 %copy-start.3 = (bf16[73,256,128]{2,1,0:T(8,128)(2,1)S(1)}, bf16[73,256,128]{2,1,0:T(8,128)(2,1)}, u32[]{:S(2)}) copy-start(bf16[73,256,128]{2,1,0:T(8,128)(2,1)} %copy-done.2) | copy-start | bytes 14352388
  (5 other events, 3.3 us)

commit v4 on v3

v4 whole, which is shorter than its diff:
```python
import functools

import jax
import jax.numpy as jnp
from jax import lax
from jax.experimental import pallas as pl
from jax.experimental.pallas import tpu as pltpu
from jax.sharding import PartitionSpec as P

LEVELS = 4
BOTH = ("tx", "ty")
SIDE = 4
GRID = 6
PLANE = GRID * GRID
BLANK = 2 * PLANE
ROWS = 256
LANES = 128
MARK = 16
EXTRA = 2 * (LANES + MARK)
DEPTH = 9 * LANES
ALL, SETTLED, ORDER, FIRST, LATE, TABLE = 0, 128, 256, 280, 288, 296
ITEMS = 66
CORNERS = ((0, 0), (0, 3), (3, 0), (3, 3))
VMEM = pl.BlockSpec(memory_space=pltpu.VMEM)
SMEM = pl.BlockSpec(memory_space=pltpu.SMEM)
HBM = pl.BlockSpec(memory_space=pltpu.HBM)
PARAMS = pltpu.CompilerParams(vmem_limit_bytes=8 * 1024 * 1024)


def partner(at, size, kind):
    if kind == "in":
        return at ^ 1
    if kind == "out":
        return (at + 1) % size if at % 2 else (at - 1) % size
    return at


def swap(value, along_x, along_y):
    size_x, size_y = lax.axis_size("tx"), lax.axis_size("ty")
    pairs = [
        (x * size_y + y, partner(x, size_x, along_x) * size_y + partner(y, size_y, along_y))
        for x in range(size_x)
        for y in range(size_y)
    ]
    return lax.ppermute(value, BOTH, pairs)


def exchange(sends):
    tx_out, tx_in, ty_out, ty_in = sends
    return swap(tx_out, "out", None), swap(tx_in, "in", None), swap(ty_out, None, "out"), swap(ty_in, None, "in")


def edges():
    odd_x = lax.rem(lax.axis_index("tx"), 2)
    odd_y = lax.rem(lax.axis_index("ty"), 2)
    return 3 * odd_x, 3 - 3 * odd_x, 3 * odd_y, 3 - 3 * odd_y


def beyond(edge):
    return (edge // 3) * 5


def own_slot(x, y):
    return PLANE + (x + 1) * GRID + y + 1


def piece(ref, at):
    return ref[at * ROWS : (at + 1) * ROWS]


def forward_kernel(tx_out, tx_in, far, near):
    _, _, out_y, in_y = edges()
    for i, ref in enumerate((tx_out, tx_in)):
        far[i * ROWS : (i + 1) * ROWS] = ref[pl.ds(pl.multiple_of(out_y * ROWS, ROWS), ROWS)]
        near[i * ROWS : (i + 1) * ROWS] = ref[pl.ds(pl.multiple_of(in_y * ROWS, ROWS), ROWS)]


def pack_kernel(earlier, tx_out, tx_in, ty_out, ty_in, sems):
    out_x, in_x, out_y, in_y = edges()
    copies = [
        pltpu.make_async_copy(earlier.at[out_x], tx_out, sems.at[0]),
        pltpu.make_async_copy(earlier.at[in_x], tx_in, sems.at[1]),
        pltpu.make_async_copy(earlier.at[:, out_y], ty_out, sems.at[2]),
        pltpu.make_async_copy(earlier.at[:, in_y], ty_in, sems.at[3]),
    ]
    for copy in copies:
        copy.start()
    for copy in copies:
        copy.wait()


def fill_table(levels, codes, table):
    def one_cell(cell, carry):
        x, y = cell // SIDE, cell % SIDE
        level = levels[x, y]
        for k in range(8):
            code = codes[x, y, k]
            old = code >= 9
            offset = jnp.where(old, code - 9, code)
            down = (offset >= 3).astype(jnp.int32) + (offset >= 6).astype(jnp.int32)
            row, column = x + down, y + offset - 3 * down
            slot = row * GRID + column + jnp.where(old, PLANE, 0)
            edge_row, edge_column = (row == 0) | (row == 5), (column == 0) | (column == 5)
            outer = edge_row & edge_column
            own_corner = ((row == 1) | (row == 4)) & ((column == 1) | (column == 4))
            waits = outer & (old == (level > 0))
            open_ = (old & (edge_row | edge_column | own_corner)) | outer
            table[ALL + 8 * cell + k] = jnp.where(waits, BLANK, slot)
            table[SETTLED + 8 * cell + k] = jnp.where(open_, BLANK, slot)
        return carry

    lax.fori_loop(0, SIDE * SIDE, one_cell, 0)
    at = jnp.int32(0)
    for level in range(LEVELS):
        table[FIRST + level] = at

        def one_place(cell, at, level=level):
            table[ORDER + at] = cell
            return at + (levels[cell // SIDE, cell % SIDE] == level).astype(jnp.int32)

        at = lax.fori_loop(0, SIDE * SIDE, one_place, at)
    table[FIRST + LEVELS] = at
    for at, (x, y) in enumerate(CORNERS):
        code = 2 * x + 2 * y // 3 + jnp.where(levels[x, y] > 0, 9, 0)
        found = jnp.int32(-1)
        for k in range(8):
            found = jnp.where(codes[x, y, k] == code, k, found)
        table[LATE + at] = found


def load_kernel(levels, codes, earlier, innovation, conditioner, chol_factor, plane, matrices, noise, sums, table, *rest):
    extras = rest[:4]
    factors, sems = rest[4:]
    copies = [
        pltpu.make_async_copy(chol_factor, factors, sems.at[0]),
        pltpu.make_async_copy(conditioner, matrices.at[:, pl.ds(0, 8 * LANES)], sems.at[1]),
        pltpu.make_async_copy(innovation, noise, sems.at[2]),
    ]
    copies += [
        pltpu.make_async_copy(
            earlier.at[pl.ds(x * SIDE, SIDE)], plane.at[pl.ds((x + 1) * GRID + 1, SIDE)], sems.at[3 + x]
        )
        for x in range(SIDE)
    ]
    for copy in copies:
        copy.start()

    def clear(at, carry):
        plane[at] = jnp.zeros(plane.shape[1:], plane.dtype)
        return carry

    lax.fori_loop(PLANE, BLANK + 1, clear, 0)
    fill_table(levels, codes, table)
    rows = lax.broadcasted_iota(jnp.int32, (LANES, LANES), 0)
    columns = lax.broadcasted_iota(jnp.int32, (LANES, LANES), 1)
    upper = rows <= columns
    copies[0].wait()

    def one_cell(cell, carry):
        factor = jnp.where(upper, factors[cell].astype(jnp.float32), 0.0)
        matrices[cell, 8 * LANES :] = factor.astype(jnp.bfloat16)
        return carry

    lax.fori_loop(0, SIDE * SIDE, one_cell, 0)
    for copy in copies[1:]:
        copy.wait()
    out_x, in_x, out_y, in_y = edges()
    for at, (x, y) in enumerate(CORNERS):
        found = table[LATE + at]
        mark = jnp.full((MARK, LANES), jnp.where(found >= 0, levels[x, y], -1).astype(jnp.float32)).astype(jnp.bfloat16)
        start = pl.multiple_of(LANES * jnp.maximum(found, 0), LANES)
        matrix = matrices[SIDE * x + y, pl.ds(start, LANES)]
        for ref, facing, place in (
            (extras[0], out_x == x, y // 3),
            (extras[1], in_x == x, y // 3),
            (extras[2], out_y == y, x // 3),
            (extras[3], in_y == y, x // 3),
        ):

            @pl.when(facing)
            def _(ref=ref, place=place, matrix=matrix, mark=mark):
                ref[place * LANES : (place + 1) * LANES] = matrix
                ref[2 * LANES + place * MARK : 2 * LANES + (place + 1) * MARK] = mark


def complete_halo(recent, plane, extras):
    out_x, in_x, out_y, in_y = edges()
    source = PLANE if recent else 0
    todo = []
    for side_x, extra_x in ((out_x, extras[0]), (in_x, extras[1])):
        for place in (0, 1):
            todo.append((beyond(side_x) * GRID + 1 + 3 * place, (side_x + 1) * GRID + 5 * place, extra_x, place))
    for side_y, extra_y in ((out_y, extras[2]), (in_y, extras[3])):
        for place in (0, 1):
            todo.append(((1 + 3 * place) * GRID + beyond(side_y), 5 * place * GRID + side_y + 1, extra_y, place))
    marks = [
        jnp.max(extra[2 * LANES + place * MARK : 2 * LANES + (place + 1) * MARK].astype(jnp.float32))
        for _, _, extra, place in todo
    ]
    for (cell, other, extra, place), mark in zip(todo, marks, strict=True):

        @pl.when(mark == recent)
        def _(cell=cell, other=other, extra=extra, place=place):
            product = jnp.dot(
                plane[source + other], extra[place * LANES : (place + 1) * LANES], preferred_element_type=jnp.float32
            )
            plane[PLANE + cell] = (plane[PLANE + cell].astype(jnp.float32) + product).astype(jnp.bfloat16)


def finish_corners(recent, table, plane, matrices, sums, levels, far, near):
    out_x, _, out_y, _ = edges()
    for at, (x, y) in enumerate(CORNERS):
        cell = SIDE * x + y

        @pl.when((levels[x, y] == recent) & (table[LATE + at] >= 0))
        def _(at=at, x=x, y=y, cell=cell):
            rows = pl.ds(pl.multiple_of(jnp.where(out_x == x, 0, ROWS), ROWS), ROWS)
            block = jnp.where(out_y == y, far[rows], near[rows])
            matrix = matrices[cell, pl.ds(pl.multiple_of(LANES * table[LATE + at], LANES), LANES)]
            summed = sums[cell] + jnp.dot(block, matrix, preferred_element_type=jnp.float32)
            plane[own_slot(x, y)] = summed.astype(jnp.bfloat16)


def store_corners(plane, far, near):
    out_x, _, out_y, _ = edges()
    for x, y in CORNERS:
        rows = pl.ds(pl.multiple_of(jnp.where(out_x == x, 0, ROWS), ROWS), ROWS)
        plane[beyond(x) * GRID + beyond(y)] = jnp.where(out_y == y, far[rows], near[rows])


def gather_product(which, cell, table, plane, matrices, noise):
    parts = [plane[table[which + 8 * cell + k]] for k in range(8)] + [noise[cell]]
    return jnp.dot(jnp.concatenate(parts, axis=1), matrices[cell], preferred_element_type=jnp.float32)


def settled_kernel(section, table, plane_in, sums_in, matrices, noise, plane, sums, items):
    def one_cell(at, count):
        cell = table[ORDER + at]
        sums[cell] = gather_product(SETTLED, cell, table, plane, matrices, noise)
        for k in range(8):
            items[1 + count] = 8 * cell + k
            count += (table[ALL + 8 * cell + k] != table[SETTLED + 8 * cell + k]).astype(jnp.int32)
        return count

    items[0] = lax.fori_loop(table[FIRST + section], table[FIRST + section + 1], one_cell, jnp.int32(0))


def store_rows(base, plane, tx_out, tx_in):
    out_x, in_x, _, _ = edges()
    for i in range(SIDE):
        plane[base + beyond(out_x) * GRID + i + 1] = piece(tx_out, i)
        plane[base + beyond(in_x) * GRID + i + 1] = piece(tx_in, i)


def rows_kernel(plane_in, tx_out, tx_in, plane):
    store_rows(PLANE, plane, tx_out, tx_in)


def store_columns(base, plane, ty_out, ty_in):
    _, _, out_y, in_y = edges()
    for i in range(SIDE):
        plane[base + (i + 1) * GRID + beyond(out_y)] = piece(ty_out, i)
        plane[base + (i + 1) * GRID + beyond(in_y)] = piece(ty_in, i)


def pack_sends(base, plane, sends):
    tx_out, tx_in, ty_out, ty_in = sends
    out_x, in_x, out_y, in_y = edges()
    for i in range(SIDE):
        rows = pl.ds(i * ROWS, ROWS)
        tx_out[rows] = plane[own_slot(out_x, i)]
        tx_in[rows] = plane[own_slot(in_x, i)]
        ty_out[rows] = plane[own_slot(i, out_y)]
        ty_in[rows] = plane[own_slot(i, in_y)]
    for i, side in enumerate((out_x, in_x)):
        rows = pl.ds((SIDE + i) * ROWS, ROWS)
        ty_out[rows] = plane[base + beyond(side) * GRID + out_y + 1]
        ty_in[rows] = plane[base + beyond(side) * GRID + in_y + 1]


def first_kernel(table, plane_in, sums_in, matrices, noise, *rest):
    halo, extras, (plane, sums, *sends) = rest[:4], rest[4:8], rest[8:]
    store_rows(0, plane, *halo[:2])
    store_columns(0, plane, *halo[2:])

    def one_cell(at, carry):
        cell = table[ORDER + at]
        summed = gather_product(ALL, cell, table, plane, matrices, noise)
        sums[cell] = summed
        plane[own_slot(cell // SIDE, cell % SIDE)] = summed.astype(jnp.bfloat16)
        return carry

    lax.fori_loop(table[FIRST], table[FIRST + 1], one_cell, 0)
    pack_sends(0, plane, sends)
    for ref, extra in zip(sends, extras, strict=True):
        ref[ref.shape[0] - EXTRA :] = extra[...]


def main_kernel(section, levels, table, items, plane_in, sums_in, matrices, ty_out, ty_in, *rest):
    extras, (plane, sums, *rest) = rest[:4], rest[4:]
    extras = [ref.at[pl.ds(ref.shape[0] - EXTRA, EXTRA)] for ref in extras]
    corners = [ref.at[pl.ds(SIDE * ROWS, 2 * ROWS)] for ref in (ty_out, ty_in)]
    store_columns(PLANE, plane, ty_out, ty_in)
    if section == 1:
        store_corners(plane, *corners)
    complete_halo(section - 1, plane, extras)
    finish_corners(section - 1, table, plane, matrices, sums, levels, *corners)

    def one_item(at, carry):
        item = items[1 + at]
        cell, k = item // 8, item % 8
        matrix = matrices[cell, pl.ds(pl.multiple_of(k * LANES, LANES), LANES)]
        sums[cell] += jnp.dot(plane[table[ALL + item]], matrix, preferred_element_type=jnp.float32)
        return carry

    lax.fori_loop(0, items[0], one_item, 0)

    def one_cell(at, carry):
        cell = table[ORDER + at]
        plane[own_slot(cell // SIDE, cell % SIDE)] = sums[cell].astype(jnp.bfloat16)
        return carry

    lax.fori_loop(table[FIRST + section], table[FIRST + section + 1], one_cell, 0)
    if section < LEVELS - 1:
        pack_sends(PLANE, plane, rest)
    else:
        result, sems = rest
        copies = [
            pltpu.make_async_copy(
                plane.at[pl.ds(own_slot(x, 0), SIDE)], result.at[pl.ds(x * SIDE, SIDE)], sems.at[x]
            )
            for x in range(SIDE)
        ]
        for copy in copies:
            copy.start()
        for copy in copies:
            copy.wait()


def corner_kernel(levels, table, plane_in, matrices, sums, far, near, result_in, plane, result, sems):
    finish_corners(LEVELS - 1, table, plane, matrices, sums, levels, far, near)
    copies = [
        pltpu.make_async_copy(plane.at[own_slot(x, y)], result.at[SIDE * x + y], sems.at[at])
        for at, (x, y) in enumerate(CORNERS)
    ]
    for copy in copies:
        copy.start()
    for copy in copies:
        copy.wait()


def cost(products, depth):
    flops = products * 2 * ROWS * depth * LANES
    return pl.CostEstimate(flops=flops, bytes_accessed=4 << 20, transcendentals=0)


def rows_of(rows):
    return jax.ShapeDtypeStruct((rows, LANES), jnp.bfloat16)


def local(earlier, innovation, conditioner, chol_factor, block_level, neighbours):
    block = earlier.shape[2:]
    tile = SIDE * SIDE
    in_hbm = lambda value: pltpu.with_memory_space_constraint(
        value.reshape(tile, *value.shape[2:]), pltpu.HBM
    )
    edge = jax.ShapeDtypeStruct((SIDE, *block), jnp.bfloat16)
    plane_shape = jax.ShapeDtypeStruct((BLANK + 1, *block), jnp.bfloat16)
    sums_shape = jax.ShapeDtypeStruct((tile, *block), jnp.float32)
    whole = jax.ShapeDtypeStruct((tile, *block), jnp.bfloat16)
    sends = pl.pallas_call(
        pack_kernel,
        out_shape=[edge] * 4,
        in_specs=[HBM],
        out_specs=[VMEM] * 4,
        scratch_shapes=[pltpu.SemaphoreType.DMA((4,))],
        compiler_params=PARAMS,
        name="pack",
    )(pltpu.with_memory_space_constraint(earlier, pltpu.HBM))
    sends = [send.reshape(SIDE * ROWS, LANES) for send in sends]
    plane, matrices, noise, sums, table, *extras = pl.pallas_call(
        load_kernel,
        out_shape=[
            plane_shape,
            jax.ShapeDtypeStruct((tile, DEPTH, LANES), jnp.bfloat16),
            whole,
            sums_shape,
            jax.ShapeDtypeStruct((TABLE,), jnp.int32),
        ]
        + [rows_of(EXTRA)] * 4,
        in_specs=[SMEM] * 2 + [HBM] * 4,
        out_specs=[VMEM] * 4 + [SMEM] + [VMEM] * 4,
        scratch_shapes=[pltpu.VMEM((tile, *chol_factor.shape[2:]), jnp.bfloat16), pltpu.SemaphoreType.DMA((7,))],
        compiler_params=PARAMS,
        cost_estimate=pl.CostEstimate(flops=0, bytes_accessed=14 << 20, transcendentals=0),
        name="load",
    )(block_level, neighbours, in_hbm(earlier), in_hbm(innovation), in_hbm(conditioner), in_hbm(chol_factor))
    halo = exchange(sends)
    plane, sums, *sends = pl.pallas_call(
        first_kernel,
        out_shape=[plane_shape, sums_shape]
        + [rows_of(SIDE * ROWS + EXTRA)] * 2
        + [rows_of((SIDE + 2) * ROWS + EXTRA)] * 2,
        in_specs=[SMEM] + [VMEM] * 12,
        out_specs=[VMEM] * 6,
        input_output_aliases={1: 0, 2: 1},
        compiler_params=PARAMS,
        cost_estimate=cost(8, DEPTH),
        name="level_0",
    )(table, plane, sums, matrices, noise, *halo, *extras)
    for section in range(1, LEVELS):
        final = section == LEVELS - 1
        halo = exchange(sends)
        if section == 1:
            extras = halo
        plane, sums, items = pl.pallas_call(
            functools.partial(settled_kernel, section),
            out_shape=[plane_shape, sums_shape, jax.ShapeDtypeStruct((ITEMS,), jnp.int32)],
            in_specs=[SMEM] + [VMEM] * 4,
            out_specs=[VMEM] * 2 + [SMEM],
            input_output_aliases={1: 0, 2: 1},
            compiler_params=PARAMS,
            cost_estimate=cost(8, DEPTH),
            name=f"settled_{section}",
        )(table, plane, sums, matrices, noise)
        if final:
            far, near = pl.pallas_call(
                forward_kernel,
                out_shape=[rows_of(2 * ROWS)] * 2,
                in_specs=[VMEM] * 2,
                out_specs=[VMEM] * 2,
                compiler_params=PARAMS,
                cost_estimate=cost(0, 0),
                name="forward",
            )(*halo[:2])
            far, near = swap(far, None, "out"), swap(near, None, "in")
        plane = pl.pallas_call(
            rows_kernel,
            out_shape=plane_shape,
            in_specs=[VMEM] * 3,
            out_specs=VMEM,
            input_output_aliases={0: 0},
            compiler_params=PARAMS,
            cost_estimate=cost(2, LANES),
            name=f"rows_{section}",
        )(plane, *halo[:2])
        plane, sums, *sends = pl.pallas_call(
            functools.partial(main_kernel, section),
            out_shape=[plane_shape, sums_shape]
            + ([whole] if final else [rows_of(SIDE * ROWS)] * 2 + [rows_of((SIDE + 2) * ROWS)] * 2),
            in_specs=[SMEM] * 3 + [VMEM] * 9,
            out_specs=[VMEM] * 2 + ([HBM] if final else [VMEM] * 4),
            scratch_shapes=[pltpu.SemaphoreType.DMA((4,))] * final,
            input_output_aliases={3: 0, 4: 1},
            compiler_params=PARAMS,
            cost_estimate=cost(16, LANES),
            name=f"level_{section}",
        )(block_level, table, items, plane, sums, matrices, *halo[2:], *extras)
    _, result = pl.pallas_call(
        corner_kernel,
        out_shape=[plane_shape, whole],
        in_specs=[SMEM] * 2 + [VMEM] * 5 + [HBM],
        out_specs=[VMEM, HBM],
        scratch_shapes=[pltpu.SemaphoreType.DMA((4,))],
        input_output_aliases={2: 0, 7: 1},
        compiler_params=PARAMS,
        cost_estimate=cost(4, LANES),
        name="last_corners",
    )(block_level, table, plane, matrices, sums, far, near, sends[0])
    return result.reshape(earlier.shape)


def solution(mesh):
    placed = (
        P("tx", "ty", None, None),
        P("tx", "ty", None, None),
        P("tx", "ty", None, None),
        P("tx", "ty", None, None),
        P("tx", "ty"),
        P("tx", "ty", None),
    )
    return jax.shard_map(
        local, mesh=mesh, in_specs=placed, out_specs=P("tx", "ty", None, None), check_vma=False
    )
```

time: 96.6 us -> 76.8 us (0.80); the launches traced: 96.2 us -> 77.4 us
  local copies, waits for them, and re-layouts: 19.8 us -> 1.97 us
  starting transfers between devices: 26 us -> 24.4 us
    unnamed x38 -> x6, local copies, waits for them, and re-layouts: 18 us -> 1.97 us
    pallas_call x1 -> x9, Pallas kernels: 1.24 us -> 10.6 us  [the longest x3 7.78 us: local(): pl.pallas_call(functools.partial(settled_kernel, section), out_shape=[pla...]
    pallas_call x4 -> x3, Pallas kernels: 16.2 us -> 6.9 us  [local(): pl.pallas_call(functools.partial(main_kernel, section), out_shape=[plane_...]
    slice x2 -> x0, local copies, waits for them, and re-layouts: 1.76 us -> none  [forward_corners(): last = jnp.stack([piece[3] for piece in blocks]).reshape(2 * ROWS, LANES)]
    ppermute x18, starting transfers between devices: 26 us -> 24.4 us  [swap(): return lax.ppermute(value, BOTH, pairs)]
  transfers between devices with their start and end apart: 18 -> 18, of which waited for: 3 -> 3; matrix products, arithmetic and copies ran while one was open for 2% -> 0% of each run, Pallas kernels for 12% -> 21%
where the time goes in v4:
time: 76.8 us; the launch traced here: 77.4 us
  waiting for transfers between devices  26.4 us (34%)
  Pallas kernels  24.5 us (32%)
  starting transfers between devices  24.4 us (32%)
  local copies, waits for them, and re-layouts  1.97 us (3%)
    ppermute x18, waiting for transfers between devices, swap(): return lax.ppermute(value, BOTH, pairs)  26.4 us
    ppermute x18, starting transfers between devices, swap(): return lax.ppermute(value, BOTH, pairs)  24.4 us
    pallas_call x3, Pallas kernels, local(): pl.pallas_call(functools.partial(settled_kernel, section), out_shape=[pla...  7.78 us
    pallas_call x3, Pallas kernels, local(): pl.pallas_call(functools.partial(main_kernel, section), out_shape=[plane_...  6.9 us
    pallas_call x1, Pallas kernels, local(): pl.pallas_call(load_kernel, out_shape=[plane_shape, jax.ShapeDtypeStruct(...  5.31 us
    unnamed x6, local copies, waits for them, and re-layouts  1.97 us
    pallas_call x1, Pallas kernels, local(): pl.pallas_call(corner_kernel, out_shape=[plane_shape, whole], in_specs=[S...  1.66 us
  transfers between devices with their start and end apart: 18, of which 3 were waited for; matrix products, arithmetic and copies ran while one was open for 0% of the time, Pallas kernels for 21%

profile of v4, /device:TPU:0, one launch (start us, length us, event | category | flops | bytes accessed | tf_op | source)
XLA Modules:
  0.0 77.4 jit_solution(4977427025882961074)
XLA Ops:
  0.0 1.2 %pack.1 = (bf16[4,256,128]{2,1,0:T(8,128)(2,1)S(1)}, bf16[4,256,128]{2,1,0:T(8,128)(2,1)S(1)}, bf16[4,256,128]{2,1,0:T(8,128)(2,1)S(1)}, bf16[4,256,128]{2,1,0:T(8,128)(2,1)S(1)}) custom-call(bf16[4,4,256,128]{3,2,1,0:T(8,128)(2,1)} %earlier.1), custom_call_target="tpu_custom_call" | custom-call | tf_op jit(solution)/shard_map/pack/pallas_call | solution.py:371
  1.2 1.7 %collective-permute-start.1 = (bf16[1024,128]{1,0:T(8,128)(2,1)S(1)}, bf16[1024,128]{1,0:T(8,128)(2,1)S(1)}, u32[]{:S(2)}, u32[]{:S(2)}) collective-permute-start(bf16[1024,128]{1,0:T(8,128)(2,1)S(1)} %bitcast.12), channel_id=1, source_target_pairs={{0,8},{1,9},{2,10},{3,11},{4,12},{5,13},{6,14},{7,15},{8,0},{9,1},... | collective-permute-start | bytes 786440 | tf_op jit(solution)/shard_map/ppermute | solution.py:45
  2.9 4.5 %collective-permute-start = (bf16[1024,128]{1,0:T(8,128)(2,1)S(1)}, bf16[1024,128]{1,0:T(8,128)(2,1)S(1)}, u32[]{:S(2)}, u32[]{:S(2)}) collective-permute-start(bf16[1024,128]{1,0:T(8,128)(2,1)S(1)} %bitcast.11), channel_id=1, source_target_pairs={{0,120},{1,121},{2,122},{3,123},{4,124},{5,125},{6,126},{7,127},{8... | collective-permute-start | bytes 786440 | tf_op jit(solution)/shard_map/ppermute | solution.py:45
  7.4 2.9 %collective-permute-start.2 = (bf16[1024,128]{1,0:T(8,128)(2,1)S(1)}, bf16[1024,128]{1,0:T(8,128)(2,1)S(1)}, u32[]{:S(2)}, u32[]{:S(2)}) collective-permute-start(bf16[1024,128]{1,0:T(8,128)(2,1)S(1)} %bitcast.10), channel_id=1, source_target_pairs={{0,7},{1,2},{2,1},{3,4},{4,3},{5,6},{6,5},{7,0},{8,15},{9,10},{10,... | collective-permute-start | bytes 786440 | tf_op jit(solution)/shard_map/ppermute | solution.py:45
  10.3 0.0 collective-permute-start.3
  10.4 0.7 copy-done
  11.0 0.7 copy-done.2
  11.7 5.3 %load.1 = (bf16[73,256,128]{2,1,0:T(8,128)(2,1)S(1)}, bf16[16,1152,128]{2,1,0:T(8,128)(2,1)S(1)}, bf16[16,256,128]{2,1,0:T(8,128)(2,1)S(1)}, f32[16,256,128]{2,1...) custom-call(s32[4,4]{1,0:T(4,128)S(1)} %copy-done, ...), custom_call_target="tpu_custom_call" | custom-call | bytes 14680064 | tf_op jit(solution)/shard_map/load/pallas_call | solution.py:381
  17.1 1.4 %level_0.1 = (bf16[73,256,128]{2,1,0:T(8,128)(2,1)S(1)}, f32[16,256,128]{2,1,0:T(8,128)S(1)}, bf16[1312,128]{1,0:T(8,128)(2,1)S(1)}, bf16[1312,128]{1,0:T(8,128)...) custom-call(s32[296]{0:T(512)S(1)} %get-tuple-element.51.table, ...), custom_call_target="tpu_custom_call", output_to_operand_aliasing={{0}: (1, {}), {1}: (2, {})} | custom-call | flops 603979776 | bytes 4194304 | tf_op jit(solution)/shard_map/level_0/pallas_call | solution.py:399
  18.5 1.6 %collective-permute-start.6 = (bf16[1824,128]{1,0:T(8,128)(2,1)S(1)}, bf16[1824,128]{1,0:T(8,128)(2,1)S(1)}, u32[]{:S(2)}, u32[]{:S(2)}) collective-permute-start(bf16[1824,128]{1,0:T(8,128)(2,1)S(1)} %get-tuple-element.71), channel_id=1, source_target_pairs={{0,7},{1,2},{2,1},{3,4},{4,3},{5,6},{6,5},{7,0},{8,15},{9,10},{10,... | collective-permute-start | bytes 1400840 | tf_op jit(solution)/shard_map/ppermute | solution.py:45
  20.1 2.5 %collective-permute-start.4 = (bf16[1312,128]{1,0:T(8,128)(2,1)S(1)}, bf16[1312,128]{1,0:T(8,128)(2,1)S(1)}, u32[]{:S(2)}, u32[]{:S(2)}) collective-permute-start(bf16[1312,128]{1,0:T(8,128)(2,1)S(1)} %get-tuple-element.68), channel_id=1, source_target_pairs={{0,120},{1,121},{2,122},{3,123},{4,124},{5,125},{6,126},{7,127},{8... | collective-permute-start | bytes 1007624 | tf_op jit(solution)/shard_map/ppermute | solution.py:45
  22.6 2.1 %settled_1.1 = (bf16[73,256,128]{2,1,0:T(8,128)(2,1)S(1)}, f32[16,256,128]{2,1,0:T(8,128)S(1)}, s32[66]{0:T(128)S(1)}) custom-call(s32[296]{0:T(512)S(1)} %get-tuple-element.51.table, bf16[73,256,128]{2,1,0:T(8,128)(2,1)S(1)} %get-tuple-element.64.plane_in, ...), custom_call_target="tpu_custom_call", output_to_operand_aliasing={{0}: (1, {}), {1}: (2, {})} | custom-call | flops 603979776 | bytes 4194304 | tf_op jit(solution)/shard_map/settled_1/pallas_call | solution.py:416
  24.7 9.1 %collective-permute-done.4.tx_out.rest_0_ = bf16[1312,128]{1,0:T(8,128)(2,1)S(1)} collective-permute-done((bf16[1312,128]{1,0:T(8,128)(2,1)S(1)}, bf16[1312,128]{1,0:T(8,128)(2,1)S(1)}, u32[]{:S(2)}, u32[]{:S(2)}) %collective-permute-start.4) | collective-permute-done | bytes 335904 | tf_op jit(solution)/shard_map/ppermute | solution.py:45
  33.8 0.1 rows_1.1.plane_in
  33.8 1.9 %level_1.1 = (bf16[73,256,128]{2,1,0:T(8,128)(2,1)S(1)}, f32[16,256,128]{2,1,0:T(8,128)S(1)}, bf16[1024,128]{1,0:T(8,128)(2,1)S(1)}, bf16[1024,128]{1,0:T(8,128)...) custom-call(s32[4,4]{1,0:T(4,128)S(1)} %copy-done, ...), custom_call_target="tpu_custom_call", output_to_operand_aliasing={{0}: (3, {}), {1}: (4, {})} | custom-call | flops 134217728 | bytes 4194304 | tf_op jit(solution)/shard_map/level_1/pallas_call | solution.py:447
  35.7 2.3 %collective-permute-start.10 = (bf16[1536,128]{1,0:T(8,128)(2,1)S(1)}, bf16[1536,128]{1,0:T(8,128)(2,1)S(1)}, u32[]{:S(2)}, u32[]{:S(2)}) collective-permute-start(bf16[1536,128]{1,0:T(8,128)(2,1)S(1)} %get-tuple-element.80), channel_id=1, source_target_pairs={{0,7},{1,2},{2,1},{3,4},{4,3},{5,6},{6,5},{7,0},{8,15},{9,10},{10,... | collective-permute-start | bytes 1179656 | tf_op jit(solution)/shard_map/ppermute | solution.py:45
  38.0 2.4 %collective-permute-start.8 = (bf16[1024,128]{1,0:T(8,128)(2,1)S(1)}, bf16[1024,128]{1,0:T(8,128)(2,1)S(1)}, u32[]{:S(2)}, u32[]{:S(2)}) collective-permute-start(bf16[1024,128]{1,0:T(8,128)(2,1)S(1)} %get-tuple-element.77), channel_id=1, source_target_pairs={{0,120},{1,121},{2,122},{3,123},{4,124},{5,125},{6,126},{7,127},{8... | collective-permute-start | bytes 786440 | tf_op jit(solution)/shard_map/ppermute | solution.py:45
  40.4 2.1 %settled_2.1 = (bf16[73,256,128]{2,1,0:T(8,128)(2,1)S(1)}, f32[16,256,128]{2,1,0:T(8,128)S(1)}, s32[66]{0:T(128)S(1)}) custom-call(s32[296]{0:T(512)S(1)} %get-tuple-element.51.table, bf16[73,256,128]{2,1,0:T(8,128)(2,1)S(1)} %get-tuple-element.73.plane_in, ...), custom_call_target="tpu_custom_call", output_to_operand_aliasing={{0}: (1, {}), {1}: (2, {})} | custom-call | flops 603979776 | bytes 4194304 | tf_op jit(solution)/shard_map/settled_2/pallas_call | solution.py:416
  42.5 7.5 %collective-permute-done.8.tx_out = bf16[1024,128]{1,0:T(8,128)(2,1)S(1)} collective-permute-done((bf16[1024,128]{1,0:T(8,128)(2,1)S(1)}, bf16[1024,128]{1,0:T(8,128)(2,1)S(1)}, u32[]{:S(2)}, u32[]{:S(2)}) %collective-permute-start.8) | collective-permute-done | bytes 262176 | tf_op jit(solution)/shard_map/ppermute | solution.py:45
  50.0 0.1 rows_2.1.plane_in
  50.1 0.6 copy-done.1
  50.7 1.7 %level_2.1 = (bf16[73,256,128]{2,1,0:T(8,128)(2,1)S(1)}, f32[16,256,128]{2,1,0:T(8,128)S(1)}, bf16[1024,128]{1,0:T(8,128)(2,1)S(1)}, bf16[1024,128]{1,0:T(8,128)...) custom-call(s32[4,4]{1,0:T(4,128)S(1)} %copy-done.1, ...), custom_call_target="tpu_custom_call", output_to_operand_aliasing={{0}: (3, {}), {1}: (4, {})} | custom-call | flops 134217728 | bytes 4194304 | tf_op jit(solution)/shard_map/level_2/pallas_call | solution.py:447
  52.4 2.2 %collective-permute-start.14 = (bf16[1536,128]{1,0:T(8,128)(2,1)S(1)}, bf16[1536,128]{1,0:T(8,128)(2,1)S(1)}, u32[]{:S(2)}, u32[]{:S(2)}) collective-permute-start(bf16[1536,128]{1,0:T(8,128)(2,1)S(1)} %get-tuple-element.89), channel_id=1, source_target_pairs={{0,7},{1,2},{2,1},{3,4},{4,3},{5,6},{6,5},{7,0},{8,15},{9,10},{10,... | collective-permute-start | bytes 1179656 | tf_op jit(solution)/shard_map/ppermute | solution.py:45
  54.6 0.7 collective-permute-start.15
  55.3 1.8 %collective-permute-start.12 = (bf16[1024,128]{1,0:T(8,128)(2,1)S(1)}, bf16[1024,128]{1,0:T(8,128)(2,1)S(1)}, u32[]{:S(2)}, u32[]{:S(2)}) collective-permute-start(bf16[1024,128]{1,0:T(8,128)(2,1)S(1)} %get-tuple-element.86), channel_id=1, source_target_pairs={{0,120},{1,121},{2,122},{3,123},{4,124},{5,125},{6,126},{7,127},{8... | collective-permute-start | bytes 786440 | tf_op jit(solution)/shard_map/ppermute | solution.py:45
  57.1 9.8 %collective-permute-done.12.tx_out = bf16[1024,128]{1,0:T(8,128)(2,1)S(1)} collective-permute-done((bf16[1024,128]{1,0:T(8,128)(2,1)S(1)}, bf16[1024,128]{1,0:T(8,128)(2,1)S(1)}, u32[]{:S(2)}, u32[]{:S(2)}) %collective-permute-start.12) | collective-permute-done | bytes 262176 | tf_op jit(solution)/shard_map/ppermute | solution.py:45
  66.9 0.1 collective-permute-start.16
  67.0 1.7 %collective-permute-start.17 = (bf16[512,128]{1,0:T(8,128)(2,1)S(1)}, bf16[512,128]{1,0:T(8,128)(2,1)S(1)}, u32[]{:S(2)}, u32[]{:S(2)}) collective-permute-start(bf16[512,128]{1,0:T(8,128)(2,1)S(1)} %get-tuple-element.94), channel_id=1, source_target_pairs={{0,1},{1,0},{2,3},{3,2},{4,5},{5,4},{6,7},{7,6},{8,9},{9,8},{10,11... | collective-permute-start | bytes 393224 | tf_op jit(solution)/shard_map/ppermute | solution.py:45
  68.7 3.6 %settled_3.1 = (bf16[73,256,128]{2,1,0:T(8,128)(2,1)S(1)}, f32[16,256,128]{2,1,0:T(8,128)S(1)}, s32[66]{0:T(128)S(1)}) custom-call(s32[296]{0:T(512)S(1)} %get-tuple-element.51.table, bf16[73,256,128]{2,1,0:T(8,128)(2,1)S(1)} %get-tuple-element.82.plane_in, ...), custom_call_target="tpu_custom_call", output_to_operand_aliasing={{0}: (1, {}), {1}: (2, {})} | custom-call | flops 603979776 | bytes 4194304 | tf_op jit(solution)/shard_map/settled_3/pallas_call | solution.py:416
  72.3 0.1 rows_3.1.plane_in
  72.4 3.3 %level_3.1 = (bf16[73,256,128]{2,1,0:T(8,128)(2,1)S(1)}, f32[16,256,128]{2,1,0:T(8,128)S(1)}, bf16[16,256,128]{2,1,0:T(8,128)(2,1)}) custom-call(s32[4,4]{1,0:T(4,128)S(1)} %copy-done.1, s32[296]{0:T(512)S(1)} %get-tuple-element.51.table, s32[66]{0:T(128)S(1)} %get-tuple-element.84.items, ...), custom_call_target="tpu_custom_call", output_to_operand_aliasing={{0}: (3, {}), {1}: (4, {})} | custom-call | flops 134217728 | bytes 4194304 | tf_op jit(solution)/shard_map/level_3/pallas_call | solution.py:447
  75.8 1.7 %last_corners.1 = (bf16[73,256,128]{2,1,0:T(8,128)(2,1)S(1)}, bf16[16,256,128]{2,1,0:T(8,128)(2,1)}) custom-call(s32[4,4]{1,0:T(4,128)S(1)} %copy-done.1, s32[296]{0:T(512)S(1)} %get-tuple-element.51.table, bf16[73,256,128]{2,1,0:T(8,128)(2,1)S(1)} %get-tuple-element.91.plane_in, ...), custom_call_target="tpu_custom_call", output_to_operand_aliasing={{0}: (2, {}), {1}: (7, {})} | custom-call | flops 33554432 | bytes 4194304 | tf_op jit(solution)/shard_map/last_corners/pallas_call | solution.py:459
  (24 shorter events, 0.1 us)
Async XLA Ops:
  1.2 15.8 %collective-permute-start.1 = (bf16[1024,128]{1,0:T(8,128)(2,1)S(1)}, bf16[1024,128]{1,0:T(8,128)(2,1)S(1)}, u32[]{:S(2)}, u32[]{:S(2)}) collective-permute-start(bf16[1024,128]{1,0:T(8,128)(2,1)S(1)} %bitcast.12), channel_id=1, source_target_pairs={{0,8},{1,9},{2,10},{3,11},{4,12},{5,13},{6,14},{7,15},{8,0},{9,1},... | collective-permute-start | bytes 786440 | tf_op jit(solution)/shard_map/ppermute | solution.py:45
  2.9 14.2 %collective-permute-start = (bf16[1024,128]{1,0:T(8,128)(2,1)S(1)}, bf16[1024,128]{1,0:T(8,128)(2,1)S(1)}, u32[]{:S(2)}, u32[]{:S(2)}) collective-permute-start(bf16[1024,128]{1,0:T(8,128)(2,1)S(1)} %bitcast.11), channel_id=1, source_target_pairs={{0,120},{1,121},{2,122},{3,123},{4,124},{5,125},{6,126},{7,127},{8... | collective-permute-start | bytes 786440 | tf_op jit(solution)/shard_map/ppermute | solution.py:45
  7.4 9.6 %collective-permute-start.2 = (bf16[1024,128]{1,0:T(8,128)(2,1)S(1)}, bf16[1024,128]{1,0:T(8,128)(2,1)S(1)}, u32[]{:S(2)}, u32[]{:S(2)}) collective-permute-start(bf16[1024,128]{1,0:T(8,128)(2,1)S(1)} %bitcast.10), channel_id=1, source_target_pairs={{0,7},{1,2},{2,1},{3,4},{4,3},{5,6},{6,5},{7,0},{8,15},{9,10},{10,... | collective-permute-start | bytes 786440 | tf_op jit(solution)/shard_map/ppermute | solution.py:45
  10.3 6.7 %collective-permute-start.3 = (bf16[1024,128]{1,0:T(8,128)(2,1)S(1)}, bf16[1024,128]{1,0:T(8,128)(2,1)S(1)}, u32[]{:S(2)}, u32[]{:S(2)}) collective-permute-start(bf16[1024,128]{1,0:T(8,128)(2,1)S(1)} %bitcast.9), channel_id=1, source_target_pairs={{0,1},{1,0},{2,3},{3,2},{4,5},{5,4},{6,7},{7,6},{8,9},{9,8},{10,11... | collective-permute-start | bytes 786440 | tf_op jit(solution)/shard_map/ppermute | solution.py:45
  10.3 0.7 copy-start
  11.0 0.7 copy-start.2
  18.5 15.3 %collective-permute-start.6 = (bf16[1824,128]{1,0:T(8,128)(2,1)S(1)}, bf16[1824,128]{1,0:T(8,128)(2,1)S(1)}, u32[]{:S(2)}, u32[]{:S(2)}) collective-permute-start(bf16[1824,128]{1,0:T(8,128)(2,1)S(1)} %get-tuple-element.71), channel_id=1, source_target_pairs={{0,7},{1,2},{2,1},{3,4},{4,3},{5,6},{6,5},{7,0},{8,15},{9,10},{10,... | collective-permute-start | bytes 1400840 | tf_op jit(solution)/shard_map/ppermute | solution.py:45
  20.1 13.7 %collective-permute-start.7 = (bf16[1824,128]{1,0:T(8,128)(2,1)S(1)}, bf16[1824,128]{1,0:T(8,128)(2,1)S(1)}, u32[]{:S(2)}, u32[]{:S(2)}) collective-permute-start(bf16[1824,128]{1,0:T(8,128)(2,1)S(1)} %get-tuple-element.72), channel_id=1, source_target_pairs={{0,1},{1,0},{2,3},{3,2},{4,5},{5,4},{6,7},{7,6},{8,9},{9,8},{10,11... | collective-permute-start | bytes 1400840 | tf_op jit(solution)/shard_map/ppermute | solution.py:45
  20.1 13.6 %collective-permute-start.4 = (bf16[1312,128]{1,0:T(8,128)(2,1)S(1)}, bf16[1312,128]{1,0:T(8,128)(2,1)S(1)}, u32[]{:S(2)}, u32[]{:S(2)}) collective-permute-start(bf16[1312,128]{1,0:T(8,128)(2,1)S(1)} %get-tuple-element.68), channel_id=1, source_target_pairs={{0,120},{1,121},{2,122},{3,123},{4,124},{5,125},{6,126},{7,127},{8... | collective-permute-start | bytes 1007624 | tf_op jit(solution)/shard_map/ppermute | solution.py:45
  22.6 11.2 %collective-permute-start.5 = (bf16[1312,128]{1,0:T(8,128)(2,1)S(1)}, bf16[1312,128]{1,0:T(8,128)(2,1)S(1)}, u32[]{:S(2)}, u32[]{:S(2)}) collective-permute-start(bf16[1312,128]{1,0:T(8,128)(2,1)S(1)} %get-tuple-element.69), channel_id=1, source_target_pairs={{0,8},{1,9},{2,10},{3,11},{4,12},{5,13},{6,14},{7,15},{8,0},{9,1},... | collective-permute-start | bytes 1007624 | tf_op jit(solution)/shard_map/ppermute | solution.py:45
  35.7 14.4 %collective-permute-start.10 = (bf16[1536,128]{1,0:T(8,128)(2,1)S(1)}, bf16[1536,128]{1,0:T(8,128)(2,1)S(1)}, u32[]{:S(2)}, u32[]{:S(2)}) collective-permute-start(bf16[1536,128]{1,0:T(8,128)(2,1)S(1)} %get-tuple-element.80), channel_id=1, source_target_pairs={{0,7},{1,2},{2,1},{3,4},{4,3},{5,6},{6,5},{7,0},{8,15},{9,10},{10,... | collective-permute-start | bytes 1179656 | tf_op jit(solution)/shard_map/ppermute | solution.py:45
  38.0 12.1 %collective-permute-start.11 = (bf16[1536,128]{1,0:T(8,128)(2,1)S(1)}, bf16[1536,128]{1,0:T(8,128)(2,1)S(1)}, u32[]{:S(2)}, u32[]{:S(2)}) collective-permute-start(bf16[1536,128]{1,0:T(8,128)(2,1)S(1)} %get-tuple-element.81), channel_id=1, source_target_pairs={{0,1},{1,0},{2,3},{3,2},{4,5},{5,4},{6,7},{7,6},{8,9},{9,8},{10,11... | collective-permute-start | bytes 1179656 | tf_op jit(solution)/shard_map/ppermute | solution.py:45
  38.0 12.0 %collective-permute-start.8 = (bf16[1024,128]{1,0:T(8,128)(2,1)S(1)}, bf16[1024,128]{1,0:T(8,128)(2,1)S(1)}, u32[]{:S(2)}, u32[]{:S(2)}) collective-permute-start(bf16[1024,128]{1,0:T(8,128)(2,1)S(1)} %get-tuple-element.77), channel_id=1, source_target_pairs={{0,120},{1,121},{2,122},{3,123},{4,124},{5,125},{6,126},{7,127},{8... | collective-permute-start | bytes 786440 | tf_op jit(solution)/shard_map/ppermute | solution.py:45
  40.4 9.6 %collective-permute-start.9 = (bf16[1024,128]{1,0:T(8,128)(2,1)S(1)}, bf16[1024,128]{1,0:T(8,128)(2,1)S(1)}, u32[]{:S(2)}, u32[]{:S(2)}) collective-permute-start(bf16[1024,128]{1,0:T(8,128)(2,1)S(1)} %get-tuple-element.78), channel_id=1, source_target_pairs={{0,8},{1,9},{2,10},{3,11},{4,12},{5,13},{6,14},{7,15},{8,0},{9,1},... | collective-permute-start | bytes 786440 | tf_op jit(solution)/shard_map/ppermute | solution.py:45
  50.0 0.7 copy-start.1
  52.4 20.0 %collective-permute-start.14 = (bf16[1536,128]{1,0:T(8,128)(2,1)S(1)}, bf16[1536,128]{1,0:T(8,128)(2,1)S(1)}, u32[]{:S(2)}, u32[]{:S(2)}) collective-permute-start(bf16[1536,128]{1,0:T(8,128)(2,1)S(1)} %get-tuple-element.89), channel_id=1, source_target_pairs={{0,7},{1,2},{2,1},{3,4},{4,3},{5,6},{6,5},{7,0},{8,15},{9,10},{10,... | collective-permute-start | bytes 1179656 | tf_op jit(solution)/shard_map/ppermute | solution.py:45
  54.6 17.8 %collective-permute-start.15 = (bf16[1536,128]{1,0:T(8,128)(2,1)S(1)}, bf16[1536,128]{1,0:T(8,128)(2,1)S(1)}, u32[]{:S(2)}, u32[]{:S(2)}) collective-permute-start(bf16[1536,128]{1,0:T(8,128)(2,1)S(1)} %get-tuple-element.90), channel_id=1, source_target_pairs={{0,1},{1,0},{2,3},{3,2},{4,5},{5,4},{6,7},{7,6},{8,9},{9,8},{10,11... | collective-permute-start | bytes 1179656 | tf_op jit(solution)/shard_map/ppermute | solution.py:45
  55.3 11.5 %collective-permute-start.12 = (bf16[1024,128]{1,0:T(8,128)(2,1)S(1)}, bf16[1024,128]{1,0:T(8,128)(2,1)S(1)}, u32[]{:S(2)}, u32[]{:S(2)}) collective-permute-start(bf16[1024,128]{1,0:T(8,128)(2,1)S(1)} %get-tuple-element.86), channel_id=1, source_target_pairs={{0,120},{1,121},{2,122},{3,123},{4,124},{5,125},{6,126},{7,127},{8... | collective-permute-start | bytes 786440 | tf_op jit(solution)/shard_map/ppermute | solution.py:45
  57.1 9.8 %collective-permute-start.13 = (bf16[1024,128]{1,0:T(8,128)(2,1)S(1)}, bf16[1024,128]{1,0:T(8,128)(2,1)S(1)}, u32[]{:S(2)}, u32[]{:S(2)}) collective-permute-start(bf16[1024,128]{1,0:T(8,128)(2,1)S(1)} %get-tuple-element.87), channel_id=1, source_target_pairs={{0,8},{1,9},{2,10},{3,11},{4,12},{5,13},{6,14},{7,15},{8,0},{9,1},... | collective-permute-start | bytes 786440 | tf_op jit(solution)/shard_map/ppermute | solution.py:45
  66.9 8.9 %collective-permute-start.16 = (bf16[512,128]{1,0:T(8,128)(2,1)S(1)}, bf16[512,128]{1,0:T(8,128)(2,1)S(1)}, u32[]{:S(2)}, u32[]{:S(2)}) collective-permute-start(bf16[512,128]{1,0:T(8,128)(2,1)S(1)} %get-tuple-element.93), channel_id=1, source_target_pairs={{0,7},{1,2},{2,1},{3,4},{4,3},{5,6},{6,5},{7,0},{8,15},{9,10},{10,... | collective-permute-start | bytes 393224 | tf_op jit(solution)/shard_map/ppermute | solution.py:45
  67.0 8.8 %collective-permute-start.17 = (bf16[512,128]{1,0:T(8,128)(2,1)S(1)}, bf16[512,128]{1,0:T(8,128)(2,1)S(1)}, u32[]{:S(2)}, u32[]{:S(2)}) collective-permute-start(bf16[512,128]{1,0:T(8,128)(2,1)S(1)} %get-tuple-element.94), channel_id=1, source_target_pairs={{0,1},{1,0},{2,3},{3,2},{4,5},{5,4},{6,7},{7,6},{8,9},{9,8},{10,11... | collective-permute-start | bytes 393224 | tf_op jit(solution)/shard_map/ppermute | solution.py:45

commit v5 on v4

v5 whole, which is shorter than its diff:
```python
import functools

import jax
import jax.numpy as jnp
from jax import lax
from jax.experimental import pallas as pl
from jax.experimental.pallas import tpu as pltpu
from jax.sharding import PartitionSpec as P

LEVELS = 4
BOTH = ("tx", "ty")
SIDE = 4
GRID = 6
PLANE = GRID * GRID
BLANK = 2 * PLANE
ROWS = 256
LANES = 128
MARK = 16
EXTRA = 2 * (LANES + MARK)
DEPTH = 9 * LANES
LEVEL, LATE, SLOT, ITEM, MARKS, COUNT, TABLE = 0, 16, 20, 148, 220, 228, 229
GROUP = 4
CORNERS = ((0, 0), (0, 3), (3, 0), (3, 3))
VMEM = pl.BlockSpec(memory_space=pltpu.VMEM)
SMEM = pl.BlockSpec(memory_space=pltpu.SMEM)
HBM = pl.BlockSpec(memory_space=pltpu.HBM)
PARAMS = pltpu.CompilerParams(vmem_limit_bytes=8 * 1024 * 1024)


def partner(at, size, kind):
    if kind == "in":
        return at ^ 1
    if kind == "out":
        return (at + 1) % size if at % 2 else (at - 1) % size
    return at


def swap(value, along_x, along_y):
    size_x, size_y = lax.axis_size("tx"), lax.axis_size("ty")
    pairs = [
        (x * size_y + y, partner(x, size_x, along_x) * size_y + partner(y, size_y, along_y))
        for x in range(size_x)
        for y in range(size_y)
    ]
    return lax.ppermute(value, BOTH, pairs)


def exchange(sends):
    tx_out, tx_in, *ty_out, ty_in = sends
    halo = [swap(tx_out, "out", None), swap(tx_in, "in", None)]
    return halo + [swap(part, None, "out") for part in ty_out] + [swap(ty_in, None, "in")]


def edges():
    odd_x = lax.rem(lax.axis_index("tx"), 2)
    odd_y = lax.rem(lax.axis_index("ty"), 2)
    return 3 * odd_x, 3 - 3 * odd_x, 3 * odd_y, 3 - 3 * odd_y


def beyond(edge):
    return (edge // 3) * 5


def own_slot(x, y):
    return PLANE + (x + 1) * GRID + y + 1


def piece(ref, at):
    return ref[at * ROWS : (at + 1) * ROWS]


def forward_kernel(plane, far, near):
    out_x, in_x, out_y, in_y = edges()
    for i, side in enumerate((out_x, in_x)):
        far[i * ROWS : (i + 1) * ROWS] = plane[PLANE + beyond(side) * GRID + out_y + 1]
        near[i * ROWS : (i + 1) * ROWS] = plane[PLANE + beyond(side) * GRID + in_y + 1]


def pack_kernel(earlier, tx_out, tx_in, ty_out, ty_in, sems):
    out_x, in_x, out_y, in_y = edges()
    copies = [
        pltpu.make_async_copy(earlier.at[out_x], tx_out, sems.at[0]),
        pltpu.make_async_copy(earlier.at[in_x], tx_in, sems.at[1]),
        pltpu.make_async_copy(earlier.at[:, out_y], ty_out, sems.at[2]),
        pltpu.make_async_copy(earlier.at[:, in_y], ty_in, sems.at[3]),
    ]
    for copy in copies:
        copy.start()
    for copy in copies:
        copy.wait()


def late_code(levels, codes, x, y):
    code = 2 * x + 2 * y // 3 + jnp.where(levels[x, y] > 0, 9, 0)
    found = jnp.int32(-1)
    for k in range(8):
        found = jnp.where(codes[x, y, k] == code, k, found)
    return found


def fill_slots(cell, level, codes, every, settled):
    x, y = cell // SIDE, cell % SIDE
    for k in range(8):
        code = codes[x, y, k]
        old = code >= 9
        offset = jnp.where(old, code - 9, code)
        down = (offset >= 3).astype(jnp.int32) + (offset >= 6).astype(jnp.int32)
        row, column = x + down, y + offset - 3 * down
        slot = row * GRID + column + jnp.where(old, PLANE, 0)
        edge_row, edge_column = (row == 0) | (row == 5), (column == 0) | (column == 5)
        outer = edge_row & edge_column
        waits = outer & (old == (level > 0))
        every[SLOT + 8 * cell + k] = jnp.where(waits, BLANK, slot)
        if settled is not None:
            own_corner = ((row == 1) | (row == 4)) & ((column == 1) | (column == 4))
            open_ = (old & (edge_row | edge_column | own_corner)) | outer
            settled[8 * cell + k] = jnp.where(open_, BLANK, slot)


def cells_of(section, table, body):
    def one_cell(cell, carry):
        @pl.when(table[LEVEL + cell] == section)
        def _():
            body(cell)

        return carry

    lax.fori_loop(0, SIDE * SIDE, one_cell, 0)


def cell_copies(cell, sources, targets, sems):
    innovation, conditioner, chol_factor = sources
    noise, matrices, factors = targets
    return (
        pltpu.make_async_copy(chol_factor.at[cell], factors.at[cell], sems.at[0, cell]),
        pltpu.make_async_copy(innovation.at[cell], noise.at[cell], sems.at[1, cell]),
        pltpu.make_async_copy(conditioner.at[cell], matrices.at[cell, pl.ds(0, 8 * LANES)], sems.at[2, cell]),
    )


def start_cell(cell, sources, targets, sems):
    for copy in cell_copies(cell, sources, targets, sems):
        copy.start()


def finish_cell(cell, sources, targets, sems):
    _, matrices, factors = targets
    copies = cell_copies(cell, sources, targets, sems)
    copies[0].wait()
    rows = lax.broadcasted_iota(jnp.int32, (LANES, LANES), 0)
    columns = lax.broadcasted_iota(jnp.int32, (LANES, LANES), 1)
    upper = jnp.where(rows <= columns, factors[cell].astype(jnp.float32), 0.0)
    matrices[cell, 8 * LANES :] = upper.astype(jnp.bfloat16)
    copies[1].wait()
    copies[2].wait()


def load_kernel(
    block_level, neighbours, earlier, innovation, conditioner, chol_factor, plane, matrices, noise, sums, table, codes, extras, *rest
):
    levels, factors, sems, more_sems = rest
    scalars = [
        pltpu.make_async_copy(block_level, levels, more_sems.at[12]),
        pltpu.make_async_copy(neighbours, codes, more_sems.at[13]),
    ]
    copies = [
        pltpu.make_async_copy(
            earlier.at[pl.ds(x * SIDE, SIDE)], plane.at[pl.ds((x + 1) * GRID + 1, SIDE)], more_sems.at[x]
        )
        for x in range(SIDE)
    ]
    for copy in scalars + copies:
        copy.start()

    def clear(at, carry):
        plane[at] = jnp.zeros(plane.shape[1:], plane.dtype)
        return carry

    lax.fori_loop(PLANE, BLANK + 1, clear, 0)
    for copy in scalars:
        copy.wait()
    for cell in range(SIDE * SIDE):
        table[LEVEL + cell] = levels[cell // SIDE, cell % SIDE]
    sources, targets = (innovation, conditioner, chol_factor), (noise, matrices, factors)
    cells_of(0, table, lambda cell: start_cell(cell, sources, targets, sems))
    out_x, _, out_y, _ = edges()
    for at, (x, y) in enumerate(CORNERS):
        late = late_code(levels, codes, x, y)
        table[LATE + at] = late
        mark = jnp.full((MARK, LANES), jnp.where(late >= 0, levels[x, y], -1).astype(jnp.float32)).astype(jnp.bfloat16)
        start = pl.multiple_of(LANES * jnp.maximum(late, 0), LANES)
        matrix = conditioner.at[SIDE * x + y, pl.ds(start, LANES)]
        for way, (side, place) in enumerate(((jnp.where(out_x == x, 0, 1), y // 3), (jnp.where(out_y == y, 2, 3), x // 3))):
            copy = pltpu.make_async_copy(
                matrix, extras.at[side, pl.ds(place * LANES, LANES)], more_sems.at[4 + 2 * at + way]
            )
            copy.start()
            copies.append(copy)
            extras[side, 2 * LANES + place * MARK : 2 * LANES + (place + 1) * MARK] = mark
    cells_of(0, table, lambda cell: fill_slots(cell, 0, codes, table, None))
    cells_of(0, table, lambda cell: finish_cell(cell, sources, targets, sems))
    for copy in copies:
        copy.wait()


def read_marks(extras):
    return [
        jnp.max(extra[2 * LANES + place * MARK : 2 * LANES + (place + 1) * MARK].astype(jnp.float32)).astype(jnp.int32)
        for extra in extras
        for place in (0, 1)
    ]


def complete_halo(recent, plane, extras, marks):
    out_x, in_x, out_y, in_y = edges()
    source = PLANE if recent else 0
    todo = []
    for side in (out_x, in_x):
        for place in (0, 1):
            todo.append((beyond(side) * GRID + 1 + 3 * place, (side + 1) * GRID + 5 * place))
    for side in (out_y, in_y):
        for place in (0, 1):
            todo.append(((1 + 3 * place) * GRID + beyond(side), 5 * place * GRID + side + 1))
    for at, (cell, other) in enumerate(todo):

        @pl.when(marks[at] == recent)
        def _(cell=cell, other=other, extra=extras[at // 2], place=at % 2):
            product = jnp.dot(
                plane[source + other], extra[place * LANES : (place + 1) * LANES], preferred_element_type=jnp.float32
            )
            plane[PLANE + cell] = (plane[PLANE + cell].astype(jnp.float32) + product).astype(jnp.bfloat16)


def finish_corners(recent, table, plane, matrices, sums, far, near):
    out_x, _, out_y, _ = edges()
    for at, (x, y) in enumerate(CORNERS):
        cell = SIDE * x + y

        @pl.when((table[LEVEL + cell] == recent) & (table[LATE + at] >= 0))
        def _(at=at, x=x, y=y, cell=cell):
            side = jnp.where(out_x == x, 0, 1)
            block = jnp.where(out_y == y, far(side), near(side))
            matrix = matrices[cell, pl.ds(pl.multiple_of(LANES * table[LATE + at], LANES), LANES)]
            summed = sums[cell] + jnp.dot(block, matrix, preferred_element_type=jnp.float32)
            plane[own_slot(x, y)] = summed.astype(jnp.bfloat16)


def block_of(ref, first):
    return lambda at: ref[pl.ds(pl.multiple_of((first + at) * ROWS, ROWS), ROWS)]


def store_corners(plane, far, near):
    out_x, _, out_y, _ = edges()
    for x, y in CORNERS:
        side = jnp.where(out_x == x, 0, 1)
        plane[beyond(x) * GRID + beyond(y)] = jnp.where(out_y == y, far(side), near(side))


def gather_product(cell, slots, first, plane, matrices, noise):
    parts = [plane[slots[first + 8 * cell + k]] for k in range(8)] + [noise[cell]]
    return jnp.dot(jnp.concatenate(parts, axis=1), matrices[cell], preferred_element_type=jnp.float32)


def settled_kernel(section, codes, table_in, plane_in, sums_in, matrices_in, noise_in, *rest):
    sources, rest = rest[:3], rest[3:]
    extras = rest[:-8]
    plane, sums, matrices, noise, table, settled, factors, sems = rest[-8:]
    targets = noise, matrices, factors
    cells_of(section, table_in, lambda cell: start_cell(cell, sources, targets, sems))
    for at in range(SLOT):
        table[at] = table_in[at]
    marks = read_marks([ref.at[pl.ds(ref.shape[0] - EXTRA, EXTRA)] for ref in extras])
    for at, mark in enumerate(marks):
        table[MARKS + at] = mark

    def one_cell(cell, count):
        def collect():
            fill_slots(cell, section, codes, table, settled)
            found = count
            for k in range(8):
                table[ITEM + found] = 8 * cell + k
                found += (table[SLOT + 8 * cell + k] != settled[8 * cell + k]).astype(jnp.int32)
            return found

        return lax.cond(table_in[LEVEL + cell] == section, collect, lambda: count)

    count = lax.fori_loop(0, SIDE * SIDE, one_cell, jnp.int32(0))
    table[COUNT] = count

    def product(cell):
        finish_cell(cell, sources, targets, sems)
        sums[cell] = gather_product(cell, settled, 0, plane, matrices, noise)

    cells_of(section, table_in, product)


def store_rows(base, plane, tx_out, tx_in):
    out_x, in_x, _, _ = edges()
    for i in range(SIDE):
        plane[base + beyond(out_x) * GRID + i + 1] = piece(tx_out, i)
        plane[base + beyond(in_x) * GRID + i + 1] = piece(tx_in, i)


def rows_kernel(plane_in, tx_out, tx_in, plane):
    store_rows(PLANE, plane, tx_out, tx_in)


def store_columns(base, plane, out_blocks, ty_in):
    _, _, out_y, in_y = edges()
    for i in range(SIDE):
        plane[base + (i + 1) * GRID + beyond(out_y)] = out_blocks[i]
        plane[base + (i + 1) * GRID + beyond(in_y)] = piece(ty_in, i)


def pack_sends(base, plane, sends):
    tx_out, tx_in, ty_out, ty_more, ty_in = sends
    out_x, in_x, out_y, in_y = edges()
    for i in range(SIDE):
        rows = pl.ds(i * ROWS, ROWS)
        tx_out[rows] = plane[own_slot(out_x, i)]
        tx_in[rows] = plane[own_slot(in_x, i)]
        ty_in[rows] = plane[own_slot(i, in_y)]
        if i < 3:
            ty_out[rows] = plane[own_slot(i, out_y)]
        else:
            ty_more[pl.ds(0, ROWS)] = plane[own_slot(i, out_y)]
    for i, side in enumerate((out_x, in_x)):
        ty_more[pl.ds((1 + i) * ROWS, ROWS)] = plane[base + beyond(side) * GRID + out_y + 1]
        ty_in[pl.ds((SIDE + i) * ROWS, ROWS)] = plane[base + beyond(side) * GRID + in_y + 1]


def first_kernel(table, plane_in, sums_in, matrices_in, noise_in, *rest):
    halo, extras, (plane, sums, matrices, noise, *sends) = rest[:4], rest[4], rest[5:]
    store_rows(0, plane, *halo[:2])
    store_columns(0, plane, [piece(halo[2], i) for i in range(SIDE)], halo[3])

    def one_cell(cell):
        summed = gather_product(cell, table, SLOT, plane, matrices, noise)
        sums[cell] = summed
        plane[own_slot(cell // SIDE, cell % SIDE)] = summed.astype(jnp.bfloat16)

    cells_of(0, table, one_cell)
    pack_sends(0, plane, sends)
    for at, ref in enumerate((sends[0], sends[1], sends[3], sends[4])):
        ref[ref.shape[0] - EXTRA :] = extras[at]


def main_kernel(section, table, plane_in, sums_in, matrices, ty_out, ty_more, ty_in, *rest):
    extras, (plane, sums, *rest) = rest[:4], rest[4:]
    extras = [ref.at[pl.ds(ref.shape[0] - EXTRA, EXTRA)] for ref in extras]
    marks = read_marks(extras) if section == 1 else [table[MARKS + at] for at in range(8)]
    corners = block_of(ty_more, 1), block_of(ty_in, SIDE)
    store_columns(PLANE, plane, [piece(ty_out, i) for i in range(3)] + [piece(ty_more, 0)], ty_in)
    if section == 1:
        store_corners(plane, *corners)
    complete_halo(section - 1, plane, extras, marks)
    finish_corners(section - 1, table, plane, matrices, sums, *corners)
    count = table[COUNT]

    def one_group(group, carry):
        products = []
        for i in range(GROUP):
            item = table[ITEM + jnp.minimum(group * GROUP + i, count - 1)]
            slot = jnp.where(group * GROUP + i < count, table[SLOT + item], BLANK)
            matrix = matrices[item // 8, pl.ds(pl.multiple_of((item % 8) * LANES, LANES), LANES)]
            products.append((item // 8, jnp.dot(plane[slot], matrix, preferred_element_type=jnp.float32)))
        for cell, product in products:
            sums[cell] += product
        return carry

    lax.fori_loop(0, (count + GROUP - 1) // GROUP, one_group, 0)

    def one_cell(cell):
        plane[own_slot(cell // SIDE, cell % SIDE)] = sums[cell].astype(jnp.bfloat16)

    cells_of(section, table, one_cell)
    if section < LEVELS - 1:
        pack_sends(PLANE, plane, rest)
    else:
        result, sems = rest
        copies = [
            pltpu.make_async_copy(
                plane.at[pl.ds(own_slot(x, 0), SIDE)], result.at[pl.ds(x * SIDE, SIDE)], sems.at[x]
            )
            for x in range(SIDE)
        ]
        for copy in copies:
            copy.start()
        for copy in copies:
            copy.wait()


def corner_kernel(table, plane_in, matrices, sums, far, near, result_in, plane, result, sems):
    finish_corners(LEVELS - 1, table, plane, matrices, sums, block_of(far, 0), block_of(near, 0))
    copies = [
        pltpu.make_async_copy(plane.at[own_slot(x, y)], result.at[SIDE * x + y], sems.at[at])
        for at, (x, y) in enumerate(CORNERS)
    ]
    for copy in copies:
        copy.start()
    for copy in copies:
        copy.wait()


def cost(products, depth):
    flops = products * 2 * ROWS * depth * LANES
    return pl.CostEstimate(flops=flops, bytes_accessed=4 << 20, transcendentals=0)


def rows_of(rows):
    return jax.ShapeDtypeStruct((rows, LANES), jnp.bfloat16)


def local(earlier, innovation, conditioner, chol_factor, block_level, neighbours):
    block = earlier.shape[2:]
    tile = SIDE * SIDE
    keep = lambda value: pltpu.with_memory_space_constraint(value, pltpu.HBM)
    flat = lambda value: keep(value.reshape(tile, *value.shape[2:]))
    edge = jax.ShapeDtypeStruct((SIDE, *block), jnp.bfloat16)
    plane_shape = jax.ShapeDtypeStruct((BLANK + 1, *block), jnp.bfloat16)
    sums_shape = jax.ShapeDtypeStruct((tile, *block), jnp.float32)
    whole = jax.ShapeDtypeStruct((tile, *block), jnp.bfloat16)
    matrices_shape = jax.ShapeDtypeStruct((tile, DEPTH, LANES), jnp.bfloat16)
    table_shape = jax.ShapeDtypeStruct((TABLE,), jnp.int32)
    factors = pltpu.VMEM((tile, *chol_factor.shape[2:]), jnp.bfloat16)
    sends = pl.pallas_call(
        pack_kernel,
        out_shape=[edge] * 4,
        in_specs=[HBM],
        out_specs=[VMEM] * 4,
        scratch_shapes=[pltpu.SemaphoreType.DMA((4,))],
        compiler_params=PARAMS,
        name="pack",
    )(keep(earlier))
    sends = [send.reshape(SIDE * ROWS, LANES) for send in sends]
    sources = flat(innovation), flat(conditioner), flat(chol_factor)
    plane, matrices, noise, sums, table, codes, extras = pl.pallas_call(
        load_kernel,
        out_shape=[
            plane_shape,
            matrices_shape,
            whole,
            sums_shape,
            table_shape,
            jax.ShapeDtypeStruct(neighbours.shape, jnp.int32),
            jax.ShapeDtypeStruct((4, EXTRA, LANES), jnp.bfloat16),
        ],
        in_specs=[HBM] * 6,
        out_specs=[VMEM] * 4 + [SMEM] * 2 + [VMEM],
        scratch_shapes=[
            pltpu.SMEM(block_level.shape, jnp.int32),
            factors,
            pltpu.SemaphoreType.DMA((3, tile)),
            pltpu.SemaphoreType.DMA((14,)),
        ],
        compiler_params=PARAMS,
        cost_estimate=pl.CostEstimate(flops=0, bytes_accessed=10 << 20, transcendentals=0),
        name="load",
    )(keep(block_level), keep(neighbours), flat(earlier), *sources)
    halo = exchange(sends)
    send_rows = lambda extra: [
        rows_of(rows)
        for rows in (4 * ROWS + extra, 4 * ROWS + extra, 3 * ROWS, 3 * ROWS + extra, 6 * ROWS + extra)
    ]
    plane, sums, matrices, noise, *sends = pl.pallas_call(
        first_kernel,
        out_shape=[plane_shape, sums_shape, matrices_shape, whole, *send_rows(EXTRA)],
        in_specs=[SMEM] + [VMEM] * 9,
        out_specs=[VMEM] * 9,
        input_output_aliases={1: 0, 2: 1, 3: 2, 4: 3},
        compiler_params=PARAMS,
        cost_estimate=cost(8, DEPTH),
        name="level_0",
    )(table, plane, sums, matrices, noise, *halo, extras)
    for section in range(1, LEVELS):
        final = section == LEVELS - 1
        halo = exchange(sends)
        if section == 1:
            extras = [halo[0], halo[1], halo[3], halo[4]]
        marks_from = extras if section > 1 else []
        plane, sums, matrices, noise, items = pl.pallas_call(
            functools.partial(settled_kernel, section),
            out_shape=[plane_shape, sums_shape, matrices_shape, whole, table_shape],
            in_specs=[SMEM] * 2 + [VMEM] * 4 + [HBM] * 3 + [VMEM] * len(marks_from),
            out_specs=[VMEM] * 4 + [SMEM],
            scratch_shapes=[
                pltpu.SMEM((8 * tile,), jnp.int32),
                factors,
                pltpu.SemaphoreType.DMA((3, tile)),
            ],
            input_output_aliases={2: 0, 3: 1, 4: 2, 5: 3},
            compiler_params=PARAMS,
            cost_estimate=cost(8, DEPTH),
            name=f"settled_{section}",
        )(codes, table, plane, sums, matrices, noise, *sources, *marks_from)
        plane = pl.pallas_call(
            rows_kernel,
            out_shape=plane_shape,
            in_specs=[VMEM] * 3,
            out_specs=VMEM,
            input_output_aliases={0: 0},
            compiler_params=PARAMS,
            cost_estimate=cost(2, LANES),
            name=f"rows_{section}",
        )(plane, *halo[:2])
        if final:
            far, near = pl.pallas_call(
                forward_kernel,
                out_shape=[rows_of(2 * ROWS)] * 2,
                in_specs=[VMEM],
                out_specs=[VMEM] * 2,
                compiler_params=PARAMS,
                cost_estimate=cost(0, 0),
                name="forward",
            )(plane)
            far, near = swap(far, None, "out"), swap(near, None, "in")
        plane, sums, *sends = pl.pallas_call(
            functools.partial(main_kernel, section),
            out_shape=[plane_shape, sums_shape] + ([whole] if final else send_rows(0)),
            in_specs=[SMEM] + [VMEM] * 10,
            out_specs=[VMEM] * 2 + ([HBM] if final else [VMEM] * 5),
            scratch_shapes=[pltpu.SemaphoreType.DMA((4,))] * final,
            input_output_aliases={1: 0, 2: 1},
            compiler_params=PARAMS,
            cost_estimate=cost(16, LANES),
            name=f"level_{section}",
        )(items, plane, sums, matrices, *halo[2:], *extras)
    _, result = pl.pallas_call(
        corner_kernel,
        out_shape=[plane_shape, whole],
        in_specs=[SMEM] + [VMEM] * 5 + [HBM],
        out_specs=[VMEM, HBM],
        scratch_shapes=[pltpu.SemaphoreType.DMA((4,))],
        input_output_aliases={1: 0, 6: 1},
        compiler_params=PARAMS,
        cost_estimate=cost(4, LANES),
        name="last_corners",
    )(items, plane, matrices, sums, far, near, sends[0])
    return result.reshape(earlier.shape)


def solution(mesh):
    placed = (
        P("tx", "ty", None, None),
        P("tx", "ty", None, None),
        P("tx", "ty", None, None),
        P("tx", "ty", None, None),
        P("tx", "ty"),
        P("tx", "ty", None),
    )
    return jax.shard_map(
        local, mesh=mesh, in_specs=placed, out_specs=P("tx", "ty", None, None), check_vma=False
    )
```

time: 76.8 us -> 67.7 us (0.88)
  waiting for transfers between devices: 26.4 us -> 6.77 us
  starting transfers between devices: 24.4 us -> 32.8 us
  Pallas kernels: 24.5 us -> 27.9 us
  local copies, waits for them, and re-layouts: 1.97 us -> 0 us
    ppermute x18 -> x21, waiting for transfers between devices: 26.4 us -> 6.77 us  [swap(): return lax.ppermute(value, BOTH, pairs)]
    ppermute x18 -> x21, starting transfers between devices: 24.4 us -> 32.8 us  [swap(): return lax.ppermute(value, BOTH, pairs)]
    pallas_call x3, Pallas kernels: 7.78 us -> 14.3 us  [local(): pl.pallas_call(functools.partial(settled_kernel, section), out_shape=[pla...]
    unnamed x6 -> x0, local copies, waits for them, and re-layouts: 1.97 us -> none
    pallas_call x2, Pallas kernels: 6.72 us -> 4.98 us  [the longest x1 3.37 us: local(): pl.pallas_call(load_kernel, out_shape=[plane_shape, matrices_shape, whole...]
    pallas_call x3, Pallas kernels: 6.9 us -> 5.84 us  [local(): pl.pallas_call(functools.partial(main_kernel, section), out_shape=[plane_...]
  transfers between devices with their start and end apart: 18 -> 21, of which waited for: 3 -> 8; matrix products, arithmetic and copies ran while one was open for 0% -> 0% of each run, Pallas kernels for 21% -> 31%
where the time goes in v5:
time: 67.7 us
  starting transfers between devices  32.8 us (48%)
  Pallas kernels  27.9 us (41%)
  waiting for transfers between devices  6.77 us (10%)
    ppermute x21, starting transfers between devices, swap(): return lax.ppermute(value, BOTH, pairs)  32.8 us
    pallas_call x3, Pallas kernels, local(): pl.pallas_call(functools.partial(settled_kernel, section), out_shape=[pla...  14.3 us
    ppermute x21, waiting for transfers between devices, swap(): return lax.ppermute(value, BOTH, pairs)  6.77 us
    pallas_call x3, Pallas kernels, local(): pl.pallas_call(functools.partial(main_kernel, section), out_shape=[plane_...  5.84 us
    pallas_call x1, Pallas kernels, local(): pl.pallas_call(load_kernel, out_shape=[plane_shape, matrices_shape, whole...  3.37 us
    pallas_call x1, Pallas kernels, local(): pl.pallas_call(first_kernel, out_shape=[plane_shape, sums_shape, matrices...  1.61 us
  transfers between devices with their start and end apart: 21, of which 8 were waited for; matrix products, arithmetic and copies ran while one was open for 0% of the time, Pallas kernels for 31%

profile of v5, /device:TPU:0, one launch (start us, length us, event | category | flops | bytes accessed | tf_op | source)
XLA Modules:
  0.0 67.7 jit_solution(14218284245791444759)
XLA Ops:
  0.0 1.2 %pack.1 = (bf16[4,256,128]{2,1,0:T(8,128)(2,1)S(1)}, bf16[4,256,128]{2,1,0:T(8,128)(2,1)S(1)}, bf16[4,256,128]{2,1,0:T(8,128)(2,1)S(1)}, bf16[4,256,128]{2,1,0:T(8,128)(2,1)S(1)}) custom-call(bf16[4,4,256,128]{3,2,1,0:T(8,128)(2,1)} %earlier.1), custom_call_target="tpu_custom_call" | custom-call | tf_op jit(solution)/shard_map/pack/pallas_call | solution.py:426
  1.2 1.7 %collective-permute-start.1 = (bf16[1024,128]{1,0:T(8,128)(2,1)S(1)}, bf16[1024,128]{1,0:T(8,128)(2,1)S(1)}, u32[]{:S(2)}, u32[]{:S(2)}) collective-permute-start(bf16[1024,128]{1,0:T(8,128)(2,1)S(1)} %bitcast.12), channel_id=1, source_target_pairs={{0,8},{1,9},{2,10},{3,11},{4,12},{5,13},{6,14},{7,15},{8,0},{9,1},... | collective-permute-start | bytes 786440 | tf_op jit(solution)/shard_map/ppermute | solution.py:45
  2.9 4.5 %collective-permute-start = (bf16[1024,128]{1,0:T(8,128)(2,1)S(1)}, bf16[1024,128]{1,0:T(8,128)(2,1)S(1)}, u32[]{:S(2)}, u32[]{:S(2)}) collective-permute-start(bf16[1024,128]{1,0:T(8,128)(2,1)S(1)} %bitcast.11), channel_id=1, source_target_pairs={{0,120},{1,121},{2,122},{3,123},{4,124},{5,125},{6,126},{7,127},{8... | collective-permute-start | bytes 786440 | tf_op jit(solution)/shard_map/ppermute | solution.py:45
  7.4 2.9 %collective-permute-start.2 = (bf16[1024,128]{1,0:T(8,128)(2,1)S(1)}, bf16[1024,128]{1,0:T(8,128)(2,1)S(1)}, u32[]{:S(2)}, u32[]{:S(2)}) collective-permute-start(bf16[1024,128]{1,0:T(8,128)(2,1)S(1)} %bitcast.10), channel_id=1, source_target_pairs={{0,7},{1,2},{2,1},{3,4},{4,3},{5,6},{6,5},{7,0},{8,15},{9,10},{10,... | collective-permute-start | bytes 786440 | tf_op jit(solution)/shard_map/ppermute | solution.py:45
  10.3 3.4 %load.1 = (bf16[73,256,128]{2,1,0:T(8,128)(2,1)S(1)}, bf16[16,1152,128]{2,1,0:T(8,128)(2,1)S(1)}, bf16[16,256,128]{2,1,0:T(8,128)(2,1)S(1)}, f32[16,256,128]{2,1...) custom-call(s32[4,4]{1,0:T(4,128)} %block_level.1, ...), custom_call_target="tpu_custom_call" | custom-call | bytes 10485760 | tf_op jit(solution)/shard_map/load/pallas_call | solution.py:437
  13.7 0.2 collective-permute-done.rest_0_
  14.0 0.5 collective-permute-done.2.rest_2_
  14.4 1.6 %level_0.1 = (bf16[73,256,128]{2,1,0:T(8,128)(2,1)S(1)}, f32[16,256,128]{2,1,0:T(8,128)S(1)}, bf16[16,1152,128]{2,1,0:T(8,128)(2,1)S(1)}, bf16[16,256,128]{2,1,0...) custom-call(s32[229]{0:T(256)S(1)} %get-tuple-element.60.table.table, ...), custom_call_target="tpu_custom_call", output_to_operand_aliasing={{0}: (1, {}), {1}: (2, {}), {2}: (3, {}), {3}: (4, {})} | custom-call | flops 603979776 | bytes 4194304 | tf_op jit(solution)/shard_map/level_0/pallas_call | solution.py:465
  16.1 0.1 collective-permute-start.8
  16.1 5.1 %collective-permute-start.4 = (bf16[1312,128]{1,0:T(8,128)(2,1)S(1)}, bf16[1312,128]{1,0:T(8,128)(2,1)S(1)}, u32[]{:S(2)}, u32[]{:S(2)}) collective-permute-start(bf16[1312,128]{1,0:T(8,128)(2,1)S(1)} %get-tuple-element.76), channel_id=1, source_target_pairs={{0,120},{1,121},{2,122},{3,123},{4,124},{5,125},{6,126},{7,127},{8... | collective-permute-start | bytes 1007624 | tf_op jit(solution)/shard_map/ppermute | solution.py:45
  21.2 3.5 %collective-permute-start.7 = (bf16[1056,128]{1,0:T(8,128)(2,1)S(1)}, bf16[1056,128]{1,0:T(8,128)(2,1)S(1)}, u32[]{:S(2)}, u32[]{:S(2)}) collective-permute-start(bf16[1056,128]{1,0:T(8,128)(2,1)S(1)} %get-tuple-element.81), channel_id=1, source_target_pairs={{0,7},{1,2},{2,1},{3,4},{4,3},{5,6},{6,5},{7,0},{8,15},{9,10},{10,... | collective-permute-start | bytes 811016 | tf_op jit(solution)/shard_map/ppermute | solution.py:45
  24.8 4.3 %settled_1.1 = (bf16[73,256,128]{2,1,0:T(8,128)(2,1)S(1)}, f32[16,256,128]{2,1,0:T(8,128)S(1)}, bf16[16,1152,128]{2,1,0:T(8,128)(2,1)S(1)}, bf16[16,256,128]{2,1,0:T(8,128)(2,1)S(1)}, s32[229]{0:T(256)S(1)}) custom-call(s32[4,4,8]{2,1,0:T(4,128)S(1)} %get-tuple-element.59.codes, ...), custom_call_target="tpu_custom_call", output_to_operand_aliasing={{0}: (2, {}), {1}: (3, {}), {2}: (4, {}), {3}: (5, {})} | custom-call | flops 603979776 | bytes 4194304 | tf_op jit(solution)/shard_map/settled_1/pallas_call | solution.py:481
  29.1 0.7 collective-permute-done.4.tx_out.rest_0_.rest_3_
  29.8 1.4 %collective-permute-done.5.tx_in.rest_1_.rest_4_ = bf16[1312,128]{1,0:T(8,128)(2,1)S(1)} collective-permute-done((bf16[1312,128]{1,0:T(8,128)(2,1)S(1)}, bf16[1312,128]{1,0:T(8,128)(2,1)S(1)}, u32[]{:S(2)}, u32[]{:S(2)}) %collective-permute-start.5) | collective-permute-done | bytes 335904 | tf_op jit(solution)/shard_map/ppermute | solution.py:45
  31.3 1.7 %level_1.1 = (bf16[73,256,128]{2,1,0:T(8,128)(2,1)S(1)}, f32[16,256,128]{2,1,0:T(8,128)S(1)}, bf16[1024,128]{1,0:T(8,128)(2,1)S(1)}, bf16[1024,128]{1,0:T(8,128)...) custom-call(s32[229]{0:T(256)S(1)} %get-tuple-element.74.table, ...), custom_call_target="tpu_custom_call", output_to_operand_aliasing={{0}: (1, {}), {1}: (2, {})} | custom-call | flops 134217728 | bytes 4194304 | tf_op jit(solution)/shard_map/level_1/pallas_call | solution.py:517
  33.0 0.1 collective-permute-start.13
  33.1 3.8 %collective-permute-start.9 = (bf16[1024,128]{1,0:T(8,128)(2,1)S(1)}, bf16[1024,128]{1,0:T(8,128)(2,1)S(1)}, u32[]{:S(2)}, u32[]{:S(2)}) collective-permute-start(bf16[1024,128]{1,0:T(8,128)(2,1)S(1)} %get-tuple-element.88), channel_id=1, source_target_pairs={{0,120},{1,121},{2,122},{3,123},{4,124},{5,125},{6,126},{7,127},{8... | collective-permute-start | bytes 786440 | tf_op jit(solution)/shard_map/ppermute | solution.py:45
  36.9 3.6 %collective-permute-start.11 = (bf16[768,128]{1,0:T(8,128)(2,1)S(1)}, bf16[768,128]{1,0:T(8,128)(2,1)S(1)}, u32[]{:S(2)}, u32[]{:S(2)}) collective-permute-start(bf16[768,128]{1,0:T(8,128)(2,1)S(1)} %get-tuple-element.92), channel_id=1, source_target_pairs={{0,7},{1,2},{2,1},{3,4},{4,3},{5,6},{6,5},{7,0},{8,15},{9,10},{10,... | collective-permute-start | bytes 589832 | tf_op jit(solution)/shard_map/ppermute | solution.py:45
  40.5 3.6 %settled_2.1 = (bf16[73,256,128]{2,1,0:T(8,128)(2,1)S(1)}, f32[16,256,128]{2,1,0:T(8,128)S(1)}, bf16[16,1152,128]{2,1,0:T(8,128)(2,1)S(1)}, bf16[16,256,128]{2,1,0:T(8,128)(2,1)S(1)}, s32[229]{0:T(256)S(1)}) custom-call(s32[4,4,8]{2,1,0:T(4,128)S(1)} %get-tuple-element.59.codes, ...), custom_call_target="tpu_custom_call", output_to_operand_aliasing={{0}: (2, {}), {1}: (3, {}), {2}: (4, {}), {3}: (5, {})} | custom-call | flops 603979776 | bytes 4194304 | tf_op jit(solution)/shard_map/settled_2/pallas_call | solution.py:481
  44.1 1.0 %collective-permute-done.9.tx_out = bf16[1024,128]{1,0:T(8,128)(2,1)S(1)} collective-permute-done((bf16[1024,128]{1,0:T(8,128)(2,1)S(1)}, bf16[1024,128]{1,0:T(8,128)(2,1)S(1)}, u32[]{:S(2)}, u32[]{:S(2)}) %collective-permute-start.9) | collective-permute-done | bytes 262176 | tf_op jit(solution)/shard_map/ppermute | solution.py:45
  45.1 0.1 collective-permute-done.10.tx_in
  45.3 1.5 %collective-permute-done.12.ty_more = bf16[768,128]{1,0:T(8,128)(2,1)S(1)} collective-permute-done((bf16[768,128]{1,0:T(8,128)(2,1)S(1)}, bf16[768,128]{1,0:T(8,128)(2,1)S(1)}, u32[]{:S(2)}, u32[]{:S(2)}) %collective-permute-start.12) | collective-permute-done | bytes 196640 | tf_op jit(solution)/shard_map/ppermute | solution.py:45
  46.8 1.3 %level_2.1 = (bf16[73,256,128]{2,1,0:T(8,128)(2,1)S(1)}, f32[16,256,128]{2,1,0:T(8,128)S(1)}, bf16[1024,128]{1,0:T(8,128)(2,1)S(1)}, bf16[1024,128]{1,0:T(8,128)...) custom-call(s32[229]{0:T(256)S(1)} %get-tuple-element.86.table, ...), custom_call_target="tpu_custom_call", output_to_operand_aliasing={{0}: (1, {}), {1}: (2, {})} | custom-call | flops 134217728 | bytes 4194304 | tf_op jit(solution)/shard_map/level_2/pallas_call | solution.py:517
  48.1 0.1 collective-permute-start.18
  48.2 2.3 %collective-permute-start.14 = (bf16[1024,128]{1,0:T(8,128)(2,1)S(1)}, bf16[1024,128]{1,0:T(8,128)(2,1)S(1)}, u32[]{:S(2)}, u32[]{:S(2)}) collective-permute-start(bf16[1024,128]{1,0:T(8,128)(2,1)S(1)} %get-tuple-element.100), channel_id=1, source_target_pairs={{0,120},{1,121},{2,122},{3,123},{4,124},{5,125},{6,126},{7,127},{8... | collective-permute-start | bytes 786440 | tf_op jit(solution)/shard_map/ppermute | solution.py:45
  50.5 0.4 collective-permute-start.15
  50.9 3.1 %collective-permute-start.16 = (bf16[768,128]{1,0:T(8,128)(2,1)S(1)}, bf16[768,128]{1,0:T(8,128)(2,1)S(1)}, u32[]{:S(2)}, u32[]{:S(2)}) collective-permute-start(bf16[768,128]{1,0:T(8,128)(2,1)S(1)} %get-tuple-element.104), channel_id=1, source_target_pairs={{0,7},{1,2},{2,1},{3,4},{4,3},{5,6},{6,5},{7,0},{8,15},{9,10},{10,... | collective-permute-start | bytes 589832 | tf_op jit(solution)/shard_map/ppermute | solution.py:45
  54.1 6.4 %settled_3.1 = (bf16[73,256,128]{2,1,0:T(8,128)(2,1)S(1)}, f32[16,256,128]{2,1,0:T(8,128)S(1)}, bf16[16,1152,128]{2,1,0:T(8,128)(2,1)S(1)}, bf16[16,256,128]{2,1,0:T(8,128)(2,1)S(1)}, s32[229]{0:T(256)S(1)}) custom-call(s32[4,4,8]{2,1,0:T(4,128)S(1)} %get-tuple-element.59.codes, ...), custom_call_target="tpu_custom_call", output_to_operand_aliasing={{0}: (2, {}), {1}: (3, {}), {2}: (4, {}), {3}: (5, {})} | custom-call | flops 603979776 | bytes 4194304 | tf_op jit(solution)/shard_map/settled_3/pallas_call | solution.py:481
  60.7 1.4 %collective-permute-start.19 = (bf16[512,128]{1,0:T(8,128)(2,1)S(1)}, bf16[512,128]{1,0:T(8,128)(2,1)S(1)}, u32[]{:S(2)}, u32[]{:S(2)}) collective-permute-start(bf16[512,128]{1,0:T(8,128)(2,1)S(1)} %get-tuple-element.109), channel_id=1, source_target_pairs={{0,7},{1,2},{2,1},{3,4},{4,3},{5,6},{6,5},{7,0},{8,15},{9,10},{10,... | collective-permute-start | bytes 393224 | tf_op jit(solution)/shard_map/ppermute | solution.py:45
  62.1 2.9 %level_3.1 = (bf16[73,256,128]{2,1,0:T(8,128)(2,1)S(1)}, f32[16,256,128]{2,1,0:T(8,128)S(1)}, bf16[16,256,128]{2,1,0:T(8,128)(2,1)}) custom-call(s32[229]{0:T(256)S(1)} %get-tuple-element.98.table, bf16[73,256,128]{2,1,0:T(8,128)(2,1)S(1)} %rows_3.1.plane_in.plane, ...), custom_call_target="tpu_custom_call", output_to_operand_aliasing={{0}: (1, {}), {1}: (2, {})} | custom-call | flops 134217728 | bytes 4194304 | tf_op jit(solution)/shard_map/level_3/pallas_call | solution.py:517
  65.0 1.3 %collective-permute-done.19.far = bf16[512,128]{1,0:T(8,128)(2,1)S(1)} collective-permute-done((bf16[512,128]{1,0:T(8,128)(2,1)S(1)}, bf16[512,128]{1,0:T(8,128)(2,1)S(1)}, u32[]{:S(2)}, u32[]{:S(2)}) %collective-permute-start.19) | collective-permute-done | bytes 131104 | tf_op jit(solution)/shard_map/ppermute | solution.py:45
  66.3 1.3 %last_corners.1 = (bf16[73,256,128]{2,1,0:T(8,128)(2,1)S(1)}, bf16[16,256,128]{2,1,0:T(8,128)(2,1)}) custom-call(s32[229]{0:T(256)S(1)} %get-tuple-element.98.table, bf16[73,256,128]{2,1,0:T(8,128)(2,1)S(1)} %get-tuple-element.107.plane_in, bf16[16,1152,128]{2,1,0:T(8,128)(2,1)S(1)} %get-tuple-element.103.matrices, ...), custom_call_target="tpu_custom_call", output_to_operand_aliasing={{0}: (1, {}), {1}: (6, {})} | custom-call | flops 33554432 | bytes 4194304 | tf_op jit(solution)/shard_map/last_corners/pallas_call | solution.py:528
  (24 shorter events, 0.4 us)
Async XLA Ops:
  1.2 12.5 %collective-permute-start.1 = (bf16[1024,128]{1,0:T(8,128)(2,1)S(1)}, bf16[1024,128]{1,0:T(8,128)(2,1)S(1)}, u32[]{:S(2)}, u32[]{:S(2)}) collective-permute-start(bf16[1024,128]{1,0:T(8,128)(2,1)S(1)} %bitcast.12), channel_id=1, source_target_pairs={{0,8},{1,9},{2,10},{3,11},{4,12},{5,13},{6,14},{7,15},{8,0},{9,1},... | collective-permute-start | bytes 786440 | tf_op jit(solution)/shard_map/ppermute | solution.py:45
  2.9 11.1 %collective-permute-start = (bf16[1024,128]{1,0:T(8,128)(2,1)S(1)}, bf16[1024,128]{1,0:T(8,128)(2,1)S(1)}, u32[]{:S(2)}, u32[]{:S(2)}) collective-permute-start(bf16[1024,128]{1,0:T(8,128)(2,1)S(1)} %bitcast.11), channel_id=1, source_target_pairs={{0,120},{1,121},{2,122},{3,123},{4,124},{5,125},{6,126},{7,127},{8... | collective-permute-start | bytes 786440 | tf_op jit(solution)/shard_map/ppermute | solution.py:45
  7.4 7.0 %collective-permute-start.2 = (bf16[1024,128]{1,0:T(8,128)(2,1)S(1)}, bf16[1024,128]{1,0:T(8,128)(2,1)S(1)}, u32[]{:S(2)}, u32[]{:S(2)}) collective-permute-start(bf16[1024,128]{1,0:T(8,128)(2,1)S(1)} %bitcast.10), channel_id=1, source_target_pairs={{0,7},{1,2},{2,1},{3,4},{4,3},{5,6},{6,5},{7,0},{8,15},{9,10},{10,... | collective-permute-start | bytes 786440 | tf_op jit(solution)/shard_map/ppermute | solution.py:45
  10.3 4.1 %collective-permute-start.3 = (bf16[1024,128]{1,0:T(8,128)(2,1)S(1)}, bf16[1024,128]{1,0:T(8,128)(2,1)S(1)}, u32[]{:S(2)}, u32[]{:S(2)}) collective-permute-start(bf16[1024,128]{1,0:T(8,128)(2,1)S(1)} %bitcast.9), channel_id=1, source_target_pairs={{0,1},{1,0},{2,3},{3,2},{4,5},{5,4},{6,7},{7,6},{8,9},{9,8},{10,11... | collective-permute-start | bytes 786440 | tf_op jit(solution)/shard_map/ppermute | solution.py:45
  16.1 15.2 %collective-permute-start.8 = (bf16[1824,128]{1,0:T(8,128)(2,1)S(1)}, bf16[1824,128]{1,0:T(8,128)(2,1)S(1)}, u32[]{:S(2)}, u32[]{:S(2)}) collective-permute-start(bf16[1824,128]{1,0:T(8,128)(2,1)S(1)} %get-tuple-element.82), channel_id=1, source_target_pairs={{0,1},{1,0},{2,3},{3,2},{4,5},{5,4},{6,7},{7,6},{8,9},{9,8},{10,11... | collective-permute-start | bytes 1400840 | tf_op jit(solution)/shard_map/ppermute | solution.py:45
  16.1 13.6 %collective-permute-start.4 = (bf16[1312,128]{1,0:T(8,128)(2,1)S(1)}, bf16[1312,128]{1,0:T(8,128)(2,1)S(1)}, u32[]{:S(2)}, u32[]{:S(2)}) collective-permute-start(bf16[1312,128]{1,0:T(8,128)(2,1)S(1)} %get-tuple-element.76), channel_id=1, source_target_pairs={{0,120},{1,121},{2,122},{3,123},{4,124},{5,125},{6,126},{7,127},{8... | collective-permute-start | bytes 1007624 | tf_op jit(solution)/shard_map/ppermute | solution.py:45
  21.2 9.9 %collective-permute-start.5 = (bf16[1312,128]{1,0:T(8,128)(2,1)S(1)}, bf16[1312,128]{1,0:T(8,128)(2,1)S(1)}, u32[]{:S(2)}, u32[]{:S(2)}) collective-permute-start(bf16[1312,128]{1,0:T(8,128)(2,1)S(1)} %get-tuple-element.77), channel_id=1, source_target_pairs={{0,8},{1,9},{2,10},{3,11},{4,12},{5,13},{6,14},{7,15},{8,0},{9,1},... | collective-permute-start | bytes 1007624 | tf_op jit(solution)/shard_map/ppermute | solution.py:45
  21.2 10.0 %collective-permute-start.7 = (bf16[1056,128]{1,0:T(8,128)(2,1)S(1)}, bf16[1056,128]{1,0:T(8,128)(2,1)S(1)}, u32[]{:S(2)}, u32[]{:S(2)}) collective-permute-start(bf16[1056,128]{1,0:T(8,128)(2,1)S(1)} %get-tuple-element.81), channel_id=1, source_target_pairs={{0,7},{1,2},{2,1},{3,4},{4,3},{5,6},{6,5},{7,0},{8,15},{9,10},{10,... | collective-permute-start | bytes 811016 | tf_op jit(solution)/shard_map/ppermute | solution.py:45
  24.7 6.5 %collective-permute-start.6 = (bf16[768,128]{1,0:T(8,128)(2,1)S(1)}, bf16[768,128]{1,0:T(8,128)(2,1)S(1)}, u32[]{:S(2)}, u32[]{:S(2)}) collective-permute-start(bf16[768,128]{1,0:T(8,128)(2,1)S(1)} %get-tuple-element.80), channel_id=1, source_target_pairs={{0,7},{1,2},{2,1},{3,4},{4,3},{5,6},{6,5},{7,0},{8,15},{9,10},{10,... | collective-permute-start | bytes 589832 | tf_op jit(solution)/shard_map/ppermute | solution.py:45
  33.0 13.8 %collective-permute-start.13 = (bf16[1536,128]{1,0:T(8,128)(2,1)S(1)}, bf16[1536,128]{1,0:T(8,128)(2,1)S(1)}, u32[]{:S(2)}, u32[]{:S(2)}) collective-permute-start(bf16[1536,128]{1,0:T(8,128)(2,1)S(1)} %get-tuple-element.94), channel_id=1, source_target_pairs={{0,1},{1,0},{2,3},{3,2},{4,5},{5,4},{6,7},{7,6},{8,9},{9,8},{10,11... | collective-permute-start | bytes 1179656 | tf_op jit(solution)/shard_map/ppermute | solution.py:45
  33.1 12.0 %collective-permute-start.9 = (bf16[1024,128]{1,0:T(8,128)(2,1)S(1)}, bf16[1024,128]{1,0:T(8,128)(2,1)S(1)}, u32[]{:S(2)}, u32[]{:S(2)}) collective-permute-start(bf16[1024,128]{1,0:T(8,128)(2,1)S(1)} %get-tuple-element.88), channel_id=1, source_target_pairs={{0,120},{1,121},{2,122},{3,123},{4,124},{5,125},{6,126},{7,127},{8... | collective-permute-start | bytes 786440 | tf_op jit(solution)/shard_map/ppermute | solution.py:45
  36.9 8.4 %collective-permute-start.10 = (bf16[1024,128]{1,0:T(8,128)(2,1)S(1)}, bf16[1024,128]{1,0:T(8,128)(2,1)S(1)}, u32[]{:S(2)}, u32[]{:S(2)}) collective-permute-start(bf16[1024,128]{1,0:T(8,128)(2,1)S(1)} %get-tuple-element.89), channel_id=1, source_target_pairs={{0,8},{1,9},{2,10},{3,11},{4,12},{5,13},{6,14},{7,15},{8,0},{9,1},... | collective-permute-start | bytes 786440 | tf_op jit(solution)/shard_map/ppermute | solution.py:45
  36.9 8.4 %collective-permute-start.11 = (bf16[768,128]{1,0:T(8,128)(2,1)S(1)}, bf16[768,128]{1,0:T(8,128)(2,1)S(1)}, u32[]{:S(2)}, u32[]{:S(2)}) collective-permute-start(bf16[768,128]{1,0:T(8,128)(2,1)S(1)} %get-tuple-element.92), channel_id=1, source_target_pairs={{0,7},{1,2},{2,1},{3,4},{4,3},{5,6},{6,5},{7,0},{8,15},{9,10},{10,... | collective-permute-start | bytes 589832 | tf_op jit(solution)/shard_map/ppermute | solution.py:45
  40.5 6.3 %collective-permute-start.12 = (bf16[768,128]{1,0:T(8,128)(2,1)S(1)}, bf16[768,128]{1,0:T(8,128)(2,1)S(1)}, u32[]{:S(2)}, u32[]{:S(2)}) collective-permute-start(bf16[768,128]{1,0:T(8,128)(2,1)S(1)} %get-tuple-element.93), channel_id=1, source_target_pairs={{0,7},{1,2},{2,1},{3,4},{4,3},{5,6},{6,5},{7,0},{8,15},{9,10},{10,... | collective-permute-start | bytes 589832 | tf_op jit(solution)/shard_map/ppermute | solution.py:45
  48.1 14.0 %collective-permute-start.18 = (bf16[1536,128]{1,0:T(8,128)(2,1)S(1)}, bf16[1536,128]{1,0:T(8,128)(2,1)S(1)}, u32[]{:S(2)}, u32[]{:S(2)}) collective-permute-start(bf16[1536,128]{1,0:T(8,128)(2,1)S(1)} %get-tuple-element.106), channel_id=1, source_target_pairs={{0,1},{1,0},{2,3},{3,2},{4,5},{5,4},{6,7},{7,6},{8,9},{9,8},{10,11... | collective-permute-start | bytes 1179656 | tf_op jit(solution)/shard_map/ppermute | solution.py:45
  48.2 12.3 %collective-permute-start.14 = (bf16[1024,128]{1,0:T(8,128)(2,1)S(1)}, bf16[1024,128]{1,0:T(8,128)(2,1)S(1)}, u32[]{:S(2)}, u32[]{:S(2)}) collective-permute-start(bf16[1024,128]{1,0:T(8,128)(2,1)S(1)} %get-tuple-element.100), channel_id=1, source_target_pairs={{0,120},{1,121},{2,122},{3,123},{4,124},{5,125},{6,126},{7,127},{8... | collective-permute-start | bytes 786440 | tf_op jit(solution)/shard_map/ppermute | solution.py:45
  50.5 10.0 %collective-permute-start.15 = (bf16[1024,128]{1,0:T(8,128)(2,1)S(1)}, bf16[1024,128]{1,0:T(8,128)(2,1)S(1)}, u32[]{:S(2)}, u32[]{:S(2)}) collective-permute-start(bf16[1024,128]{1,0:T(8,128)(2,1)S(1)} %get-tuple-element.101), channel_id=1, source_target_pairs={{0,8},{1,9},{2,10},{3,11},{4,12},{5,13},{6,14},{7,15},{8,0},{9,1},... | collective-permute-start | bytes 786440 | tf_op jit(solution)/shard_map/ppermute | solution.py:45
  50.9 11.1 %collective-permute-start.16 = (bf16[768,128]{1,0:T(8,128)(2,1)S(1)}, bf16[768,128]{1,0:T(8,128)(2,1)S(1)}, u32[]{:S(2)}, u32[]{:S(2)}) collective-permute-start(bf16[768,128]{1,0:T(8,128)(2,1)S(1)} %get-tuple-element.104), channel_id=1, source_target_pairs={{0,7},{1,2},{2,1},{3,4},{4,3},{5,6},{6,5},{7,0},{8,15},{9,10},{10,... | collective-permute-start | bytes 589832 | tf_op jit(solution)/shard_map/ppermute | solution.py:45
  54.0 8.1 %collective-permute-start.17 = (bf16[768,128]{1,0:T(8,128)(2,1)S(1)}, bf16[768,128]{1,0:T(8,128)(2,1)S(1)}, u32[]{:S(2)}, u32[]{:S(2)}) collective-permute-start(bf16[768,128]{1,0:T(8,128)(2,1)S(1)} %get-tuple-element.105), channel_id=1, source_target_pairs={{0,7},{1,2},{2,1},{3,4},{4,3},{5,6},{6,5},{7,0},{8,15},{9,10},{10,... | collective-permute-start | bytes 589832 | tf_op jit(solution)/shard_map/ppermute | solution.py:45
  60.7 5.7 %collective-permute-start.19 = (bf16[512,128]{1,0:T(8,128)(2,1)S(1)}, bf16[512,128]{1,0:T(8,128)(2,1)S(1)}, u32[]{:S(2)}, u32[]{:S(2)}) collective-permute-start(bf16[512,128]{1,0:T(8,128)(2,1)S(1)} %get-tuple-element.109), channel_id=1, source_target_pairs={{0,7},{1,2},{2,1},{3,4},{4,3},{5,6},{6,5},{7,0},{8,15},{9,10},{10,... | collective-permute-start | bytes 393224 | tf_op jit(solution)/shard_map/ppermute | solution.py:45
  62.1 4.3 %collective-permute-start.20 = (bf16[512,128]{1,0:T(8,128)(2,1)S(1)}, bf16[512,128]{1,0:T(8,128)(2,1)S(1)}, u32[]{:S(2)}, u32[]{:S(2)}) collective-permute-start(bf16[512,128]{1,0:T(8,128)(2,1)S(1)} %get-tuple-element.110), channel_id=1, source_target_pairs={{0,1},{1,0},{2,3},{3,2},{4,5},{5,4},{6,7},{7,6},{8,9},{9,8},{10,11... | collective-permute-start | bytes 393224 | tf_op jit(solution)/shard_map/ppermute | solution.py:45

commit v6 on v5

--- a/solution.py
+++ b/solution.py
@@ -18,7 +18,7 @@
 MARK = 16
 EXTRA = 2 * (LANES + MARK)
 DEPTH = 9 * LANES
-LEVEL, LATE, SLOT, ITEM, MARKS, COUNT, TABLE = 0, 16, 20, 148, 220, 228, 229
+LEVEL, SLOT, ITEM, CELLS, COUNT, CHOSEN, TABLE = 0, 16, 144, 216, 236, 237, 238
 GROUP = 4
 CORNERS = ((0, 0), (0, 3), (3, 0), (3, 3))
 VMEM = pl.BlockSpec(memory_space=pltpu.VMEM)
@@ -117,15 +117,31 @@
             settled[8 * cell + k] = jnp.where(open_, BLANK, slot)
 
 
-def cells_of(section, table, body):
-    def one_cell(cell, carry):
-        @pl.when(table[LEVEL + cell] == section)
-        def _():
-            body(cell)
-
+def choose(section, levels, table):
+    def one_cell(cell, at):
+        table[CELLS + at] = cell
+        return at + (levels[LEVEL + cell] == section).astype(jnp.int32)
+
+    table[CHOSEN] = lax.fori_loop(0, SIDE * SIDE, one_cell, jnp.int32(0))
+
+
+def each_cell(table, body):
+    def one_cell(at, carry):
+        body(table[CELLS + at])
         return carry
 
-    lax.fori_loop(0, SIDE * SIDE, one_cell, 0)
+    lax.fori_loop(0, table[CHOSEN], one_cell, 0)
+
+
+def each_pair(table, body):
+    count = table[CHOSEN]
+
+    def one_pair(pair, carry):
+        second = jnp.minimum(2 * pair + 1, count - 1)
+        body(table[CELLS + 2 * pair], table[CELLS + second], 2 * pair + 1 < count)
+        return carry
+
+    lax.fori_loop(0, (count + 1) // 2, one_pair, 0)
 
 
 def cell_copies(cell, sources, targets, sems):
@@ -182,11 +198,11 @@
     for cell in range(SIDE * SIDE):
         table[LEVEL + cell] = levels[cell // SIDE, cell % SIDE]
     sources, targets = (innovation, conditioner, chol_factor), (noise, matrices, factors)
-    cells_of(0, table, lambda cell: start_cell(cell, sources, targets, sems))
+    choose(0, table, table)
+    each_cell(table, lambda cell: start_cell(cell, sources, targets, sems))
     out_x, _, out_y, _ = edges()
     for at, (x, y) in enumerate(CORNERS):
         late = late_code(levels, codes, x, y)
-        table[LATE + at] = late
         mark = jnp.full((MARK, LANES), jnp.where(late >= 0, levels[x, y], -1).astype(jnp.float32)).astype(jnp.bfloat16)
         start = pl.multiple_of(LANES * jnp.maximum(late, 0), LANES)
         matrix = conditioner.at[SIDE * x + y, pl.ds(start, LANES)]
@@ -197,21 +213,17 @@
             copy.start()
             copies.append(copy)
             extras[side, 2 * LANES + place * MARK : 2 * LANES + (place + 1) * MARK] = mark
-    cells_of(0, table, lambda cell: fill_slots(cell, 0, codes, table, None))
-    cells_of(0, table, lambda cell: finish_cell(cell, sources, targets, sems))
+    each_cell(table, lambda cell: fill_slots(cell, 0, codes, table, None))
+    each_cell(table, lambda cell: finish_cell(cell, sources, targets, sems))
     for copy in copies:
         copy.wait()
 
 
-def read_marks(extras):
-    return [
-        jnp.max(extra[2 * LANES + place * MARK : 2 * LANES + (place + 1) * MARK].astype(jnp.float32)).astype(jnp.int32)
-        for extra in extras
-        for place in (0, 1)
-    ]
-
-
-def complete_halo(recent, plane, extras, marks):
+def read_mark(extra, place):
+    return jnp.max(extra[2 * LANES + place * MARK : 2 * LANES + (place + 1) * MARK].astype(jnp.float32))
+
+
+def complete_halo(recent, plane, extras):
     out_x, in_x, out_y, in_y = edges()
     source = PLANE if recent else 0
     todo = []
@@ -221,6 +233,7 @@
     for side in (out_y, in_y):
         for place in (0, 1):
             todo.append(((1 + 3 * place) * GRID + beyond(side), 5 * place * GRID + side + 1))
+    marks = [read_mark(extra, place) for extra in extras for place in (0, 1)]
     for at, (cell, other) in enumerate(todo):
 
         @pl.when(marks[at] == recent)
@@ -231,18 +244,22 @@
             plane[PLANE + cell] = (plane[PLANE + cell].astype(jnp.float32) + product).astype(jnp.bfloat16)
 
 
-def finish_corners(recent, table, plane, matrices, sums, far, near):
+def finish_corners(recent, extras, plane, sums, far, near):
     out_x, _, out_y, _ = edges()
-    for at, (x, y) in enumerate(CORNERS):
-        cell = SIDE * x + y
-
-        @pl.when((table[LEVEL + cell] == recent) & (table[LATE + at] >= 0))
-        def _(at=at, x=x, y=y, cell=cell):
+    facing = [extras.at[jnp.where(out_y == y, 2, 3)] for _, y in CORNERS]
+    places = [x // 3 for x, _ in CORNERS]
+    marks = [read_mark(extra, place) for extra, place in zip(facing, places, strict=True)]
+    for (x, y), extra, place, mark in zip(CORNERS, facing, places, marks, strict=True):
+
+        @pl.when(mark == recent)
+        def _(x=x, y=y, extra=extra, place=place):
             side = jnp.where(out_x == x, 0, 1)
             block = jnp.where(out_y == y, far(side), near(side))
-            matrix = matrices[cell, pl.ds(pl.multiple_of(LANES * table[LATE + at], LANES), LANES)]
-            summed = sums[cell] + jnp.dot(block, matrix, preferred_element_type=jnp.float32)
+            matrix = extra[place * LANES : (place + 1) * LANES]
+            summed = sums[SIDE * x + y] + jnp.dot(block, matrix, preferred_element_type=jnp.float32)
             plane[own_slot(x, y)] = summed.astype(jnp.bfloat16)
+
+    return [mark == recent for mark in marks]
 
 
 def block_of(ref, first):
@@ -263,35 +280,33 @@
 
 def settled_kernel(section, codes, table_in, plane_in, sums_in, matrices_in, noise_in, *rest):
     sources, rest = rest[:3], rest[3:]
-    extras = rest[:-8]
-    plane, sums, matrices, noise, table, settled, factors, sems = rest[-8:]
+    plane, sums, matrices, noise, table, settled, factors, sems = rest
     targets = noise, matrices, factors
-    cells_of(section, table_in, lambda cell: start_cell(cell, sources, targets, sems))
-    for at in range(SLOT):
-        table[at] = table_in[at]
-    marks = read_marks([ref.at[pl.ds(ref.shape[0] - EXTRA, EXTRA)] for ref in extras])
-    for at, mark in enumerate(marks):
-        table[MARKS + at] = mark
-
-    def one_cell(cell, count):
-        def collect():
-            fill_slots(cell, section, codes, table, settled)
-            found = count
-            for k in range(8):
-                table[ITEM + found] = 8 * cell + k
-                found += (table[SLOT + 8 * cell + k] != settled[8 * cell + k]).astype(jnp.int32)
-            return found
-
-        return lax.cond(table_in[LEVEL + cell] == section, collect, lambda: count)
-
-    count = lax.fori_loop(0, SIDE * SIDE, one_cell, jnp.int32(0))
-    table[COUNT] = count
-
-    def product(cell):
-        finish_cell(cell, sources, targets, sems)
-        sums[cell] = gather_product(cell, settled, 0, plane, matrices, noise)
-
-    cells_of(section, table_in, product)
+    choose(section, table_in, table)
+    each_cell(table, lambda cell: start_cell(cell, sources, targets, sems))
+
+    def one_cell(at, found):
+        cell = table[CELLS + at]
+        fill_slots(cell, section, codes, table, settled)
+        for k in range(8):
+            table[ITEM + found] = 8 * cell + k
+            found += (table[SLOT + 8 * cell + k] != settled[8 * cell + k]).astype(jnp.int32)
+        return found
+
+    table[COUNT] = lax.fori_loop(0, table[CHOSEN], one_cell, jnp.int32(0))
+
+    def products(first, second, fresh):
+        finish_cell(first, sources, targets, sems)
+
+        @pl.when(fresh)
+        def _():
+            finish_cell(second, sources, targets, sems)
+
+        both = [gather_product(cell, settled, 0, plane, matrices, noise) for cell in (first, second)]
+        sums[first] = both[0]
+        sums[second] = both[1]
+
+    each_pair(table, products)
 
 
 def store_rows(base, plane, tx_out, tx_in):
@@ -329,32 +344,45 @@
         ty_in[pl.ds((SIDE + i) * ROWS, ROWS)] = plane[base + beyond(side) * GRID + in_y + 1]
 
 
-def first_kernel(table, plane_in, sums_in, matrices_in, noise_in, *rest):
-    halo, extras, (plane, sums, matrices, noise, *sends) = rest[:4], rest[4], rest[5:]
+def fetch(table, scalars, sem):
+    copy = pltpu.make_async_copy(table, scalars, sem)
+    copy.start()
+    return copy.wait
+
+
+def first_kernel(table_in, plane_in, sums_in, matrices_in, noise_in, *rest):
+    halo, extras, (plane, sums, matrices, noise, *sends) = rest[:4], rest[4], rest[5:-2]
+    table, sem = rest[-2:]
+    wait = fetch(table_in, table, sem)
     store_rows(0, plane, *halo[:2])
     store_columns(0, plane, [piece(halo[2], i) for i in range(SIDE)], halo[3])
-
-    def one_cell(cell):
-        summed = gather_product(cell, table, SLOT, plane, matrices, noise)
-        sums[cell] = summed
-        plane[own_slot(cell // SIDE, cell % SIDE)] = summed.astype(jnp.bfloat16)
-
-    cells_of(0, table, one_cell)
-    pack_sends(0, plane, sends)
     for at, ref in enumerate((sends[0], sends[1], sends[3], sends[4])):
         ref[ref.shape[0] - EXTRA :] = extras[at]
-
-
-def main_kernel(section, table, plane_in, sums_in, matrices, ty_out, ty_more, ty_in, *rest):
-    extras, (plane, sums, *rest) = rest[:4], rest[4:]
+    wait()
+
+    def products(first, second, fresh):
+        cells = first, second
+        both = [gather_product(cell, table, SLOT, plane, matrices, noise) for cell in cells]
+        for cell, summed in zip(cells, both, strict=True):
+            sums[cell] = summed
+            plane[own_slot(cell // SIDE, cell % SIDE)] = summed.astype(jnp.bfloat16)
+
+    each_pair(table, products)
+    pack_sends(0, plane, sends)
+
+
+def main_kernel(section, table_in, plane_in, sums_in, matrices, own, ty_out, ty_more, ty_in, *rest):
+    extras, rest = rest[:4], rest[4:]
+    plane, sums, *rest, table, sem = rest
+    wait = fetch(table_in, table, sem)
     extras = [ref.at[pl.ds(ref.shape[0] - EXTRA, EXTRA)] for ref in extras]
-    marks = read_marks(extras) if section == 1 else [table[MARKS + at] for at in range(8)]
     corners = block_of(ty_more, 1), block_of(ty_in, SIDE)
     store_columns(PLANE, plane, [piece(ty_out, i) for i in range(3)] + [piece(ty_more, 0)], ty_in)
     if section == 1:
         store_corners(plane, *corners)
-    complete_halo(section - 1, plane, extras, marks)
-    finish_corners(section - 1, table, plane, matrices, sums, *corners)
+    complete_halo(section - 1, plane, extras)
+    finish_corners(section - 1, own, plane, sums, *corners)
+    wait()
     count = table[COUNT]
 
     def one_group(group, carry):
@@ -373,7 +401,7 @@
     def one_cell(cell):
         plane[own_slot(cell // SIDE, cell % SIDE)] = sums[cell].astype(jnp.bfloat16)
 
-    cells_of(section, table, one_cell)
+    each_cell(table, one_cell)
     if section < LEVELS - 1:
         pack_sends(PLANE, plane, rest)
     else:
@@ -390,16 +418,16 @@
             copy.wait()
 
 
-def corner_kernel(table, plane_in, matrices, sums, far, near, result_in, plane, result, sems):
-    finish_corners(LEVELS - 1, table, plane, matrices, sums, block_of(far, 0), block_of(near, 0))
+def corner_kernel(plane_in, own, sums, far, near, result_in, plane, result, sems):
+    changed = finish_corners(LEVELS - 1, own, plane, sums, block_of(far, 0), block_of(near, 0))
     copies = [
         pltpu.make_async_copy(plane.at[own_slot(x, y)], result.at[SIDE * x + y], sems.at[at])
         for at, (x, y) in enumerate(CORNERS)
     ]
-    for copy in copies:
-        copy.start()
-    for copy in copies:
-        copy.wait()
+    for copy, needed in zip(copies, changed, strict=True):
+        pl.when(needed)(copy.start)
+    for copy, needed in zip(copies, changed, strict=True):
+        pl.when(needed)(copy.wait)
 
 
 def cost(products, depth):
@@ -422,6 +450,7 @@
     whole = jax.ShapeDtypeStruct((tile, *block), jnp.bfloat16)
     matrices_shape = jax.ShapeDtypeStruct((tile, DEPTH, LANES), jnp.bfloat16)
     table_shape = jax.ShapeDtypeStruct((TABLE,), jnp.int32)
+    scalars = [pltpu.SMEM((TABLE,), jnp.int32), pltpu.SemaphoreType.DMA]
     factors = pltpu.VMEM((tile, *chol_factor.shape[2:]), jnp.bfloat16)
     sends = pl.pallas_call(
         pack_kernel,
@@ -434,7 +463,7 @@
     )(keep(earlier))
     sends = [send.reshape(SIDE * ROWS, LANES) for send in sends]
     sources = flat(innovation), flat(conditioner), flat(chol_factor)
-    plane, matrices, noise, sums, table, codes, extras = pl.pallas_call(
+    plane, matrices, noise, sums, table, codes, own = pl.pallas_call(
         load_kernel,
         out_shape=[
             plane_shape,
@@ -465,23 +494,23 @@
     plane, sums, matrices, noise, *sends = pl.pallas_call(
         first_kernel,
         out_shape=[plane_shape, sums_shape, matrices_shape, whole, *send_rows(EXTRA)],
-        in_specs=[SMEM] + [VMEM] * 9,
+        in_specs=[VMEM] * 10,
         out_specs=[VMEM] * 9,
+        scratch_shapes=scalars,
         input_output_aliases={1: 0, 2: 1, 3: 2, 4: 3},
         compiler_params=PARAMS,
         cost_estimate=cost(8, DEPTH),
         name="level_0",
-    )(table, plane, sums, matrices, noise, *halo, extras)
+    )(table, plane, sums, matrices, noise, *halo, own)
     for section in range(1, LEVELS):
         final = section == LEVELS - 1
         halo = exchange(sends)
         if section == 1:
             extras = [halo[0], halo[1], halo[3], halo[4]]
-        marks_from = extras if section > 1 else []
         plane, sums, matrices, noise, items = pl.pallas_call(
             functools.partial(settled_kernel, section),
             out_shape=[plane_shape, sums_shape, matrices_shape, whole, table_shape],
-            in_specs=[SMEM] * 2 + [VMEM] * 4 + [HBM] * 3 + [VMEM] * len(marks_from),
+            in_specs=[SMEM] * 2 + [VMEM] * 4 + [HBM] * 3,
             out_specs=[VMEM] * 4 + [SMEM],
             scratch_shapes=[
                 pltpu.SMEM((8 * tile,), jnp.int32),
@@ -492,7 +521,7 @@
             compiler_params=PARAMS,
             cost_estimate=cost(8, DEPTH),
             name=f"settled_{section}",
-        )(codes, table, plane, sums, matrices, noise, *sources, *marks_from)
+        )(codes, table, plane, sums, matrices, noise, *sources)
         plane = pl.pallas_call(
             rows_kernel,
             out_shape=plane_shape,
@@ -517,25 +546,25 @@
         plane, sums, *sends = pl.pallas_call(
             functools.partial(main_kernel, section),
             out_shape=[plane_shape, sums_shape] + ([whole] if final else send_rows(0)),
-            in_specs=[SMEM] + [VMEM] * 10,
+            in_specs=[VMEM] * 12,
             out_specs=[VMEM] * 2 + ([HBM] if final else [VMEM] * 5),
-            scratch_shapes=[pltpu.SemaphoreType.DMA((4,))] * final,
+            scratch_shapes=[pltpu.SemaphoreType.DMA((4,))] * final + scalars,
             input_output_aliases={1: 0, 2: 1},
             compiler_params=PARAMS,
             cost_estimate=cost(16, LANES),
             name=f"level_{section}",
-        )(items, plane, sums, matrices, *halo[2:], *extras)
+        )(items, plane, sums, matrices, own, *halo[2:], *extras)
     _, result = pl.pallas_call(
         corner_kernel,
         out_shape=[plane_shape, whole],
-        in_specs=[SMEM] + [VMEM] * 5 + [HBM],
+        in_specs=[VMEM] * 5 + [HBM],
         out_specs=[VMEM, HBM],
         scratch_shapes=[pltpu.SemaphoreType.DMA((4,))],
-        input_output_aliases={1: 0, 6: 1},
+        input_output_aliases={0: 0, 5: 1},
         compiler_params=PARAMS,
         cost_estimate=cost(4, LANES),
         name="last_corners",
-    )(items, plane, matrices, sums, far, near, sends[0])
+    )(plane, own, sums, far, near, sends[0])
     return result.reshape(earlier.shape)
 
 

time: 67.7 us -> 65.4 us (0.966)
  Pallas kernels: 27.9 us -> 24 us
  waiting for transfers between devices: 6.77 us -> 7.91 us
  starting transfers between devices: 32.8 us -> 33.8 us
    pallas_call x1, Pallas kernels: 1.32 us -> 0.18 us  [local(): pl.pallas_call(corner_kernel, out_shape=[plane_shape, whole], in_specs=[V...]
    ppermute x21, waiting for transfers between devices: 6.77 us -> 7.91 us  [swap(): return lax.ppermute(value, BOTH, pairs)]
    pallas_call x3, Pallas kernels: 14.3 us -> 13.2 us  [local(): pl.pallas_call(functools.partial(settled_kernel, section), out_shape=[pla...]
    pallas_call x3, Pallas kernels: 5.84 us -> 4.73 us  [local(): pl.pallas_call(functools.partial(main_kernel, section), out_shape=[plane_...]
    ppermute x21, starting transfers between devices: 32.8 us -> 33.8 us  [swap(): return lax.ppermute(value, BOTH, pairs)]
  transfers between devices with their start and end apart: 21 -> 21, of which waited for: 8 -> 8; matrix products, arithmetic and copies ran while one was open for 0% -> 0% of each run, Pallas kernels for 31% -> 29%
where the time goes in v6:
time: 65.4 us; the launch traced here: 65.9 us
  starting transfers between devices  33.8 us (52%)
  Pallas kernels  24 us (37%)
  waiting for transfers between devices  7.91 us (12%)
    ppermute x21, starting transfers between devices, swap(): return lax.ppermute(value, BOTH, pairs)  33.8 us
    pallas_call x3, Pallas kernels, local(): pl.pallas_call(functools.partial(settled_kernel, section), out_shape=[pla...  13.2 us
    ppermute x21, waiting for transfers between devices, swap(): return lax.ppermute(value, BOTH, pairs)  7.91 us
    pallas_call x3, Pallas kernels, local(): pl.pallas_call(functools.partial(main_kernel, section), out_shape=[plane_...  4.73 us
    pallas_call x1, Pallas kernels, local(): pl.pallas_call(load_kernel, out_shape=[plane_shape, matrices_shape, whole...  3.32 us
  transfers between devices with their start and end apart: 21, of which 8 were waited for; matrix products, arithmetic and copies ran while one was open for 0% of the time, Pallas kernels for 29%

profile of v6, /device:TPU:0, one launch (start us, length us, event | category | flops | bytes accessed | tf_op | source)
XLA Modules:
  0.0 65.9 jit_solution(13622746173569853583)
XLA Ops:
  0.0 1.2 %pack.1 = (bf16[4,256,128]{2,1,0:T(8,128)(2,1)S(1)}, bf16[4,256,128]{2,1,0:T(8,128)(2,1)S(1)}, bf16[4,256,128]{2,1,0:T(8,128)(2,1)S(1)}, bf16[4,256,128]{2,1,0:T(8,128)(2,1)S(1)}) custom-call(bf16[4,4,256,128]{3,2,1,0:T(8,128)(2,1)} %earlier.1), custom_call_target="tpu_custom_call" | custom-call | tf_op jit(solution)/shard_map/pack/pallas_call | solution.py:455
  1.2 1.7 %collective-permute-start.1 = (bf16[1024,128]{1,0:T(8,128)(2,1)S(1)}, bf16[1024,128]{1,0:T(8,128)(2,1)S(1)}, u32[]{:S(2)}, u32[]{:S(2)}) collective-permute-start(bf16[1024,128]{1,0:T(8,128)(2,1)S(1)} %bitcast.12), channel_id=1, source_target_pairs={{0,8},{1,9},{2,10},{3,11},{4,12},{5,13},{6,14},{7,15},{8,0},{9,1},... | collective-permute-start | bytes 786440 | tf_op jit(solution)/shard_map/ppermute | solution.py:45
  2.9 4.5 %collective-permute-start = (bf16[1024,128]{1,0:T(8,128)(2,1)S(1)}, bf16[1024,128]{1,0:T(8,128)(2,1)S(1)}, u32[]{:S(2)}, u32[]{:S(2)}) collective-permute-start(bf16[1024,128]{1,0:T(8,128)(2,1)S(1)} %bitcast.11), channel_id=1, source_target_pairs={{0,120},{1,121},{2,122},{3,123},{4,124},{5,125},{6,126},{7,127},{8... | collective-permute-start | bytes 786440 | tf_op jit(solution)/shard_map/ppermute | solution.py:45
  7.4 2.9 %collective-permute-start.2 = (bf16[1024,128]{1,0:T(8,128)(2,1)S(1)}, bf16[1024,128]{1,0:T(8,128)(2,1)S(1)}, u32[]{:S(2)}, u32[]{:S(2)}) collective-permute-start(bf16[1024,128]{1,0:T(8,128)(2,1)S(1)} %bitcast.10), channel_id=1, source_target_pairs={{0,7},{1,2},{2,1},{3,4},{4,3},{5,6},{6,5},{7,0},{8,15},{9,10},{10,... | collective-permute-start | bytes 786440 | tf_op jit(solution)/shard_map/ppermute | solution.py:45
  10.3 3.3 %load.1 = (bf16[73,256,128]{2,1,0:T(8,128)(2,1)S(1)}, bf16[16,1152,128]{2,1,0:T(8,128)(2,1)S(1)}, bf16[16,256,128]{2,1,0:T(8,128)(2,1)S(1)}, f32[16,256,128]{2,1...) custom-call(s32[4,4]{1,0:T(4,128)} %block_level.1, ...), custom_call_target="tpu_custom_call" | custom-call | bytes 10485760 | tf_op jit(solution)/shard_map/load/pallas_call | solution.py:466
  13.7 0.3 collective-permute-done.rest_0_
  14.0 0.5 collective-permute-done.2.rest_2_
  14.4 1.1 %level_0.1 = (bf16[73,256,128]{2,1,0:T(8,128)(2,1)S(1)}, f32[16,256,128]{2,1,0:T(8,128)S(1)}, bf16[16,1152,128]{2,1,0:T(8,128)(2,1)S(1)}, bf16[16,256,128]{2,1,0...) custom-call(s32[238]{0:T(256)S(1)} %get-tuple-element.60.table_in, ...), custom_call_target="tpu_custom_call", output_to_operand_aliasing={{0}: (1, {}), {1}: (2, {}), {2}: (3, {}), {3}: (4, {})} | custom-call | flops 603979776 | bytes 4194304 | tf_op jit(solution)/shard_map/level_0/pallas_call | solution.py:494
  15.6 0.1 collective-permute-start.8
  15.7 5.6 %collective-permute-start.4 = (bf16[1312,128]{1,0:T(8,128)(2,1)S(1)}, bf16[1312,128]{1,0:T(8,128)(2,1)S(1)}, u32[]{:S(2)}, u32[]{:S(2)}) collective-permute-start(bf16[1312,128]{1,0:T(8,128)(2,1)S(1)} %get-tuple-element.76), channel_id=1, source_target_pairs={{0,120},{1,121},{2,122},{3,123},{4,124},{5,125},{6,126},{7,127},{8... | collective-permute-start | bytes 1007624 | tf_op jit(solution)/shard_map/ppermute | solution.py:45
  21.3 3.8 %collective-permute-start.7 = (bf16[1056,128]{1,0:T(8,128)(2,1)S(1)}, bf16[1056,128]{1,0:T(8,128)(2,1)S(1)}, u32[]{:S(2)}, u32[]{:S(2)}) collective-permute-start(bf16[1056,128]{1,0:T(8,128)(2,1)S(1)} %get-tuple-element.81), channel_id=1, source_target_pairs={{0,7},{1,2},{2,1},{3,4},{4,3},{5,6},{6,5},{7,0},{8,15},{9,10},{10,... | collective-permute-start | bytes 811016 | tf_op jit(solution)/shard_map/ppermute | solution.py:45
  25.1 3.4 %settled_1.1 = (bf16[73,256,128]{2,1,0:T(8,128)(2,1)S(1)}, f32[16,256,128]{2,1,0:T(8,128)S(1)}, bf16[16,1152,128]{2,1,0:T(8,128)(2,1)S(1)}, bf16[16,256,128]{2,1,0:T(8,128)(2,1)S(1)}, s32[238]{0:T(256)S(1)}) custom-call(s32[4,4,8]{2,1,0:T(4,128)S(1)} %get-tuple-element.59.codes, ...), custom_call_target="tpu_custom_call", output_to_operand_aliasing={{0}: (2, {}), {1}: (3, {}), {2}: (4, {}), {3}: (5, {})} | custom-call | flops 603979776 | bytes 4194304 | tf_op jit(solution)/shard_map/settled_1/pallas_call | solution.py:510
  28.5 1.2 %collective-permute-done.4.tx_out.rest_0_ = bf16[1312,128]{1,0:T(8,128)(2,1)S(1)} collective-permute-done((bf16[1312,128]{1,0:T(8,128)(2,1)S(1)}, bf16[1312,128]{1,0:T(8,128)(2,1)S(1)}, u32[]{:S(2)}, u32[]{:S(2)}) %collective-permute-start.4) | collective-permute-done | bytes 335904 | tf_op jit(solution)/shard_map/ppermute | solution.py:45
  29.7 1.5 %collective-permute-done.5.tx_in.rest_1_ = bf16[1312,128]{1,0:T(8,128)(2,1)S(1)} collective-permute-done((bf16[1312,128]{1,0:T(8,128)(2,1)S(1)}, bf16[1312,128]{1,0:T(8,128)(2,1)S(1)}, u32[]{:S(2)}, u32[]{:S(2)}) %collective-permute-start.5) | collective-permute-done | bytes 335904 | tf_op jit(solution)/shard_map/ppermute | solution.py:45
  31.3 0.1 collective-permute-done.6.ty_out
  31.4 0.9 %level_1.1 = (bf16[73,256,128]{2,1,0:T(8,128)(2,1)S(1)}, f32[16,256,128]{2,1,0:T(8,128)S(1)}, bf16[1024,128]{1,0:T(8,128)(2,1)S(1)}, bf16[1024,128]{1,0:T(8,128)...) custom-call(s32[238]{0:T(256)S(1)} %get-tuple-element.74.table_in, ...), custom_call_target="tpu_custom_call", output_to_operand_aliasing={{0}: (1, {}), {1}: (2, {})} | custom-call | flops 134217728 | bytes 4194304 | tf_op jit(solution)/shard_map/level_1/pallas_call | solution.py:546
  32.3 0.1 collective-permute-start.13
  32.4 3.5 %collective-permute-start.9 = (bf16[1024,128]{1,0:T(8,128)(2,1)S(1)}, bf16[1024,128]{1,0:T(8,128)(2,1)S(1)}, u32[]{:S(2)}, u32[]{:S(2)}) collective-permute-start(bf16[1024,128]{1,0:T(8,128)(2,1)S(1)} %get-tuple-element.88), channel_id=1, source_target_pairs={{0,120},{1,121},{2,122},{3,123},{4,124},{5,125},{6,126},{7,127},{8... | collective-permute-start | bytes 786440 | tf_op jit(solution)/shard_map/ppermute | solution.py:45
  35.9 4.0 %collective-permute-start.11 = (bf16[768,128]{1,0:T(8,128)(2,1)S(1)}, bf16[768,128]{1,0:T(8,128)(2,1)S(1)}, u32[]{:S(2)}, u32[]{:S(2)}) collective-permute-start(bf16[768,128]{1,0:T(8,128)(2,1)S(1)} %get-tuple-element.92), channel_id=1, source_target_pairs={{0,7},{1,2},{2,1},{3,4},{4,3},{5,6},{6,5},{7,0},{8,15},{9,10},{10,... | collective-permute-start | bytes 589832 | tf_op jit(solution)/shard_map/ppermute | solution.py:45
  40.0 5.4 %settled_2.1 = (bf16[73,256,128]{2,1,0:T(8,128)(2,1)S(1)}, f32[16,256,128]{2,1,0:T(8,128)S(1)}, bf16[16,1152,128]{2,1,0:T(8,128)(2,1)S(1)}, bf16[16,256,128]{2,1,0:T(8,128)(2,1)S(1)}, s32[238]{0:T(256)S(1)}) custom-call(s32[4,4,8]{2,1,0:T(4,128)S(1)} %get-tuple-element.59.codes, ...), custom_call_target="tpu_custom_call", output_to_operand_aliasing={{0}: (2, {}), {1}: (3, {}), {2}: (4, {}), {3}: (5, {})} | custom-call | flops 603979776 | bytes 4194304 | tf_op jit(solution)/shard_map/settled_2/pallas_call | solution.py:510
  45.4 0.8 %collective-permute-done.12.ty_more = bf16[768,128]{1,0:T(8,128)(2,1)S(1)} collective-permute-done((bf16[768,128]{1,0:T(8,128)(2,1)S(1)}, bf16[768,128]{1,0:T(8,128)(2,1)S(1)}, u32[]{:S(2)}, u32[]{:S(2)}) %collective-permute-start.12) | collective-permute-done | bytes 196640 | tf_op jit(solution)/shard_map/ppermute | solution.py:45
  46.2 1.6 %level_2.1 = (bf16[73,256,128]{2,1,0:T(8,128)(2,1)S(1)}, f32[16,256,128]{2,1,0:T(8,128)S(1)}, bf16[1024,128]{1,0:T(8,128)(2,1)S(1)}, bf16[1024,128]{1,0:T(8,128)...) custom-call(s32[238]{0:T(256)S(1)} %get-tuple-element.86.table_in, ...), custom_call_target="tpu_custom_call", output_to_operand_aliasing={{0}: (1, {}), {1}: (2, {})} | custom-call | flops 134217728 | bytes 4194304 | tf_op jit(solution)/shard_map/level_2/pallas_call | solution.py:546
  47.8 0.1 collective-permute-start.18
  47.9 1.2 %collective-permute-start.14 = (bf16[1024,128]{1,0:T(8,128)(2,1)S(1)}, bf16[1024,128]{1,0:T(8,128)(2,1)S(1)}, u32[]{:S(2)}, u32[]{:S(2)}) collective-permute-start(bf16[1024,128]{1,0:T(8,128)(2,1)S(1)} %get-tuple-element.100), channel_id=1, source_target_pairs={{0,120},{1,121},{2,122},{3,123},{4,124},{5,125},{6,126},{7,127},{8... | collective-permute-start | bytes 786440 | tf_op jit(solution)/shard_map/ppermute | solution.py:45
  49.1 0.4 collective-permute-start.15
  49.5 3.9 %collective-permute-start.16 = (bf16[768,128]{1,0:T(8,128)(2,1)S(1)}, bf16[768,128]{1,0:T(8,128)(2,1)S(1)}, u32[]{:S(2)}, u32[]{:S(2)}) collective-permute-start(bf16[768,128]{1,0:T(8,128)(2,1)S(1)} %get-tuple-element.104), channel_id=1, source_target_pairs={{0,7},{1,2},{2,1},{3,4},{4,3},{5,6},{6,5},{7,0},{8,15},{9,10},{10,... | collective-permute-start | bytes 589832 | tf_op jit(solution)/shard_map/ppermute | solution.py:45
  53.4 4.4 %settled_3.1 = (bf16[73,256,128]{2,1,0:T(8,128)(2,1)S(1)}, f32[16,256,128]{2,1,0:T(8,128)S(1)}, bf16[16,1152,128]{2,1,0:T(8,128)(2,1)S(1)}, bf16[16,256,128]{2,1,0:T(8,128)(2,1)S(1)}, s32[238]{0:T(256)S(1)}) custom-call(s32[4,4,8]{2,1,0:T(4,128)S(1)} %get-tuple-element.59.codes, ...), custom_call_target="tpu_custom_call", output_to_operand_aliasing={{0}: (2, {}), {1}: (3, {}), {2}: (4, {}), {3}: (5, {})} | custom-call | flops 603979776 | bytes 4194304 | tf_op jit(solution)/shard_map/settled_3/pallas_call | solution.py:510
  57.9 2.1 %collective-permute-done.14.tx_out = bf16[1024,128]{1,0:T(8,128)(2,1)S(1)} collective-permute-done((bf16[1024,128]{1,0:T(8,128)(2,1)S(1)}, bf16[1024,128]{1,0:T(8,128)(2,1)S(1)}, u32[]{:S(2)}, u32[]{:S(2)}) %collective-permute-start.14) | collective-permute-done | bytes 262176 | tf_op jit(solution)/shard_map/ppermute | solution.py:45
  60.0 1.9 %collective-permute-start.19 = (bf16[512,128]{1,0:T(8,128)(2,1)S(1)}, bf16[512,128]{1,0:T(8,128)(2,1)S(1)}, u32[]{:S(2)}, u32[]{:S(2)}) collective-permute-start(bf16[512,128]{1,0:T(8,128)(2,1)S(1)} %get-tuple-element.109), channel_id=1, source_target_pairs={{0,7},{1,2},{2,1},{3,4},{4,3},{5,6},{6,5},{7,0},{8,15},{9,10},{10,... | collective-permute-start | bytes 393224 | tf_op jit(solution)/shard_map/ppermute | solution.py:45
  62.0 2.2 %level_3.1 = (bf16[73,256,128]{2,1,0:T(8,128)(2,1)S(1)}, f32[16,256,128]{2,1,0:T(8,128)S(1)}, bf16[16,256,128]{2,1,0:T(8,128)(2,1)}) custom-call(s32[238]{0:T(256)S(1)} %get-tuple-element.98.table_in, bf16[73,256,128]{2,1,0:T(8,128)(2,1)S(1)} %rows_3.1.plane_in.plane, ...), custom_call_target="tpu_custom_call", output_to_operand_aliasing={{0}: (1, {}), {1}: (2, {})} | custom-call | flops 134217728 | bytes 4194304 | tf_op jit(solution)/shard_map/level_3/pallas_call | solution.py:546
  64.2 1.5 %collective-permute-done.19.far = bf16[512,128]{1,0:T(8,128)(2,1)S(1)} collective-permute-done((bf16[512,128]{1,0:T(8,128)(2,1)S(1)}, bf16[512,128]{1,0:T(8,128)(2,1)S(1)}, u32[]{:S(2)}, u32[]{:S(2)}) %collective-permute-start.19) | collective-permute-done | bytes 131104 | tf_op jit(solution)/shard_map/ppermute | solution.py:45
  65.7 0.2 last_corners.1
  (24 shorter events, 0.4 us)
Async XLA Ops:
  1.2 12.5 %collective-permute-start.1 = (bf16[1024,128]{1,0:T(8,128)(2,1)S(1)}, bf16[1024,128]{1,0:T(8,128)(2,1)S(1)}, u32[]{:S(2)}, u32[]{:S(2)}) collective-permute-start(bf16[1024,128]{1,0:T(8,128)(2,1)S(1)} %bitcast.12), channel_id=1, source_target_pairs={{0,8},{1,9},{2,10},{3,11},{4,12},{5,13},{6,14},{7,15},{8,0},{9,1},... | collective-permute-start | bytes 786440 | tf_op jit(solution)/shard_map/ppermute | solution.py:45
  2.9 11.1 %collective-permute-start = (bf16[1024,128]{1,0:T(8,128)(2,1)S(1)}, bf16[1024,128]{1,0:T(8,128)(2,1)S(1)}, u32[]{:S(2)}, u32[]{:S(2)}) collective-permute-start(bf16[1024,128]{1,0:T(8,128)(2,1)S(1)} %bitcast.11), channel_id=1, source_target_pairs={{0,120},{1,121},{2,122},{3,123},{4,124},{5,125},{6,126},{7,127},{8... | collective-permute-start | bytes 786440 | tf_op jit(solution)/shard_map/ppermute | solution.py:45
  7.4 7.0 %collective-permute-start.2 = (bf16[1024,128]{1,0:T(8,128)(2,1)S(1)}, bf16[1024,128]{1,0:T(8,128)(2,1)S(1)}, u32[]{:S(2)}, u32[]{:S(2)}) collective-permute-start(bf16[1024,128]{1,0:T(8,128)(2,1)S(1)} %bitcast.10), channel_id=1, source_target_pairs={{0,7},{1,2},{2,1},{3,4},{4,3},{5,6},{6,5},{7,0},{8,15},{9,10},{10,... | collective-permute-start | bytes 786440 | tf_op jit(solution)/shard_map/ppermute | solution.py:45
  10.3 4.1 %collective-permute-start.3 = (bf16[1024,128]{1,0:T(8,128)(2,1)S(1)}, bf16[1024,128]{1,0:T(8,128)(2,1)S(1)}, u32[]{:S(2)}, u32[]{:S(2)}) collective-permute-start(bf16[1024,128]{1,0:T(8,128)(2,1)S(1)} %bitcast.9), channel_id=1, source_target_pairs={{0,1},{1,0},{2,3},{3,2},{4,5},{5,4},{6,7},{7,6},{8,9},{9,8},{10,11... | collective-permute-start | bytes 786440 | tf_op jit(solution)/shard_map/ppermute | solution.py:45
  15.6 15.8 %collective-permute-start.8 = (bf16[1824,128]{1,0:T(8,128)(2,1)S(1)}, bf16[1824,128]{1,0:T(8,128)(2,1)S(1)}, u32[]{:S(2)}, u32[]{:S(2)}) collective-permute-start(bf16[1824,128]{1,0:T(8,128)(2,1)S(1)} %get-tuple-element.82), channel_id=1, source_target_pairs={{0,1},{1,0},{2,3},{3,2},{4,5},{5,4},{6,7},{7,6},{8,9},{9,8},{10,11... | collective-permute-start | bytes 1400840 | tf_op jit(solution)/shard_map/ppermute | solution.py:45
  15.7 14.0 %collective-permute-start.4 = (bf16[1312,128]{1,0:T(8,128)(2,1)S(1)}, bf16[1312,128]{1,0:T(8,128)(2,1)S(1)}, u32[]{:S(2)}, u32[]{:S(2)}) collective-permute-start(bf16[1312,128]{1,0:T(8,128)(2,1)S(1)} %get-tuple-element.76), channel_id=1, source_target_pairs={{0,120},{1,121},{2,122},{3,123},{4,124},{5,125},{6,126},{7,127},{8... | collective-permute-start | bytes 1007624 | tf_op jit(solution)/shard_map/ppermute | solution.py:45
  21.3 9.9 %collective-permute-start.5 = (bf16[1312,128]{1,0:T(8,128)(2,1)S(1)}, bf16[1312,128]{1,0:T(8,128)(2,1)S(1)}, u32[]{:S(2)}, u32[]{:S(2)}) collective-permute-start(bf16[1312,128]{1,0:T(8,128)(2,1)S(1)} %get-tuple-element.77), channel_id=1, source_target_pairs={{0,8},{1,9},{2,10},{3,11},{4,12},{5,13},{6,14},{7,15},{8,0},{9,1},... | collective-permute-start | bytes 1007624 | tf_op jit(solution)/shard_map/ppermute | solution.py:45
  21.3 10.1 %collective-permute-start.7 = (bf16[1056,128]{1,0:T(8,128)(2,1)S(1)}, bf16[1056,128]{1,0:T(8,128)(2,1)S(1)}, u32[]{:S(2)}, u32[]{:S(2)}) collective-permute-start(bf16[1056,128]{1,0:T(8,128)(2,1)S(1)} %get-tuple-element.81), channel_id=1, source_target_pairs={{0,7},{1,2},{2,1},{3,4},{4,3},{5,6},{6,5},{7,0},{8,15},{9,10},{10,... | collective-permute-start | bytes 811016 | tf_op jit(solution)/shard_map/ppermute | solution.py:45
  25.0 6.3 %collective-permute-start.6 = (bf16[768,128]{1,0:T(8,128)(2,1)S(1)}, bf16[768,128]{1,0:T(8,128)(2,1)S(1)}, u32[]{:S(2)}, u32[]{:S(2)}) collective-permute-start(bf16[768,128]{1,0:T(8,128)(2,1)S(1)} %get-tuple-element.80), channel_id=1, source_target_pairs={{0,7},{1,2},{2,1},{3,4},{4,3},{5,6},{6,5},{7,0},{8,15},{9,10},{10,... | collective-permute-start | bytes 589832 | tf_op jit(solution)/shard_map/ppermute | solution.py:45
  32.3 13.9 %collective-permute-start.13 = (bf16[1536,128]{1,0:T(8,128)(2,1)S(1)}, bf16[1536,128]{1,0:T(8,128)(2,1)S(1)}, u32[]{:S(2)}, u32[]{:S(2)}) collective-permute-start(bf16[1536,128]{1,0:T(8,128)(2,1)S(1)} %get-tuple-element.94), channel_id=1, source_target_pairs={{0,1},{1,0},{2,3},{3,2},{4,5},{5,4},{6,7},{7,6},{8,9},{9,8},{10,11... | collective-permute-start | bytes 1179656 | tf_op jit(solution)/shard_map/ppermute | solution.py:45
  32.4 12.9 %collective-permute-start.9 = (bf16[1024,128]{1,0:T(8,128)(2,1)S(1)}, bf16[1024,128]{1,0:T(8,128)(2,1)S(1)}, u32[]{:S(2)}, u32[]{:S(2)}) collective-permute-start(bf16[1024,128]{1,0:T(8,128)(2,1)S(1)} %get-tuple-element.88), channel_id=1, source_target_pairs={{0,120},{1,121},{2,122},{3,123},{4,124},{5,125},{6,126},{7,127},{8... | collective-permute-start | bytes 786440 | tf_op jit(solution)/shard_map/ppermute | solution.py:45
  35.9 9.4 %collective-permute-start.10 = (bf16[1024,128]{1,0:T(8,128)(2,1)S(1)}, bf16[1024,128]{1,0:T(8,128)(2,1)S(1)}, u32[]{:S(2)}, u32[]{:S(2)}) collective-permute-start(bf16[1024,128]{1,0:T(8,128)(2,1)S(1)} %get-tuple-element.89), channel_id=1, source_target_pairs={{0,8},{1,9},{2,10},{3,11},{4,12},{5,13},{6,14},{7,15},{8,0},{9,1},... | collective-permute-start | bytes 786440 | tf_op jit(solution)/shard_map/ppermute | solution.py:45
  35.9 9.5 %collective-permute-start.11 = (bf16[768,128]{1,0:T(8,128)(2,1)S(1)}, bf16[768,128]{1,0:T(8,128)(2,1)S(1)}, u32[]{:S(2)}, u32[]{:S(2)}) collective-permute-start(bf16[768,128]{1,0:T(8,128)(2,1)S(1)} %get-tuple-element.92), channel_id=1, source_target_pairs={{0,7},{1,2},{2,1},{3,4},{4,3},{5,6},{6,5},{7,0},{8,15},{9,10},{10,... | collective-permute-start | bytes 589832 | tf_op jit(solution)/shard_map/ppermute | solution.py:45
  39.9 6.3 %collective-permute-start.12 = (bf16[768,128]{1,0:T(8,128)(2,1)S(1)}, bf16[768,128]{1,0:T(8,128)(2,1)S(1)}, u32[]{:S(2)}, u32[]{:S(2)}) collective-permute-start(bf16[768,128]{1,0:T(8,128)(2,1)S(1)} %get-tuple-element.93), channel_id=1, source_target_pairs={{0,7},{1,2},{2,1},{3,4},{4,3},{5,6},{6,5},{7,0},{8,15},{9,10},{10,... | collective-permute-start | bytes 589832 | tf_op jit(solution)/shard_map/ppermute | solution.py:45
  47.8 14.2 %collective-permute-start.18 = (bf16[1536,128]{1,0:T(8,128)(2,1)S(1)}, bf16[1536,128]{1,0:T(8,128)(2,1)S(1)}, u32[]{:S(2)}, u32[]{:S(2)}) collective-permute-start(bf16[1536,128]{1,0:T(8,128)(2,1)S(1)} %get-tuple-element.106), channel_id=1, source_target_pairs={{0,1},{1,0},{2,3},{3,2},{4,5},{5,4},{6,7},{7,6},{8,9},{9,8},{10,11... | collective-permute-start | bytes 1179656 | tf_op jit(solution)/shard_map/ppermute | solution.py:45
  47.9 12.0 %collective-permute-start.14 = (bf16[1024,128]{1,0:T(8,128)(2,1)S(1)}, bf16[1024,128]{1,0:T(8,128)(2,1)S(1)}, u32[]{:S(2)}, u32[]{:S(2)}) collective-permute-start(bf16[1024,128]{1,0:T(8,128)(2,1)S(1)} %get-tuple-element.100), channel_id=1, source_target_pairs={{0,120},{1,121},{2,122},{3,123},{4,124},{5,125},{6,126},{7,127},{8... | collective-permute-start | bytes 786440 | tf_op jit(solution)/shard_map/ppermute | solution.py:45
  49.1 10.8 %collective-permute-start.15 = (bf16[1024,128]{1,0:T(8,128)(2,1)S(1)}, bf16[1024,128]{1,0:T(8,128)(2,1)S(1)}, u32[]{:S(2)}, u32[]{:S(2)}) collective-permute-start(bf16[1024,128]{1,0:T(8,128)(2,1)S(1)} %get-tuple-element.101), channel_id=1, source_target_pairs={{0,8},{1,9},{2,10},{3,11},{4,12},{5,13},{6,14},{7,15},{8,0},{9,1},... | collective-permute-start | bytes 786440 | tf_op jit(solution)/shard_map/ppermute | solution.py:45
  49.5 12.5 %collective-permute-start.16 = (bf16[768,128]{1,0:T(8,128)(2,1)S(1)}, bf16[768,128]{1,0:T(8,128)(2,1)S(1)}, u32[]{:S(2)}, u32[]{:S(2)}) collective-permute-start(bf16[768,128]{1,0:T(8,128)(2,1)S(1)} %get-tuple-element.104), channel_id=1, source_target_pairs={{0,7},{1,2},{2,1},{3,4},{4,3},{5,6},{6,5},{7,0},{8,15},{9,10},{10,... | collective-permute-start | bytes 589832 | tf_op jit(solution)/shard_map/ppermute | solution.py:45
  53.4 8.6 %collective-permute-start.17 = (bf16[768,128]{1,0:T(8,128)(2,1)S(1)}, bf16[768,128]{1,0:T(8,128)(2,1)S(1)}, u32[]{:S(2)}, u32[]{:S(2)}) collective-permute-start(bf16[768,128]{1,0:T(8,128)(2,1)S(1)} %get-tuple-element.105), channel_id=1, source_target_pairs={{0,7},{1,2},{2,1},{3,4},{4,3},{5,6},{6,5},{7,0},{8,15},{9,10},{10,... | collective-permute-start | bytes 589832 | tf_op jit(solution)/shard_map/ppermute | solution.py:45
  60.0 5.7 %collective-permute-start.19 = (bf16[512,128]{1,0:T(8,128)(2,1)S(1)}, bf16[512,128]{1,0:T(8,128)(2,1)S(1)}, u32[]{:S(2)}, u32[]{:S(2)}) collective-permute-start(bf16[512,128]{1,0:T(8,128)(2,1)S(1)} %get-tuple-element.109), channel_id=1, source_target_pairs={{0,7},{1,2},{2,1},{3,4},{4,3},{5,6},{6,5},{7,0},{8,15},{9,10},{10,... | collective-permute-start | bytes 393224 | tf_op jit(solution)/shard_map/ppermute | solution.py:45
  62.0 3.8 %collective-permute-start.20 = (bf16[512,128]{1,0:T(8,128)(2,1)S(1)}, bf16[512,128]{1,0:T(8,128)(2,1)S(1)}, u32[]{:S(2)}, u32[]{:S(2)}) collective-permute-start(bf16[512,128]{1,0:T(8,128)(2,1)S(1)} %get-tuple-element.110), channel_id=1, source_target_pairs={{0,1},{1,0},{2,3},{3,2},{4,5},{5,4},{6,7},{7,6},{8,9},{9,8},{10,11... | collective-permute-start | bytes 393224 | tf_op jit(solution)/shard_map/ppermute | solution.py:45

commit v7 on v6

--- a/solution.py
+++ b/solution.py
@@ -46,9 +46,8 @@
 
 
 def exchange(sends):
-    tx_out, tx_in, *ty_out, ty_in = sends
-    halo = [swap(tx_out, "out", None), swap(tx_in, "in", None)]
-    return halo + [swap(part, None, "out") for part in ty_out] + [swap(ty_in, None, "in")]
+    tx_out, tx_in, ty_out, ty_in = sends
+    return swap(tx_out, "out", None), swap(tx_in, "in", None), swap(ty_out, None, "out"), swap(ty_in, None, "in")
 
 
 def edges():
@@ -309,39 +308,48 @@
     each_pair(table, products)
 
 
-def store_rows(base, plane, tx_out, tx_in):
+def rows_kernel(base, outward, plane_in, halo, plane):
     out_x, in_x, _, _ = edges()
+    row = beyond(out_x if outward else in_x)
     for i in range(SIDE):
-        plane[base + beyond(out_x) * GRID + i + 1] = piece(tx_out, i)
-        plane[base + beyond(in_x) * GRID + i + 1] = piece(tx_in, i)
-
-
-def rows_kernel(plane_in, tx_out, tx_in, plane):
-    store_rows(PLANE, plane, tx_out, tx_in)
-
-
-def store_columns(base, plane, out_blocks, ty_in):
+        plane[base + row * GRID + i + 1] = piece(halo, i)
+
+
+def take_rows(base, plane, halo, name):
+    for outward, part, products in ((True, halo[0], 16), (False, halo[1], 64)):
+        plane = pl.pallas_call(
+            functools.partial(rows_kernel, base, outward),
+            out_shape=jax.ShapeDtypeStruct(plane.shape, plane.dtype),
+            in_specs=[VMEM] * 2,
+            out_specs=VMEM,
+            input_output_aliases={0: 0},
+            compiler_params=PARAMS,
+            cost_estimate=cost(products, DEPTH),
+            name=f"{name}_{'out' if outward else 'in'}",
+        )(plane, part)
+    return plane
+
+
+def store_columns(base, plane, ty_out, ty_in):
     _, _, out_y, in_y = edges()
     for i in range(SIDE):
-        plane[base + (i + 1) * GRID + beyond(out_y)] = out_blocks[i]
+        plane[base + (i + 1) * GRID + beyond(out_y)] = piece(ty_out, i)
         plane[base + (i + 1) * GRID + beyond(in_y)] = piece(ty_in, i)
 
 
 def pack_sends(base, plane, sends):
-    tx_out, tx_in, ty_out, ty_more, ty_in = sends
+    tx_out, tx_in, ty_out, ty_in = sends
     out_x, in_x, out_y, in_y = edges()
     for i in range(SIDE):
         rows = pl.ds(i * ROWS, ROWS)
         tx_out[rows] = plane[own_slot(out_x, i)]
         tx_in[rows] = plane[own_slot(in_x, i)]
+        ty_out[rows] = plane[own_slot(i, out_y)]
         ty_in[rows] = plane[own_slot(i, in_y)]
-        if i < 3:
-            ty_out[rows] = plane[own_slot(i, out_y)]
-        else:
-            ty_more[pl.ds(0, ROWS)] = plane[own_slot(i, out_y)]
     for i, side in enumerate((out_x, in_x)):
-        ty_more[pl.ds((1 + i) * ROWS, ROWS)] = plane[base + beyond(side) * GRID + out_y + 1]
-        ty_in[pl.ds((SIDE + i) * ROWS, ROWS)] = plane[base + beyond(side) * GRID + in_y + 1]
+        rows = pl.ds((SIDE + i) * ROWS, ROWS)
+        ty_out[rows] = plane[base + beyond(side) * GRID + out_y + 1]
+        ty_in[rows] = plane[base + beyond(side) * GRID + in_y + 1]
 
 
 def fetch(table, scalars, sem):
@@ -351,12 +359,11 @@
 
 
 def first_kernel(table_in, plane_in, sums_in, matrices_in, noise_in, *rest):
-    halo, extras, (plane, sums, matrices, noise, *sends) = rest[:4], rest[4], rest[5:-2]
+    halo, extras, (plane, sums, matrices, noise, *sends) = rest[:2], rest[2], rest[3:-2]
     table, sem = rest[-2:]
     wait = fetch(table_in, table, sem)
-    store_rows(0, plane, *halo[:2])
-    store_columns(0, plane, [piece(halo[2], i) for i in range(SIDE)], halo[3])
-    for at, ref in enumerate((sends[0], sends[1], sends[3], sends[4])):
+    store_columns(0, plane, *halo)
+    for at, ref in enumerate(sends):
         ref[ref.shape[0] - EXTRA :] = extras[at]
     wait()
 
@@ -371,13 +378,13 @@
     pack_sends(0, plane, sends)
 
 
-def main_kernel(section, table_in, plane_in, sums_in, matrices, own, ty_out, ty_more, ty_in, *rest):
+def main_kernel(section, table_in, plane_in, sums_in, matrices, own, ty_out, ty_in, *rest):
     extras, rest = rest[:4], rest[4:]
     plane, sums, *rest, table, sem = rest
     wait = fetch(table_in, table, sem)
     extras = [ref.at[pl.ds(ref.shape[0] - EXTRA, EXTRA)] for ref in extras]
-    corners = block_of(ty_more, 1), block_of(ty_in, SIDE)
-    store_columns(PLANE, plane, [piece(ty_out, i) for i in range(3)] + [piece(ty_more, 0)], ty_in)
+    corners = block_of(ty_out, SIDE), block_of(ty_in, SIDE)
+    store_columns(PLANE, plane, ty_out, ty_in)
     if section == 1:
         store_corners(plane, *corners)
     complete_halo(section - 1, plane, extras)
@@ -487,26 +494,24 @@
         name="load",
     )(keep(block_level), keep(neighbours), flat(earlier), *sources)
     halo = exchange(sends)
-    send_rows = lambda extra: [
-        rows_of(rows)
-        for rows in (4 * ROWS + extra, 4 * ROWS + extra, 3 * ROWS, 3 * ROWS + extra, 6 * ROWS + extra)
-    ]
+    plane = take_rows(0, plane, halo, "rows_0")
+    send_rows = lambda extra: [rows_of(4 * ROWS + extra)] * 2 + [rows_of(6 * ROWS + extra)] * 2
     plane, sums, matrices, noise, *sends = pl.pallas_call(
         first_kernel,
         out_shape=[plane_shape, sums_shape, matrices_shape, whole, *send_rows(EXTRA)],
-        in_specs=[VMEM] * 10,
-        out_specs=[VMEM] * 9,
+        in_specs=[VMEM] * 8,
+        out_specs=[VMEM] * 8,
         scratch_shapes=scalars,
         input_output_aliases={1: 0, 2: 1, 3: 2, 4: 3},
         compiler_params=PARAMS,
         cost_estimate=cost(8, DEPTH),
         name="level_0",
-    )(table, plane, sums, matrices, noise, *halo, own)
+    )(table, plane, sums, matrices, noise, *halo[2:], own)
     for section in range(1, LEVELS):
         final = section == LEVELS - 1
         halo = exchange(sends)
         if section == 1:
-            extras = [halo[0], halo[1], halo[3], halo[4]]
+            extras = halo
         plane, sums, matrices, noise, items = pl.pallas_call(
             functools.partial(settled_kernel, section),
             out_shape=[plane_shape, sums_shape, matrices_shape, whole, table_shape],
@@ -522,16 +527,7 @@
             cost_estimate=cost(8, DEPTH),
             name=f"settled_{section}",
         )(codes, table, plane, sums, matrices, noise, *sources)
-        plane = pl.pallas_call(
-            rows_kernel,
-            out_shape=plane_shape,
-            in_specs=[VMEM] * 3,
-            out_specs=VMEM,
-            input_output_aliases={0: 0},
-            compiler_params=PARAMS,
-            cost_estimate=cost(2, LANES),
-            name=f"rows_{section}",
-        )(plane, *halo[:2])
+        plane = take_rows(PLANE, plane, halo, f"rows_{section}")
         if final:
             far, near = pl.pallas_call(
                 forward_kernel,
@@ -546,8 +542,8 @@
         plane, sums, *sends = pl.pallas_call(
             functools.partial(main_kernel, section),
             out_shape=[plane_shape, sums_shape] + ([whole] if final else send_rows(0)),
-            in_specs=[VMEM] * 12,
-            out_specs=[VMEM] * 2 + ([HBM] if final else [VMEM] * 5),
+            in_specs=[VMEM] * 11,
+            out_specs=[VMEM] * 2 + ([HBM] if final else [VMEM] * 4),
             scratch_shapes=[pltpu.SemaphoreType.DMA((4,))] * final + scalars,
             input_output_aliases={1: 0, 2: 1},
             compiler_params=PARAMS,

time: 65.4 us -> 62.7 us (0.959)
  the two profiles are of different devices: /device:TPU:0 before, /device:TPU:1 now
where the time goes in v7:
time: 62.7 us; the launch traced here: 62.4 us
  starting transfers between devices  35 us (56%)
  Pallas kernels  25 us (40%)
  waiting for transfers between devices  2.22 us (4%)
    ppermute x18, starting transfers between devices, swap(): return lax.ppermute(value, BOTH, pairs)  35 us
    pallas_call x3, Pallas kernels, local(): pl.pallas_call(functools.partial(settled_kernel, section), out_shape=[pla...  13.2 us
    pallas_call x3, Pallas kernels, local(): pl.pallas_call(functools.partial(main_kernel, section), out_shape=[plane_...  4.75 us
    pallas_call x1, Pallas kernels, local(): pl.pallas_call(load_kernel, out_shape=[plane_shape, matrices_shape, whole...  3.32 us
    ppermute x18, waiting for transfers between devices, swap(): return lax.ppermute(value, BOTH, pairs)  2.22 us
  transfers between devices with their start and end apart: 18, of which 1 were waited for; matrix products, arithmetic and copies ran while one was open for 0% of the time, Pallas kernels for 31%

profile of v7, /device:TPU:1, one launch (start us, length us, event | category | flops | bytes accessed | tf_op | source)
XLA Modules:
  0.0 62.4 jit_solution(6494699198028442157)
XLA Ops:
  0.0 1.2 %pack.1 = (bf16[4,256,128]{2,1,0:T(8,128)(2,1)S(1)}, bf16[4,256,128]{2,1,0:T(8,128)(2,1)S(1)}, bf16[4,256,128]{2,1,0:T(8,128)(2,1)S(1)}, bf16[4,256,128]{2,1,0:T(8,128)(2,1)S(1)}) custom-call(bf16[4,4,256,128]{3,2,1,0:T(8,128)(2,1)} %earlier.1), custom_call_target="tpu_custom_call" | custom-call | tf_op jit(solution)/shard_map/pack/pallas_call | solution.py:462
  1.2 5.8 %collective-permute-start = (bf16[1024,128]{1,0:T(8,128)(2,1)S(1)}, bf16[1024,128]{1,0:T(8,128)(2,1)S(1)}, u32[]{:S(2)}, u32[]{:S(2)}) collective-permute-start(bf16[1024,128]{1,0:T(8,128)(2,1)S(1)} %bitcast.12), channel_id=1, source_target_pairs={{0,120},{1,121},{2,122},{3,123},{4,124},{5,125},{6,126},{7,127},{8... | collective-permute-start | bytes 786440 | tf_op jit(solution)/shard_map/ppermute | solution.py:45
  7.1 0.0 collective-permute-start.1
  7.1 2.5 %collective-permute-start.2 = (bf16[1024,128]{1,0:T(8,128)(2,1)S(1)}, bf16[1024,128]{1,0:T(8,128)(2,1)S(1)}, u32[]{:S(2)}, u32[]{:S(2)}) collective-permute-start(bf16[1024,128]{1,0:T(8,128)(2,1)S(1)} %bitcast.10), channel_id=1, source_target_pairs={{0,7},{1,2},{2,1},{3,4},{4,3},{5,6},{6,5},{7,0},{8,15},{9,10},{10,... | collective-permute-start | bytes 786440 | tf_op jit(solution)/shard_map/ppermute | solution.py:45
  9.5 1.7 %collective-permute-start.3 = (bf16[1024,128]{1,0:T(8,128)(2,1)S(1)}, bf16[1024,128]{1,0:T(8,128)(2,1)S(1)}, u32[]{:S(2)}, u32[]{:S(2)}) collective-permute-start(bf16[1024,128]{1,0:T(8,128)(2,1)S(1)} %bitcast.9), channel_id=1, source_target_pairs={{0,1},{1,0},{2,3},{3,2},{4,5},{5,4},{6,7},{7,6},{8,9},{9,8},{10,11... | collective-permute-start | bytes 786440 | tf_op jit(solution)/shard_map/ppermute | solution.py:45
  11.2 3.3 %load.1 = (bf16[73,256,128]{2,1,0:T(8,128)(2,1)S(1)}, bf16[16,1152,128]{2,1,0:T(8,128)(2,1)S(1)}, bf16[16,256,128]{2,1,0:T(8,128)(2,1)S(1)}, f32[16,256,128]{2,1...) custom-call(s32[4,4]{1,0:T(4,128)} %block_level.1, ...), custom_call_target="tpu_custom_call" | custom-call | bytes 10485760 | tf_op jit(solution)/shard_map/load/pallas_call | solution.py:473
  14.6 0.0 collective-permute-done.1.halo
  14.7 0.0 collective-permute-done.2.rest_0_
  14.7 0.0 collective-permute-done.3.rest_1_
  14.7 1.1 %level_0.1 = (bf16[73,256,128]{2,1,0:T(8,128)(2,1)S(1)}, f32[16,256,128]{2,1,0:T(8,128)S(1)}, bf16[16,1152,128]{2,1,0:T(8,128)(2,1)S(1)}, bf16[16,256,128]{2,1,0...) custom-call(s32[238]{0:T(256)S(1)} %get-tuple-element.57.table_in, ...), custom_call_target="tpu_custom_call", output_to_operand_aliasing={{0}: (1, {}), {1}: (2, {}), {2}: (3, {}), {3}: (4, {})} | custom-call | flops 603979776 | bytes 4194304 | tf_op jit(solution)/shard_map/level_0/pallas_call | solution.py:499
  15.8 3.5 %collective-permute-start.4 = (bf16[1312,128]{1,0:T(8,128)(2,1)S(1)}, bf16[1312,128]{1,0:T(8,128)(2,1)S(1)}, u32[]{:S(2)}, u32[]{:S(2)}) collective-permute-start(bf16[1312,128]{1,0:T(8,128)(2,1)S(1)} %get-tuple-element.73), channel_id=1, source_target_pairs={{0,120},{1,121},{2,122},{3,123},{4,124},{5,125},{6,126},{7,127},{8... | collective-permute-start | bytes 1007624 | tf_op jit(solution)/shard_map/ppermute | solution.py:45
  19.4 0.0 collective-permute-start.5
  19.4 4.3 %collective-permute-start.6 = (bf16[1824,128]{1,0:T(8,128)(2,1)S(1)}, bf16[1824,128]{1,0:T(8,128)(2,1)S(1)}, u32[]{:S(2)}, u32[]{:S(2)}) collective-permute-start(bf16[1824,128]{1,0:T(8,128)(2,1)S(1)} %get-tuple-element.77), channel_id=1, source_target_pairs={{0,7},{1,2},{2,1},{3,4},{4,3},{5,6},{6,5},{7,0},{8,15},{9,10},{10,... | collective-permute-start | bytes 1400840 | tf_op jit(solution)/shard_map/ppermute | solution.py:45
  23.7 0.8 %collective-permute-start.7 = (bf16[1824,128]{1,0:T(8,128)(2,1)S(1)}, bf16[1824,128]{1,0:T(8,128)(2,1)S(1)}, u32[]{:S(2)}, u32[]{:S(2)}) collective-permute-start(bf16[1824,128]{1,0:T(8,128)(2,1)S(1)} %get-tuple-element.78), channel_id=1, source_target_pairs={{0,1},{1,0},{2,3},{3,2},{4,5},{5,4},{6,7},{7,6},{8,9},{9,8},{10,11... | collective-permute-start | bytes 1400840 | tf_op jit(solution)/shard_map/ppermute | solution.py:45
  24.5 3.4 %settled_1.1 = (bf16[73,256,128]{2,1,0:T(8,128)(2,1)S(1)}, f32[16,256,128]{2,1,0:T(8,128)S(1)}, bf16[16,1152,128]{2,1,0:T(8,128)(2,1)S(1)}, bf16[16,256,128]{2,1,0:T(8,128)(2,1)S(1)}, s32[238]{0:T(256)S(1)}) custom-call(s32[4,4,8]{2,1,0:T(4,128)S(1)} %get-tuple-element.56.codes, ...), custom_call_target="tpu_custom_call", output_to_operand_aliasing={{0}: (2, {}), {1}: (3, {}), {2}: (4, {}), {3}: (5, {})} | custom-call | flops 603979776 | bytes 4194304 | tf_op jit(solution)/shard_map/settled_1/pallas_call | solution.py:515
  28.0 2.2 %collective-permute-done.6.ty_out.rest_2_ = bf16[1824,128]{1,0:T(8,128)(2,1)S(1)} collective-permute-done((bf16[1824,128]{1,0:T(8,128)(2,1)S(1)}, bf16[1824,128]{1,0:T(8,128)(2,1)S(1)}, u32[]{:S(2)}, u32[]{:S(2)}) %collective-permute-start.6) | collective-permute-done | bytes 466976 | tf_op jit(solution)/shard_map/ppermute | solution.py:45
  30.2 1.0 %level_1.1 = (bf16[73,256,128]{2,1,0:T(8,128)(2,1)S(1)}, f32[16,256,128]{2,1,0:T(8,128)S(1)}, bf16[1024,128]{1,0:T(8,128)(2,1)S(1)}, bf16[1024,128]{1,0:T(8,128)...) custom-call(s32[238]{0:T(256)S(1)} %get-tuple-element.71.table_in, ...), custom_call_target="tpu_custom_call", output_to_operand_aliasing={{0}: (1, {}), {1}: (2, {})} | custom-call | flops 134217728 | bytes 4194304 | tf_op jit(solution)/shard_map/level_1/pallas_call | solution.py:542
  31.2 1.3 %collective-permute-start.8 = (bf16[1024,128]{1,0:T(8,128)(2,1)S(1)}, bf16[1024,128]{1,0:T(8,128)(2,1)S(1)}, u32[]{:S(2)}, u32[]{:S(2)}) collective-permute-start(bf16[1024,128]{1,0:T(8,128)(2,1)S(1)} %get-tuple-element.84), channel_id=1, source_target_pairs={{0,120},{1,121},{2,122},{3,123},{4,124},{5,125},{6,126},{7,127},{8... | collective-permute-start | bytes 786440 | tf_op jit(solution)/shard_map/ppermute | solution.py:45
  32.6 0.4 collective-permute-start.9
  33.0 4.2 %collective-permute-start.10 = (bf16[1536,128]{1,0:T(8,128)(2,1)S(1)}, bf16[1536,128]{1,0:T(8,128)(2,1)S(1)}, u32[]{:S(2)}, u32[]{:S(2)}) collective-permute-start(bf16[1536,128]{1,0:T(8,128)(2,1)S(1)} %get-tuple-element.88), channel_id=1, source_target_pairs={{0,7},{1,2},{2,1},{3,4},{4,3},{5,6},{6,5},{7,0},{8,15},{9,10},{10,... | collective-permute-start | bytes 1179656 | tf_op jit(solution)/shard_map/ppermute | solution.py:45
  37.1 1.6 %collective-permute-start.11 = (bf16[1536,128]{1,0:T(8,128)(2,1)S(1)}, bf16[1536,128]{1,0:T(8,128)(2,1)S(1)}, u32[]{:S(2)}, u32[]{:S(2)}) collective-permute-start(bf16[1536,128]{1,0:T(8,128)(2,1)S(1)} %get-tuple-element.89), channel_id=1, source_target_pairs={{0,1},{1,0},{2,3},{3,2},{4,5},{5,4},{6,7},{7,6},{8,9},{9,8},{10,11... | collective-permute-start | bytes 1179656 | tf_op jit(solution)/shard_map/ppermute | solution.py:45
  38.7 4.4 %settled_2.1 = (bf16[73,256,128]{2,1,0:T(8,128)(2,1)S(1)}, f32[16,256,128]{2,1,0:T(8,128)S(1)}, bf16[16,1152,128]{2,1,0:T(8,128)(2,1)S(1)}, bf16[16,256,128]{2,1,0:T(8,128)(2,1)S(1)}, s32[238]{0:T(256)S(1)}) custom-call(s32[4,4,8]{2,1,0:T(4,128)S(1)} %get-tuple-element.56.codes, ...), custom_call_target="tpu_custom_call", output_to_operand_aliasing={{0}: (2, {}), {1}: (3, {}), {2}: (4, {}), {3}: (5, {})} | custom-call | flops 603979776 | bytes 4194304 | tf_op jit(solution)/shard_map/settled_2/pallas_call | solution.py:515
  43.3 1.3 %level_2.1 = (bf16[73,256,128]{2,1,0:T(8,128)(2,1)S(1)}, f32[16,256,128]{2,1,0:T(8,128)S(1)}, bf16[1024,128]{1,0:T(8,128)(2,1)S(1)}, bf16[1024,128]{1,0:T(8,128)...) custom-call(s32[238]{0:T(256)S(1)} %get-tuple-element.82.table_in, ...), custom_call_target="tpu_custom_call", output_to_operand_aliasing={{0}: (1, {}), {1}: (2, {})} | custom-call | flops 134217728 | bytes 4194304 | tf_op jit(solution)/shard_map/level_2/pallas_call | solution.py:542
  44.5 0.1 collective-permute-start.12
  44.6 2.5 %collective-permute-start.13 = (bf16[1024,128]{1,0:T(8,128)(2,1)S(1)}, bf16[1024,128]{1,0:T(8,128)(2,1)S(1)}, u32[]{:S(2)}, u32[]{:S(2)}) collective-permute-start(bf16[1024,128]{1,0:T(8,128)(2,1)S(1)} %get-tuple-element.96), channel_id=1, source_target_pairs={{0,8},{1,9},{2,10},{3,11},{4,12},{5,13},{6,14},{7,15},{8,0},{9,1},... | collective-permute-start | bytes 786440 | tf_op jit(solution)/shard_map/ppermute | solution.py:45
  47.2 0.8 %collective-permute-start.14 = (bf16[1536,128]{1,0:T(8,128)(2,1)S(1)}, bf16[1536,128]{1,0:T(8,128)(2,1)S(1)}, u32[]{:S(2)}, u32[]{:S(2)}) collective-permute-start(bf16[1536,128]{1,0:T(8,128)(2,1)S(1)} %get-tuple-element.99), channel_id=1, source_target_pairs={{0,7},{1,2},{2,1},{3,4},{4,3},{5,6},{6,5},{7,0},{8,15},{9,10},{10,... | collective-permute-start | bytes 1179656 | tf_op jit(solution)/shard_map/ppermute | solution.py:45
  48.0 2.4 %collective-permute-start.15 = (bf16[1536,128]{1,0:T(8,128)(2,1)S(1)}, bf16[1536,128]{1,0:T(8,128)(2,1)S(1)}, u32[]{:S(2)}, u32[]{:S(2)}) collective-permute-start(bf16[1536,128]{1,0:T(8,128)(2,1)S(1)} %get-tuple-element.100), channel_id=1, source_target_pairs={{0,1},{1,0},{2,3},{3,2},{4,5},{5,4},{6,7},{7,6},{8,9},{9,8},{10,11... | collective-permute-start | bytes 1179656 | tf_op jit(solution)/shard_map/ppermute | solution.py:45
  50.5 5.4 %settled_3.1 = (bf16[73,256,128]{2,1,0:T(8,128)(2,1)S(1)}, f32[16,256,128]{2,1,0:T(8,128)S(1)}, bf16[16,1152,128]{2,1,0:T(8,128)(2,1)S(1)}, bf16[16,256,128]{2,1,0:T(8,128)(2,1)S(1)}, s32[238]{0:T(256)S(1)}) custom-call(s32[4,4,8]{2,1,0:T(4,128)S(1)} %get-tuple-element.56.codes, ...), custom_call_target="tpu_custom_call", output_to_operand_aliasing={{0}: (2, {}), {1}: (3, {}), {2}: (4, {}), {3}: (5, {})} | custom-call | flops 603979776 | bytes 4194304 | tf_op jit(solution)/shard_map/settled_3/pallas_call | solution.py:515
  56.0 0.8 %collective-permute-start.16 = (bf16[512,128]{1,0:T(8,128)(2,1)S(1)}, bf16[512,128]{1,0:T(8,128)(2,1)S(1)}, u32[]{:S(2)}, u32[]{:S(2)}) collective-permute-start(bf16[512,128]{1,0:T(8,128)(2,1)S(1)} %get-tuple-element.103), channel_id=1, source_target_pairs={{0,7},{1,2},{2,1},{3,4},{4,3},{5,6},{6,5},{7,0},{8,15},{9,10},{10,... | collective-permute-start | bytes 393224 | tf_op jit(solution)/shard_map/ppermute | solution.py:45
  56.8 2.2 %collective-permute-start.17 = (bf16[512,128]{1,0:T(8,128)(2,1)S(1)}, bf16[512,128]{1,0:T(8,128)(2,1)S(1)}, u32[]{:S(2)}, u32[]{:S(2)}) collective-permute-start(bf16[512,128]{1,0:T(8,128)(2,1)S(1)} %get-tuple-element.104), channel_id=1, source_target_pairs={{0,1},{1,0},{2,3},{3,2},{4,5},{5,4},{6,7},{7,6},{8,9},{9,8},{10,11... | collective-permute-start | bytes 393224 | tf_op jit(solution)/shard_map/ppermute | solution.py:45
  59.0 2.5 %level_3.1 = (bf16[73,256,128]{2,1,0:T(8,128)(2,1)S(1)}, f32[16,256,128]{2,1,0:T(8,128)S(1)}, bf16[16,256,128]{2,1,0:T(8,128)(2,1)}) custom-call(s32[238]{0:T(256)S(1)} %get-tuple-element.93.table_in, bf16[73,256,128]{2,1,0:T(8,128)(2,1)S(1)} %rows_3_in.1.plane_in.plane, ...), custom_call_target="tpu_custom_call", output_to_operand_aliasing={{0}: (1, {}), {1}: (2, {})} | custom-call | flops 134217728 | bytes 4194304 | tf_op jit(solution)/shard_map/level_3/pallas_call | solution.py:542
  61.5 1.0 %last_corners.1 = (bf16[73,256,128]{2,1,0:T(8,128)(2,1)S(1)}, bf16[16,256,128]{2,1,0:T(8,128)(2,1)}) custom-call(bf16[73,256,128]{2,1,0:T(8,128)(2,1)S(1)} %get-tuple-element.101.plane_in, bf16[4,288,128]{2,1,0:T(8,128)(2,1)S(1)} %get-tuple-element.66.rest_2_.own, ...), custom_call_target="tpu_custom_call", output_to_operand_aliasing={{0}: (0, {}), {1}: (5, {})} | custom-call | flops 33554432 | bytes 4194304 | tf_op jit(solution)/shard_map/last_corners/pallas_call | solution.py:553
  (23 shorter events, 0.4 us)
Async XLA Ops:
  1.2 13.3 %collective-permute-start = (bf16[1024,128]{1,0:T(8,128)(2,1)S(1)}, bf16[1024,128]{1,0:T(8,128)(2,1)S(1)}, u32[]{:S(2)}, u32[]{:S(2)}) collective-permute-start(bf16[1024,128]{1,0:T(8,128)(2,1)S(1)} %bitcast.12), channel_id=1, source_target_pairs={{0,120},{1,121},{2,122},{3,123},{4,124},{5,125},{6,126},{7,127},{8... | collective-permute-start | bytes 786440 | tf_op jit(solution)/shard_map/ppermute | solution.py:45
  7.1 7.6 %collective-permute-start.1 = (bf16[1024,128]{1,0:T(8,128)(2,1)S(1)}, bf16[1024,128]{1,0:T(8,128)(2,1)S(1)}, u32[]{:S(2)}, u32[]{:S(2)}) collective-permute-start(bf16[1024,128]{1,0:T(8,128)(2,1)S(1)} %bitcast.11), channel_id=1, source_target_pairs={{0,8},{1,9},{2,10},{3,11},{4,12},{5,13},{6,14},{7,15},{8,0},{9,1},... | collective-permute-start | bytes 786440 | tf_op jit(solution)/shard_map/ppermute | solution.py:45
  7.1 7.6 %collective-permute-start.2 = (bf16[1024,128]{1,0:T(8,128)(2,1)S(1)}, bf16[1024,128]{1,0:T(8,128)(2,1)S(1)}, u32[]{:S(2)}, u32[]{:S(2)}) collective-permute-start(bf16[1024,128]{1,0:T(8,128)(2,1)S(1)} %bitcast.10), channel_id=1, source_target_pairs={{0,7},{1,2},{2,1},{3,4},{4,3},{5,6},{6,5},{7,0},{8,15},{9,10},{10,... | collective-permute-start | bytes 786440 | tf_op jit(solution)/shard_map/ppermute | solution.py:45
  9.5 5.1 %collective-permute-start.3 = (bf16[1024,128]{1,0:T(8,128)(2,1)S(1)}, bf16[1024,128]{1,0:T(8,128)(2,1)S(1)}, u32[]{:S(2)}, u32[]{:S(2)}) collective-permute-start(bf16[1024,128]{1,0:T(8,128)(2,1)S(1)} %bitcast.9), channel_id=1, source_target_pairs={{0,1},{1,0},{2,3},{3,2},{4,5},{5,4},{6,7},{7,6},{8,9},{9,8},{10,11... | collective-permute-start | bytes 786440 | tf_op jit(solution)/shard_map/ppermute | solution.py:45
  15.8 12.1 %collective-permute-start.4 = (bf16[1312,128]{1,0:T(8,128)(2,1)S(1)}, bf16[1312,128]{1,0:T(8,128)(2,1)S(1)}, u32[]{:S(2)}, u32[]{:S(2)}) collective-permute-start(bf16[1312,128]{1,0:T(8,128)(2,1)S(1)} %get-tuple-element.73), channel_id=1, source_target_pairs={{0,120},{1,121},{2,122},{3,123},{4,124},{5,125},{6,126},{7,127},{8... | collective-permute-start | bytes 1007624 | tf_op jit(solution)/shard_map/ppermute | solution.py:45
  19.4 8.6 %collective-permute-start.5 = (bf16[1312,128]{1,0:T(8,128)(2,1)S(1)}, bf16[1312,128]{1,0:T(8,128)(2,1)S(1)}, u32[]{:S(2)}, u32[]{:S(2)}) collective-permute-start(bf16[1312,128]{1,0:T(8,128)(2,1)S(1)} %get-tuple-element.74), channel_id=1, source_target_pairs={{0,8},{1,9},{2,10},{3,11},{4,12},{5,13},{6,14},{7,15},{8,0},{9,1},... | collective-permute-start | bytes 1007624 | tf_op jit(solution)/shard_map/ppermute | solution.py:45
  19.4 10.8 %collective-permute-start.6 = (bf16[1824,128]{1,0:T(8,128)(2,1)S(1)}, bf16[1824,128]{1,0:T(8,128)(2,1)S(1)}, u32[]{:S(2)}, u32[]{:S(2)}) collective-permute-start(bf16[1824,128]{1,0:T(8,128)(2,1)S(1)} %get-tuple-element.77), channel_id=1, source_target_pairs={{0,7},{1,2},{2,1},{3,4},{4,3},{5,6},{6,5},{7,0},{8,15},{9,10},{10,... | collective-permute-start | bytes 1400840 | tf_op jit(solution)/shard_map/ppermute | solution.py:45
  23.7 6.5 %collective-permute-start.7 = (bf16[1824,128]{1,0:T(8,128)(2,1)S(1)}, bf16[1824,128]{1,0:T(8,128)(2,1)S(1)}, u32[]{:S(2)}, u32[]{:S(2)}) collective-permute-start(bf16[1824,128]{1,0:T(8,128)(2,1)S(1)} %get-tuple-element.78), channel_id=1, source_target_pairs={{0,1},{1,0},{2,3},{3,2},{4,5},{5,4},{6,7},{7,6},{8,9},{9,8},{10,11... | collective-permute-start | bytes 1400840 | tf_op jit(solution)/shard_map/ppermute | solution.py:45
  31.2 11.9 %collective-permute-start.8 = (bf16[1024,128]{1,0:T(8,128)(2,1)S(1)}, bf16[1024,128]{1,0:T(8,128)(2,1)S(1)}, u32[]{:S(2)}, u32[]{:S(2)}) collective-permute-start(bf16[1024,128]{1,0:T(8,128)(2,1)S(1)} %get-tuple-element.84), channel_id=1, source_target_pairs={{0,120},{1,121},{2,122},{3,123},{4,124},{5,125},{6,126},{7,127},{8... | collective-permute-start | bytes 786440 | tf_op jit(solution)/shard_map/ppermute | solution.py:45
  32.6 10.6 %collective-permute-start.9 = (bf16[1024,128]{1,0:T(8,128)(2,1)S(1)}, bf16[1024,128]{1,0:T(8,128)(2,1)S(1)}, u32[]{:S(2)}, u32[]{:S(2)}) collective-permute-start(bf16[1024,128]{1,0:T(8,128)(2,1)S(1)} %get-tuple-element.85), channel_id=1, source_target_pairs={{0,8},{1,9},{2,10},{3,11},{4,12},{5,13},{6,14},{7,15},{8,0},{9,1},... | collective-permute-start | bytes 786440 | tf_op jit(solution)/shard_map/ppermute | solution.py:45
  33.0 10.3 %collective-permute-start.10 = (bf16[1536,128]{1,0:T(8,128)(2,1)S(1)}, bf16[1536,128]{1,0:T(8,128)(2,1)S(1)}, u32[]{:S(2)}, u32[]{:S(2)}) collective-permute-start(bf16[1536,128]{1,0:T(8,128)(2,1)S(1)} %get-tuple-element.88), channel_id=1, source_target_pairs={{0,7},{1,2},{2,1},{3,4},{4,3},{5,6},{6,5},{7,0},{8,15},{9,10},{10,... | collective-permute-start | bytes 1179656 | tf_op jit(solution)/shard_map/ppermute | solution.py:45
  37.1 6.1 %collective-permute-start.11 = (bf16[1536,128]{1,0:T(8,128)(2,1)S(1)}, bf16[1536,128]{1,0:T(8,128)(2,1)S(1)}, u32[]{:S(2)}, u32[]{:S(2)}) collective-permute-start(bf16[1536,128]{1,0:T(8,128)(2,1)S(1)} %get-tuple-element.89), channel_id=1, source_target_pairs={{0,1},{1,0},{2,3},{3,2},{4,5},{5,4},{6,7},{7,6},{8,9},{9,8},{10,11... | collective-permute-start | bytes 1179656 | tf_op jit(solution)/shard_map/ppermute | solution.py:45
  44.5 11.3 %collective-permute-start.12 = (bf16[1024,128]{1,0:T(8,128)(2,1)S(1)}, bf16[1024,128]{1,0:T(8,128)(2,1)S(1)}, u32[]{:S(2)}, u32[]{:S(2)}) collective-permute-start(bf16[1024,128]{1,0:T(8,128)(2,1)S(1)} %get-tuple-element.95), channel_id=1, source_target_pairs={{0,120},{1,121},{2,122},{3,123},{4,124},{5,125},{6,126},{7,127},{8... | collective-permute-start | bytes 786440 | tf_op jit(solution)/shard_map/ppermute | solution.py:45
  44.6 11.3 %collective-permute-start.13 = (bf16[1024,128]{1,0:T(8,128)(2,1)S(1)}, bf16[1024,128]{1,0:T(8,128)(2,1)S(1)}, u32[]{:S(2)}, u32[]{:S(2)}) collective-permute-start(bf16[1024,128]{1,0:T(8,128)(2,1)S(1)} %get-tuple-element.96), channel_id=1, source_target_pairs={{0,8},{1,9},{2,10},{3,11},{4,12},{5,13},{6,14},{7,15},{8,0},{9,1},... | collective-permute-start | bytes 786440 | tf_op jit(solution)/shard_map/ppermute | solution.py:45
  47.2 11.8 %collective-permute-start.14 = (bf16[1536,128]{1,0:T(8,128)(2,1)S(1)}, bf16[1536,128]{1,0:T(8,128)(2,1)S(1)}, u32[]{:S(2)}, u32[]{:S(2)}) collective-permute-start(bf16[1536,128]{1,0:T(8,128)(2,1)S(1)} %get-tuple-element.99), channel_id=1, source_target_pairs={{0,7},{1,2},{2,1},{3,4},{4,3},{5,6},{6,5},{7,0},{8,15},{9,10},{10,... | collective-permute-start | bytes 1179656 | tf_op jit(solution)/shard_map/ppermute | solution.py:45
  48.0 10.9 %collective-permute-start.15 = (bf16[1536,128]{1,0:T(8,128)(2,1)S(1)}, bf16[1536,128]{1,0:T(8,128)(2,1)S(1)}, u32[]{:S(2)}, u32[]{:S(2)}) collective-permute-start(bf16[1536,128]{1,0:T(8,128)(2,1)S(1)} %get-tuple-element.100), channel_id=1, source_target_pairs={{0,1},{1,0},{2,3},{3,2},{4,5},{5,4},{6,7},{7,6},{8,9},{9,8},{10,11... | collective-permute-start | bytes 1179656 | tf_op jit(solution)/shard_map/ppermute | solution.py:45
  56.0 5.5 %collective-permute-start.16 = (bf16[512,128]{1,0:T(8,128)(2,1)S(1)}, bf16[512,128]{1,0:T(8,128)(2,1)S(1)}, u32[]{:S(2)}, u32[]{:S(2)}) collective-permute-start(bf16[512,128]{1,0:T(8,128)(2,1)S(1)} %get-tuple-element.103), channel_id=1, source_target_pairs={{0,7},{1,2},{2,1},{3,4},{4,3},{5,6},{6,5},{7,0},{8,15},{9,10},{10,... | collective-permute-start | bytes 393224 | tf_op jit(solution)/shard_map/ppermute | solution.py:45
  56.8 4.7 %collective-permute-start.17 = (bf16[512,128]{1,0:T(8,128)(2,1)S(1)}, bf16[512,128]{1,0:T(8,128)(2,1)S(1)}, u32[]{:S(2)}, u32[]{:S(2)}) collective-permute-start(bf16[512,128]{1,0:T(8,128)(2,1)S(1)} %get-tuple-element.104), channel_id=1, source_target_pairs={{0,1},{1,0},{2,3},{3,2},{4,5},{5,4},{6,7},{7,6},{8,9},{9,8},{10,11... | collective-permute-start | bytes 393224 | tf_op jit(solution)/shard_map/ppermute | solution.py:45

commit v8 on v7

--- a/solution.py
+++ b/solution.py
@@ -116,6 +116,17 @@
             settled[8 * cell + k] = jnp.where(open_, BLANK, slot)
 
 
+def cells_of(section, table, body):
+    def one_cell(cell, carry):
+        @pl.when(table[LEVEL + cell] == section)
+        def _():
+            body(cell)
+
+        return carry
+
+    lax.fori_loop(0, SIDE * SIDE, one_cell, 0)
+
+
 def choose(section, levels, table):
     def one_cell(cell, at):
         table[CELLS + at] = cell
@@ -132,15 +143,15 @@
     lax.fori_loop(0, table[CHOSEN], one_cell, 0)
 
 
-def each_pair(table, body):
+def each_group(table, body):
     count = table[CHOSEN]
 
-    def one_pair(pair, carry):
-        second = jnp.minimum(2 * pair + 1, count - 1)
-        body(table[CELLS + 2 * pair], table[CELLS + second], 2 * pair + 1 < count)
+    def one_group(group, carry):
+        first = group * GROUP
+        body([table[CELLS + jnp.minimum(first + i, count - 1)] for i in range(GROUP)], count - first)
         return carry
 
-    lax.fori_loop(0, (count + 1) // 2, one_pair, 0)
+    lax.fori_loop(0, (count + GROUP - 1) // GROUP, one_group, 0)
 
 
 def cell_copies(cell, sources, targets, sems):
@@ -282,7 +293,10 @@
     plane, sums, matrices, noise, table, settled, factors, sems = rest
     targets = noise, matrices, factors
     choose(section, table_in, table)
-    each_cell(table, lambda cell: start_cell(cell, sources, targets, sems))
+    if section == 1:
+        each_cell(table, lambda cell: start_cell(cell, sources, targets, sems))
+    if section + 1 < LEVELS:
+        cells_of(section + 1, table_in, lambda cell: start_cell(cell, sources, targets, sems))
 
     def one_cell(at, found):
         cell = table[CELLS + at]
@@ -294,18 +308,21 @@
 
     table[COUNT] = lax.fori_loop(0, table[CHOSEN], one_cell, jnp.int32(0))
 
-    def products(first, second, fresh):
-        finish_cell(first, sources, targets, sems)
-
-        @pl.when(fresh)
-        def _():
-            finish_cell(second, sources, targets, sems)
-
-        both = [gather_product(cell, settled, 0, plane, matrices, noise) for cell in (first, second)]
-        sums[first] = both[0]
-        sums[second] = both[1]
-
-    each_pair(table, products)
+    def products(cells, fresh):
+        if section == 1:
+            for i, cell in enumerate(cells):
+
+                @pl.when(i < fresh)
+                def _(cell=cell):
+                    finish_cell(cell, sources, targets, sems)
+
+        results = [gather_product(cell, settled, 0, plane, matrices, noise) for cell in cells]
+        for cell, summed in zip(cells, results, strict=True):
+            sums[cell] = summed
+
+    each_group(table, products)
+    if section + 1 < LEVELS:
+        cells_of(section + 1, table_in, lambda cell: finish_cell(cell, sources, targets, sems))
 
 
 def rows_kernel(base, outward, plane_in, halo, plane):
@@ -367,14 +384,13 @@
         ref[ref.shape[0] - EXTRA :] = extras[at]
     wait()
 
-    def products(first, second, fresh):
-        cells = first, second
-        both = [gather_product(cell, table, SLOT, plane, matrices, noise) for cell in cells]
-        for cell, summed in zip(cells, both, strict=True):
+    def products(cells, fresh):
+        results = [gather_product(cell, table, SLOT, plane, matrices, noise) for cell in cells]
+        for cell, summed in zip(cells, results, strict=True):
             sums[cell] = summed
             plane[own_slot(cell // SIDE, cell % SIDE)] = summed.astype(jnp.bfloat16)
 
-    each_pair(table, products)
+    each_group(table, products)
     pack_sends(0, plane, sends)
 
 

time: 62.7 us -> 60.9 us (0.971)
  the two profiles are of different devices: /device:TPU:1 before, /device:TPU:0 now
where the time goes in v8:
time: 60.9 us; the launch traced here: 59.7 us
  starting transfers between devices  25.5 us (42%)
  Pallas kernels  22.9 us (38%)
  waiting for transfers between devices  11.1 us (18%)
    ppermute x18, starting transfers between devices, swap(): return lax.ppermute(value, BOTH, pairs)  25.5 us
    ppermute x18, waiting for transfers between devices, swap(): return lax.ppermute(value, BOTH, pairs)  11.1 us
    pallas_call x3, Pallas kernels, local(): pl.pallas_call(functools.partial(settled_kernel, section), out_shape=[pla...  10.7 us
    pallas_call x1, Pallas kernels, local(): pl.pallas_call(load_kernel, out_shape=[plane_shape, matrices_shape, whole...  4.08 us
    pallas_call x3, Pallas kernels, local(): pl.pallas_call(functools.partial(main_kernel, section), out_shape=[plane_...  4.02 us
    pallas_call x1, Pallas kernels, local(): pl.pallas_call(first_kernel, out_shape=[plane_shape, sums_shape, matrices...  2.31 us
    pallas_call x1, Pallas kernels, local(): pl.pallas_call(pack_kernel, out_shape=[edge] * 4, in_specs=[HBM], out_spe...  1.22 us
  transfers between devices with their start and end apart: 18, of which 7 were waited for; matrix products, arithmetic and copies ran while one was open for 0% of the time, Pallas kernels for 29%

profile of v8, /device:TPU:0, one launch (start us, length us, event | category | flops | bytes accessed | tf_op | source)
XLA Modules:
  0.0 59.7 jit_solution(330310021661025088)
XLA Ops:
  0.0 1.2 %pack.1 = (bf16[4,256,128]{2,1,0:T(8,128)(2,1)S(1)}, bf16[4,256,128]{2,1,0:T(8,128)(2,1)S(1)}, bf16[4,256,128]{2,1,0:T(8,128)(2,1)S(1)}, bf16[4,256,128]{2,1,0:T(8,128)(2,1)S(1)}) custom-call(bf16[4,4,256,128]{3,2,1,0:T(8,128)(2,1)} %earlier.1), custom_call_target="tpu_custom_call" | custom-call | tf_op jit(solution)/shard_map/pack/pallas_call | solution.py:478
  1.2 5.4 %collective-permute-start = (bf16[1024,128]{1,0:T(8,128)(2,1)S(1)}, bf16[1024,128]{1,0:T(8,128)(2,1)S(1)}, u32[]{:S(2)}, u32[]{:S(2)}) collective-permute-start(bf16[1024,128]{1,0:T(8,128)(2,1)S(1)} %bitcast.12), channel_id=1, source_target_pairs={{0,120},{1,121},{2,122},{3,123},{4,124},{5,125},{6,126},{7,127},{8... | collective-permute-start | bytes 786440 | tf_op jit(solution)/shard_map/ppermute | solution.py:45
  6.6 0.0 collective-permute-start.1
  6.6 3.2 %collective-permute-start.2 = (bf16[1024,128]{1,0:T(8,128)(2,1)S(1)}, bf16[1024,128]{1,0:T(8,128)(2,1)S(1)}, u32[]{:S(2)}, u32[]{:S(2)}) collective-permute-start(bf16[1024,128]{1,0:T(8,128)(2,1)S(1)} %bitcast.10), channel_id=1, source_target_pairs={{0,7},{1,2},{2,1},{3,4},{4,3},{5,6},{6,5},{7,0},{8,15},{9,10},{10,... | collective-permute-start | bytes 786440 | tf_op jit(solution)/shard_map/ppermute | solution.py:45
  9.8 0.0 collective-permute-start.3
  9.8 4.1 %load.1 = (bf16[73,256,128]{2,1,0:T(8,128)(2,1)S(1)}, bf16[16,1152,128]{2,1,0:T(8,128)(2,1)S(1)}, bf16[16,256,128]{2,1,0:T(8,128)(2,1)S(1)}, f32[16,256,128]{2,1...) custom-call(s32[4,4]{1,0:T(4,128)} %block_level.1, ...), custom_call_target="tpu_custom_call" | custom-call | bytes 10485760 | tf_op jit(solution)/shard_map/load/pallas_call | solution.py:489
  13.9 0.0 collective-permute-done.halo
  14.0 0.4 collective-permute-done.1.halo
  14.4 2.3 %level_0.1 = (bf16[73,256,128]{2,1,0:T(8,128)(2,1)S(1)}, f32[16,256,128]{2,1,0:T(8,128)S(1)}, bf16[16,1152,128]{2,1,0:T(8,128)(2,1)S(1)}, bf16[16,256,128]{2,1,0...) custom-call(s32[238]{0:T(256)S(1)} %get-tuple-element.57.table_in, ...), custom_call_target="tpu_custom_call", output_to_operand_aliasing={{0}: (1, {}), {1}: (2, {}), {2}: (3, {}), {3}: (4, {})} | custom-call | flops 603979776 | bytes 4194304 | tf_op jit(solution)/shard_map/level_0/pallas_call | solution.py:515
  16.8 2.9 %collective-permute-start.4 = (bf16[1312,128]{1,0:T(8,128)(2,1)S(1)}, bf16[1312,128]{1,0:T(8,128)(2,1)S(1)}, u32[]{:S(2)}, u32[]{:S(2)}) collective-permute-start(bf16[1312,128]{1,0:T(8,128)(2,1)S(1)} %get-tuple-element.73), channel_id=1, source_target_pairs={{0,120},{1,121},{2,122},{3,123},{4,124},{5,125},{6,126},{7,127},{8... | collective-permute-start | bytes 1007624 | tf_op jit(solution)/shard_map/ppermute | solution.py:45
  19.7 2.3 %collective-permute-start.6 = (bf16[1824,128]{1,0:T(8,128)(2,1)S(1)}, bf16[1824,128]{1,0:T(8,128)(2,1)S(1)}, u32[]{:S(2)}, u32[]{:S(2)}) collective-permute-start(bf16[1824,128]{1,0:T(8,128)(2,1)S(1)} %get-tuple-element.77), channel_id=1, source_target_pairs={{0,7},{1,2},{2,1},{3,4},{4,3},{5,6},{6,5},{7,0},{8,15},{9,10},{10,... | collective-permute-start | bytes 1400840 | tf_op jit(solution)/shard_map/ppermute | solution.py:45
  22.0 4.2 %settled_1.1 = (bf16[73,256,128]{2,1,0:T(8,128)(2,1)S(1)}, f32[16,256,128]{2,1,0:T(8,128)S(1)}, bf16[16,1152,128]{2,1,0:T(8,128)(2,1)S(1)}, bf16[16,256,128]{2,1,0:T(8,128)(2,1)S(1)}, s32[238]{0:T(256)S(1)}) custom-call(s32[4,4,8]{2,1,0:T(4,128)S(1)} %get-tuple-element.56.codes, ...), custom_call_target="tpu_custom_call", output_to_operand_aliasing={{0}: (2, {}), {1}: (3, {}), {2}: (4, {}), {3}: (5, {})} | custom-call | flops 603979776 | bytes 4194304 | tf_op jit(solution)/shard_map/settled_1/pallas_call | solution.py:531
  26.2 2.3 %collective-permute-done.4.halo.rest_0_ = bf16[1312,128]{1,0:T(8,128)(2,1)S(1)} collective-permute-done((bf16[1312,128]{1,0:T(8,128)(2,1)S(1)}, bf16[1312,128]{1,0:T(8,128)(2,1)S(1)}, u32[]{:S(2)}, u32[]{:S(2)}) %collective-permute-start.4) | collective-permute-done | bytes 335904 | tf_op jit(solution)/shard_map/ppermute | solution.py:45
  28.5 0.4 collective-permute-done.5.halo.rest_1_
  29.0 1.2 %level_1.1 = (bf16[73,256,128]{2,1,0:T(8,128)(2,1)S(1)}, f32[16,256,128]{2,1,0:T(8,128)S(1)}, bf16[1024,128]{1,0:T(8,128)(2,1)S(1)}, bf16[1024,128]{1,0:T(8,128)...) custom-call(s32[238]{0:T(256)S(1)} %get-tuple-element.71.table_in, ...), custom_call_target="tpu_custom_call", output_to_operand_aliasing={{0}: (1, {}), {1}: (2, {})} | custom-call | flops 134217728 | bytes 4194304 | tf_op jit(solution)/shard_map/level_1/pallas_call | solution.py:558
  30.2 4.0 %collective-permute-start.8 = (bf16[1024,128]{1,0:T(8,128)(2,1)S(1)}, bf16[1024,128]{1,0:T(8,128)(2,1)S(1)}, u32[]{:S(2)}, u32[]{:S(2)}) collective-permute-start(bf16[1024,128]{1,0:T(8,128)(2,1)S(1)} %get-tuple-element.84), channel_id=1, source_target_pairs={{0,120},{1,121},{2,122},{3,123},{4,124},{5,125},{6,126},{7,127},{8... | collective-permute-start | bytes 786440 | tf_op jit(solution)/shard_map/ppermute | solution.py:45
  34.3 0.4 collective-permute-start.10
  34.7 0.6 %collective-permute-start.11 = (bf16[1536,128]{1,0:T(8,128)(2,1)S(1)}, bf16[1536,128]{1,0:T(8,128)(2,1)S(1)}, u32[]{:S(2)}, u32[]{:S(2)}) collective-permute-start(bf16[1536,128]{1,0:T(8,128)(2,1)S(1)} %get-tuple-element.89), channel_id=1, source_target_pairs={{0,1},{1,0},{2,3},{3,2},{4,5},{5,4},{6,7},{7,6},{8,9},{9,8},{10,11... | collective-permute-start | bytes 1179656 | tf_op jit(solution)/shard_map/ppermute | solution.py:45
  35.3 3.2 %settled_2.1 = (bf16[73,256,128]{2,1,0:T(8,128)(2,1)S(1)}, f32[16,256,128]{2,1,0:T(8,128)S(1)}, bf16[16,1152,128]{2,1,0:T(8,128)(2,1)S(1)}, bf16[16,256,128]{2,1,0:T(8,128)(2,1)S(1)}, s32[238]{0:T(256)S(1)}) custom-call(s32[4,4,8]{2,1,0:T(4,128)S(1)} %get-tuple-element.56.codes, ...), custom_call_target="tpu_custom_call", output_to_operand_aliasing={{0}: (2, {}), {1}: (3, {}), {2}: (4, {}), {3}: (5, {})} | custom-call | flops 603979776 | bytes 4194304 | tf_op jit(solution)/shard_map/settled_2/pallas_call | solution.py:531
  38.5 2.6 %collective-permute-done.8.halo = bf16[1024,128]{1,0:T(8,128)(2,1)S(1)} collective-permute-done((bf16[1024,128]{1,0:T(8,128)(2,1)S(1)}, bf16[1024,128]{1,0:T(8,128)(2,1)S(1)}, u32[]{:S(2)}, u32[]{:S(2)}) %collective-permute-start.8) | collective-permute-done | bytes 262176 | tf_op jit(solution)/shard_map/ppermute | solution.py:45
  41.2 1.4 %collective-permute-done.10.ty_out = bf16[1536,128]{1,0:T(8,128)(2,1)S(1)} collective-permute-done((bf16[1536,128]{1,0:T(8,128)(2,1)S(1)}, bf16[1536,128]{1,0:T(8,128)(2,1)S(1)}, u32[]{:S(2)}, u32[]{:S(2)}) %collective-permute-start.10) | collective-permute-done | bytes 393248 | tf_op jit(solution)/shard_map/ppermute | solution.py:45
  42.7 0.7 %level_2.1 = (bf16[73,256,128]{2,1,0:T(8,128)(2,1)S(1)}, f32[16,256,128]{2,1,0:T(8,128)S(1)}, bf16[1024,128]{1,0:T(8,128)(2,1)S(1)}, bf16[1024,128]{1,0:T(8,128)...) custom-call(s32[238]{0:T(256)S(1)} %get-tuple-element.82.table_in, ...), custom_call_target="tpu_custom_call", output_to_operand_aliasing={{0}: (1, {}), {1}: (2, {})} | custom-call | flops 134217728 | bytes 4194304 | tf_op jit(solution)/shard_map/level_2/pallas_call | solution.py:558
  43.4 1.9 %collective-permute-start.12 = (bf16[1024,128]{1,0:T(8,128)(2,1)S(1)}, bf16[1024,128]{1,0:T(8,128)(2,1)S(1)}, u32[]{:S(2)}, u32[]{:S(2)}) collective-permute-start(bf16[1024,128]{1,0:T(8,128)(2,1)S(1)} %get-tuple-element.95), channel_id=1, source_target_pairs={{0,120},{1,121},{2,122},{3,123},{4,124},{5,125},{6,126},{7,127},{8... | collective-permute-start | bytes 786440 | tf_op jit(solution)/shard_map/ppermute | solution.py:45
  45.3 0.9 %collective-permute-start.13 = (bf16[1024,128]{1,0:T(8,128)(2,1)S(1)}, bf16[1024,128]{1,0:T(8,128)(2,1)S(1)}, u32[]{:S(2)}, u32[]{:S(2)}) collective-permute-start(bf16[1024,128]{1,0:T(8,128)(2,1)S(1)} %get-tuple-element.96), channel_id=1, source_target_pairs={{0,8},{1,9},{2,10},{3,11},{4,12},{5,13},{6,14},{7,15},{8,0},{9,1},... | collective-permute-start | bytes 786440 | tf_op jit(solution)/shard_map/ppermute | solution.py:45
  46.2 1.2 %collective-permute-start.14 = (bf16[1536,128]{1,0:T(8,128)(2,1)S(1)}, bf16[1536,128]{1,0:T(8,128)(2,1)S(1)}, u32[]{:S(2)}, u32[]{:S(2)}) collective-permute-start(bf16[1536,128]{1,0:T(8,128)(2,1)S(1)} %get-tuple-element.99), channel_id=1, source_target_pairs={{0,7},{1,2},{2,1},{3,4},{4,3},{5,6},{6,5},{7,0},{8,15},{9,10},{10,... | collective-permute-start | bytes 1179656 | tf_op jit(solution)/shard_map/ppermute | solution.py:45
  47.4 3.3 %settled_3.1 = (bf16[73,256,128]{2,1,0:T(8,128)(2,1)S(1)}, f32[16,256,128]{2,1,0:T(8,128)S(1)}, bf16[16,1152,128]{2,1,0:T(8,128)(2,1)S(1)}, bf16[16,256,128]{2,1,0:T(8,128)(2,1)S(1)}, s32[238]{0:T(256)S(1)}) custom-call(s32[4,4,8]{2,1,0:T(4,128)S(1)} %get-tuple-element.56.codes, ...), custom_call_target="tpu_custom_call", output_to_operand_aliasing={{0}: (2, {}), {1}: (3, {}), {2}: (4, {}), {3}: (5, {})} | custom-call | flops 603979776 | bytes 4194304 | tf_op jit(solution)/shard_map/settled_3/pallas_call | solution.py:531
  50.7 3.0 %collective-permute-done.12.halo = bf16[1024,128]{1,0:T(8,128)(2,1)S(1)} collective-permute-done((bf16[1024,128]{1,0:T(8,128)(2,1)S(1)}, bf16[1024,128]{1,0:T(8,128)(2,1)S(1)}, u32[]{:S(2)}, u32[]{:S(2)}) %collective-permute-start.12) | collective-permute-done | bytes 262176 | tf_op jit(solution)/shard_map/ppermute | solution.py:45
  53.9 2.2 %collective-permute-start.16 = (bf16[512,128]{1,0:T(8,128)(2,1)S(1)}, bf16[512,128]{1,0:T(8,128)(2,1)S(1)}, u32[]{:S(2)}, u32[]{:S(2)}) collective-permute-start(bf16[512,128]{1,0:T(8,128)(2,1)S(1)} %get-tuple-element.103), channel_id=1, source_target_pairs={{0,7},{1,2},{2,1},{3,4},{4,3},{5,6},{6,5},{7,0},{8,15},{9,10},{10,... | collective-permute-start | bytes 393224 | tf_op jit(solution)/shard_map/ppermute | solution.py:45
  56.0 0.4 collective-permute-start.17
  56.5 2.1 %level_3.1 = (bf16[73,256,128]{2,1,0:T(8,128)(2,1)S(1)}, f32[16,256,128]{2,1,0:T(8,128)S(1)}, bf16[16,256,128]{2,1,0:T(8,128)(2,1)}) custom-call(s32[238]{0:T(256)S(1)} %get-tuple-element.93.table_in, bf16[73,256,128]{2,1,0:T(8,128)(2,1)S(1)} %rows_3_in.1.plane_in.plane, ...), custom_call_target="tpu_custom_call", output_to_operand_aliasing={{0}: (1, {}), {1}: (2, {})} | custom-call | flops 134217728 | bytes 4194304 | tf_op jit(solution)/shard_map/level_3/pallas_call | solution.py:558
  58.7 0.9 %collective-permute-done.16.far = bf16[512,128]{1,0:T(8,128)(2,1)S(1)} collective-permute-done((bf16[512,128]{1,0:T(8,128)(2,1)S(1)}, bf16[512,128]{1,0:T(8,128)(2,1)S(1)}, u32[]{:S(2)}, u32[]{:S(2)}) %collective-permute-start.16) | collective-permute-done | bytes 131104 | tf_op jit(solution)/shard_map/ppermute | solution.py:45
  59.6 0.2 last_corners.1
  (23 shorter events, 0.4 us)
Async XLA Ops:
  1.2 12.7 %collective-permute-start = (bf16[1024,128]{1,0:T(8,128)(2,1)S(1)}, bf16[1024,128]{1,0:T(8,128)(2,1)S(1)}, u32[]{:S(2)}, u32[]{:S(2)}) collective-permute-start(bf16[1024,128]{1,0:T(8,128)(2,1)S(1)} %bitcast.12), channel_id=1, source_target_pairs={{0,120},{1,121},{2,122},{3,123},{4,124},{5,125},{6,126},{7,127},{8... | collective-permute-start | bytes 786440 | tf_op jit(solution)/shard_map/ppermute | solution.py:45
  6.6 7.8 %collective-permute-start.1 = (bf16[1024,128]{1,0:T(8,128)(2,1)S(1)}, bf16[1024,128]{1,0:T(8,128)(2,1)S(1)}, u32[]{:S(2)}, u32[]{:S(2)}) collective-permute-start(bf16[1024,128]{1,0:T(8,128)(2,1)S(1)} %bitcast.11), channel_id=1, source_target_pairs={{0,8},{1,9},{2,10},{3,11},{4,12},{5,13},{6,14},{7,15},{8,0},{9,1},... | collective-permute-start | bytes 786440 | tf_op jit(solution)/shard_map/ppermute | solution.py:45
  6.6 7.8 %collective-permute-start.2 = (bf16[1024,128]{1,0:T(8,128)(2,1)S(1)}, bf16[1024,128]{1,0:T(8,128)(2,1)S(1)}, u32[]{:S(2)}, u32[]{:S(2)}) collective-permute-start(bf16[1024,128]{1,0:T(8,128)(2,1)S(1)} %bitcast.10), channel_id=1, source_target_pairs={{0,7},{1,2},{2,1},{3,4},{4,3},{5,6},{6,5},{7,0},{8,15},{9,10},{10,... | collective-permute-start | bytes 786440 | tf_op jit(solution)/shard_map/ppermute | solution.py:45
  9.8 4.6 %collective-permute-start.3 = (bf16[1024,128]{1,0:T(8,128)(2,1)S(1)}, bf16[1024,128]{1,0:T(8,128)(2,1)S(1)}, u32[]{:S(2)}, u32[]{:S(2)}) collective-permute-start(bf16[1024,128]{1,0:T(8,128)(2,1)S(1)} %bitcast.9), channel_id=1, source_target_pairs={{0,1},{1,0},{2,3},{3,2},{4,5},{5,4},{6,7},{7,6},{8,9},{9,8},{10,11... | collective-permute-start | bytes 786440 | tf_op jit(solution)/shard_map/ppermute | solution.py:45
  16.8 11.7 %collective-permute-start.4 = (bf16[1312,128]{1,0:T(8,128)(2,1)S(1)}, bf16[1312,128]{1,0:T(8,128)(2,1)S(1)}, u32[]{:S(2)}, u32[]{:S(2)}) collective-permute-start(bf16[1312,128]{1,0:T(8,128)(2,1)S(1)} %get-tuple-element.73), channel_id=1, source_target_pairs={{0,120},{1,121},{2,122},{3,123},{4,124},{5,125},{6,126},{7,127},{8... | collective-permute-start | bytes 1007624 | tf_op jit(solution)/shard_map/ppermute | solution.py:45
  19.7 9.3 %collective-permute-start.5 = (bf16[1312,128]{1,0:T(8,128)(2,1)S(1)}, bf16[1312,128]{1,0:T(8,128)(2,1)S(1)}, u32[]{:S(2)}, u32[]{:S(2)}) collective-permute-start(bf16[1312,128]{1,0:T(8,128)(2,1)S(1)} %get-tuple-element.74), channel_id=1, source_target_pairs={{0,8},{1,9},{2,10},{3,11},{4,12},{5,13},{6,14},{7,15},{8,0},{9,1},... | collective-permute-start | bytes 1007624 | tf_op jit(solution)/shard_map/ppermute | solution.py:45
  19.7 9.3 %collective-permute-start.6 = (bf16[1824,128]{1,0:T(8,128)(2,1)S(1)}, bf16[1824,128]{1,0:T(8,128)(2,1)S(1)}, u32[]{:S(2)}, u32[]{:S(2)}) collective-permute-start(bf16[1824,128]{1,0:T(8,128)(2,1)S(1)} %get-tuple-element.77), channel_id=1, source_target_pairs={{0,7},{1,2},{2,1},{3,4},{4,3},{5,6},{6,5},{7,0},{8,15},{9,10},{10,... | collective-permute-start | bytes 1400840 | tf_op jit(solution)/shard_map/ppermute | solution.py:45
  22.0 7.0 %collective-permute-start.7 = (bf16[1824,128]{1,0:T(8,128)(2,1)S(1)}, bf16[1824,128]{1,0:T(8,128)(2,1)S(1)}, u32[]{:S(2)}, u32[]{:S(2)}) collective-permute-start(bf16[1824,128]{1,0:T(8,128)(2,1)S(1)} %get-tuple-element.78), channel_id=1, source_target_pairs={{0,1},{1,0},{2,3},{3,2},{4,5},{5,4},{6,7},{7,6},{8,9},{9,8},{10,11... | collective-permute-start | bytes 1400840 | tf_op jit(solution)/shard_map/ppermute | solution.py:45
  30.2 10.9 %collective-permute-start.8 = (bf16[1024,128]{1,0:T(8,128)(2,1)S(1)}, bf16[1024,128]{1,0:T(8,128)(2,1)S(1)}, u32[]{:S(2)}, u32[]{:S(2)}) collective-permute-start(bf16[1024,128]{1,0:T(8,128)(2,1)S(1)} %get-tuple-element.84), channel_id=1, source_target_pairs={{0,120},{1,121},{2,122},{3,123},{4,124},{5,125},{6,126},{7,127},{8... | collective-permute-start | bytes 786440 | tf_op jit(solution)/shard_map/ppermute | solution.py:45
  34.3 6.9 %collective-permute-start.9 = (bf16[1024,128]{1,0:T(8,128)(2,1)S(1)}, bf16[1024,128]{1,0:T(8,128)(2,1)S(1)}, u32[]{:S(2)}, u32[]{:S(2)}) collective-permute-start(bf16[1024,128]{1,0:T(8,128)(2,1)S(1)} %get-tuple-element.85), channel_id=1, source_target_pairs={{0,8},{1,9},{2,10},{3,11},{4,12},{5,13},{6,14},{7,15},{8,0},{9,1},... | collective-permute-start | bytes 786440 | tf_op jit(solution)/shard_map/ppermute | solution.py:45
  34.3 8.4 %collective-permute-start.10 = (bf16[1536,128]{1,0:T(8,128)(2,1)S(1)}, bf16[1536,128]{1,0:T(8,128)(2,1)S(1)}, u32[]{:S(2)}, u32[]{:S(2)}) collective-permute-start(bf16[1536,128]{1,0:T(8,128)(2,1)S(1)} %get-tuple-element.88), channel_id=1, source_target_pairs={{0,7},{1,2},{2,1},{3,4},{4,3},{5,6},{6,5},{7,0},{8,15},{9,10},{10,... | collective-permute-start | bytes 1179656 | tf_op jit(solution)/shard_map/ppermute | solution.py:45
  34.7 8.0 %collective-permute-start.11 = (bf16[1536,128]{1,0:T(8,128)(2,1)S(1)}, bf16[1536,128]{1,0:T(8,128)(2,1)S(1)}, u32[]{:S(2)}, u32[]{:S(2)}) collective-permute-start(bf16[1536,128]{1,0:T(8,128)(2,1)S(1)} %get-tuple-element.89), channel_id=1, source_target_pairs={{0,1},{1,0},{2,3},{3,2},{4,5},{5,4},{6,7},{7,6},{8,9},{9,8},{10,11... | collective-permute-start | bytes 1179656 | tf_op jit(solution)/shard_map/ppermute | solution.py:45
  43.4 10.3 %collective-permute-start.12 = (bf16[1024,128]{1,0:T(8,128)(2,1)S(1)}, bf16[1024,128]{1,0:T(8,128)(2,1)S(1)}, u32[]{:S(2)}, u32[]{:S(2)}) collective-permute-start(bf16[1024,128]{1,0:T(8,128)(2,1)S(1)} %get-tuple-element.95), channel_id=1, source_target_pairs={{0,120},{1,121},{2,122},{3,123},{4,124},{5,125},{6,126},{7,127},{8... | collective-permute-start | bytes 786440 | tf_op jit(solution)/shard_map/ppermute | solution.py:45
  45.3 8.5 %collective-permute-start.13 = (bf16[1024,128]{1,0:T(8,128)(2,1)S(1)}, bf16[1024,128]{1,0:T(8,128)(2,1)S(1)}, u32[]{:S(2)}, u32[]{:S(2)}) collective-permute-start(bf16[1024,128]{1,0:T(8,128)(2,1)S(1)} %get-tuple-element.96), channel_id=1, source_target_pairs={{0,8},{1,9},{2,10},{3,11},{4,12},{5,13},{6,14},{7,15},{8,0},{9,1},... | collective-permute-start | bytes 786440 | tf_op jit(solution)/shard_map/ppermute | solution.py:45
  46.2 10.3 %collective-permute-start.14 = (bf16[1536,128]{1,0:T(8,128)(2,1)S(1)}, bf16[1536,128]{1,0:T(8,128)(2,1)S(1)}, u32[]{:S(2)}, u32[]{:S(2)}) collective-permute-start(bf16[1536,128]{1,0:T(8,128)(2,1)S(1)} %get-tuple-element.99), channel_id=1, source_target_pairs={{0,7},{1,2},{2,1},{3,4},{4,3},{5,6},{6,5},{7,0},{8,15},{9,10},{10,... | collective-permute-start | bytes 1179656 | tf_op jit(solution)/shard_map/ppermute | solution.py:45
  47.4 9.1 %collective-permute-start.15 = (bf16[1536,128]{1,0:T(8,128)(2,1)S(1)}, bf16[1536,128]{1,0:T(8,128)(2,1)S(1)}, u32[]{:S(2)}, u32[]{:S(2)}) collective-permute-start(bf16[1536,128]{1,0:T(8,128)(2,1)S(1)} %get-tuple-element.100), channel_id=1, source_target_pairs={{0,1},{1,0},{2,3},{3,2},{4,5},{5,4},{6,7},{7,6},{8,9},{9,8},{10,11... | collective-permute-start | bytes 1179656 | tf_op jit(solution)/shard_map/ppermute | solution.py:45
  53.9 5.7 %collective-permute-start.16 = (bf16[512,128]{1,0:T(8,128)(2,1)S(1)}, bf16[512,128]{1,0:T(8,128)(2,1)S(1)}, u32[]{:S(2)}, u32[]{:S(2)}) collective-permute-start(bf16[512,128]{1,0:T(8,128)(2,1)S(1)} %get-tuple-element.103), channel_id=1, source_target_pairs={{0,7},{1,2},{2,1},{3,4},{4,3},{5,6},{6,5},{7,0},{8,15},{9,10},{10,... | collective-permute-start | bytes 393224 | tf_op jit(solution)/shard_map/ppermute | solution.py:45
  56.0 3.5 %collective-permute-start.17 = (bf16[512,128]{1,0:T(8,128)(2,1)S(1)}, bf16[512,128]{1,0:T(8,128)(2,1)S(1)}, u32[]{:S(2)}, u32[]{:S(2)}) collective-permute-start(bf16[512,128]{1,0:T(8,128)(2,1)S(1)} %get-tuple-element.104), channel_id=1, source_target_pairs={{0,1},{1,0},{2,3},{3,2},{4,5},{5,4},{6,7},{7,6},{8,9},{9,8},{10,11... | collective-permute-start | bytes 393224 | tf_op jit(solution)/shard_map/ppermute | solution.py:45

commit v9 on v7

--- a/solution.py
+++ b/solution.py
@@ -367,14 +367,17 @@
         ref[ref.shape[0] - EXTRA :] = extras[at]
     wait()
 
-    def products(first, second, fresh):
-        cells = first, second
-        both = [gather_product(cell, table, SLOT, plane, matrices, noise) for cell in cells]
-        for cell, summed in zip(cells, both, strict=True):
+    count = table[CHOSEN]
+
+    def one_group(group, carry):
+        cells = [table[CELLS + jnp.minimum(GROUP * group + i, count - 1)] for i in range(GROUP)]
+        products = [gather_product(cell, table, SLOT, plane, matrices, noise) for cell in cells]
+        for cell, summed in zip(cells, products, strict=True):
             sums[cell] = summed
             plane[own_slot(cell // SIDE, cell % SIDE)] = summed.astype(jnp.bfloat16)
-
-    each_pair(table, products)
+        return carry
+
+    lax.fori_loop(0, (count + GROUP - 1) // GROUP, one_group, 0)
     pack_sends(0, plane, sends)
 
 

time: 62.7 us -> 61.3 us (0.978)
  the two profiles are of different devices: /device:TPU:1 before, /device:TPU:0 now
where the time goes in v9:
time: 61.3 us; the launch traced here: 60.1 us
  starting transfers between devices  25.2 us (41%)
  Pallas kernels  24.8 us (40%)
  waiting for transfers between devices  9.96 us (16%)
    ppermute x18, starting transfers between devices, swap(): return lax.ppermute(value, BOTH, pairs)  25.2 us
    pallas_call x3, Pallas kernels, local(): pl.pallas_call(functools.partial(settled_kernel, section), out_shape=[pla...  13.2 us
    ppermute x18, waiting for transfers between devices, swap(): return lax.ppermute(value, BOTH, pairs)  9.96 us
    pallas_call x3, Pallas kernels, local(): pl.pallas_call(functools.partial(main_kernel, section), out_shape=[plane_...  4.98 us
    pallas_call x1, Pallas kernels, local(): pl.pallas_call(load_kernel, out_shape=[plane_shape, matrices_shape, whole...  3.32 us
    pallas_call x1, Pallas kernels, local(): pl.pallas_call(first_kernel, out_shape=[plane_shape, sums_shape, matrices...  1.49 us
  transfers between devices with their start and end apart: 18, of which 7 were waited for; matrix products, arithmetic and copies ran while one was open for 0% of the time, Pallas kernels for 33%

profile of v9, /device:TPU:0, one launch (start us, length us, event | category | flops | bytes accessed | tf_op | source)
XLA Modules:
  0.0 60.1 jit_solution(10309576697751752806)
XLA Ops:
  0.0 1.2 %pack.1 = (bf16[4,256,128]{2,1,0:T(8,128)(2,1)S(1)}, bf16[4,256,128]{2,1,0:T(8,128)(2,1)S(1)}, bf16[4,256,128]{2,1,0:T(8,128)(2,1)S(1)}, bf16[4,256,128]{2,1,0:T(8,128)(2,1)S(1)}) custom-call(bf16[4,4,256,128]{3,2,1,0:T(8,128)(2,1)} %earlier.1), custom_call_target="tpu_custom_call" | custom-call | tf_op jit(solution)/shard_map/pack/pallas_call | solution.py:465
  1.2 5.4 %collective-permute-start = (bf16[1024,128]{1,0:T(8,128)(2,1)S(1)}, bf16[1024,128]{1,0:T(8,128)(2,1)S(1)}, u32[]{:S(2)}, u32[]{:S(2)}) collective-permute-start(bf16[1024,128]{1,0:T(8,128)(2,1)S(1)} %bitcast.12), channel_id=1, source_target_pairs={{0,120},{1,121},{2,122},{3,123},{4,124},{5,125},{6,126},{7,127},{8... | collective-permute-start | bytes 786440 | tf_op jit(solution)/shard_map/ppermute | solution.py:45
  6.6 0.0 collective-permute-start.1
  6.6 3.2 %collective-permute-start.2 = (bf16[1024,128]{1,0:T(8,128)(2,1)S(1)}, bf16[1024,128]{1,0:T(8,128)(2,1)S(1)}, u32[]{:S(2)}, u32[]{:S(2)}) collective-permute-start(bf16[1024,128]{1,0:T(8,128)(2,1)S(1)} %bitcast.10), channel_id=1, source_target_pairs={{0,7},{1,2},{2,1},{3,4},{4,3},{5,6},{6,5},{7,0},{8,15},{9,10},{10,... | collective-permute-start | bytes 786440 | tf_op jit(solution)/shard_map/ppermute | solution.py:45
  9.8 3.3 %load.1 = (bf16[73,256,128]{2,1,0:T(8,128)(2,1)S(1)}, bf16[16,1152,128]{2,1,0:T(8,128)(2,1)S(1)}, bf16[16,256,128]{2,1,0:T(8,128)(2,1)S(1)}, f32[16,256,128]{2,1...) custom-call(s32[4,4]{1,0:T(4,128)} %block_level.1, ...), custom_call_target="tpu_custom_call" | custom-call | bytes 10485760 | tf_op jit(solution)/shard_map/load/pallas_call | solution.py:476
  13.2 1.2 %collective-permute-done.1.halo = bf16[1024,128]{1,0:T(8,128)(2,1)S(1)} collective-permute-done((bf16[1024,128]{1,0:T(8,128)(2,1)S(1)}, bf16[1024,128]{1,0:T(8,128)(2,1)S(1)}, u32[]{:S(2)}, u32[]{:S(2)}) %collective-permute-start.1) | collective-permute-done | bytes 262176 | tf_op jit(solution)/shard_map/ppermute | solution.py:45
  14.4 0.0 collective-permute-done.3.rest_1_
  14.4 1.5 %level_0.1 = (bf16[73,256,128]{2,1,0:T(8,128)(2,1)S(1)}, f32[16,256,128]{2,1,0:T(8,128)S(1)}, bf16[16,1152,128]{2,1,0:T(8,128)(2,1)S(1)}, bf16[16,256,128]{2,1,0...) custom-call(s32[238]{0:T(256)S(1)} %get-tuple-element.57.table_in, ...), custom_call_target="tpu_custom_call", output_to_operand_aliasing={{0}: (1, {}), {1}: (2, {}), {2}: (3, {}), {3}: (4, {})} | custom-call | flops 603979776 | bytes 4194304 | tf_op jit(solution)/shard_map/level_0/pallas_call | solution.py:502
  15.9 3.7 %collective-permute-start.4 = (bf16[1312,128]{1,0:T(8,128)(2,1)S(1)}, bf16[1312,128]{1,0:T(8,128)(2,1)S(1)}, u32[]{:S(2)}, u32[]{:S(2)}) collective-permute-start(bf16[1312,128]{1,0:T(8,128)(2,1)S(1)} %get-tuple-element.73), channel_id=1, source_target_pairs={{0,120},{1,121},{2,122},{3,123},{4,124},{5,125},{6,126},{7,127},{8... | collective-permute-start | bytes 1007624 | tf_op jit(solution)/shard_map/ppermute | solution.py:45
  19.7 0.0 collective-permute-start.5
  19.7 2.3 %collective-permute-start.6 = (bf16[1824,128]{1,0:T(8,128)(2,1)S(1)}, bf16[1824,128]{1,0:T(8,128)(2,1)S(1)}, u32[]{:S(2)}, u32[]{:S(2)}) collective-permute-start(bf16[1824,128]{1,0:T(8,128)(2,1)S(1)} %get-tuple-element.77), channel_id=1, source_target_pairs={{0,7},{1,2},{2,1},{3,4},{4,3},{5,6},{6,5},{7,0},{8,15},{9,10},{10,... | collective-permute-start | bytes 1400840 | tf_op jit(solution)/shard_map/ppermute | solution.py:45
  22.0 0.0 collective-permute-start.7
  22.0 3.9 %settled_1.1 = (bf16[73,256,128]{2,1,0:T(8,128)(2,1)S(1)}, f32[16,256,128]{2,1,0:T(8,128)S(1)}, bf16[16,1152,128]{2,1,0:T(8,128)(2,1)S(1)}, bf16[16,256,128]{2,1,0:T(8,128)(2,1)S(1)}, s32[238]{0:T(256)S(1)}) custom-call(s32[4,4,8]{2,1,0:T(4,128)S(1)} %get-tuple-element.56.codes, ...), custom_call_target="tpu_custom_call", output_to_operand_aliasing={{0}: (2, {}), {1}: (3, {}), {2}: (4, {}), {3}: (5, {})} | custom-call | flops 603979776 | bytes 4194304 | tf_op jit(solution)/shard_map/settled_1/pallas_call | solution.py:518
  25.9 2.9 %collective-permute-done.4.halo.rest_0_ = bf16[1312,128]{1,0:T(8,128)(2,1)S(1)} collective-permute-done((bf16[1312,128]{1,0:T(8,128)(2,1)S(1)}, bf16[1312,128]{1,0:T(8,128)(2,1)S(1)}, u32[]{:S(2)}, u32[]{:S(2)}) %collective-permute-start.4) | collective-permute-done | bytes 335904 | tf_op jit(solution)/shard_map/ppermute | solution.py:45
  28.8 0.1 collective-permute-done.5.halo.rest_1_
  29.0 0.0 collective-permute-done.7.ty_in.rest_3_
  29.0 1.0 %level_1.1 = (bf16[73,256,128]{2,1,0:T(8,128)(2,1)S(1)}, f32[16,256,128]{2,1,0:T(8,128)S(1)}, bf16[1024,128]{1,0:T(8,128)(2,1)S(1)}, bf16[1024,128]{1,0:T(8,128)...) custom-call(s32[238]{0:T(256)S(1)} %get-tuple-element.71.table_in, ...), custom_call_target="tpu_custom_call", output_to_operand_aliasing={{0}: (1, {}), {1}: (2, {})} | custom-call | flops 134217728 | bytes 4194304 | tf_op jit(solution)/shard_map/level_1/pallas_call | solution.py:545
  30.1 3.9 %collective-permute-start.8 = (bf16[1024,128]{1,0:T(8,128)(2,1)S(1)}, bf16[1024,128]{1,0:T(8,128)(2,1)S(1)}, u32[]{:S(2)}, u32[]{:S(2)}) collective-permute-start(bf16[1024,128]{1,0:T(8,128)(2,1)S(1)} %get-tuple-element.84), channel_id=1, source_target_pairs={{0,120},{1,121},{2,122},{3,123},{4,124},{5,125},{6,126},{7,127},{8... | collective-permute-start | bytes 786440 | tf_op jit(solution)/shard_map/ppermute | solution.py:45
  33.9 0.8 %collective-permute-start.10 = (bf16[1536,128]{1,0:T(8,128)(2,1)S(1)}, bf16[1536,128]{1,0:T(8,128)(2,1)S(1)}, u32[]{:S(2)}, u32[]{:S(2)}) collective-permute-start(bf16[1536,128]{1,0:T(8,128)(2,1)S(1)} %get-tuple-element.88), channel_id=1, source_target_pairs={{0,7},{1,2},{2,1},{3,4},{4,3},{5,6},{6,5},{7,0},{8,15},{9,10},{10,... | collective-permute-start | bytes 1179656 | tf_op jit(solution)/shard_map/ppermute | solution.py:45
  34.7 0.4 collective-permute-start.11
  35.2 3.9 %settled_2.1 = (bf16[73,256,128]{2,1,0:T(8,128)(2,1)S(1)}, f32[16,256,128]{2,1,0:T(8,128)S(1)}, bf16[16,1152,128]{2,1,0:T(8,128)(2,1)S(1)}, bf16[16,256,128]{2,1,0:T(8,128)(2,1)S(1)}, s32[238]{0:T(256)S(1)}) custom-call(s32[4,4,8]{2,1,0:T(4,128)S(1)} %get-tuple-element.56.codes, ...), custom_call_target="tpu_custom_call", output_to_operand_aliasing={{0}: (2, {}), {1}: (3, {}), {2}: (4, {}), {3}: (5, {})} | custom-call | flops 603979776 | bytes 4194304 | tf_op jit(solution)/shard_map/settled_2/pallas_call | solution.py:518
  39.1 1.9 %collective-permute-done.8.halo = bf16[1024,128]{1,0:T(8,128)(2,1)S(1)} collective-permute-done((bf16[1024,128]{1,0:T(8,128)(2,1)S(1)}, bf16[1024,128]{1,0:T(8,128)(2,1)S(1)}, u32[]{:S(2)}, u32[]{:S(2)}) %collective-permute-start.8) | collective-permute-done | bytes 262176 | tf_op jit(solution)/shard_map/ppermute | solution.py:45
  41.1 1.2 %collective-permute-done.10.ty_out = bf16[1536,128]{1,0:T(8,128)(2,1)S(1)} collective-permute-done((bf16[1536,128]{1,0:T(8,128)(2,1)S(1)}, bf16[1536,128]{1,0:T(8,128)(2,1)S(1)}, u32[]{:S(2)}, u32[]{:S(2)}) %collective-permute-start.10) | collective-permute-done | bytes 393248 | tf_op jit(solution)/shard_map/ppermute | solution.py:45
  42.3 1.0 %level_2.1 = (bf16[73,256,128]{2,1,0:T(8,128)(2,1)S(1)}, f32[16,256,128]{2,1,0:T(8,128)S(1)}, bf16[1024,128]{1,0:T(8,128)(2,1)S(1)}, bf16[1024,128]{1,0:T(8,128)...) custom-call(s32[238]{0:T(256)S(1)} %get-tuple-element.82.table_in, ...), custom_call_target="tpu_custom_call", output_to_operand_aliasing={{0}: (1, {}), {1}: (2, {})} | custom-call | flops 134217728 | bytes 4194304 | tf_op jit(solution)/shard_map/level_2/pallas_call | solution.py:545
  43.3 2.6 %collective-permute-start.12 = (bf16[1024,128]{1,0:T(8,128)(2,1)S(1)}, bf16[1024,128]{1,0:T(8,128)(2,1)S(1)}, u32[]{:S(2)}, u32[]{:S(2)}) collective-permute-start(bf16[1024,128]{1,0:T(8,128)(2,1)S(1)} %get-tuple-element.95), channel_id=1, source_target_pairs={{0,120},{1,121},{2,122},{3,123},{4,124},{5,125},{6,126},{7,127},{8... | collective-permute-start | bytes 786440 | tf_op jit(solution)/shard_map/ppermute | solution.py:45
  46.0 1.2 %collective-permute-start.14 = (bf16[1536,128]{1,0:T(8,128)(2,1)S(1)}, bf16[1536,128]{1,0:T(8,128)(2,1)S(1)}, u32[]{:S(2)}, u32[]{:S(2)}) collective-permute-start(bf16[1536,128]{1,0:T(8,128)(2,1)S(1)} %get-tuple-element.99), channel_id=1, source_target_pairs={{0,7},{1,2},{2,1},{3,4},{4,3},{5,6},{6,5},{7,0},{8,15},{9,10},{10,... | collective-permute-start | bytes 1179656 | tf_op jit(solution)/shard_map/ppermute | solution.py:45
  47.2 5.4 %settled_3.1 = (bf16[73,256,128]{2,1,0:T(8,128)(2,1)S(1)}, f32[16,256,128]{2,1,0:T(8,128)S(1)}, bf16[16,1152,128]{2,1,0:T(8,128)(2,1)S(1)}, bf16[16,256,128]{2,1,0:T(8,128)(2,1)S(1)}, s32[238]{0:T(256)S(1)}) custom-call(s32[4,4,8]{2,1,0:T(4,128)S(1)} %get-tuple-element.56.codes, ...), custom_call_target="tpu_custom_call", output_to_operand_aliasing={{0}: (2, {}), {1}: (3, {}), {2}: (4, {}), {3}: (5, {})} | custom-call | flops 603979776 | bytes 4194304 | tf_op jit(solution)/shard_map/settled_3/pallas_call | solution.py:518
  52.6 1.5 %collective-permute-done.12.halo = bf16[1024,128]{1,0:T(8,128)(2,1)S(1)} collective-permute-done((bf16[1024,128]{1,0:T(8,128)(2,1)S(1)}, bf16[1024,128]{1,0:T(8,128)(2,1)S(1)}, u32[]{:S(2)}, u32[]{:S(2)}) %collective-permute-start.12) | collective-permute-done | bytes 262176 | tf_op jit(solution)/shard_map/ppermute | solution.py:45
  54.3 1.6 %collective-permute-start.16 = (bf16[512,128]{1,0:T(8,128)(2,1)S(1)}, bf16[512,128]{1,0:T(8,128)(2,1)S(1)}, u32[]{:S(2)}, u32[]{:S(2)}) collective-permute-start(bf16[512,128]{1,0:T(8,128)(2,1)S(1)} %get-tuple-element.103), channel_id=1, source_target_pairs={{0,7},{1,2},{2,1},{3,4},{4,3},{5,6},{6,5},{7,0},{8,15},{9,10},{10,... | collective-permute-start | bytes 393224 | tf_op jit(solution)/shard_map/ppermute | solution.py:45
  55.9 3.0 %level_3.1 = (bf16[73,256,128]{2,1,0:T(8,128)(2,1)S(1)}, f32[16,256,128]{2,1,0:T(8,128)S(1)}, bf16[16,256,128]{2,1,0:T(8,128)(2,1)}) custom-call(s32[238]{0:T(256)S(1)} %get-tuple-element.93.table_in, bf16[73,256,128]{2,1,0:T(8,128)(2,1)S(1)} %rows_3_in.1.plane_in.plane, ...), custom_call_target="tpu_custom_call", output_to_operand_aliasing={{0}: (1, {}), {1}: (2, {})} | custom-call | flops 134217728 | bytes 4194304 | tf_op jit(solution)/shard_map/level_3/pallas_call | solution.py:545
  58.8 1.1 %collective-permute-done.16.far = bf16[512,128]{1,0:T(8,128)(2,1)S(1)} collective-permute-done((bf16[512,128]{1,0:T(8,128)(2,1)S(1)}, bf16[512,128]{1,0:T(8,128)(2,1)S(1)}, u32[]{:S(2)}, u32[]{:S(2)}) %collective-permute-start.16) | collective-permute-done | bytes 131104 | tf_op jit(solution)/shard_map/ppermute | solution.py:45
  60.0 0.2 last_corners.1
  (23 shorter events, 0.4 us)
Async XLA Ops:
  1.2 11.9 %collective-permute-start = (bf16[1024,128]{1,0:T(8,128)(2,1)S(1)}, bf16[1024,128]{1,0:T(8,128)(2,1)S(1)}, u32[]{:S(2)}, u32[]{:S(2)}) collective-permute-start(bf16[1024,128]{1,0:T(8,128)(2,1)S(1)} %bitcast.12), channel_id=1, source_target_pairs={{0,120},{1,121},{2,122},{3,123},{4,124},{5,125},{6,126},{7,127},{8... | collective-permute-start | bytes 786440 | tf_op jit(solution)/shard_map/ppermute | solution.py:45
  6.6 7.8 %collective-permute-start.1 = (bf16[1024,128]{1,0:T(8,128)(2,1)S(1)}, bf16[1024,128]{1,0:T(8,128)(2,1)S(1)}, u32[]{:S(2)}, u32[]{:S(2)}) collective-permute-start(bf16[1024,128]{1,0:T(8,128)(2,1)S(1)} %bitcast.11), channel_id=1, source_target_pairs={{0,8},{1,9},{2,10},{3,11},{4,12},{5,13},{6,14},{7,15},{8,0},{9,1},... | collective-permute-start | bytes 786440 | tf_op jit(solution)/shard_map/ppermute | solution.py:45
  6.6 7.8 %collective-permute-start.2 = (bf16[1024,128]{1,0:T(8,128)(2,1)S(1)}, bf16[1024,128]{1,0:T(8,128)(2,1)S(1)}, u32[]{:S(2)}, u32[]{:S(2)}) collective-permute-start(bf16[1024,128]{1,0:T(8,128)(2,1)S(1)} %bitcast.10), channel_id=1, source_target_pairs={{0,7},{1,2},{2,1},{3,4},{4,3},{5,6},{6,5},{7,0},{8,15},{9,10},{10,... | collective-permute-start | bytes 786440 | tf_op jit(solution)/shard_map/ppermute | solution.py:45
  9.8 4.6 %collective-permute-start.3 = (bf16[1024,128]{1,0:T(8,128)(2,1)S(1)}, bf16[1024,128]{1,0:T(8,128)(2,1)S(1)}, u32[]{:S(2)}, u32[]{:S(2)}) collective-permute-start(bf16[1024,128]{1,0:T(8,128)(2,1)S(1)} %bitcast.9), channel_id=1, source_target_pairs={{0,1},{1,0},{2,3},{3,2},{4,5},{5,4},{6,7},{7,6},{8,9},{9,8},{10,11... | collective-permute-start | bytes 786440 | tf_op jit(solution)/shard_map/ppermute | solution.py:45
  15.9 12.9 %collective-permute-start.4 = (bf16[1312,128]{1,0:T(8,128)(2,1)S(1)}, bf16[1312,128]{1,0:T(8,128)(2,1)S(1)}, u32[]{:S(2)}, u32[]{:S(2)}) collective-permute-start(bf16[1312,128]{1,0:T(8,128)(2,1)S(1)} %get-tuple-element.73), channel_id=1, source_target_pairs={{0,120},{1,121},{2,122},{3,123},{4,124},{5,125},{6,126},{7,127},{8... | collective-permute-start | bytes 1007624 | tf_op jit(solution)/shard_map/ppermute | solution.py:45
  19.7 9.3 %collective-permute-start.5 = (bf16[1312,128]{1,0:T(8,128)(2,1)S(1)}, bf16[1312,128]{1,0:T(8,128)(2,1)S(1)}, u32[]{:S(2)}, u32[]{:S(2)}) collective-permute-start(bf16[1312,128]{1,0:T(8,128)(2,1)S(1)} %get-tuple-element.74), channel_id=1, source_target_pairs={{0,8},{1,9},{2,10},{3,11},{4,12},{5,13},{6,14},{7,15},{8,0},{9,1},... | collective-permute-start | bytes 1007624 | tf_op jit(solution)/shard_map/ppermute | solution.py:45
  19.7 9.3 %collective-permute-start.6 = (bf16[1824,128]{1,0:T(8,128)(2,1)S(1)}, bf16[1824,128]{1,0:T(8,128)(2,1)S(1)}, u32[]{:S(2)}, u32[]{:S(2)}) collective-permute-start(bf16[1824,128]{1,0:T(8,128)(2,1)S(1)} %get-tuple-element.77), channel_id=1, source_target_pairs={{0,7},{1,2},{2,1},{3,4},{4,3},{5,6},{6,5},{7,0},{8,15},{9,10},{10,... | collective-permute-start | bytes 1400840 | tf_op jit(solution)/shard_map/ppermute | solution.py:45
  22.0 7.0 %collective-permute-start.7 = (bf16[1824,128]{1,0:T(8,128)(2,1)S(1)}, bf16[1824,128]{1,0:T(8,128)(2,1)S(1)}, u32[]{:S(2)}, u32[]{:S(2)}) collective-permute-start(bf16[1824,128]{1,0:T(8,128)(2,1)S(1)} %get-tuple-element.78), channel_id=1, source_target_pairs={{0,1},{1,0},{2,3},{3,2},{4,5},{5,4},{6,7},{7,6},{8,9},{9,8},{10,11... | collective-permute-start | bytes 1400840 | tf_op jit(solution)/shard_map/ppermute | solution.py:45
  30.1 11.0 %collective-permute-start.8 = (bf16[1024,128]{1,0:T(8,128)(2,1)S(1)}, bf16[1024,128]{1,0:T(8,128)(2,1)S(1)}, u32[]{:S(2)}, u32[]{:S(2)}) collective-permute-start(bf16[1024,128]{1,0:T(8,128)(2,1)S(1)} %get-tuple-element.84), channel_id=1, source_target_pairs={{0,120},{1,121},{2,122},{3,123},{4,124},{5,125},{6,126},{7,127},{8... | collective-permute-start | bytes 786440 | tf_op jit(solution)/shard_map/ppermute | solution.py:45
  33.9 7.1 %collective-permute-start.9 = (bf16[1024,128]{1,0:T(8,128)(2,1)S(1)}, bf16[1024,128]{1,0:T(8,128)(2,1)S(1)}, u32[]{:S(2)}, u32[]{:S(2)}) collective-permute-start(bf16[1024,128]{1,0:T(8,128)(2,1)S(1)} %get-tuple-element.85), channel_id=1, source_target_pairs={{0,8},{1,9},{2,10},{3,11},{4,12},{5,13},{6,14},{7,15},{8,0},{9,1},... | collective-permute-start | bytes 786440 | tf_op jit(solution)/shard_map/ppermute | solution.py:45
  33.9 8.4 %collective-permute-start.10 = (bf16[1536,128]{1,0:T(8,128)(2,1)S(1)}, bf16[1536,128]{1,0:T(8,128)(2,1)S(1)}, u32[]{:S(2)}, u32[]{:S(2)}) collective-permute-start(bf16[1536,128]{1,0:T(8,128)(2,1)S(1)} %get-tuple-element.88), channel_id=1, source_target_pairs={{0,7},{1,2},{2,1},{3,4},{4,3},{5,6},{6,5},{7,0},{8,15},{9,10},{10,... | collective-permute-start | bytes 1179656 | tf_op jit(solution)/shard_map/ppermute | solution.py:45
  34.7 7.6 %collective-permute-start.11 = (bf16[1536,128]{1,0:T(8,128)(2,1)S(1)}, bf16[1536,128]{1,0:T(8,128)(2,1)S(1)}, u32[]{:S(2)}, u32[]{:S(2)}) collective-permute-start(bf16[1536,128]{1,0:T(8,128)(2,1)S(1)} %get-tuple-element.89), channel_id=1, source_target_pairs={{0,1},{1,0},{2,3},{3,2},{4,5},{5,4},{6,7},{7,6},{8,9},{9,8},{10,11... | collective-permute-start | bytes 1179656 | tf_op jit(solution)/shard_map/ppermute | solution.py:45
  43.3 10.8 %collective-permute-start.12 = (bf16[1024,128]{1,0:T(8,128)(2,1)S(1)}, bf16[1024,128]{1,0:T(8,128)(2,1)S(1)}, u32[]{:S(2)}, u32[]{:S(2)}) collective-permute-start(bf16[1024,128]{1,0:T(8,128)(2,1)S(1)} %get-tuple-element.95), channel_id=1, source_target_pairs={{0,120},{1,121},{2,122},{3,123},{4,124},{5,125},{6,126},{7,127},{8... | collective-permute-start | bytes 786440 | tf_op jit(solution)/shard_map/ppermute | solution.py:45
  46.0 8.2 %collective-permute-start.13 = (bf16[1024,128]{1,0:T(8,128)(2,1)S(1)}, bf16[1024,128]{1,0:T(8,128)(2,1)S(1)}, u32[]{:S(2)}, u32[]{:S(2)}) collective-permute-start(bf16[1024,128]{1,0:T(8,128)(2,1)S(1)} %get-tuple-element.96), channel_id=1, source_target_pairs={{0,8},{1,9},{2,10},{3,11},{4,12},{5,13},{6,14},{7,15},{8,0},{9,1},... | collective-permute-start | bytes 786440 | tf_op jit(solution)/shard_map/ppermute | solution.py:45
  46.0 9.9 %collective-permute-start.14 = (bf16[1536,128]{1,0:T(8,128)(2,1)S(1)}, bf16[1536,128]{1,0:T(8,128)(2,1)S(1)}, u32[]{:S(2)}, u32[]{:S(2)}) collective-permute-start(bf16[1536,128]{1,0:T(8,128)(2,1)S(1)} %get-tuple-element.99), channel_id=1, source_target_pairs={{0,7},{1,2},{2,1},{3,4},{4,3},{5,6},{6,5},{7,0},{8,15},{9,10},{10,... | collective-permute-start | bytes 1179656 | tf_op jit(solution)/shard_map/ppermute | solution.py:45
  47.2 8.6 %collective-permute-start.15 = (bf16[1536,128]{1,0:T(8,128)(2,1)S(1)}, bf16[1536,128]{1,0:T(8,128)(2,1)S(1)}, u32[]{:S(2)}, u32[]{:S(2)}) collective-permute-start(bf16[1536,128]{1,0:T(8,128)(2,1)S(1)} %get-tuple-element.100), channel_id=1, source_target_pairs={{0,1},{1,0},{2,3},{3,2},{4,5},{5,4},{6,7},{7,6},{8,9},{9,8},{10,11... | collective-permute-start | bytes 1179656 | tf_op jit(solution)/shard_map/ppermute | solution.py:45
  54.3 5.7 %collective-permute-start.16 = (bf16[512,128]{1,0:T(8,128)(2,1)S(1)}, bf16[512,128]{1,0:T(8,128)(2,1)S(1)}, u32[]{:S(2)}, u32[]{:S(2)}) collective-permute-start(bf16[512,128]{1,0:T(8,128)(2,1)S(1)} %get-tuple-element.103), channel_id=1, source_target_pairs={{0,7},{1,2},{2,1},{3,4},{4,3},{5,6},{6,5},{7,0},{8,15},{9,10},{10,... | collective-permute-start | bytes 393224 | tf_op jit(solution)/shard_map/ppermute | solution.py:45
  55.8 4.1 %collective-permute-start.17 = (bf16[512,128]{1,0:T(8,128)(2,1)S(1)}, bf16[512,128]{1,0:T(8,128)(2,1)S(1)}, u32[]{:S(2)}, u32[]{:S(2)}) collective-permute-start(bf16[512,128]{1,0:T(8,128)(2,1)S(1)} %get-tuple-element.104), channel_id=1, source_target_pairs={{0,1},{1,0},{2,3},{3,2},{4,5},{5,4},{6,7},{7,6},{8,9},{9,8},{10,11... | collective-permute-start | bytes 393224 | tf_op jit(solution)/shard_map/ppermute | solution.py:45
